TPU v7x, 32 devices: a whole 2x2x4 slice. The times are simulated.
32 devices in a mesh: expert: 16 (over z, y, x), tensor: 2 (over core).
Axes of the slice: x: 2, y: 2, z: 4, core: 2. Of those that a mesh axis runs over, the one named last changes fastest.
Arguments:
- batch_one: bfloat16 [2048, 1536], P(('expert', 'tensor')), may hold values from -6 to 6
- batch_two: bfloat16 [2048, 1536], P(('expert', 'tensor')), may hold values from -6 to 6
- norm_gain: bfloat16 [1536], replicated, may hold values from 0.25 to 1.75
- slots_one: int32 [2048, 8], P(('expert', 'tensor')), may hold values from 0 to 15, all different within a row; in each aligned block of 64 rows (0 to 63, 64 to 127, ...) at most 36 rows name the same one
- slots_two: int32 [2048, 8], P(('expert', 'tensor')), may hold values from 0 to 15, all different within a row; in each aligned block of 64 rows (0 to 63, 64 to 127, ...) at most 36 rows name the same one
- gates_one: float32 [2048, 8], P(('expert', 'tensor')), may hold values from 0.2 to 1
- gates_two: float32 [2048, 8], P(('expert', 'tensor')), may hold values from 0.2 to 1
- table_old: int32 [16], replicated, may hold values from 0 to 39, as said below
- table_new: int32 [16], replicated, may hold values from 0 to 39, as said below
- gate_old: bfloat16 [16, 1536, 512], P('expert', 'tensor'), as said below
- up_old: bfloat16 [16, 1536, 512], P('expert', 'tensor'), as said below
- down_old: bfloat16 [16, 512, 1536], P('expert', None, 'tensor'), as said below
Outputs:
- mixed_one: bfloat16 [2048, 1536], P(('expert', 'tensor'))
- mixed_two: bfloat16 [2048, 1536], P(('expert', 'tensor'))
Inputs may be any that keep to these rules, and one draw needn't show every extreme that they name: `slots_one`: the 8 routes of a token name different slots; among the 64 tokens of one device no slot is named by more than 36 routes, a bound that some block reaches. `slots_two`: the 8 routes of a token name different slots; among the 64 tokens of one device no slot is named by more than 36 routes, a bound that some block reaches. `table_old`: when 16 >= 40 every expert is held by at least one slot; several slots may hold the same expert. table_new[s] equals table_old at slot s, s - 1 or s + 1 (modulo 16), and each of the three cases occurs. `gate_old`: slots that hold the same expert under table_old hold equal weights. `up_old`: slots that hold the same expert under table_old hold equal weights. `down_old`: slots that hold the same expert under table_old hold equal weights.
All inputs are finite; a program needn't handle non-finite values.
Results may differ from a plain program's by a relative error of at most 0.0071.
Values may be sent and summed in bfloat16 or wider, within the bound.
No kernel may reach another device: no remote copies, remote signals or barrier semaphores. Data moves between devices by JAX's collectives and lax.ppermute only.
A program may use at most 128 MiB of HBM per device.

v0:
```python
import jax
import jax.numpy as jnp
from jax import lax
from jax.sharding import PartitionSpec as P

EPS = 1e-05


def shifted(block, axis, distance):
    devices = range(lax.axis_size(axis))
    route = [((i - distance) % len(devices), i) for i in devices]
    return lax.ppermute(block, axis, route)


def rms_rows(tokens, norm_gain):
    values = tokens.astype(jnp.float32)
    square = jnp.mean(values * values, axis=-1, keepdims=True)
    return (values * lax.rsqrt(square + EPS) * norm_gain.astype(jnp.float32)).astype(jnp.bfloat16)


def gather_full(shards):
    return (
        lax.all_gather(shards[0], "tensor", axis=0, tiled=True),
        lax.all_gather(shards[1], "tensor", axis=0, tiled=True),
        lax.all_gather(shards[2], "tensor", axis=1, tiled=True),
    )


def expert_block(weights, received):
    gate_full, up_full, down_full = weights
    sources, block_len, features = received.shape
    row_block = received.reshape(sources * block_len, features)
    gate_act = jnp.dot(row_block, gate_full, preferred_element_type=jnp.float32)
    up_act = jnp.dot(row_block, up_full, preferred_element_type=jnp.float32)
    hidden = (jax.nn.silu(gate_act) * up_act).astype(jnp.bfloat16)
    result = jnp.dot(hidden, down_full, preferred_element_type=jnp.float32).astype(jnp.bfloat16)
    result = result.reshape(sources, block_len, features)
    return lax.all_to_all(result, "expert", split_axis=0, concat_axis=0, tiled=True)


def moe_batch(tokens, norm_gain, route_slots, route_gates, weights):
    normed = rms_rows(tokens, norm_gain)
    tok_rows = normed.shape[0]
    top_count = route_slots.shape[1]
    group_size = lax.axis_size("expert")
    capacity = 9 * tok_rows // group_size
    flat_slot = route_slots.reshape(-1)
    onehot = (flat_slot[:, None] == jnp.arange(group_size, dtype=jnp.int32)[None, :]).astype(
        jnp.int32
    )
    running = jnp.cumsum(onehot, axis=0) - 1
    position = jnp.sum(running * onehot, axis=1)
    target = flat_slot * capacity + position
    places = jnp.arange(group_size * capacity, dtype=jnp.int32)
    picker = jnp.any(
        places[:, None, None] == target.reshape(tok_rows, top_count)[None, :, :], axis=2
    ).astype(jnp.bfloat16)
    outgoing = jnp.dot(picker, normed, preferred_element_type=jnp.float32).astype(jnp.bfloat16)
    outgoing = outgoing.reshape(group_size, capacity, normed.shape[1])
    returned = expert_block(
        weights, lax.all_to_all(outgoing, "expert", split_axis=0, concat_axis=0, tiled=True)
    )
    flat_back = returned.reshape(group_size * capacity, normed.shape[1])
    picked = (
        jnp.take(flat_back, target, axis=0)
        .astype(jnp.float32)
        .reshape(tok_rows, top_count, normed.shape[1])
    )
    return jnp.sum(picked * route_gates[:, :, None], axis=1).astype(jnp.bfloat16)


def flatten_all(pieces):
    return jnp.concatenate([piece.reshape(-1) for piece in pieces])


def unflatten(flat, templates):
    pieces = []
    begin = 0
    for template in templates:
        length = template.size
        pieces.append(flat[begin : begin + length].reshape(template.shape))
        begin = begin + length
    return tuple(pieces)


def shard_neighbours(flat):
    found = []
    for offset in (1, -1):
        found.append(shifted(flat, "expert", offset))
    return found


def local(
    batch_one,
    batch_two,
    norm_gain,
    slots_one,
    slots_two,
    gates_one,
    gates_two,
    table_old,
    table_new,
    gate_old,
    up_old,
    down_old,
):
    shards = (gate_old[0], up_old[0], down_old[0])
    full_old = gather_full(shards)
    mixed_one = moe_batch(batch_one, norm_gain, slots_one, gates_one, full_old)
    slot_index = lax.axis_index("expert")
    group = table_old.shape[0]
    wanted = table_new[slot_index]
    keep_own = wanted == table_old[slot_index]
    from_left = wanted == table_old[(slot_index - 1) % group]
    mine = flatten_all(shards)
    beside = shard_neighbours(mine)
    fresh = jnp.where(keep_own, mine, jnp.where(from_left, beside[0], beside[1]))
    full_new = gather_full(unflatten(fresh, shards))
    mixed_two = moe_batch(batch_two, norm_gain, slots_two, gates_two, full_new)
    return (mixed_one, mixed_two)


def solution(mesh):
    in_specs = (
        P(("expert", "tensor"), None),
        P(("expert", "tensor"), None),
        P(),
        P(("expert", "tensor"), None),
        P(("expert", "tensor"), None),
        P(("expert", "tensor"), None),
        P(("expert", "tensor"), None),
        P(),
        P(),
        P("expert", "tensor", None),
        P("expert", "tensor", None),
        P("expert", None, "tensor"),
    )
    out_specs = (P(("expert", "tensor"), None), P(("expert", "tensor"), None))
    return jax.shard_map(local, mesh=mesh, in_specs=in_specs, out_specs=out_specs, check_vma=False)
```

profile of v0, /device:TPU:0, one launch (start us, length us, event | category | flops | bytes accessed | tf_op | source)
XLA Modules:
  0.0 305.3 jit_solution(12491493111559348174)
XLA Ops:
  13.1 2.9 collective-permute-start
  16.0 4.0 %collective-permute-start.1 = (bf16[1179648]{0:T(1024)(128)(2,1)}, bf16[1179648]{0:T(1024)(128)(2,1)}, u32[]{:S(2)}, u32[]{:S(2)}) collective-permute-start(bf16[1179648]{0:T(1024)(128)(2,1)} %constant_dynamic-update-slice_fusion), channel_id=1, source_target_pairs={{2,0},{4,2},{6,4},{8,6},{10,8},{12,10},{14,12},{16,14},{18,16},{20... | collective-permute-start | bytes 7077896 | tf_op jit(solution)/shard_map/ppermute | solution.py:12
  23.4 1.5 reshape.146
  24.9 4.6 %all-to-all-start = ((bf16[16,36,1536]{2,1,0:T(8,128)(2,1)}), bf16[16,36,1536]{2,1,0:T(8,128)(2,1)}, u32[]{:S(2)}, u32[]{:S(2)}) async-start(bf16[16,36,1536]{2,1,0:T(8,128)(2,1)} %reshape.146), calls=%async_computation | async-start | bytes 3932160 | tf_op jit(solution)/shard_map/all_to_all | solution.py:61
  37.5 1.5 reshape.153
  39.1 95.3 %collective-permute-done = bf16[1179648]{0:T(1024)(128)(2,1)} collective-permute-done((bf16[1179648]{0:T(1024)(128)(2,1)}, bf16[1179648]{0:T(1024)(128)(2,1)}, u32[]{:S(2)}, u32[]{:S(2)}) %collective-permute-start) | collective-permute-done | bytes 2359328 | tf_op jit(solution)/shard_map/ppermute | solution.py:12
  134.3 2.1 collective-permute-done.1
  136.4 1.8 select_select_fusion
  138.2 2.3 all-to-all-done
  140.6 10.6 %all-to-all-start.2 = ((bf16[16,36,1536]{2,1,0:T(8,128)(2,1)}), bf16[16,36,1536]{2,1,0:T(8,128)(2,1)}, u32[]{:S(2)}, u32[]{:S(2)}) async-start(bf16[16,36,1536]{2,1,0:T(8,128)(2,1)} %reshape.153), calls=%async_computation.2 | async-start | bytes 3932160 | tf_op jit(solution)/shard_map/all_to_all | solution.py:61
  152.5 2.3 slice.56
  156.3 2.4 reshape.147
  158.8 3.6 %fusion.5 = f32[576,512]{1,0:T(8,128)} fusion(bf16[576,1536]{1,0:T(8,128)(2,1)S(1)} %reshape.147, bf16[1,1536,512]{2,1,0:T(8,128)(2,1)} %all-gather.16.cloned.1.call-done), kind=kOutput, calls=%fused_computation.14 | convolution fusion | flops 905969664 | bytes 4521984 | tf_op jit(solution)/shard_map/dot_general | solution.py:33
  162.4 5.8 %convolution_convert_fusion.3 = bf16[576,1536]{1,0:T(8,128)(2,1)} fusion(bf16[1,512,1536]{2,1,0:T(8,128)(2,1)} %all-gather.20.cloned.1.call-done, bf16[576,1536]{1,0:T(8,128)(2,1)S(1)} %reshape.147, bf16[1,1536,512]{2,1,0:T(8,128)(2,1)} %all-gather.18.cloned.1.call-done, f32[576,512]{1,0:T(8,128)} %fusion.5), kind=kOutput, calls=%fused_computation.9 | convolution fusion | flops 1814593536 | bytes 7864320 | tf_op jit(solution)/shard_map/dot_general | solution.py:36
  168.2 3.5 %reshape.148 = bf16[16,36,1536]{2,1,0:T(8,128)(2,1)} reshape(bf16[576,1536]{1,0:T(8,128)(2,1)} %convolution_convert_fusion.3) | data formatting | bytes 3538944 | tf_op jit(solution)/shard_map/reshape | solution.py:37
  171.7 19.8 %all-to-all-done.2 = bf16[16,36,1536]{2,1,0:T(8,128)(2,1)} async-done(((bf16[16,36,1536]{2,1,0:T(8,128)(2,1)}), bf16[16,36,1536]{2,1,0:T(8,128)(2,1)}, u32[]{:S(2)}, u32[]{:S(2)}) %all-to-all-start.2) | async-done | bytes 1769504 | tf_op jit(solution)/shard_map/all_to_all | solution.py:61
  191.5 9.1 %all-to-all-start.1 = ((bf16[16,36,1536]{2,1,0:T(8,128)(2,1)}), bf16[16,36,1536]{2,1,0:T(8,128)(2,1)S(1)}, u32[]{:S(2)}, u32[]{:S(2)}) async-start(bf16[16,36,1536]{2,1,0:T(8,128)(2,1)} %reshape.148), calls=%async_computation.1 | async-start | bytes 3932160 | tf_op jit(solution)/shard_map/all_to_all | solution.py:38
  200.8 1.6 slice.60
  202.4 3.5 %reshape.154 = bf16[576,1536]{1,0:T(8,128)(2,1)} reshape(bf16[16,36,1536]{2,1,0:T(8,128)(2,1)} %all-to-all-done.2) | data formatting | bytes 3538944 | tf_op jit(solution)/shard_map/reshape | solution.py:32
  206.0 3.0 fusion.42
  209.0 4.8 %all-gather.14.cloned.1.call-done = bf16[512,1536]{1,0:T(8,128)(2,1)} async-done(((bf16[512,768]{1,0:T(8,128)(2,1)}), bf16[512,1536]{1,0:T(8,128)(2,1)}) %all-gather.14.cloned.1.call-update) | async-done | bytes 1572880 | tf_op jit(solution)/shard_map/all_gather | solution.py:25
  213.8 5.8 %convolution_convert_fusion.2 = bf16[576,1536]{1,0:T(8,128)(2,1)} fusion(bf16[512,1536]{1,0:T(8,128)(2,1)} %all-gather.14.cloned.1.call-done, bf16[576,1536]{1,0:T(8,128)(2,1)} %reshape.154, bf16[1536,512]{1,0:T(8,128)(2,1)} %all-gather.12.cloned.1.call-done, f32[576,512]{1,0:T(8,128)S(1)} %fusion.42), kind=kOutput, calls=%fused_computation.8 | convolution fusion | flops 1814593536 | bytes 7864320 | tf_op jit(solution)/shard_map/dot_general | solution.py:36
  219.5 3.5 %reshape.155 = bf16[16,36,1536]{2,1,0:T(8,128)(2,1)} reshape(bf16[576,1536]{1,0:T(8,128)(2,1)} %convolution_convert_fusion.2) | data formatting | bytes 3538944 | tf_op jit(solution)/shard_map/reshape | solution.py:37
  223.0 17.9 %all-to-all-done.1 = bf16[16,36,1536]{2,1,0:T(8,128)(2,1)S(1)} async-done(((bf16[16,36,1536]{2,1,0:T(8,128)(2,1)}), bf16[16,36,1536]{2,1,0:T(8,128)(2,1)S(1)}, u32[]{:S(2)}, u32[]{:S(2)}) %all-to-all-start.1) | async-done | bytes 1769504 | tf_op jit(solution)/shard_map/all_to_all | solution.py:38
  242.2 9.2 %all-to-all-start.3 = ((bf16[16,36,1536]{2,1,0:T(8,128)(2,1)}), bf16[16,36,1536]{2,1,0:T(8,128)(2,1)}, u32[]{:S(2)}, u32[]{:S(2)}) async-start(bf16[16,36,1536]{2,1,0:T(8,128)(2,1)} %reshape.155), calls=%async_computation.3 | async-start | bytes 3932160 | tf_op jit(solution)/shard_map/all_to_all | solution.py:38
  251.6 2.4 reshape.149
  254.0 2.1 gather_fusion
  256.2 2.1 fusion.1
  258.3 33.5 %all-to-all-done.3 = bf16[16,36,1536]{2,1,0:T(8,128)(2,1)} async-done(((bf16[16,36,1536]{2,1,0:T(8,128)(2,1)}), bf16[16,36,1536]{2,1,0:T(8,128)(2,1)}, u32[]{:S(2)}, u32[]{:S(2)}) %all-to-all-start.3) | async-done | bytes 1769504 | tf_op jit(solution)/shard_map/all_to_all | solution.py:38
  291.8 2.4 reshape.156
  294.2 2.1 gather_fusion.1
  296.4 2.1 fusion
  (96 shorter events, 19.0 us)
Async XLA Ops:
  7.2 1.5 copy-start.2
  7.2 151.6 %all-gather.16.cloned.1.call-start = ((), (), s32[]{:S(2)}) async-start(), calls=%async_computation.7 | async-start | bytes 2359296 | tf_op jit(solution)/shard_map/all_gather | solution.py:23
  7.9 154.5 %all-gather.18.cloned.1.call-start = ((), (), s32[]{:S(2)}) async-start(), calls=%async_computation.8 | async-start | bytes 2359296 | tf_op jit(solution)/shard_map/all_gather | solution.py:24
  8.7 1.3 copy-start.3
  9.0 1.5 copy-start.4
  11.2 8.8 %copy-start.7 = (s32[64,8]{0,1:T(8,128)S(1)}, s32[64,8]{0,1:T(8,128)}, u32[]{:S(2)}) copy-start(s32[64,8]{0,1:T(8,128)} %param.17) | copy-start | bytes 6148
  11.2 9.1 %copy-start.9 = (bf16[1536]{0:T(1024)(128)(2,1)S(1)}, bf16[1536]{0:T(1024)(128)(2,1)}, u32[]{:S(2)}) copy-start(bf16[1536]{0:T(1024)(128)(2,1)} %param.16) | copy-start | bytes 9220
  11.2 10.9 %copy-start.5 = (bf16[64,1536]{1,0:T(8,128)(2,1)S(1)}, bf16[64,1536]{1,0:T(8,128)(2,1)}, u32[]{:S(2)}) copy-start(bf16[64,1536]{1,0:T(8,128)(2,1)} %param.14) | copy-start | bytes 589828
  13.1 121.3 %collective-permute-start = (bf16[1179648]{0:T(1024)(128)(2,1)}, bf16[1179648]{0:T(1024)(128)(2,1)}, u32[]{:S(2)}, u32[]{:S(2)}) collective-permute-start(bf16[1179648]{0:T(1024)(128)(2,1)} %constant_dynamic-update-slice_fusion), channel_id=1, source_target_pairs={{30,0},{0,2},{2,4},{4,6},{6,8},{8,10},{10,12},{12,14},{14,16},{16,... | collective-permute-start | bytes 7077896 | tf_op jit(solution)/shard_map/ppermute | solution.py:12
  16.0 120.4 %collective-permute-start.1 = (bf16[1179648]{0:T(1024)(128)(2,1)}, bf16[1179648]{0:T(1024)(128)(2,1)}, u32[]{:S(2)}, u32[]{:S(2)}) collective-permute-start(bf16[1179648]{0:T(1024)(128)(2,1)} %constant_dynamic-update-slice_fusion), channel_id=1, source_target_pairs={{2,0},{4,2},{6,4},{8,6},{10,8},{12,10},{14,12},{16,14},{18,16},{20... | collective-permute-start | bytes 7077896 | tf_op jit(solution)/shard_map/ppermute | solution.py:12
  24.9 5.4 %copy-start.8 = (s32[64,8]{0,1:T(8,128)S(1)}, s32[64,8]{0,1:T(8,128)}, u32[]{:S(2)}) copy-start(s32[64,8]{0,1:T(8,128)} %param.18) | copy-start | bytes 6148
  24.9 5.6 %copy-start.13 = (s32[16]{0:T(128)S(1)}, s32[16]{0:T(128)}, u32[]{:S(2)}) copy-start(s32[16]{0:T(128)} %param.22) | copy-start | bytes 196
  24.9 6.2 %copy-start.12 = (s32[16]{0:T(128)S(1)}, s32[16]{0:T(128)}, u32[]{:S(2)}) copy-start(s32[16]{0:T(128)} %param.21) | copy-start | bytes 196
  24.9 11.3 %copy-start.6 = (bf16[64,1536]{1,0:T(8,128)(2,1)S(1)}, bf16[64,1536]{1,0:T(8,128)(2,1)}, u32[]{:S(2)}) copy-start(bf16[64,1536]{1,0:T(8,128)(2,1)} %param.15) | copy-start | bytes 589828
  24.9 115.6 %all-to-all-start = ((bf16[16,36,1536]{2,1,0:T(8,128)(2,1)}), bf16[16,36,1536]{2,1,0:T(8,128)(2,1)}, u32[]{:S(2)}, u32[]{:S(2)}) async-start(bf16[16,36,1536]{2,1,0:T(8,128)(2,1)} %reshape.146), calls=%async_computation | async-start | bytes 3932160 | tf_op jit(solution)/shard_map/all_to_all | solution.py:61
  29.5 132.9 %all-gather.20.cloned.1.call-start = ((), (), s32[]{:S(2)}) async-start(), calls=%async_computation.9 | async-start | bytes 2359296 | tf_op jit(solution)/shard_map/all_gather | solution.py:25
  140.6 50.9 %all-to-all-start.2 = ((bf16[16,36,1536]{2,1,0:T(8,128)(2,1)}), bf16[16,36,1536]{2,1,0:T(8,128)(2,1)}, u32[]{:S(2)}, u32[]{:S(2)}) async-start(bf16[16,36,1536]{2,1,0:T(8,128)(2,1)} %reshape.153), calls=%async_computation.2 | async-start | bytes 3932160 | tf_op jit(solution)/shard_map/all_to_all | solution.py:61
  151.2 54.8 %all-gather.10.cloned.1.call-start = ((), (), s32[]{:S(2)}) async-start(), calls=%async_computation.4 | async-start | bytes 2359296 | tf_op jit(solution)/shard_map/all_gather | solution.py:23
  152.5 2.4 copy-start.1
  154.9 54.1 %all-gather.12.cloned.1.call-start = ((), (), s32[]{:S(2)}) async-start(), calls=%async_computation.5 | async-start | bytes 2359296 | tf_op jit(solution)/shard_map/all_gather | solution.py:24
  191.5 49.4 %all-to-all-start.1 = ((bf16[16,36,1536]{2,1,0:T(8,128)(2,1)}), bf16[16,36,1536]{2,1,0:T(8,128)(2,1)S(1)}, u32[]{:S(2)}, u32[]{:S(2)}) async-start(bf16[16,36,1536]{2,1,0:T(8,128)(2,1)} %reshape.148), calls=%async_computation.1 | async-start | bytes 3932160 | tf_op jit(solution)/shard_map/all_to_all | solution.py:38
  200.6 13.2 %all-gather.14.cloned.1.call-start = ((), (), s32[]{:S(2)}) async-start(), calls=%async_computation.6 | async-start | bytes 2359296 | tf_op jit(solution)/shard_map/all_gather | solution.py:25
  223.0 28.3 %copy-start.10 = (f32[64,8]{0,1:T(8,128)S(1)}, f32[64,8]{0,1:T(8,128)}, u32[]{:S(2)}) copy-start(f32[64,8]{0,1:T(8,128)} %param.20) | copy-start | bytes 6148
  223.0 28.4 %copy-start.11 = (f32[64,8]{0,1:T(8,128)S(1)}, f32[64,8]{0,1:T(8,128)}, u32[]{:S(2)}) copy-start(f32[64,8]{0,1:T(8,128)} %param.19) | copy-start | bytes 6148
  240.9 1.3 copy-start
  242.2 49.6 %all-to-all-start.3 = ((bf16[16,36,1536]{2,1,0:T(8,128)(2,1)}), bf16[16,36,1536]{2,1,0:T(8,128)(2,1)}, u32[]{:S(2)}, u32[]{:S(2)}) async-start(bf16[16,36,1536]{2,1,0:T(8,128)(2,1)} %reshape.155), calls=%async_computation.3 | async-start | bytes 3932160 | tf_op jit(solution)/shard_map/all_to_all | solution.py:38
Sparse Core Ops, SparseCore 0:
  9.6 12.5 all-gather.15
  23.7 10.9 all-gather.17
  36.2 10.9 all-gather.19
  155.0 11.0 all-gather.9
  167.5 10.9 all-gather.11
  202.7 11.0 all-gather.13
where the time goes:
time: 310 us; the launch traced here: 305 us
  waiting for transfers between devices  178 us (57%)
  starting transfers between devices  40.8 us (13%)
  local copies, waits for them, and re-layouts  40.1 us (13%)
  matrix products  19.6 us (6%)
  between operations  17.1 us (6%)
  other arithmetic  9.9 us (3%)
    ppermute x2, waiting for transfers between devices, shifted(): return lax.ppermute(block, axis, route)  97.4 us
    all_to_all x2, waiting for transfers between devices, expert_block(): lax.all_to_all(result, 'expert', split_axis=0, concat_axis=0, tiled=True)  51.4 us
    all_to_all x2, waiting for transfers between devices, moe_batch(): lax.all_to_all(outgoing, 'expert', split_axis=0, concat_axis=0, tiled=True)  22.1 us
    all_to_all x2, starting transfers between devices, expert_block(): lax.all_to_all(result, 'expert', split_axis=0, concat_axis=0, tiled=True)  18.2 us
    all_to_all x2, starting transfers between devices, moe_batch(): lax.all_to_all(outgoing, 'expert', split_axis=0, concat_axis=0, tiled=True)  15.2 us
    dot_general x2, matrix products, expert_block(): jnp.dot(hidden, down_full, preferred_element_type=jnp.float32)  11.6 us
    reshape x2, local copies, waits for them, and re-layouts, expert_block(): result = result.reshape(sources, block_len, features)  6.95 us
    ppermute x2, starting transfers between devices, shifted(): return lax.ppermute(block, axis, route)  6.93 us
  transfers between devices with their start and end apart: 12, of which 7 were waited for; matrix products, arithmetic and copies ran while one was open for 20% of the time, Pallas kernels for 0%

commit v1 on v0

v1 whole, which is shorter than its diff:
```python
import jax
import jax.numpy as jnp
from jax import lax
from jax.sharding import PartitionSpec as P

EPS = 1e-05


def rms_rows(tokens, norm_gain):
    values = tokens.astype(jnp.float32)
    square = jnp.mean(values * values, axis=-1, keepdims=True)
    return (values * lax.rsqrt(square + EPS) * norm_gain.astype(jnp.float32)).astype(jnp.bfloat16)


def gather_tensor(shard, axis):
    if lax.axis_size("tensor") != 2:
        return lax.all_gather(shard, "tensor", axis=axis, tiled=True)
    other = lax.ppermute(shard, "tensor", [(0, 1), (1, 0)])
    first = lax.axis_index("tensor") == 0
    return jnp.concatenate(
        [jnp.where(first, shard, other), jnp.where(first, other, shard)], axis=axis
    )


def source_slots(table_old, table_new):
    group = table_old.shape[0]
    slot_index = jnp.arange(group, dtype=jnp.int32)
    picked = jnp.where(
        table_new == jnp.roll(table_old, 1), (slot_index - 1) % group, (slot_index + 1) % group
    )
    return jnp.where(table_new == table_old, slot_index, picked).astype(jnp.int32)


def slot_weights(route_slots, route_gates, held_by):
    group = held_by.shape[0]
    hit = route_slots[:, :, None] == jnp.arange(group, dtype=jnp.int32)
    by_slot = jnp.sum(jnp.where(hit, route_gates[:, :, None], 0.0), axis=1)
    moved = held_by[:, None] == jnp.arange(group, dtype=jnp.int32)
    return jnp.sum(jnp.where(moved[None], by_slot[:, :, None], 0.0), axis=1)


def expert_part(rows, weight, gate_full, up_full, down_full):
    gate_act = jnp.dot(rows, gate_full, preferred_element_type=jnp.float32)
    up_act = jnp.dot(rows, up_full, preferred_element_type=jnp.float32)
    hidden = (jax.nn.silu(gate_act) * up_act).astype(jnp.bfloat16)
    result = jnp.dot(hidden, down_full, preferred_element_type=jnp.float32).astype(jnp.bfloat16)
    return (result.astype(jnp.float32) * weight[:, None]).astype(jnp.bfloat16)


def local(
    batch_one,
    batch_two,
    norm_gain,
    slots_one,
    slots_two,
    gates_one,
    gates_two,
    table_old,
    table_new,
    gate_old,
    up_old,
    down_old,
):
    group = table_old.shape[0]
    me = lax.axis_index("expert")
    gate_full = gather_tensor(gate_old[0], 0)
    up_full = gather_tensor(up_old[0], 0)
    down_full = gather_tensor(down_old[0], 1)
    rows_one = lax.all_gather(rms_rows(batch_one, norm_gain), "expert", axis=0, tiled=True)
    rows_two = lax.all_gather(rms_rows(batch_two, norm_gain), "expert", axis=0, tiled=True)
    own = jnp.arange(group, dtype=jnp.int32)
    weights = jnp.stack(
        [
            slot_weights(slots_one, gates_one, own),
            slot_weights(slots_two, gates_two, source_slots(table_old, table_new)),
        ]
    )
    all_weights = lax.all_gather(weights, "expert", axis=1, tiled=True)
    mine = lax.dynamic_index_in_dim(all_weights, me, axis=2, keepdims=False)
    outs = []
    for rows, weight in ((rows_one, mine[0]), (rows_two, mine[1])):
        part = expert_part(rows, weight, gate_full, up_full, down_full)
        outs.append(lax.psum_scatter(part, "expert", scatter_dimension=0, tiled=True))
    return tuple(outs)


def solution(mesh):
    in_specs = (
        P(("expert", "tensor"), None),
        P(("expert", "tensor"), None),
        P(),
        P(("expert", "tensor"), None),
        P(("expert", "tensor"), None),
        P(("expert", "tensor"), None),
        P(("expert", "tensor"), None),
        P(),
        P(),
        P("expert", "tensor", None),
        P("expert", "tensor", None),
        P("expert", None, "tensor"),
    )
    out_specs = (P(("expert", "tensor"), None), P(("expert", "tensor"), None))
    return jax.shard_map(local, mesh=mesh, in_specs=in_specs, out_specs=out_specs, check_vma=False)
```

time: 310 us -> 435 us (1.40); the launches traced: 305 us -> 435 us
  waiting for transfers between devices: 178 us -> 318 us
  blocking collectives: 0 us -> 52.6 us
  starting transfers between devices: 40.8 us -> 1.37 us
  local copies, waits for them, and re-layouts: 40.1 us -> 9.49 us
  matrix products: 19.6 us -> 26.3 us
    reduce_scatter x0 -> x2, waiting for transfers between devices: none -> 257 us  [local(): lax.psum_scatter(part, 'expert', scatter_dimension=0, tiled=True)]
    ppermute x2 -> x3, waiting for transfers between devices: 97.4 us -> 0.01 us  [gather_tensor(): other = lax.ppermute(shard, 'tensor', [(0, 1), (1, 0)])]
    all_to_all x4 -> x0, waiting for transfers between devices: 73.5 us -> none  [the longest x2 51.4 us: expert_block(): lax.all_to_all(result, 'expert', split_axis=0, concat_axis=0, tiled=True)]
    all_gather x6 -> x2, waiting for transfers between devices: 4.81 us -> 60.5 us  [the longest x1 56.6 us: local(): lax.all_gather(rms_rows(batch_one, norm_gain), 'expert', axis=0, tiled=True)]
    all_gather x0 -> x1, blocking collectives: none -> 52.6 us  [local(): all_weights = lax.all_gather(weights, 'expert', axis=1, tiled=True)]
    all_to_all x4 -> x0, starting transfers between devices: 33.4 us -> none  [the longest x2 18.2 us: expert_block(): lax.all_to_all(result, 'expert', split_axis=0, concat_axis=0, tiled=True)]
    reshape x8 -> x0, local copies, waits for them, and re-layouts: 20.8 us -> none  [the longest x2 6.95 us: expert_block(): result = result.reshape(sources, block_len, features)]
    dot_general x6 -> x4, matrix products: 19.6 us -> 26.3 us  [the longest x2 16.2 us: expert_part(): jnp.dot(hidden, down_full, preferred_element_type=jnp.float32)]
  transfers between devices with their start and end apart: 12 -> 7, of which waited for: 7 -> 4; matrix products, arithmetic and copies ran while one was open for 20% -> 10% of each run, Pallas kernels for 0% -> 0%
where the time goes in v1:
time: 435 us
  waiting for transfers between devices  318 us (73%)
  blocking collectives  52.6 us (12%)
  matrix products  26.3 us (6%)
  between operations  13.9 us (3%)
  other arithmetic  13.1 us (3%)
  local copies, waits for them, and re-layouts  9.49 us (2%)
    reduce_scatter x2, waiting for transfers between devices, local(): lax.psum_scatter(part, 'expert', scatter_dimension=0, tiled=True)  257 us
    all_gather x1, waiting for transfers between devices, local(): lax.all_gather(rms_rows(batch_one, norm_gain), 'expert', axis=0, tiled=True)  56.6 us
    all_gather x1, blocking collectives, local(): all_weights = lax.all_gather(weights, 'expert', axis=1, tiled=True)  52.6 us
    dot_general x2, matrix products, expert_part(): jnp.dot(hidden, down_full, preferred_element_type=jnp.float32)  16.2 us
    dot_general x2, matrix products, expert_part(): gate_act = jnp.dot(rows, gate_full, preferred_element_type=jnp.float32)  10.1 us
  transfers between devices with their start and end apart: 7, of which 4 were waited for; matrix products, arithmetic and copies ran while one was open for 10% of the time, Pallas kernels for 0%

profile of v1, /device:TPU:0, one launch (start us, length us, event | category | flops | bytes accessed | tf_op | source)
XLA Modules:
  0.0 435.1 jit_solution(15090231416935503374)
XLA Ops:
  7.2 1.1 fusion.6
  8.4 1.1 fusion.9
  9.4 0.7 convert_element_type.41
  10.1 1.9 fusion.11
  12.1 0.0 all-gather.3.cloned.1.call-start
  12.1 0.7 all-gather.3.cloned.1.call-update
  12.8 0.0 reduce-scatter.5.cloned.1.call-start
  12.9 0.5 collective-permute-start
  13.4 0.1 collective-permute-start.1
  13.5 0.4 collective-permute-start.2
  13.9 1.2 slice.16
  15.2 1.4 compare_select_fusion.5
  16.5 0.1 iota_compare_fusion.2
  16.6 0.7 select_reduce_fusion.2
  17.3 0.7 select_reduce_fusion.3
  18.1 0.1 select_reduce_fusion
  18.2 0.1 select_reduce_fusion.1
  18.3 0.1 copy.31
  18.4 52.6 %all_gather.10 = f32[2,1024,16]{2,0,1:T(2,128)S(1)} all-gather(f32[2,64,16]{2,0,1:T(2,128)S(1)} %copy.31), channel_id=1, replica_groups=mesh['expert'=16,'tensor'=2] {'expert'}, dimensions={1}, use_global_device_ids=true | all-gather | bytes 139264 | tf_op jit(solution)/shard_map/all_gather | solution.py:78
  71.0 8.1 %dynamic-slice_reduce_fusion = (f32[1024]{0:T(1024)S(1)}, f32[1024]{0:T(1024)S(1)}) fusion(f32[2,1024,16]{2,0,1:T(2,128)S(1)} %all_gather.10, s32[]{:T(128)S(6)} %add.56, s32[]{:T(128)S(6)} %select_n.84), kind=kLoop, calls=%fused_computation.21 | loop fusion | bytes 16392 | tf_op jit(solution)/shard_map/slice | solution.py:81
  79.2 2.5 broadcast_select_fusion.5
  81.7 1.3 broadcast_select_fusion.3
  83.0 1.4 broadcast_select_fusion.1
  84.4 3.9 all-gather.5.cloned.1.call-done
  88.4 5.1 %fusion.4 = f32[1024,512]{1,0:T(8,128)} fusion(bf16[1024,1536]{1,0:T(8,128)(2,1)} %all-gather.5.cloned.1.call-done, bf16[768,512]{1,0:T(8,128)(2,1)S(1)} %copy-done.4, bf16[768,512]{1,0:T(8,128)(2,1)S(1)} %copy-done.3), kind=kOutput, calls=%fused_computation.13 | convolution fusion | flops 1613758464 | bytes 6815744 | tf_op jit(solution)/shard_map/dot_general | solution.py:43
  93.5 8.1 %multiply_convert_fusion = bf16[1024,1536]{1,0:T(8,128)(2,1)} fusion(f32[1024]{0:T(1024)S(1)} %get-tuple-element.2, f32[1024,512]{1,0:T(8,128)} %fusion.4, bf16[512,768]{1,0:T(8,128)(2,1)} %get-tuple-element.7, bf16[512,768]{1,0:T(8,128)(2,1)} %get-tuple-element.6, bf16[1024,1536]{1,0:T(8,128)(2,1)} %all-gather.5.cloned.1.call-done, ...), kind=kOutput, calls=%fused_computation | convolution fusion | flops 3236954112 | bytes 11538432 | tf_op jit(solution)/shard_map/dot_general | solution.py:46
  101.6 0.2 reduce-scatter.3.cloned.1.call-start
  101.8 56.6 %all-gather.3.cloned.1.call-done = bf16[1024,1536]{1,0:T(8,128)(2,1)} async-done(((bf16[64,1536]{1,0:T(8,128)(2,1)}), bf16[1024,1536]{1,0:T(8,128)(2,1)}) %all-gather.3.cloned.1.call-update) | async-done | bytes 3145744 | tf_op jit(solution)/shard_map/all_gather | solution.py:69
  158.4 5.0 %fusion.5 = f32[1024,512]{1,0:T(8,128)} fusion(bf16[1024,1536]{1,0:T(8,128)(2,1)} %all-gather.3.cloned.1.call-done, bf16[768,512]{1,0:T(8,128)(2,1)S(1)} %copy-done.4, bf16[768,512]{1,0:T(8,128)(2,1)S(1)} %copy-done.3), kind=kOutput, calls=%fused_computation.14 | convolution fusion | flops 1613758464 | bytes 6815744 | tf_op jit(solution)/shard_map/dot_general | solution.py:43
  163.4 8.1 %multiply_convert_fusion.1 = bf16[1024,1536]{1,0:T(8,128)(2,1)} fusion(f32[1024]{0:T(1024)S(1)} %get-tuple-element.3, f32[1024,512]{1,0:T(8,128)} %fusion.5, bf16[512,768]{1,0:T(8,128)(2,1)} %get-tuple-element.7, bf16[512,768]{1,0:T(8,128)(2,1)} %get-tuple-element.6, bf16[1024,1536]{1,0:T(8,128)(2,1)} %all-gather.3.cloned.1.call-done, ...), kind=kOutput, calls=%fused_computation.1 | convolution fusion | flops 3236954112 | bytes 11538432 | tf_op jit(solution)/shard_map/dot_general | solution.py:46
  171.6 121.6 %reduce-scatter.5.cloned.1.call-done = bf16[64,1536]{1,0:T(8,128)(2,1)} async-done(((bf16[1024,1536]{1,0:T(8,128)(2,1)}), bf16[64,1536]{1,0:T(8,128)(2,1)}) %reduce-scatter.5.cloned.1.call-update) | async-done | bytes 196624 | tf_op jit(solution)/shard_map/reduce_scatter | solution.py:83
  293.2 135.4 %reduce-scatter.3.cloned.1.call-done = bf16[64,1536]{1,0:T(8,128)(2,1)} async-done(((bf16[1024,1536]{1,0:T(8,128)(2,1)}), bf16[64,1536]{1,0:T(8,128)(2,1)}) %reduce-scatter.3.cloned.1.call-update) | async-done | bytes 196624 | tf_op jit(solution)/shard_map/reduce_scatter | solution.py:83
  (24 shorter events, 0.1 us)
Async XLA Ops:
  7.2 72.0 %copy-start = (bf16[1,768,512]{2,1,0:T(8,128)(2,1)S(1)}, bf16[1,768,512]{2,1,0:T(8,128)(2,1)}, u32[]{:S(2)}) copy-start(bf16[1,768,512]{2,1,0:T(8,128)(2,1)} %param.21) | copy-start | bytes 2359300
  7.2 81.2 %all-gather.5.cloned.1.call-start = ((), (), s32[]{:S(2)}) async-start(), calls=%async_computation.4 | async-start | bytes 3342336 | tf_op jit(solution)/shard_map/all_gather | solution.py:70
  12.1 69.6 %copy-start.1 = (bf16[1,768,512]{2,1,0:T(8,128)(2,1)S(1)}, bf16[1,768,512]{2,1,0:T(8,128)(2,1)}, u32[]{:S(2)}) copy-start(bf16[1,768,512]{2,1,0:T(8,128)(2,1)} %param.22) | copy-start | bytes 2359300
  12.1 146.3 %all-gather.3.cloned.1.call-start = ((), (), s32[]{:S(2)}) async-start(), calls=%async_computation.2 | async-start | bytes 3342336 | tf_op jit(solution)/shard_map/all_gather | solution.py:69
  12.8 280.4 %reduce-scatter.5.cloned.1.call-start = ((), (), s32[]{:S(2)}) async-start(), calls=%async_computation.5 | async-start | bytes 3342336 | tf_op jit(solution)/shard_map/reduce_scatter | solution.py:83
  12.9 66.3 %collective-permute-start = (bf16[768,512]{1,0:T(8,128)(2,1)}, bf16[768,512]{1,0:T(8,128)(2,1)}, u32[]{:S(2)}, u32[]{:S(2)}) collective-permute-start(bf16[768,512]{1,0:T(8,128)(2,1)} %bitcast.16), channel_id=1, source_target_pairs={{0,1},{1,0},{2,3},{3,2},{4,5},{5,4},{6,7},{7,6},{8,9},{9,8},{10,11... | collective-permute-start | bytes 2359304 | tf_op jit(solution)/shard_map/ppermute | solution.py:18
  13.4 68.3 %collective-permute-start.1 = (bf16[768,512]{1,0:T(8,128)(2,1)}, bf16[768,512]{1,0:T(8,128)(2,1)S(1)}, u32[]{:S(2)}, u32[]{:S(2)}) collective-permute-start(bf16[768,512]{1,0:T(8,128)(2,1)} %bitcast.17), channel_id=1, source_target_pairs={{0,1},{1,0},{2,3},{3,2},{4,5},{5,4},{6,7},{7,6},{8,9},{9,8},{10,11... | collective-permute-start | bytes 2359304 | tf_op jit(solution)/shard_map/ppermute | solution.py:18
  13.5 69.5 %collective-permute-start.2 = (bf16[512,768]{1,0:T(8,128)(2,1)}, bf16[512,768]{1,0:T(8,128)(2,1)S(1)}, u32[]{:S(2)}, u32[]{:S(2)}) collective-permute-start(bf16[512,768]{1,0:T(8,128)(2,1)} %bitcast.18), channel_id=1, source_target_pairs={{0,1},{1,0},{2,3},{3,2},{4,5},{5,4},{6,7},{7,6},{8,9},{9,8},{10,11... | collective-permute-start | bytes 2359304 | tf_op jit(solution)/shard_map/ppermute | solution.py:18
  79.2 3.8 copy-start.2
  81.7 6.7 %copy-start.3 = (bf16[768,512]{1,0:T(8,128)(2,1)S(1)}, bf16[768,512]{1,0:T(8,128)(2,1)}, u32[]{:S(2)}) copy-start(bf16[768,512]{1,0:T(8,128)(2,1)} %get-tuple-element.8) | copy-start | bytes 2359300
  83.0 5.3 %copy-start.4 = (bf16[768,512]{1,0:T(8,128)(2,1)S(1)}, bf16[768,512]{1,0:T(8,128)(2,1)}, u32[]{:S(2)}) copy-start(bf16[768,512]{1,0:T(8,128)(2,1)} %get-tuple-element.9) | copy-start | bytes 2359300
  88.4 5.1 %copy-start.5 = (bf16[768,512]{1,0:T(8,128)(2,1)S(1)}, bf16[768,512]{1,0:T(8,128)(2,1)}, u32[]{:S(2)}) copy-start(bf16[768,512]{1,0:T(8,128)(2,1)} %get-tuple-element.4) | copy-start | bytes 2359300
  88.4 5.1 %copy-start.6 = (bf16[768,512]{1,0:T(8,128)(2,1)S(1)}, bf16[768,512]{1,0:T(8,128)(2,1)}, u32[]{:S(2)}) copy-start(bf16[768,512]{1,0:T(8,128)(2,1)} %get-tuple-element.5) | copy-start | bytes 2359300
  101.6 327.0 %reduce-scatter.3.cloned.1.call-start = ((), (), s32[]{:S(2)}) async-start(), calls=%async_computation.3 | async-start | bytes 3342336 | tf_op jit(solution)/shard_map/reduce_scatter | solution.py:83
Sparse Core Ops, SparseCore 0:
  12.2 76.0 all-gather.4
  91.7 66.6 all-gather.2
  164.0 129.1 reduce-scatter.4
  298.6 129.9 reduce-scatter.2

commit v2 on v1

--- a/solution.py
+++ b/solution.py
@@ -1,25 +1,22 @@
+import functools
+
 import jax
 import jax.numpy as jnp
 from jax import lax
+from jax.experimental import pallas as pl
+from jax.experimental.pallas import tpu as pltpu
 from jax.sharding import PartitionSpec as P
 
 EPS = 1e-05
+PACK = 128
+VMEM_LIMIT = 48 * 1024 * 1024
+X, Y, Z_LOW, Z_HIGH = 1, 2, 4, 8
 
 
 def rms_rows(tokens, norm_gain):
     values = tokens.astype(jnp.float32)
     square = jnp.mean(values * values, axis=-1, keepdims=True)
     return (values * lax.rsqrt(square + EPS) * norm_gain.astype(jnp.float32)).astype(jnp.bfloat16)
-
-
-def gather_tensor(shard, axis):
-    if lax.axis_size("tensor") != 2:
-        return lax.all_gather(shard, "tensor", axis=axis, tiled=True)
-    other = lax.ppermute(shard, "tensor", [(0, 1), (1, 0)])
-    first = lax.axis_index("tensor") == 0
-    return jnp.concatenate(
-        [jnp.where(first, shard, other), jnp.where(first, other, shard)], axis=axis
-    )
 
 
 def source_slots(table_old, table_new):
@@ -43,11 +40,11 @@
     gate_act = jnp.dot(rows, gate_full, preferred_element_type=jnp.float32)
     up_act = jnp.dot(rows, up_full, preferred_element_type=jnp.float32)
     hidden = (jax.nn.silu(gate_act) * up_act).astype(jnp.bfloat16)
-    result = jnp.dot(hidden, down_full, preferred_element_type=jnp.float32).astype(jnp.bfloat16)
-    return (result.astype(jnp.float32) * weight[:, None]).astype(jnp.bfloat16)
-
-
-def local(
+    result = jnp.dot(hidden, down_full, preferred_element_type=jnp.float32)
+    return (result * weight[:, None]).astype(jnp.bfloat16)
+
+
+def local_any(
     batch_one,
     batch_two,
     norm_gain,
@@ -63,9 +60,9 @@
 ):
     group = table_old.shape[0]
     me = lax.axis_index("expert")
-    gate_full = gather_tensor(gate_old[0], 0)
-    up_full = gather_tensor(up_old[0], 0)
-    down_full = gather_tensor(down_old[0], 1)
+    gate_full = lax.all_gather(gate_old[0], "tensor", axis=0, tiled=True)
+    up_full = lax.all_gather(up_old[0], "tensor", axis=0, tiled=True)
+    down_full = lax.all_gather(down_old[0], "tensor", axis=1, tiled=True)
     rows_one = lax.all_gather(rms_rows(batch_one, norm_gain), "expert", axis=0, tiled=True)
     rows_two = lax.all_gather(rms_rows(batch_two, norm_gain), "expert", axis=0, tiled=True)
     own = jnp.arange(group, dtype=jnp.int32)
@@ -84,6 +81,270 @@
     return tuple(outs)
 
 
+def call(body, outs, ins, flops=0, moved=0, scratch=()):
+    smem = pl.BlockSpec(memory_space=pltpu.SMEM)
+    vmem = pl.BlockSpec(memory_space=pltpu.VMEM)
+    return pl.pallas_call(
+        body,
+        out_shape=outs,
+        in_specs=[smem if x.ndim == 1 and x.dtype == jnp.int32 else vmem for x in ins],
+        out_specs=jax.tree.map(lambda _: vmem, outs),
+        scratch_shapes=list(scratch),
+        compiler_params=pltpu.CompilerParams(vmem_limit_bytes=VMEM_LIMIT),
+        cost_estimate=pl.CostEstimate(flops=flops, bytes_accessed=moved, transcendentals=0),
+    )(*ins)
+
+
+def prepare_kernel(
+    source_ref, one_ref, two_ref, gain_ref, slots_one_ref, slots_two_ref, gates_one_ref, gates_two_ref,
+    out_one_ref, out_two_ref,
+):
+    group = source_ref.shape[0]
+    gain = gain_ref[...].astype(jnp.float32)
+    width = one_ref.shape[1]
+    for tokens_ref, slots_ref, gates_ref, out_ref, moved in (
+        (one_ref, slots_one_ref, gates_one_ref, out_one_ref, False),
+        (two_ref, slots_two_ref, gates_two_ref, out_two_ref, True),
+    ):
+        values = tokens_ref[...].astype(jnp.float32)
+        square = jnp.mean(values * values, axis=-1, keepdims=True)
+        out_ref[:, :width] = (values * lax.rsqrt(square + EPS) * gain).astype(jnp.bfloat16)
+        slots = slots_ref[...]
+        if moved:
+            holder = jnp.zeros_like(slots)
+            for s in range(group):
+                holder = jnp.where(slots == s, source_ref[s], holder)
+            slots = holder
+        gates = gates_ref[...]
+        lane = lax.broadcasted_iota(jnp.int32, (slots.shape[0], PACK), 1)
+        expert = lane & (group - 1)
+        total = jnp.zeros((slots.shape[0], PACK), jnp.float32)
+        for k in range(slots.shape[1]):
+            total += jnp.where(expert == slots[:, k : k + 1], gates[:, k : k + 1], 0.0)
+        high = total.astype(jnp.bfloat16).astype(jnp.float32)
+        rest = total - high
+        middle = rest.astype(jnp.bfloat16).astype(jnp.float32)
+        low = rest - middle
+        piece = lane // group
+        packed = jnp.where(
+            piece == 0, high, jnp.where(piece == 1, middle, jnp.where(piece == 2, low, 0.0))
+        )
+        out_ref[:, width:] = packed.astype(jnp.bfloat16)
+
+
+def hidden_of(place, rows_ref, gate_refs, up_refs, begin, count):
+    depth = gate_refs[0].shape[0]
+    acts = []
+    for refs in (gate_refs, up_refs):
+        act = None
+        for which, ref in enumerate(refs):
+            half = place if which == 0 else 1 - place
+            columns = pl.ds(pl.multiple_of(half * depth, depth), depth)
+            term = jnp.dot(
+                rows_ref[pl.ds(begin, count), columns], ref[...], preferred_element_type=jnp.float32
+            )
+            act = term if act is None else act + term
+        acts.append(act)
+    gate_act, up_act = acts
+    return (gate_act / (1.0 + jnp.exp(-gate_act)) * up_act).astype(jnp.bfloat16)
+
+
+def weight_of(expert, group, packed):
+    lane = lax.broadcasted_iota(jnp.int32, packed.shape, 1)
+    chosen = (lane & (group - 1)) == expert
+    return jnp.sum(jnp.where(chosen, packed.astype(jnp.float32), 0.0), axis=1, keepdims=True)
+
+
+def own_kernel(pieces, group, place_ref, *refs):
+    piece_refs, refs = refs[:pieces], refs[pieces:]
+    gate_a, gate_b, up_a, up_b, down_a, down_b, total_ref, rows_ref = refs
+    tok = piece_refs[0].shape[0]
+    width = total_ref.shape[1]
+    for i, ref in enumerate(piece_refs):
+        rows_ref[i * tok : (i + 1) * tok, :] = ref[...]
+    place = place_ref[0]
+    block = 256
+
+    @pl.loop(0, rows_ref.shape[0] // block)
+    def _(step):
+        begin = pl.multiple_of(step * block, block)
+        hidden = hidden_of(place, rows_ref, (gate_a, gate_b), (up_a, up_b), begin, block)
+        weight = weight_of(place_ref[1], group, rows_ref[pl.ds(begin, block), width:])
+        for which, ref in enumerate((down_a, down_b)):
+            half = place if which == 0 else 1 - place
+            columns = pl.ds(pl.multiple_of(half * ref.shape[1], ref.shape[1]), ref.shape[1])
+            part = jnp.dot(hidden, ref[...], preferred_element_type=jnp.float32)
+            total_ref[pl.ds(begin, block), columns] = part * weight
+
+
+def beside_kernel(pieces, group, place_ref, *refs):
+    piece_refs, refs = refs[:pieces], refs[pieces:]
+    gate_a, gate_b, up_a, up_b, hidden_ref, weight_ref, rows_ref = refs
+    tok = piece_refs[0].shape[0]
+    width = rows_ref.shape[1] - PACK
+    for i, ref in enumerate(piece_refs):
+        rows_ref[i * tok : (i + 1) * tok, :] = ref[...]
+    block = 256
+
+    @pl.loop(0, rows_ref.shape[0] // block)
+    def _(step):
+        begin = pl.multiple_of(step * block, block)
+        hidden_ref[pl.ds(begin, block), :] = hidden_of(
+            place_ref[0], rows_ref, (gate_a, gate_b), (up_a, up_b), begin, block
+        )
+        weight = weight_of(place_ref[1] ^ Z_LOW, group, rows_ref[pl.ds(begin, block), width:])
+        weight_ref[pl.ds(begin, block), :] = jnp.broadcast_to(weight, (block, PACK))
+
+
+def join_kernel(place_ref, hidden_ref, weight_ref, total_ref, down_a, down_b, send_a, send_b, keep_a, keep_b):
+    place = place_ref[0]
+    count = send_a.shape[0]
+    for pair, outs in ((0, (send_a, send_b)), (1, (keep_a, keep_b))):
+        rows = slice(pair * 2 * count, (pair + 1) * 2 * count)
+        weight = weight_ref[rows, :1]
+        for which, ref in enumerate((down_a, down_b)):
+            half = place if which == 0 else 1 - place
+            columns = pl.ds(pl.multiple_of(half * ref.shape[1], ref.shape[1]), ref.shape[1])
+            part = jnp.dot(hidden_ref[rows, :], ref[...], preferred_element_type=jnp.float32)
+            part = part * weight + total_ref[rows, columns]
+            outs[0][:, columns] = part[:count].astype(outs[0].dtype)
+            outs[1][:, columns] = part[count:].astype(outs[1].dtype)
+
+
+def first_sum_kernel(keep_ref, got_ref, send_ref, held_ref):
+    half = held_ref.shape[0]
+    held_ref[...] = keep_ref[:half] + got_ref[:half].astype(jnp.float32)
+    send_ref[...] = (keep_ref[half:] + got_ref[half:].astype(jnp.float32)).astype(jnp.bfloat16)
+
+
+def second_sum_kernel(keep_a, got_a, keep_b, got_b, send_ref, held_ref):
+    half = keep_a.shape[0] // 2
+    for i, (keep, got) in enumerate(((keep_a, got_a), (keep_b, got_b))):
+        rows = slice(i * half, (i + 1) * half)
+        held_ref[rows, :] = keep[:half] + got[:half].astype(jnp.float32)
+        send_ref[rows, :] = (keep[half:] + got[half:].astype(jnp.float32)).astype(jnp.bfloat16)
+
+
+def last_sum_kernel(keep_ref, got_ref, out_ref):
+    out_ref[...] = (keep_ref[...] + got_ref[...].astype(jnp.float32)).astype(jnp.bfloat16)
+
+
+def swap(block, distance):
+    count = lax.axis_size("expert")
+    return lax.ppermute(block, "expert", [(i, i ^ distance) for i in range(count)])
+
+
+def swap_core(block):
+    return lax.ppermute(block, "tensor", [(0, 1), (1, 0)])
+
+
+def spread(own):
+    half = own.shape[0] // 2
+    far = swap(own, Z_HIGH)
+    a1 = jnp.concatenate([own[:half], far[:half]])
+    b1 = jnp.concatenate([own[half:], far[half:]])
+    a2, b2 = swap(a1, X), swap(b1, Y)
+    a3, b3 = swap(a1, Y), swap(b1, X)
+    a4, b4 = swap(a2, Y), swap(b2, X)
+    return [a3, a4, b3, b4, a1, a2, b1, b2]
+
+
+def send_back(send_a, send_b, keep_a, keep_b):
+    quarter, width = keep_a.shape[0] // 2, keep_a.shape[1]
+    bf = jax.ShapeDtypeStruct((quarter, width), jnp.bfloat16)
+    f32 = jax.ShapeDtypeStruct((quarter, width), jnp.float32)
+    size = quarter * width
+    got_a, got_b = swap(send_a, Y), swap(send_b, X)
+    next_a, held_a = call(first_sum_kernel, (bf, f32), (keep_a, got_a), size, 18 * size)
+    next_b, held_b = call(first_sum_kernel, (bf, f32), (keep_b, got_b), size, 18 * size)
+    got_a, got_b = swap(next_a, X), swap(next_b, Y)
+    next_z, held_z = call(
+        second_sum_kernel, (bf, f32), (held_a, got_a, held_b, got_b), size, 18 * size
+    )
+    got_z = swap(next_z, Z_HIGH)
+    return call(last_sum_kernel, bf, (held_z, got_z), size, 8 * size)
+
+
+def local_pairs(
+    batch_one,
+    batch_two,
+    norm_gain,
+    slots_one,
+    slots_two,
+    gates_one,
+    gates_two,
+    table_old,
+    table_new,
+    gate_old,
+    up_old,
+    down_old,
+):
+    group = table_old.shape[0]
+    tok, width = batch_one.shape
+    place = jnp.stack([lax.axis_index("tensor"), lax.axis_index("expert")]).astype(jnp.int32)
+    mine = (gate_old[0], up_old[0], down_old[0])
+    own = call(
+        prepare_kernel,
+        (jax.ShapeDtypeStruct((tok, width + PACK), jnp.bfloat16),) * 2,
+        (
+            source_slots(table_old, table_new),
+            batch_one,
+            batch_two,
+            norm_gain.reshape(1, width),
+            slots_one,
+            slots_two,
+            gates_one,
+            gates_two,
+        ),
+        10 * tok * width,
+        8 * tok * width,
+    )
+    twins = tuple(swap_core(w) for w in mine)
+    beside = tuple(swap(w, Z_LOW) for w in mine)
+    beside_twins = tuple(swap_core(w) for w in beside)
+    ff = gate_old.shape[2]
+    rows = 8 * tok
+    pieces = [spread(x) for x in own]
+    scratch = (pltpu.VMEM((rows, width + PACK), jnp.bfloat16),)
+    totals = [
+        call(
+            functools.partial(own_kernel, 8, group),
+            jax.ShapeDtypeStruct((rows, width), jnp.float32),
+            (place, *p, mine[0], twins[0], mine[1], twins[1], mine[2], twins[2]),
+            6 * rows * width * ff,
+            6 * width * ff + 6 * rows * width,
+            scratch,
+        )
+        for p in pieces
+    ]
+    hidden = [
+        call(
+            functools.partial(beside_kernel, 8, group),
+            (
+                jax.ShapeDtypeStruct((rows, ff), jnp.bfloat16),
+                jax.ShapeDtypeStruct((rows, PACK), jnp.float32),
+            ),
+            (place, *p, beside[0], beside_twins[0], beside[1], beside_twins[1]),
+            4 * rows * width * ff,
+            4 * width * ff + 2 * rows * width,
+            scratch,
+        )
+        for p in pieces
+    ]
+    outs = []
+    for total, (hid, weight) in zip(totals, hidden):
+        parts = call(
+            join_kernel,
+            (jax.ShapeDtypeStruct((2 * tok, width), jnp.bfloat16),) * 2
+            + (jax.ShapeDtypeStruct((2 * tok, width), jnp.float32),) * 2,
+            (place, hid, weight, total, beside[2], beside_twins[2]),
+            2 * rows * width * ff,
+            2 * width * ff + 8 * rows * width,
+        )
+        outs.append(send_back(*parts))
+    return tuple(outs)
+
+
 def solution(mesh):
     in_specs = (
         P(("expert", "tensor"), None),
@@ -100,4 +361,5 @@
         P("expert", None, "tensor"),
     )
     out_specs = (P(("expert", "tensor"), None), P(("expert", "tensor"), None))
+    local = local_pairs if (mesh.shape["expert"], mesh.shape["tensor"]) == (16, 2) else local_any
     return jax.shard_map(local, mesh=mesh, in_specs=in_specs, out_specs=out_specs, check_vma=False)

time: 435 us -> 175 us (0.40)
  waiting for transfers between devices: 318 us -> 84.3 us
  blocking collectives: 52.6 us -> 0 us
  starting transfers between devices: 1.37 us -> 36.4 us
  Pallas kernels: 0 us -> 30 us
  matrix products: 26.3 us -> 0 us
  between operations: 13.9 us -> 1.02 us
  other arithmetic: 13.1 us -> 1.6 us
  local copies, waits for them, and re-layouts: 9.49 us -> 20.8 us
    reduce_scatter x2 -> x0, waiting for transfers between devices: 257 us -> none  [local(): lax.psum_scatter(part, 'expert', scatter_dimension=0, tiled=True)]
    ppermute x3 -> x33, waiting for transfers between devices: 0.01 us -> 84.3 us  [the longest x27 84.2 us: swap(): lax.ppermute(block, 'expert', [(i, i ^ distance) for i in range(count)])]
    all_gather x2 -> x0, waiting for transfers between devices: 60.5 us -> none  [the longest x1 56.6 us: local(): lax.all_gather(rms_rows(batch_one, norm_gain), 'expert', axis=0, tiled=True)]
    all_gather x1 -> x0, blocking collectives: 52.6 us -> none  [local(): all_weights = lax.all_gather(weights, 'expert', axis=1, tiled=True)]
    ppermute x3 -> x33, starting transfers between devices: 1.03 us -> 36.4 us  [the longest x27 35.9 us: swap(): lax.ppermute(block, 'expert', [(i, i ^ distance) for i in range(count)])]
    pallas_call x0 -> x15, Pallas kernels: none -> 30 us  [call(): pl.pallas_call(body, out_shape=outs, in_specs=[smem if x.ndim == 1 and x....]
    dot_general x4 -> x0, matrix products: 26.3 us -> none  [the longest x2 16.2 us: expert_part(): jnp.dot(hidden, down_full, preferred_element_type=jnp.float32)]
    unnamed x14 -> x82, local copies, waits for them, and re-layouts: 0.03 us -> 18.7 us
  transfers between devices with their start and end apart: 7 -> 33, of which waited for: 4 -> 14; matrix products, arithmetic and copies ran while one was open for 10% -> 0% of each run, Pallas kernels for 0% -> 14%
where the time goes in v2:
time: 175 us; the launch traced here: 174 us
  waiting for transfers between devices  84.3 us (48%)
  starting transfers between devices  36.4 us (21%)
  Pallas kernels  30 us (17%)
  local copies, waits for them, and re-layouts  20.8 us (12%)
    ppermute x27, waiting for transfers between devices, swap(): lax.ppermute(block, 'expert', [(i, i ^ distance) for i in range(count)])  84.2 us
    ppermute x27, starting transfers between devices, swap(): lax.ppermute(block, 'expert', [(i, i ^ distance) for i in range(count)])  35.9 us
    pallas_call x15, Pallas kernels, call(): pl.pallas_call(body, out_shape=outs, in_specs=[smem if x.ndim == 1 and x....  30 us
    unnamed x82, local copies, waits for them, and re-layouts  18.7 us
  transfers between devices with their start and end apart: 33, of which 14 were waited for; matrix products, arithmetic and copies ran while one was open for 0% of the time, Pallas kernels for 14%

profile of v2, /device:TPU:0, one launch (start us, length us, event | category | flops | bytes accessed | tf_op | source)
XLA Modules:
  0.0 174.2 jit_solution(9890049417982471858)
XLA Ops:
  5.8 1.5 compare_select_fusion.5.source_ref
  10.2 4.1 %collective-permute-start = (bf16[64,1664]{1,0:T(8,128)(2,1)S(1)}, bf16[64,1664]{1,0:T(8,128)(2,1)S(1)}, u32[]{:S(2)}, u32[]{:S(2)}) collective-permute-start(bf16[64,1664]{1,0:T(8,128)(2,1)S(1)} %get-tuple-element.28), channel_id=1, source_target_pairs={{0,16},{2,18},{4,20},{6,22},{8,24},{10,26},{12,28},{14,30},{16,0},... | collective-permute-start | bytes 638984 | tf_op jit(solution)/shard_map/ppermute | solution.py:234
  14.4 15.1 %collective-permute-done = bf16[64,1664]{1,0:T(8,128)(2,1)S(1)} collective-permute-done((bf16[64,1664]{1,0:T(8,128)(2,1)S(1)}, bf16[64,1664]{1,0:T(8,128)(2,1)S(1)}, u32[]{:S(2)}, u32[]{:S(2)}) %collective-permute-start) | collective-permute-done | bytes 213024 | tf_op jit(solution)/shard_map/ppermute | solution.py:234
  29.5 1.9 %collective-permute-start.5 = (bf16[64,1664]{1,0:T(8,128)(2,1)S(1)}, bf16[64,1664]{1,0:T(8,128)(2,1)S(1)}, u32[]{:S(2)}, u32[]{:S(2)}) collective-permute-start(bf16[64,1664]{1,0:T(8,128)(2,1)S(1)} %pad_maximum_fusion.1.refs_6_), channel_id=1, source_target_pairs={{0,4},{2,6},{4,0},{6,2},{8,12},{10,14},{12,8},{14,10},{16,20},{18,... | collective-permute-start | bytes 638984 | tf_op jit(solution)/shard_map/ppermute | solution.py:234
  31.5 1.5 collective-permute-start.4
  35.7 2.4 %collective-permute-start.23 = (bf16[64,1664]{1,0:T(8,128)(2,1)S(1)}, bf16[64,1664]{1,0:T(8,128)(2,1)S(1)}, u32[]{:S(2)}, u32[]{:S(2)}) collective-permute-start(bf16[64,1664]{1,0:T(8,128)(2,1)S(1)} %pad_maximum_fusion.2.refs_4_), channel_id=1, source_target_pairs={{0,2},{2,0},{4,6},{6,4},{8,10},{10,8},{12,14},{14,12},{16,18},{18,... | collective-permute-start | bytes 638984 | tf_op jit(solution)/shard_map/ppermute | solution.py:234
  38.2 1.5 collective-permute-done.4.refs_2_
  40.5 3.4 %collective-permute-done.2.refs_5_ = bf16[64,1664]{1,0:T(8,128)(2,1)S(1)} collective-permute-done((bf16[64,1664]{1,0:T(8,128)(2,1)S(1)}, bf16[64,1664]{1,0:T(8,128)(2,1)S(1)}, u32[]{:S(2)}, u32[]{:S(2)}) %collective-permute-start.2) | collective-permute-done | bytes 213024 | tf_op jit(solution)/shard_map/ppermute | solution.py:234
  53.0 1.5 collective-permute-start.27
  55.9 1.5 collective-permute-start.14
  57.4 1.5 collective-permute-done.27.refs_3_
  60.1 10.5 %collective-permute-done.7.refs_8_ = bf16[768,512]{1,0:T(8,128)(2,1)} collective-permute-done((bf16[768,512]{1,0:T(8,128)(2,1)S(1)}, bf16[768,512]{1,0:T(8,128)(2,1)}, u32[]{:S(2)}, u32[]{:S(2)}) %collective-permute-start.7) | collective-permute-done | bytes 786464 | tf_op jit(solution)/shard_map/ppermute | solution.py:234
  70.6 16.8 %collective-permute-done.9.refs_10_ = bf16[768,512]{1,0:T(8,128)(2,1)} collective-permute-done((bf16[768,512]{1,0:T(8,128)(2,1)S(1)}, bf16[768,512]{1,0:T(8,128)(2,1)}, u32[]{:S(2)}, u32[]{:S(2)}) %collective-permute-start.9) | collective-permute-done | bytes 786464 | tf_op jit(solution)/shard_map/ppermute | solution.py:234
  87.4 11.5 %collective-permute-done.14.down_a = bf16[512,768]{1,0:T(8,128)(2,1)} collective-permute-done((bf16[512,768]{1,0:T(8,128)(2,1)S(1)}, bf16[512,768]{1,0:T(8,128)(2,1)}, u32[]{:S(2)}, u32[]{:S(2)}) %collective-permute-start.14) | collective-permute-done | bytes 786464 | tf_op jit(solution)/shard_map/ppermute | solution.py:234
  99.0 1.5 collective-permute-start.6
  100.5 1.5 collective-permute-start.3
  109.5 6.3 %shard_map.140.total_ref = f32[512,1536]{1,0:T(8,128)} custom-call(s32[2]{0:T(128)S(1)} %pad_add_fusion.place_ref, bf16[64,1664]{1,0:T(8,128)(2,1)S(1)} %copy-done.23, bf16[64,1664]{1,0:T(8,128)(2,1)S(1)} %copy-done.32, bf16[64,1664]{1,0:T(8,128)(2,1)S(1)} %copy-done.29, bf16[64,1664]{1,0:T(8,128)(2,1)S(1)} %copy-done.35, bf16[64,1664]{1,0:T(8,128)(2,1)S(1)} %copy-done.6, ...), custom_call_target="tpu_custom_call" | custom-call | flops 2415919104 | bytes 9437184 | tf_op jit(solution)/shard_map/pallas_call | solution.py:87
  115.9 6.3 %shard_map.133.total_ref = f32[512,1536]{1,0:T(8,128)} custom-call(s32[2]{0:T(128)S(1)} %pad_add_fusion.place_ref, bf16[64,1664]{1,0:T(8,128)(2,1)S(1)} %copy-done.18, bf16[64,1664]{1,0:T(8,128)(2,1)S(1)} %collective-permute-done.3.refs_1_, bf16[64,1664]{1,0:T(8,128)(2,1)S(1)} %copy-done.14, bf16[64,1664]{1,0:T(8,128)(2,1)S(1)} %collective-permute-done.6.refs_3_, ...), custom_call_target="tpu_custom_call" | custom-call | flops 2415919104 | bytes 9437184 | tf_op jit(solution)/shard_map/pallas_call | solution.py:87
  122.3 4.0 %shard_map.139 = (bf16[512,512]{1,0:T(8,128)(2,1)S(1)}, f32[512,128]{1,0:T(8,128)S(1)}) custom-call(s32[2]{0:T(128)S(1)} %pad_add_fusion.place_ref, bf16[64,1664]{1,0:T(8,128)(2,1)S(1)} %copy-done.24, bf16[64,1664]{1,0:T(8,128)(2,1)S(1)} %copy-done.33, bf16[64,1664]{1,0:T(8,128)(2,1)S(1)} %copy-done.30, bf16[64,1664]{1,0:T(8,128)(2,1)S(1)} %copy-done.36, ...), custom_call_target="tpu_custom_call" | custom-call | flops 1610612736 | bytes 4718592 | tf_op jit(solution)/shard_map/pallas_call | solution.py:87
  126.3 3.3 %shard_map.141 = (bf16[128,1536]{1,0:T(8,128)(2,1)S(1)}, bf16[128,1536]{1,0:T(8,128)(2,1)S(1)}, f32[128,1536]{1,0:T(8,128)S(1)}, f32[128,1536]{1,0:T(8,128)S(1)}) custom-call(s32[2]{0:T(128)S(1)} %pad_add_fusion.place_ref, bf16[512,512]{1,0:T(8,128)(2,1)S(1)} %get-tuple-element.42.hidden_ref, f32[512,128]{1,0:T(8,128)S(1)} %get-tuple-element.43.weight_ref, ...), custom_call_target="tpu_custom_call" | custom-call | flops 805306368 | bytes 7864320 | tf_op jit(solution)/shard_map/pallas_call | solution.py:87
  130.7 3.9 %shard_map.132 = (bf16[512,512]{1,0:T(8,128)(2,1)S(1)}, f32[512,128]{1,0:T(8,128)S(1)}) custom-call(s32[2]{0:T(128)S(1)} %pad_add_fusion.place_ref, bf16[64,1664]{1,0:T(8,128)(2,1)S(1)} %copy-done.18, bf16[64,1664]{1,0:T(8,128)(2,1)S(1)} %collective-permute-done.3.refs_1_, bf16[64,1664]{1,0:T(8,128)(2,1)S(1)} %copy-done.14, ...), custom_call_target="tpu_custom_call" | custom-call | flops 1610612736 | bytes 4718592 | tf_op jit(solution)/shard_map/pallas_call | solution.py:87
  134.7 3.3 %shard_map.134 = (bf16[128,1536]{1,0:T(8,128)(2,1)S(1)}, bf16[128,1536]{1,0:T(8,128)(2,1)S(1)}, f32[128,1536]{1,0:T(8,128)S(1)}, f32[128,1536]{1,0:T(8,128)S(1)}) custom-call(s32[2]{0:T(128)S(1)} %pad_add_fusion.place_ref, bf16[512,512]{1,0:T(8,128)(2,1)S(1)} %get-tuple-element.29.hidden_ref, f32[512,128]{1,0:T(8,128)S(1)} %get-tuple-element.30.weight_ref, ...), custom_call_target="tpu_custom_call" | custom-call | flops 805306368 | bytes 7864320 | tf_op jit(solution)/shard_map/pallas_call | solution.py:87
  138.1 1.6 collective-permute-start.16
  139.6 1.5 collective-permute-start.18
  143.0 7.2 %collective-permute-done.16.got_ref = bf16[128,1536]{1,0:T(8,128)(2,1)S(1)} collective-permute-done((bf16[128,1536]{1,0:T(8,128)(2,1)S(1)}, bf16[128,1536]{1,0:T(8,128)(2,1)S(1)}, u32[]{:S(2)}, u32[]{:S(2)}) %collective-permute-start.16) | collective-permute-done | bytes 393248 | tf_op jit(solution)/shard_map/ppermute | solution.py:234
  150.2 1.6 collective-permute-start.17
  151.9 1.6 collective-permute-start.19
  153.5 2.5 %collective-permute-done.29.got_a = bf16[64,1536]{1,0:T(8,128)(2,1)S(1)} collective-permute-done((bf16[64,1536]{1,0:T(8,128)(2,1)S(1)}, bf16[64,1536]{1,0:T(8,128)(2,1)S(1)}, u32[]{:S(2)}, u32[]{:S(2)}) %collective-permute-start.29) | collective-permute-done | bytes 196640 | tf_op jit(solution)/shard_map/ppermute | solution.py:234
  156.0 3.4 %collective-permute-start.32 = (bf16[64,1536]{1,0:T(8,128)(2,1)S(1)}, bf16[64,1536]{1,0:T(8,128)(2,1)S(1)}, u32[]{:S(2)}, u32[]{:S(2)}) collective-permute-start(bf16[64,1536]{1,0:T(8,128)(2,1)S(1)} %get-tuple-element.53), channel_id=1, source_target_pairs={{0,16},{2,18},{4,20},{6,22},{8,24},{10,26},{12,28},{14,30},{16,0},... | collective-permute-start | bytes 589832 | tf_op jit(solution)/shard_map/ppermute | solution.py:234
  159.5 2.1 %collective-permute-start.20 = (bf16[64,1536]{1,0:T(8,128)(2,1)S(1)}, bf16[64,1536]{1,0:T(8,128)(2,1)S(1)}, u32[]{:S(2)}, u32[]{:S(2)}) collective-permute-start(bf16[64,1536]{1,0:T(8,128)(2,1)S(1)} %get-tuple-element.40), channel_id=1, source_target_pairs={{0,16},{2,18},{4,20},{6,22},{8,24},{10,26},{12,28},{14,30},{16,0},... | collective-permute-start | bytes 589832 | tf_op jit(solution)/shard_map/ppermute | solution.py:234
  161.6 9.7 %collective-permute-done.32.got_ref = bf16[64,1536]{1,0:T(8,128)(2,1)S(1)} collective-permute-done((bf16[64,1536]{1,0:T(8,128)(2,1)S(1)}, bf16[64,1536]{1,0:T(8,128)(2,1)S(1)}, u32[]{:S(2)}, u32[]{:S(2)}) %collective-permute-start.32) | collective-permute-done | bytes 196640 | tf_op jit(solution)/shard_map/ppermute | solution.py:234
  172.1 1.4 collective-permute-done.20.got_ref
  (142 shorter events, 35.7 us)
Async XLA Ops:
  10.2 19.3 %collective-permute-start = (bf16[64,1664]{1,0:T(8,128)(2,1)S(1)}, bf16[64,1664]{1,0:T(8,128)(2,1)S(1)}, u32[]{:S(2)}, u32[]{:S(2)}) collective-permute-start(bf16[64,1664]{1,0:T(8,128)(2,1)S(1)} %get-tuple-element.28), channel_id=1, source_target_pairs={{0,16},{2,18},{4,20},{6,22},{8,24},{10,26},{12,28},{14,30},{16,0},... | collective-permute-start | bytes 638984 | tf_op jit(solution)/shard_map/ppermute | solution.py:234
  14.3 19.3 %collective-permute-start.21 = (bf16[64,1664]{1,0:T(8,128)(2,1)S(1)}, bf16[64,1664]{1,0:T(8,128)(2,1)S(1)}, u32[]{:S(2)}, u32[]{:S(2)}) collective-permute-start(bf16[64,1664]{1,0:T(8,128)(2,1)S(1)} %get-tuple-element.41), channel_id=1, source_target_pairs={{0,16},{2,18},{4,20},{6,22},{8,24},{10,26},{12,28},{14,30},{16,0},... | collective-permute-start | bytes 638984 | tf_op jit(solution)/shard_map/ppermute | solution.py:234
  14.4 45.2 %collective-permute-start.11 = (bf16[768,512]{1,0:T(8,128)(2,1)}, bf16[768,512]{1,0:T(8,128)(2,1)S(1)}, u32[]{:S(2)}, u32[]{:S(2)}) collective-permute-start(bf16[768,512]{1,0:T(8,128)(2,1)} %bitcast.6), channel_id=1, source_target_pairs={{0,1},{1,0},{2,3},{3,2},{4,5},{5,4},{6,7},{7,6},{8,9},{9,8},{10,11... | collective-permute-start | bytes 2359304 | tf_op jit(solution)/shard_map/ppermute | solution.py:238
  29.5 6.2 %collective-permute-start.5 = (bf16[64,1664]{1,0:T(8,128)(2,1)S(1)}, bf16[64,1664]{1,0:T(8,128)(2,1)S(1)}, u32[]{:S(2)}, u32[]{:S(2)}) collective-permute-start(bf16[64,1664]{1,0:T(8,128)(2,1)S(1)} %pad_maximum_fusion.1.refs_6_), channel_id=1, source_target_pairs={{0,4},{2,6},{4,0},{6,2},{8,12},{10,14},{12,8},{14,10},{16,20},{18,... | collective-permute-start | bytes 638984 | tf_op jit(solution)/shard_map/ppermute | solution.py:234
  31.5 8.2 %collective-permute-start.4 = (bf16[64,1664]{1,0:T(8,128)(2,1)S(1)}, bf16[64,1664]{1,0:T(8,128)(2,1)S(1)}, u32[]{:S(2)}, u32[]{:S(2)}) collective-permute-start(bf16[64,1664]{1,0:T(8,128)(2,1)S(1)} %pad_maximum_fusion.1.refs_6_), channel_id=1, source_target_pairs={{0,2},{2,0},{4,6},{6,4},{8,10},{10,8},{12,14},{14,12},{16,18},{18,... | collective-permute-start | bytes 638984 | tf_op jit(solution)/shard_map/ppermute | solution.py:234
  33.0 11.0 %collective-permute-start.2 = (bf16[64,1664]{1,0:T(8,128)(2,1)S(1)}, bf16[64,1664]{1,0:T(8,128)(2,1)S(1)}, u32[]{:S(2)}, u32[]{:S(2)}) collective-permute-start(bf16[64,1664]{1,0:T(8,128)(2,1)S(1)} %pad_maximum_fusion.refs_4_), channel_id=1, source_target_pairs={{0,2},{2,0},{4,6},{6,4},{8,10},{10,8},{12,14},{14,12},{16,18},{18,... | collective-permute-start | bytes 638984 | tf_op jit(solution)/shard_map/ppermute | solution.py:234
  33.6 10.4 %collective-permute-start.1 = (bf16[64,1664]{1,0:T(8,128)(2,1)S(1)}, bf16[64,1664]{1,0:T(8,128)(2,1)S(1)}, u32[]{:S(2)}, u32[]{:S(2)}) collective-permute-start(bf16[64,1664]{1,0:T(8,128)(2,1)S(1)} %pad_maximum_fusion.refs_4_), channel_id=1, source_target_pairs={{0,4},{2,6},{4,0},{6,2},{8,12},{10,14},{12,8},{14,10},{16,20},{18,... | collective-permute-start | bytes 638984 | tf_op jit(solution)/shard_map/ppermute | solution.py:234
  35.7 11.9 %collective-permute-start.23 = (bf16[64,1664]{1,0:T(8,128)(2,1)S(1)}, bf16[64,1664]{1,0:T(8,128)(2,1)S(1)}, u32[]{:S(2)}, u32[]{:S(2)}) collective-permute-start(bf16[64,1664]{1,0:T(8,128)(2,1)S(1)} %pad_maximum_fusion.2.refs_4_), channel_id=1, source_target_pairs={{0,2},{2,0},{4,6},{6,4},{8,10},{10,8},{12,14},{14,12},{16,18},{18,... | collective-permute-start | bytes 638984 | tf_op jit(solution)/shard_map/ppermute | solution.py:234
  40.4 8.9 %collective-permute-start.22 = (bf16[64,1664]{1,0:T(8,128)(2,1)S(1)}, bf16[64,1664]{1,0:T(8,128)(2,1)S(1)}, u32[]{:S(2)}, u32[]{:S(2)}) collective-permute-start(bf16[64,1664]{1,0:T(8,128)(2,1)S(1)} %pad_maximum_fusion.2.refs_4_), channel_id=1, source_target_pairs={{0,4},{2,6},{4,0},{6,2},{8,12},{10,14},{12,8},{14,10},{16,20},{18,... | collective-permute-start | bytes 638984 | tf_op jit(solution)/shard_map/ppermute | solution.py:234
  44.0 7.5 %collective-permute-start.26 = (bf16[64,1664]{1,0:T(8,128)(2,1)S(1)}, bf16[64,1664]{1,0:T(8,128)(2,1)S(1)}, u32[]{:S(2)}, u32[]{:S(2)}) collective-permute-start(bf16[64,1664]{1,0:T(8,128)(2,1)S(1)} %pad_maximum_fusion.3.refs_6_), channel_id=1, source_target_pairs={{0,4},{2,6},{4,0},{6,2},{8,12},{10,14},{12,8},{14,10},{16,20},{18,... | collective-permute-start | bytes 638984 | tf_op jit(solution)/shard_map/ppermute | solution.py:234
  44.7 7.6 %collective-permute-start.25 = (bf16[64,1664]{1,0:T(8,128)(2,1)S(1)}, bf16[64,1664]{1,0:T(8,128)(2,1)S(1)}, u32[]{:S(2)}, u32[]{:S(2)}) collective-permute-start(bf16[64,1664]{1,0:T(8,128)(2,1)S(1)} %pad_maximum_fusion.3.refs_6_), channel_id=1, source_target_pairs={{0,2},{2,0},{4,6},{6,4},{8,10},{10,8},{12,14},{14,12},{16,18},{18,... | collective-permute-start | bytes 638984 | tf_op jit(solution)/shard_map/ppermute | solution.py:234
  47.6 7.6 %collective-permute-start.24 = (bf16[64,1664]{1,0:T(8,128)(2,1)S(1)}, bf16[64,1664]{1,0:T(8,128)(2,1)S(1)}, u32[]{:S(2)}, u32[]{:S(2)}) collective-permute-start(bf16[64,1664]{1,0:T(8,128)(2,1)S(1)} %collective-permute-done.23.refs_5_), channel_id=1, source_target_pairs={{0,4},{2,6},{4,0},{6,2},{8,12},{10,14},{12,8},{14,10},{16,20},{18,... | collective-permute-start | bytes 638984 | tf_op jit(solution)/shard_map/ppermute | solution.py:234
  50.0 20.6 %collective-permute-start.7 = (bf16[768,512]{1,0:T(8,128)(2,1)S(1)}, bf16[768,512]{1,0:T(8,128)(2,1)}, u32[]{:S(2)}, u32[]{:S(2)}) collective-permute-start(bf16[768,512]{1,0:T(8,128)(2,1)S(1)} %bitcast.7), channel_id=1, source_target_pairs={{0,8},{2,10},{4,12},{6,14},{8,0},{10,2},{12,4},{14,6},{16,24},{18,... | collective-permute-start | bytes 2359304 | tf_op jit(solution)/shard_map/ppermute | solution.py:234
  51.4 36.0 %collective-permute-start.9 = (bf16[768,512]{1,0:T(8,128)(2,1)S(1)}, bf16[768,512]{1,0:T(8,128)(2,1)}, u32[]{:S(2)}, u32[]{:S(2)}) collective-permute-start(bf16[768,512]{1,0:T(8,128)(2,1)S(1)} %bitcast.10), channel_id=1, source_target_pairs={{0,8},{2,10},{4,12},{6,14},{8,0},{10,2},{12,4},{14,6},{16,24},{18,... | collective-permute-start | bytes 2359304 | tf_op jit(solution)/shard_map/ppermute | solution.py:234
  55.9 43.0 %collective-permute-start.14 = (bf16[512,768]{1,0:T(8,128)(2,1)S(1)}, bf16[512,768]{1,0:T(8,128)(2,1)}, u32[]{:S(2)}, u32[]{:S(2)}) collective-permute-start(bf16[512,768]{1,0:T(8,128)(2,1)S(1)} %bitcast.14), channel_id=1, source_target_pairs={{0,8},{2,10},{4,12},{6,14},{8,0},{10,2},{12,4},{14,6},{16,24},{18,... | collective-permute-start | bytes 2359304 | tf_op jit(solution)/shard_map/ppermute | solution.py:234
  59.6 39.5 %collective-permute-start.12 = (bf16[768,512]{1,0:T(8,128)(2,1)S(1)}, bf16[768,512]{1,0:T(8,128)(2,1)}, u32[]{:S(2)}, u32[]{:S(2)}) collective-permute-start(bf16[768,512]{1,0:T(8,128)(2,1)S(1)} %bitcast.11), channel_id=1, source_target_pairs={{0,1},{1,0},{2,3},{3,2},{4,5},{5,4},{6,7},{7,6},{8,9},{9,8},{10,11... | collective-permute-start | bytes 2359304 | tf_op jit(solution)/shard_map/ppermute | solution.py:238
  59.6 41.0 %collective-permute-start.13 = (bf16[512,768]{1,0:T(8,128)(2,1)S(1)}, bf16[512,768]{1,0:T(8,128)(2,1)}, u32[]{:S(2)}, u32[]{:S(2)}) collective-permute-start(bf16[512,768]{1,0:T(8,128)(2,1)S(1)} %bitcast.15), channel_id=1, source_target_pairs={{0,1},{1,0},{2,3},{3,2},{4,5},{5,4},{6,7},{7,6},{8,9},{9,8},{10,11... | collective-permute-start | bytes 2359304 | tf_op jit(solution)/shard_map/ppermute | solution.py:238
  70.6 51.7 %collective-permute-start.8 = (bf16[768,512]{1,0:T(8,128)(2,1)}, bf16[768,512]{1,0:T(8,128)(2,1)}, u32[]{:S(2)}, u32[]{:S(2)}) collective-permute-start(bf16[768,512]{1,0:T(8,128)(2,1)} %collective-permute-done.7.refs_8_), channel_id=1, source_target_pairs={{0,1},{1,0},{2,3},{3,2},{4,5},{5,4},{6,7},{7,6},{8,9},{9,8},{10,11... | collective-permute-start | bytes 2359304 | tf_op jit(solution)/shard_map/ppermute | solution.py:238
  87.4 34.8 %collective-permute-start.10 = (bf16[768,512]{1,0:T(8,128)(2,1)}, bf16[768,512]{1,0:T(8,128)(2,1)}, u32[]{:S(2)}, u32[]{:S(2)}) collective-permute-start(bf16[768,512]{1,0:T(8,128)(2,1)} %collective-permute-done.9.refs_10_), channel_id=1, source_target_pairs={{0,1},{1,0},{2,3},{3,2},{4,5},{5,4},{6,7},{7,6},{8,9},{9,8},{10,11... | collective-permute-start | bytes 2359304 | tf_op jit(solution)/shard_map/ppermute | solution.py:238
  98.9 27.4 %collective-permute-start.15 = (bf16[512,768]{1,0:T(8,128)(2,1)}, bf16[512,768]{1,0:T(8,128)(2,1)}, u32[]{:S(2)}, u32[]{:S(2)}) collective-permute-start(bf16[512,768]{1,0:T(8,128)(2,1)} %collective-permute-done.14.down_a), channel_id=1, source_target_pairs={{0,1},{1,0},{2,3},{3,2},{4,5},{5,4},{6,7},{7,6},{8,9},{9,8},{10,11... | collective-permute-start | bytes 2359304 | tf_op jit(solution)/shard_map/ppermute | solution.py:238
  99.0 16.8 %collective-permute-start.6 = (bf16[64,1664]{1,0:T(8,128)(2,1)}, bf16[64,1664]{1,0:T(8,128)(2,1)S(1)}, u32[]{:S(2)}, u32[]{:S(2)}) collective-permute-start(bf16[64,1664]{1,0:T(8,128)(2,1)} %copy-done.11), channel_id=1, source_target_pairs={{0,2},{2,0},{4,6},{6,4},{8,10},{10,8},{12,14},{14,12},{16,18},{18,... | collective-permute-start | bytes 638984 | tf_op jit(solution)/shard_map/ppermute | solution.py:234
  100.5 15.3 %collective-permute-start.3 = (bf16[64,1664]{1,0:T(8,128)(2,1)}, bf16[64,1664]{1,0:T(8,128)(2,1)S(1)}, u32[]{:S(2)}, u32[]{:S(2)}) collective-permute-start(bf16[64,1664]{1,0:T(8,128)(2,1)} %copy-done.15), channel_id=1, source_target_pairs={{0,4},{2,6},{4,0},{6,2},{8,12},{10,14},{12,8},{14,10},{16,20},{18,... | collective-permute-start | bytes 638984 | tf_op jit(solution)/shard_map/ppermute | solution.py:234
  129.6 11.5 %collective-permute-start.28 = (bf16[128,1536]{1,0:T(8,128)(2,1)S(1)}, bf16[128,1536]{1,0:T(8,128)(2,1)S(1)}, u32[]{:S(2)}, u32[]{:S(2)}) collective-permute-start(bf16[128,1536]{1,0:T(8,128)(2,1)S(1)} %get-tuple-element.45), channel_id=1, source_target_pairs={{0,4},{2,6},{4,0},{6,2},{8,12},{10,14},{12,8},{14,10},{16,20},{18,... | collective-permute-start | bytes 1179656 | tf_op jit(solution)/shard_map/ppermute | solution.py:234
  130.2 11.6 %collective-permute-start.30 = (bf16[128,1536]{1,0:T(8,128)(2,1)S(1)}, bf16[128,1536]{1,0:T(8,128)(2,1)S(1)}, u32[]{:S(2)}, u32[]{:S(2)}) collective-permute-start(bf16[128,1536]{1,0:T(8,128)(2,1)S(1)} %get-tuple-element.49), channel_id=1, source_target_pairs={{0,2},{2,0},{4,6},{6,4},{8,10},{10,8},{12,14},{14,12},{16,18},{18,... | collective-permute-start | bytes 1179656 | tf_op jit(solution)/shard_map/ppermute | solution.py:234
  138.1 12.1 %collective-permute-start.16 = (bf16[128,1536]{1,0:T(8,128)(2,1)S(1)}, bf16[128,1536]{1,0:T(8,128)(2,1)S(1)}, u32[]{:S(2)}, u32[]{:S(2)}) collective-permute-start(bf16[128,1536]{1,0:T(8,128)(2,1)S(1)} %get-tuple-element.32), channel_id=1, source_target_pairs={{0,4},{2,6},{4,0},{6,2},{8,12},{10,14},{12,8},{14,10},{16,20},{18,... | collective-permute-start | bytes 1179656 | tf_op jit(solution)/shard_map/ppermute | solution.py:234
  139.6 12.2 %collective-permute-start.18 = (bf16[128,1536]{1,0:T(8,128)(2,1)S(1)}, bf16[128,1536]{1,0:T(8,128)(2,1)S(1)}, u32[]{:S(2)}, u32[]{:S(2)}) collective-permute-start(bf16[128,1536]{1,0:T(8,128)(2,1)S(1)} %get-tuple-element.36), channel_id=1, source_target_pairs={{0,2},{2,0},{4,6},{6,4},{8,10},{10,8},{12,14},{14,12},{16,18},{18,... | collective-permute-start | bytes 1179656 | tf_op jit(solution)/shard_map/ppermute | solution.py:234
  141.2 14.7 %collective-permute-start.29 = (bf16[64,1536]{1,0:T(8,128)(2,1)S(1)}, bf16[64,1536]{1,0:T(8,128)(2,1)S(1)}, u32[]{:S(2)}, u32[]{:S(2)}) collective-permute-start(bf16[64,1536]{1,0:T(8,128)(2,1)S(1)} %get-tuple-element.47), channel_id=1, source_target_pairs={{0,2},{2,0},{4,6},{6,4},{8,10},{10,8},{12,14},{14,12},{16,18},{18,... | collective-permute-start | bytes 589832 | tf_op jit(solution)/shard_map/ppermute | solution.py:234
  141.9 14.0 %collective-permute-start.31 = (bf16[64,1536]{1,0:T(8,128)(2,1)S(1)}, bf16[64,1536]{1,0:T(8,128)(2,1)S(1)}, u32[]{:S(2)}, u32[]{:S(2)}) collective-permute-start(bf16[64,1536]{1,0:T(8,128)(2,1)S(1)} %get-tuple-element.51), channel_id=1, source_target_pairs={{0,4},{2,6},{4,0},{6,2},{8,12},{10,14},{12,8},{14,10},{16,20},{18,... | collective-permute-start | bytes 589832 | tf_op jit(solution)/shard_map/ppermute | solution.py:234
  150.2 9.2 %collective-permute-start.17 = (bf16[64,1536]{1,0:T(8,128)(2,1)S(1)}, bf16[64,1536]{1,0:T(8,128)(2,1)S(1)}, u32[]{:S(2)}, u32[]{:S(2)}) collective-permute-start(bf16[64,1536]{1,0:T(8,128)(2,1)S(1)} %get-tuple-element.34), channel_id=1, source_target_pairs={{0,2},{2,0},{4,6},{6,4},{8,10},{10,8},{12,14},{14,12},{16,18},{18,... | collective-permute-start | bytes 589832 | tf_op jit(solution)/shard_map/ppermute | solution.py:234
  151.9 7.6 %collective-permute-start.19 = (bf16[64,1536]{1,0:T(8,128)(2,1)S(1)}, bf16[64,1536]{1,0:T(8,128)(2,1)S(1)}, u32[]{:S(2)}, u32[]{:S(2)}) collective-permute-start(bf16[64,1536]{1,0:T(8,128)(2,1)S(1)} %get-tuple-element.38), channel_id=1, source_target_pairs={{0,4},{2,6},{4,0},{6,2},{8,12},{10,14},{12,8},{14,10},{16,20},{18,... | collective-permute-start | bytes 589832 | tf_op jit(solution)/shard_map/ppermute | solution.py:234
  156.0 15.3 %collective-permute-start.32 = (bf16[64,1536]{1,0:T(8,128)(2,1)S(1)}, bf16[64,1536]{1,0:T(8,128)(2,1)S(1)}, u32[]{:S(2)}, u32[]{:S(2)}) collective-permute-start(bf16[64,1536]{1,0:T(8,128)(2,1)S(1)} %get-tuple-element.53), channel_id=1, source_target_pairs={{0,16},{2,18},{4,20},{6,22},{8,24},{10,26},{12,28},{14,30},{16,0},... | collective-permute-start | bytes 589832 | tf_op jit(solution)/shard_map/ppermute | solution.py:234
  159.5 13.9 %collective-permute-start.20 = (bf16[64,1536]{1,0:T(8,128)(2,1)S(1)}, bf16[64,1536]{1,0:T(8,128)(2,1)S(1)}, u32[]{:S(2)}, u32[]{:S(2)}) collective-permute-start(bf16[64,1536]{1,0:T(8,128)(2,1)S(1)} %get-tuple-element.40), channel_id=1, source_target_pairs={{0,16},{2,18},{4,20},{6,22},{8,24},{10,26},{12,28},{14,30},{16,0},... | collective-permute-start | bytes 589832 | tf_op jit(solution)/shard_map/ppermute | solution.py:234
  (40 other events, 518.9 us)

commit v3 on v2

--- a/solution.py
+++ b/solution.py
@@ -9,7 +9,6 @@
 
 EPS = 1e-05
 PACK = 128
-VMEM_LIMIT = 48 * 1024 * 1024
 X, Y, Z_LOW, Z_HIGH = 1, 2, 4, 8
 
 
@@ -81,71 +80,80 @@
     return tuple(outs)
 
 
-def call(body, outs, ins, flops=0, moved=0, scratch=()):
+def call(body, outs, ins, vmem_mb, flops=0, moved=0, scratch=(), specs=None):
     smem = pl.BlockSpec(memory_space=pltpu.SMEM)
     vmem = pl.BlockSpec(memory_space=pltpu.VMEM)
     return pl.pallas_call(
         body,
         out_shape=outs,
-        in_specs=[smem if x.ndim == 1 and x.dtype == jnp.int32 else vmem for x in ins],
+        in_specs=specs
+        or [smem if x.ndim == 1 and x.dtype == jnp.int32 else vmem for x in ins],
         out_specs=jax.tree.map(lambda _: vmem, outs),
         scratch_shapes=list(scratch),
-        compiler_params=pltpu.CompilerParams(vmem_limit_bytes=VMEM_LIMIT),
+        compiler_params=pltpu.CompilerParams(vmem_limit_bytes=vmem_mb * 1024 * 1024),
         cost_estimate=pl.CostEstimate(flops=flops, bytes_accessed=moved, transcendentals=0),
     )(*ins)
 
 
-def prepare_kernel(
-    source_ref, one_ref, two_ref, gain_ref, slots_one_ref, slots_two_ref, gates_one_ref, gates_two_ref,
-    out_one_ref, out_two_ref,
-):
-    group = source_ref.shape[0]
-    gain = gain_ref[...].astype(jnp.float32)
-    width = one_ref.shape[1]
-    for tokens_ref, slots_ref, gates_ref, out_ref, moved in (
-        (one_ref, slots_one_ref, gates_one_ref, out_one_ref, False),
-        (two_ref, slots_two_ref, gates_two_ref, out_two_ref, True),
-    ):
+def prepare_kernel(old_ref, new_ref, *refs):
+    hbm, outs, held, sems = refs[:7], refs[7:9], refs[9:16], refs[16]
+    copies = [pltpu.make_async_copy(a, b, sems.at[i]) for i, (a, b) in enumerate(zip(hbm, held))]
+    for copy in copies:
+        copy.start()
+    group = old_ref.shape[0]
+    sources = []
+    for s in range(group):
+        left, right = (s - 1) % group, (s + 1) % group
+        wanted = new_ref[s]
+        other = jnp.where(wanted == old_ref[left], left, right)
+        sources.append(jnp.where(wanted == old_ref[s], s, other))
+    for copy in copies:
+        copy.wait()
+    gain = held[0][...].astype(jnp.float32).reshape(1, -1)
+    for b in range(2):
+        tokens_ref, slots_ref, gates_ref = held[1 + b], held[3 + b], held[5 + b]
+        out_ref = outs[b]
+        tok, width = tokens_ref.shape
         values = tokens_ref[...].astype(jnp.float32)
         square = jnp.mean(values * values, axis=-1, keepdims=True)
         out_ref[:, :width] = (values * lax.rsqrt(square + EPS) * gain).astype(jnp.bfloat16)
-        slots = slots_ref[...]
-        if moved:
+        slots, gates = slots_ref[...], gates_ref[...]
+        if b == 1:
             holder = jnp.zeros_like(slots)
             for s in range(group):
-                holder = jnp.where(slots == s, source_ref[s], holder)
+                holder = jnp.where(slots == s, sources[s], holder)
             slots = holder
-        gates = gates_ref[...]
-        lane = lax.broadcasted_iota(jnp.int32, (slots.shape[0], PACK), 1)
-        expert = lane & (group - 1)
-        total = jnp.zeros((slots.shape[0], PACK), jnp.float32)
-        for k in range(slots.shape[1]):
-            total += jnp.where(expert == slots[:, k : k + 1], gates[:, k : k + 1], 0.0)
-        high = total.astype(jnp.bfloat16).astype(jnp.float32)
-        rest = total - high
-        middle = rest.astype(jnp.bfloat16).astype(jnp.float32)
-        low = rest - middle
-        piece = lane // group
-        packed = jnp.where(
-            piece == 0, high, jnp.where(piece == 1, middle, jnp.where(piece == 2, low, 0.0))
-        )
-        out_ref[:, width:] = packed.astype(jnp.bfloat16)
-
-
-def hidden_of(place, rows_ref, gate_refs, up_refs, begin, count):
-    depth = gate_refs[0].shape[0]
-    acts = []
-    for refs in (gate_refs, up_refs):
-        act = None
-        for which, ref in enumerate(refs):
-            half = place if which == 0 else 1 - place
-            columns = pl.ds(pl.multiple_of(half * depth, depth), depth)
-            term = jnp.dot(
-                rows_ref[pl.ds(begin, count), columns], ref[...], preferred_element_type=jnp.float32
-            )
-            act = term if act is None else act + term
-        acts.append(act)
-    gate_act, up_act = acts
+        expert = lax.broadcasted_iota(jnp.int32, (group, tok), 0)
+        total = jnp.zeros((group, tok), jnp.float32)
+        for k in range(slots.shape[0]):
+            total += jnp.where(expert == slots[k : k + 1, :], gates[k : k + 1, :], 0.0)
+        high = total.astype(jnp.bfloat16)
+        rest = total - high.astype(jnp.float32)
+        middle = rest.astype(jnp.bfloat16)
+        low = (rest - middle.astype(jnp.float32)).astype(jnp.bfloat16)
+        packed = jnp.concatenate([high, middle, low], axis=0)
+        row = lax.broadcasted_iota(jnp.int32, (3 * group, PACK), 0)
+        lane = lax.broadcasted_iota(jnp.int32, (3 * group, PACK), 1)
+        turned = lax.dot_general(
+            packed,
+            (row == lane).astype(jnp.bfloat16),
+            (((0,), (0,)), ((), ())),
+            preferred_element_type=jnp.float32,
+        )
+        out_ref[:, width:] = turned.astype(jnp.bfloat16)
+
+
+def hidden_of(place, rows_ref, both_refs, begin, count):
+    depth, ff = both_refs[0].shape[0], both_refs[0].shape[1] // 2
+    acts = None
+    for which, ref in enumerate(both_refs):
+        half = place if which == 0 else 1 - place
+        columns = pl.ds(pl.multiple_of(half * depth, depth), depth)
+        term = jnp.dot(
+            rows_ref[pl.ds(begin, count), columns], ref[...], preferred_element_type=jnp.float32
+        )
+        acts = term if acts is None else acts + term
+    gate_act, up_act = acts[:, :ff], acts[:, ff:]
     return (gate_act / (1.0 + jnp.exp(-gate_act)) * up_act).astype(jnp.bfloat16)
 
 
@@ -157,7 +165,7 @@
 
 def own_kernel(pieces, group, place_ref, *refs):
     piece_refs, refs = refs[:pieces], refs[pieces:]
-    gate_a, gate_b, up_a, up_b, down_a, down_b, total_ref, rows_ref = refs
+    both_a, both_b, down_a, down_b, total_ref, rows_ref = refs
     tok = piece_refs[0].shape[0]
     width = total_ref.shape[1]
     for i, ref in enumerate(piece_refs):
@@ -168,7 +176,7 @@
     @pl.loop(0, rows_ref.shape[0] // block)
     def _(step):
         begin = pl.multiple_of(step * block, block)
-        hidden = hidden_of(place, rows_ref, (gate_a, gate_b), (up_a, up_b), begin, block)
+        hidden = hidden_of(place, rows_ref, (both_a, both_b), begin, block)
         weight = weight_of(place_ref[1], group, rows_ref[pl.ds(begin, block), width:])
         for which, ref in enumerate((down_a, down_b)):
             half = place if which == 0 else 1 - place
@@ -179,7 +187,7 @@
 
 def beside_kernel(pieces, group, place_ref, *refs):
     piece_refs, refs = refs[:pieces], refs[pieces:]
-    gate_a, gate_b, up_a, up_b, hidden_ref, weight_ref, rows_ref = refs
+    both_a, both_b, hidden_ref, weight_ref, rows_ref = refs
     tok = piece_refs[0].shape[0]
     width = rows_ref.shape[1] - PACK
     for i, ref in enumerate(piece_refs):
@@ -190,7 +198,7 @@
     def _(step):
         begin = pl.multiple_of(step * block, block)
         hidden_ref[pl.ds(begin, block), :] = hidden_of(
-            place_ref[0], rows_ref, (gate_a, gate_b), (up_a, up_b), begin, block
+            place_ref[0], rows_ref, (both_a, both_b), begin, block
         )
         weight = weight_of(place_ref[1] ^ Z_LOW, group, rows_ref[pl.ds(begin, block), width:])
         weight_ref[pl.ds(begin, block), :] = jnp.broadcast_to(weight, (block, PACK))
@@ -255,14 +263,14 @@
     f32 = jax.ShapeDtypeStruct((quarter, width), jnp.float32)
     size = quarter * width
     got_a, got_b = swap(send_a, Y), swap(send_b, X)
-    next_a, held_a = call(first_sum_kernel, (bf, f32), (keep_a, got_a), size, 18 * size)
-    next_b, held_b = call(first_sum_kernel, (bf, f32), (keep_b, got_b), size, 18 * size)
+    next_a, held_a = call(first_sum_kernel, (bf, f32), (keep_a, got_a), 8, size, 18 * size)
+    next_b, held_b = call(first_sum_kernel, (bf, f32), (keep_b, got_b), 8, size, 18 * size)
     got_a, got_b = swap(next_a, X), swap(next_b, Y)
     next_z, held_z = call(
-        second_sum_kernel, (bf, f32), (held_a, got_a, held_b, got_b), size, 18 * size
+        second_sum_kernel, (bf, f32), (held_a, got_a, held_b, got_b), 8, size, 18 * size
     )
     got_z = swap(next_z, Z_HIGH)
-    return call(last_sum_kernel, bf, (held_z, got_z), size, 8 * size)
+    return call(last_sum_kernel, bf, (held_z, got_z), 8, size, 8 * size)
 
 
 def local_pairs(
@@ -282,35 +290,37 @@
     group = table_old.shape[0]
     tok, width = batch_one.shape
     place = jnp.stack([lax.axis_index("tensor"), lax.axis_index("expert")]).astype(jnp.int32)
-    mine = (gate_old[0], up_old[0], down_old[0])
+    tables = [pl.BlockSpec(memory_space=pltpu.SMEM)] * 2
+    ins = (
+        norm_gain, batch_one, batch_two, slots_one.T, slots_two.T, gates_one.T, gates_two.T
+    )
     own = call(
         prepare_kernel,
         (jax.ShapeDtypeStruct((tok, width + PACK), jnp.bfloat16),) * 2,
-        (
-            source_slots(table_old, table_new),
-            batch_one,
-            batch_two,
-            norm_gain.reshape(1, width),
-            slots_one,
-            slots_two,
-            gates_one,
-            gates_two,
-        ),
+        (table_old, table_new, *ins),
+        8,
         10 * tok * width,
         8 * tok * width,
-    )
-    twins = tuple(swap_core(w) for w in mine)
-    beside = tuple(swap(w, Z_LOW) for w in mine)
-    beside_twins = tuple(swap_core(w) for w in beside)
+        [pltpu.VMEM(x.shape, x.dtype) for x in ins] + [pltpu.SemaphoreType.DMA((len(ins),))],
+        tables + [pl.BlockSpec(memory_space=pl.ANY)] * len(ins),
+    )
+    both = jnp.concatenate([gate_old[0], up_old[0]], axis=1)
+    down = down_old[0]
+    beside_both = swap(both, Z_LOW)
+    twin_both, twin_down = swap_core(both), swap_core(down)
+    pieces = [spread(x) for x in own]
+    down_later, beside_both, pieces = lax.optimization_barrier((down, beside_both, pieces))
+    beside_down = swap(down_later, Z_LOW)
+    beside_twin_both = swap_core(beside_both)
     ff = gate_old.shape[2]
     rows = 8 * tok
-    pieces = [spread(x) for x in own]
     scratch = (pltpu.VMEM((rows, width + PACK), jnp.bfloat16),)
     totals = [
         call(
             functools.partial(own_kernel, 8, group),
             jax.ShapeDtypeStruct((rows, width), jnp.float32),
-            (place, *p, mine[0], twins[0], mine[1], twins[1], mine[2], twins[2]),
+            (place, *p, both, twin_both, down, twin_down),
+            20,
             6 * rows * width * ff,
             6 * width * ff + 6 * rows * width,
             scratch,
@@ -324,20 +334,24 @@
                 jax.ShapeDtypeStruct((rows, ff), jnp.bfloat16),
                 jax.ShapeDtypeStruct((rows, PACK), jnp.float32),
             ),
-            (place, *p, beside[0], beside_twins[0], beside[1], beside_twins[1]),
+            (place, *p, beside_both, beside_twin_both),
+            16,
             4 * rows * width * ff,
             4 * width * ff + 2 * rows * width,
             scratch,
         )
         for p in pieces
     ]
+    beside_down, totals, hidden[0] = lax.optimization_barrier((beside_down, totals, hidden[0]))
+    beside_twin_down = swap_core(beside_down)
     outs = []
     for total, (hid, weight) in zip(totals, hidden):
         parts = call(
             join_kernel,
             (jax.ShapeDtypeStruct((2 * tok, width), jnp.bfloat16),) * 2
             + (jax.ShapeDtypeStruct((2 * tok, width), jnp.float32),) * 2,
-            (place, hid, weight, total, beside[2], beside_twins[2]),
+            (place, hid, weight, total, beside_down, beside_twin_down),
+            14,
             2 * rows * width * ff,
             2 * width * ff + 8 * rows * width,
         )

time: 175 us -> 142 us (0.81)
  waiting for transfers between devices: 84.3 us -> 54.1 us
  Pallas kernels: 30 us -> 24.9 us
    ppermute x27 -> x26, waiting for transfers between devices: 84.2 us -> 50.9 us  [swap(): lax.ppermute(block, 'expert', [(i, i ^ distance) for i in range(count)])]
    pallas_call x15, Pallas kernels: 30 us -> 24.9 us  [call(): pl.pallas_call(body, out_shape=outs, in_specs=specs or [smem if x.ndim ==...]
    unnamed x82 -> x92, local copies, waits for them, and re-layouts: 18.7 us -> 22.1 us
    ppermute x6 -> x4, waiting for transfers between devices: 0.02 us -> 3.21 us  [swap_core(): return lax.ppermute(block, 'tensor', [(0, 1), (1, 0)])]
    ppermute x27 -> x26, starting transfers between devices: 35.9 us -> 36.9 us  [swap(): lax.ppermute(block, 'expert', [(i, i ^ distance) for i in range(count)])]
  transfers between devices with their start and end apart: 33 -> 30, of which waited for: 14 -> 18; matrix products, arithmetic and copies ran while one was open for 0% -> 1% of each run, Pallas kernels for 14% -> 15%
where the time goes in v3:
time: 142 us
  waiting for transfers between devices  54.1 us (38%)
  starting transfers between devices  37.6 us (26%)
  Pallas kernels  24.9 us (18%)
  local copies, waits for them, and re-layouts  22.2 us (16%)
  other arithmetic  1.7 us (1%)
    ppermute x26, waiting for transfers between devices, swap(): lax.ppermute(block, 'expert', [(i, i ^ distance) for i in range(count)])  50.9 us
    ppermute x26, starting transfers between devices, swap(): lax.ppermute(block, 'expert', [(i, i ^ distance) for i in range(count)])  36.9 us
    pallas_call x15, Pallas kernels, call(): pl.pallas_call(body, out_shape=outs, in_specs=specs or [smem if x.ndim ==...  24.9 us
    unnamed x92, local copies, waits for them, and re-layouts  22.1 us
    ppermute x4, waiting for transfers between devices, swap_core(): return lax.ppermute(block, 'tensor', [(0, 1), (1, 0)])  3.21 us
  transfers between devices with their start and end apart: 30, of which 18 were waited for; matrix products, arithmetic and copies ran while one was open for 1% of the time, Pallas kernels for 15%

profile of v3, /device:TPU:0, one launch (start us, length us, event | category | flops | bytes accessed | tf_op | source)
XLA Modules:
  0.0 141.7 jit_solution(14903296749051822106)
XLA Ops:
  8.6 4.1 %collective-permute-start.8 = (bf16[64,1664]{1,0:T(8,128)(2,1)S(1)}, bf16[64,1664]{1,0:T(8,128)(2,1)S(1)}, u32[]{:S(2)}, u32[]{:S(2)}) collective-permute-start(bf16[64,1664]{1,0:T(8,128)(2,1)S(1)} %get-tuple-element.52), channel_id=1, source_target_pairs={{0,16},{2,18},{4,20},{6,22},{8,24},{10,26},{12,28},{14,30},{16,0},... | collective-permute-start | bytes 638984 | tf_op jit(solution)/shard_map/ppermute | solution.py:242
  14.4 1.9 %collective-permute-start = (bf16[768,1024]{1,0:T(8,128)(2,1)S(1)}, bf16[768,1024]{1,0:T(8,128)(2,1)}, u32[]{:S(2)}, u32[]{:S(2)}) collective-permute-start(bf16[768,1024]{1,0:T(8,128)(2,1)S(1)} %pad_maximum_fusion.refs_8_), channel_id=1, source_target_pairs={{0,8},{2,10},{4,12},{6,14},{8,0},{10,2},{12,4},{14,6},{16,24},{18,... | collective-permute-start | bytes 4718600 | tf_op jit(solution)/shard_map/ppermute | solution.py:242
  16.3 11.7 %collective-permute-done.8 = bf16[64,1664]{1,0:T(8,128)(2,1)S(1)} collective-permute-done((bf16[64,1664]{1,0:T(8,128)(2,1)S(1)}, bf16[64,1664]{1,0:T(8,128)(2,1)S(1)}, u32[]{:S(2)}, u32[]{:S(2)}) %collective-permute-start.8) | collective-permute-done | bytes 213024 | tf_op jit(solution)/shard_map/ppermute | solution.py:242
  28.1 1.9 %collective-permute-start.10 = (bf16[64,1664]{1,0:T(8,128)(2,1)S(1)}, bf16[64,1664]{1,0:T(8,128)(2,1)S(1)}, u32[]{:S(2)}, u32[]{:S(2)}) collective-permute-start(bf16[64,1664]{1,0:T(8,128)(2,1)S(1)} %pad_maximum_fusion.3.refs_4_), channel_id=1, source_target_pairs={{0,2},{2,0},{4,6},{6,4},{8,10},{10,8},{12,14},{14,12},{16,18},{18,... | collective-permute-start | bytes 638984 | tf_op jit(solution)/shard_map/ppermute | solution.py:242
  30.0 1.6 %collective-permute-start.13 = (bf16[64,1664]{1,0:T(8,128)(2,1)S(1)}, bf16[64,1664]{1,0:T(8,128)(2,1)S(1)}, u32[]{:S(2)}, u32[]{:S(2)}) collective-permute-start(bf16[64,1664]{1,0:T(8,128)(2,1)S(1)} %pad_maximum_fusion.4.refs_6_), channel_id=1, source_target_pairs={{0,4},{2,6},{4,0},{6,2},{8,12},{10,14},{12,8},{14,10},{16,20},{18,... | collective-permute-start | bytes 638984 | tf_op jit(solution)/shard_map/ppermute | solution.py:242
  31.8 1.6 %collective-permute-start.3 = (bf16[64,1664]{1,0:T(8,128)(2,1)S(1)}, bf16[64,1664]{1,0:T(8,128)(2,1)S(1)}, u32[]{:S(2)}, u32[]{:S(2)}) collective-permute-start(bf16[64,1664]{1,0:T(8,128)(2,1)S(1)} %pad_maximum_fusion.1.refs_4_), channel_id=1, source_target_pairs={{0,2},{2,0},{4,6},{6,4},{8,10},{10,8},{12,14},{14,12},{16,18},{18,... | collective-permute-start | bytes 638984 | tf_op jit(solution)/shard_map/ppermute | solution.py:242
  33.5 1.6 %collective-permute-start.6 = (bf16[64,1664]{1,0:T(8,128)(2,1)S(1)}, bf16[64,1664]{1,0:T(8,128)(2,1)S(1)}, u32[]{:S(2)}, u32[]{:S(2)}) collective-permute-start(bf16[64,1664]{1,0:T(8,128)(2,1)S(1)} %pad_maximum_fusion.2.refs_6_), channel_id=1, source_target_pairs={{0,4},{2,6},{4,0},{6,2},{8,12},{10,14},{12,8},{14,10},{16,20},{18,... | collective-permute-start | bytes 638984 | tf_op jit(solution)/shard_map/ppermute | solution.py:242
  35.1 1.6 %collective-permute-start.12 = (bf16[64,1664]{1,0:T(8,128)(2,1)S(1)}, bf16[64,1664]{1,0:T(8,128)(2,1)S(1)}, u32[]{:S(2)}, u32[]{:S(2)}) collective-permute-start(bf16[64,1664]{1,0:T(8,128)(2,1)S(1)} %pad_maximum_fusion.4.refs_6_), channel_id=1, source_target_pairs={{0,2},{2,0},{4,6},{6,4},{8,10},{10,8},{12,14},{14,12},{16,18},{18,... | collective-permute-start | bytes 638984 | tf_op jit(solution)/shard_map/ppermute | solution.py:242
  40.1 1.6 %collective-permute-done.6.refs_7_ = bf16[64,1664]{1,0:T(8,128)(2,1)S(1)} collective-permute-done((bf16[64,1664]{1,0:T(8,128)(2,1)S(1)}, bf16[64,1664]{1,0:T(8,128)(2,1)S(1)}, u32[]{:S(2)}, u32[]{:S(2)}) %collective-permute-start.6) | collective-permute-done | bytes 213024 | tf_op jit(solution)/shard_map/ppermute | solution.py:242
  43.8 2.0 %collective-permute-start.9 = (bf16[64,1664]{1,0:T(8,128)(2,1)S(1)}, bf16[64,1664]{1,0:T(8,128)(2,1)S(1)}, u32[]{:S(2)}, u32[]{:S(2)}) collective-permute-start(bf16[64,1664]{1,0:T(8,128)(2,1)S(1)} %pad_maximum_fusion.3.refs_4_), channel_id=1, source_target_pairs={{0,4},{2,6},{4,0},{6,2},{8,12},{10,14},{12,8},{14,10},{16,20},{18,... | collective-permute-start | bytes 638984 | tf_op jit(solution)/shard_map/ppermute | solution.py:242
  48.7 1.6 %collective-permute-start.14 = (bf16[64,1664]{1,0:T(8,128)(2,1)S(1)}, bf16[64,1664]{1,0:T(8,128)(2,1)S(1)}, u32[]{:S(2)}, u32[]{:S(2)}) collective-permute-start(bf16[64,1664]{1,0:T(8,128)(2,1)S(1)} %collective-permute-done.13.refs_7_), channel_id=1, source_target_pairs={{0,2},{2,0},{4,6},{6,4},{8,10},{10,8},{12,14},{14,12},{16,18},{18,... | collective-permute-start | bytes 638984 | tf_op jit(solution)/shard_map/ppermute | solution.py:242
  52.7 2.0 %collective-permute-start.4 = (bf16[64,1664]{1,0:T(8,128)(2,1)S(1)}, bf16[64,1664]{1,0:T(8,128)(2,1)S(1)}, u32[]{:S(2)}, u32[]{:S(2)}) collective-permute-start(bf16[64,1664]{1,0:T(8,128)(2,1)S(1)} %collective-permute-done.3.refs_5_), channel_id=1, source_target_pairs={{0,4},{2,6},{4,0},{6,2},{8,12},{10,14},{12,8},{14,10},{16,20},{18,... | collective-permute-start | bytes 638984 | tf_op jit(solution)/shard_map/ppermute | solution.py:242
  57.2 2.0 %collective-permute-start.7 = (bf16[64,1664]{1,0:T(8,128)(2,1)S(1)}, bf16[64,1664]{1,0:T(8,128)(2,1)S(1)}, u32[]{:S(2)}, u32[]{:S(2)}) collective-permute-start(bf16[64,1664]{1,0:T(8,128)(2,1)S(1)} %collective-permute-done.6.refs_7_), channel_id=1, source_target_pairs={{0,2},{2,0},{4,6},{6,4},{8,10},{10,8},{12,14},{14,12},{16,18},{18,... | collective-permute-start | bytes 638984 | tf_op jit(solution)/shard_map/ppermute | solution.py:242
  61.3 1.8 %collective-permute-done.7.refs_3_ = bf16[64,1664]{1,0:T(8,128)(2,1)S(1)} collective-permute-done((bf16[64,1664]{1,0:T(8,128)(2,1)S(1)}, bf16[64,1664]{1,0:T(8,128)(2,1)S(1)}, u32[]{:S(2)}, u32[]{:S(2)}) %collective-permute-start.7) | collective-permute-done | bytes 213024 | tf_op jit(solution)/shard_map/ppermute | solution.py:242
  65.5 3.2 %collective-permute-done.17.refs_11_ = bf16[512,768]{1,0:T(8,128)(2,1)} collective-permute-done((bf16[512,768]{1,0:T(8,128)(2,1)}, bf16[512,768]{1,0:T(8,128)(2,1)}, u32[]{:S(2)}, u32[]{:S(2)}) %collective-permute-start.17) | collective-permute-done | bytes 786464 | tf_op jit(solution)/shard_map/ppermute | solution.py:246
  75.3 4.6 %shard_map.133.total_ref = f32[512,1536]{1,0:T(8,128)S(1)} custom-call(s32[2]{0:T(128)S(1)} %pad_add_fusion.place_ref, bf16[64,1664]{1,0:T(8,128)(2,1)S(1)} %copy-done.23, bf16[64,1664]{1,0:T(8,128)(2,1)S(1)} %copy-done.26, bf16[64,1664]{1,0:T(8,128)(2,1)S(1)} %copy-done.14, bf16[64,1664]{1,0:T(8,128)(2,1)S(1)} %copy-done.29, ...), custom_call_target="tpu_custom_call" | custom-call | flops 2415919104 | bytes 9437184 | tf_op jit(solution)/shard_map/pallas_call | solution.py:86
  80.0 4.5 %shard_map.132.total_ref = f32[512,1536]{1,0:T(8,128)S(1)} custom-call(s32[2]{0:T(128)S(1)} %pad_add_fusion.place_ref, bf16[64,1664]{1,0:T(8,128)(2,1)S(1)} %copy-done.21, bf16[64,1664]{1,0:T(8,128)(2,1)S(1)} %copy-done.34, bf16[64,1664]{1,0:T(8,128)(2,1)S(1)} %copy-done.32, bf16[64,1664]{1,0:T(8,128)(2,1)S(1)} %copy-done.36, ...), custom_call_target="tpu_custom_call" | custom-call | flops 2415919104 | bytes 9437184 | tf_op jit(solution)/shard_map/pallas_call | solution.py:86
  84.7 4.1 %shard_map.134 = (bf16[512,512]{1,0:T(8,128)(2,1)S(1)}, f32[512,128]{1,0:T(8,128)S(1)}) custom-call(s32[2]{0:T(128)S(1)} %pad_add_fusion.place_ref, bf16[64,1664]{1,0:T(8,128)(2,1)S(1)} %copy-done.21, bf16[64,1664]{1,0:T(8,128)(2,1)S(1)} %copy-done.34, bf16[64,1664]{1,0:T(8,128)(2,1)S(1)} %copy-done.32, bf16[64,1664]{1,0:T(8,128)(2,1)S(1)} %copy-done.36, ...), custom_call_target="tpu_custom_call" | custom-call | flops 1610612736 | bytes 4718592 | tf_op jit(solution)/shard_map/pallas_call | solution.py:86
  89.0 4.0 %shard_map.140 = (bf16[512,512]{1,0:T(8,128)(2,1)S(1)}, f32[512,128]{1,0:T(8,128)S(1)}) custom-call(s32[2]{0:T(128)S(1)} %pad_add_fusion.place_ref, bf16[64,1664]{1,0:T(8,128)(2,1)S(1)} %copy-done.24, bf16[64,1664]{1,0:T(8,128)(2,1)S(1)} %copy-done.27, bf16[64,1664]{1,0:T(8,128)(2,1)S(1)} %copy-done.15, bf16[64,1664]{1,0:T(8,128)(2,1)S(1)} %copy-done.30, ...), custom_call_target="tpu_custom_call" | custom-call | flops 1610612736 | bytes 4718592 | tf_op jit(solution)/shard_map/pallas_call | solution.py:86
  93.1 2.2 %shard_map.141 = (bf16[128,1536]{1,0:T(8,128)(2,1)S(1)}, bf16[128,1536]{1,0:T(8,128)(2,1)S(1)}, f32[128,1536]{1,0:T(8,128)S(1)}, f32[128,1536]{1,0:T(8,128)S(1)}) custom-call(s32[2]{0:T(128)S(1)} %pad_add_fusion.place_ref, bf16[512,512]{1,0:T(8,128)(2,1)S(1)} %get-tuple-element.87.hidden_ref, f32[512,128]{1,0:T(8,128)S(1)} %get-tuple-element.88.weight_ref, ...), custom_call_target="tpu_custom_call" | custom-call | flops 805306368 | bytes 7864320 | tf_op jit(solution)/shard_map/pallas_call | solution.py:86
  95.3 2.0 %collective-permute-start.27 = (bf16[128,1536]{1,0:T(8,128)(2,1)S(1)}, bf16[128,1536]{1,0:T(8,128)(2,1)S(1)}, u32[]{:S(2)}, u32[]{:S(2)}) collective-permute-start(bf16[128,1536]{1,0:T(8,128)(2,1)S(1)} %get-tuple-element.95), channel_id=1, source_target_pairs={{0,2},{2,0},{4,6},{6,4},{8,10},{10,8},{12,14},{14,12},{16,18},{18,... | collective-permute-start | bytes 1179656 | tf_op jit(solution)/shard_map/ppermute | solution.py:242
  98.8 2.2 %shard_map.135 = (bf16[128,1536]{1,0:T(8,128)(2,1)S(1)}, bf16[128,1536]{1,0:T(8,128)(2,1)S(1)}, f32[128,1536]{1,0:T(8,128)S(1)}, f32[128,1536]{1,0:T(8,128)S(1)}) custom-call(s32[2]{0:T(128)S(1)} %pad_add_fusion.place_ref, bf16[512,512]{1,0:T(8,128)(2,1)S(1)} %get-tuple-element.73.hidden_ref, f32[512,128]{1,0:T(8,128)S(1)} %get-tuple-element.74.weight_ref, ...), custom_call_target="tpu_custom_call" | custom-call | flops 805306368 | bytes 7864320 | tf_op jit(solution)/shard_map/pallas_call | solution.py:86
  101.7 5.7 %collective-permute-done.27.got_ref = bf16[128,1536]{1,0:T(8,128)(2,1)S(1)} collective-permute-done((bf16[128,1536]{1,0:T(8,128)(2,1)S(1)}, bf16[128,1536]{1,0:T(8,128)(2,1)S(1)}, u32[]{:S(2)}, u32[]{:S(2)}) %collective-permute-start.27) | collective-permute-done | bytes 393248 | tf_op jit(solution)/shard_map/ppermute | solution.py:242
  107.4 1.6 %collective-permute-start.28 = (bf16[64,1536]{1,0:T(8,128)(2,1)S(1)}, bf16[64,1536]{1,0:T(8,128)(2,1)S(1)}, u32[]{:S(2)}, u32[]{:S(2)}) collective-permute-start(bf16[64,1536]{1,0:T(8,128)(2,1)S(1)} %get-tuple-element.97), channel_id=1, source_target_pairs={{0,4},{2,6},{4,0},{6,2},{8,12},{10,14},{12,8},{14,10},{16,20},{18,... | collective-permute-start | bytes 589832 | tf_op jit(solution)/shard_map/ppermute | solution.py:242
  109.3 1.7 %collective-permute-start.26 = (bf16[64,1536]{1,0:T(8,128)(2,1)S(1)}, bf16[64,1536]{1,0:T(8,128)(2,1)S(1)}, u32[]{:S(2)}, u32[]{:S(2)}) collective-permute-start(bf16[64,1536]{1,0:T(8,128)(2,1)S(1)} %get-tuple-element.93), channel_id=1, source_target_pairs={{0,2},{2,0},{4,6},{6,4},{8,10},{10,8},{12,14},{14,12},{16,18},{18,... | collective-permute-start | bytes 589832 | tf_op jit(solution)/shard_map/ppermute | solution.py:242
  111.0 4.7 %collective-permute-done.22.got_ref = bf16[128,1536]{1,0:T(8,128)(2,1)S(1)} collective-permute-done((bf16[128,1536]{1,0:T(8,128)(2,1)S(1)}, bf16[128,1536]{1,0:T(8,128)(2,1)S(1)}, u32[]{:S(2)}, u32[]{:S(2)}) %collective-permute-start.22) | collective-permute-done | bytes 393248 | tf_op jit(solution)/shard_map/ppermute | solution.py:242
  115.8 1.6 %collective-permute-start.23 = (bf16[64,1536]{1,0:T(8,128)(2,1)S(1)}, bf16[64,1536]{1,0:T(8,128)(2,1)S(1)}, u32[]{:S(2)}, u32[]{:S(2)}) collective-permute-start(bf16[64,1536]{1,0:T(8,128)(2,1)S(1)} %get-tuple-element.84), channel_id=1, source_target_pairs={{0,4},{2,6},{4,0},{6,2},{8,12},{10,14},{12,8},{14,10},{16,20},{18,... | collective-permute-start | bytes 589832 | tf_op jit(solution)/shard_map/ppermute | solution.py:242
  117.8 1.7 %collective-permute-start.21 = (bf16[64,1536]{1,0:T(8,128)(2,1)S(1)}, bf16[64,1536]{1,0:T(8,128)(2,1)S(1)}, u32[]{:S(2)}, u32[]{:S(2)}) collective-permute-start(bf16[64,1536]{1,0:T(8,128)(2,1)S(1)} %get-tuple-element.80), channel_id=1, source_target_pairs={{0,2},{2,0},{4,6},{6,4},{8,10},{10,8},{12,14},{14,12},{16,18},{18,... | collective-permute-start | bytes 589832 | tf_op jit(solution)/shard_map/ppermute | solution.py:242
  119.5 2.4 %collective-permute-done.28.got_b = bf16[64,1536]{1,0:T(8,128)(2,1)S(1)} collective-permute-done((bf16[64,1536]{1,0:T(8,128)(2,1)S(1)}, bf16[64,1536]{1,0:T(8,128)(2,1)S(1)}, u32[]{:S(2)}, u32[]{:S(2)}) %collective-permute-start.28) | collective-permute-done | bytes 196640 | tf_op jit(solution)/shard_map/ppermute | solution.py:242
  122.1 3.2 %collective-permute-done.23.got_b = bf16[64,1536]{1,0:T(8,128)(2,1)S(1)} collective-permute-done((bf16[64,1536]{1,0:T(8,128)(2,1)S(1)}, bf16[64,1536]{1,0:T(8,128)(2,1)S(1)}, u32[]{:S(2)}, u32[]{:S(2)}) %collective-permute-start.23) | collective-permute-done | bytes 196640 | tf_op jit(solution)/shard_map/ppermute | solution.py:242
  125.6 12.5 %collective-permute-done.29.got_ref = bf16[64,1536]{1,0:T(8,128)(2,1)S(1)} collective-permute-done((bf16[64,1536]{1,0:T(8,128)(2,1)S(1)}, bf16[64,1536]{1,0:T(8,128)(2,1)S(1)}, u32[]{:S(2)}, u32[]{:S(2)}) %collective-permute-start.29) | collective-permute-done | bytes 196640 | tf_op jit(solution)/shard_map/ppermute | solution.py:242
  138.8 2.1 %collective-permute-done.24.got_ref = bf16[64,1536]{1,0:T(8,128)(2,1)S(1)} collective-permute-done((bf16[64,1536]{1,0:T(8,128)(2,1)S(1)}, bf16[64,1536]{1,0:T(8,128)(2,1)S(1)}, u32[]{:S(2)}, u32[]{:S(2)}) %collective-permute-start.24) | collective-permute-done | bytes 196640 | tf_op jit(solution)/shard_map/ppermute | solution.py:242
  (144 shorter events, 39.5 us)
Async XLA Ops:
  8.6 19.4 %collective-permute-start.8 = (bf16[64,1664]{1,0:T(8,128)(2,1)S(1)}, bf16[64,1664]{1,0:T(8,128)(2,1)S(1)}, u32[]{:S(2)}, u32[]{:S(2)}) collective-permute-start(bf16[64,1664]{1,0:T(8,128)(2,1)S(1)} %get-tuple-element.52), channel_id=1, source_target_pairs={{0,16},{2,18},{4,20},{6,22},{8,24},{10,26},{12,28},{14,30},{16,0},... | collective-permute-start | bytes 638984 | tf_op jit(solution)/shard_map/ppermute | solution.py:242
  12.7 19.0 %collective-permute-start.1 = (bf16[64,1664]{1,0:T(8,128)(2,1)S(1)}, bf16[64,1664]{1,0:T(8,128)(2,1)S(1)}, u32[]{:S(2)}, u32[]{:S(2)}) collective-permute-start(bf16[64,1664]{1,0:T(8,128)(2,1)S(1)} %get-tuple-element.51), channel_id=1, source_target_pairs={{0,16},{2,18},{4,20},{6,22},{8,24},{10,26},{12,28},{14,30},{16,0},... | collective-permute-start | bytes 638984 | tf_op jit(solution)/shard_map/ppermute | solution.py:242
  14.4 49.4 %collective-permute-start = (bf16[768,1024]{1,0:T(8,128)(2,1)S(1)}, bf16[768,1024]{1,0:T(8,128)(2,1)}, u32[]{:S(2)}, u32[]{:S(2)}) collective-permute-start(bf16[768,1024]{1,0:T(8,128)(2,1)S(1)} %pad_maximum_fusion.refs_8_), channel_id=1, source_target_pairs={{0,8},{2,10},{4,12},{6,14},{8,0},{10,2},{12,4},{14,6},{16,24},{18,... | collective-permute-start | bytes 4718600 | tf_op jit(solution)/shard_map/ppermute | solution.py:242
  28.1 7.0 %collective-permute-start.10 = (bf16[64,1664]{1,0:T(8,128)(2,1)S(1)}, bf16[64,1664]{1,0:T(8,128)(2,1)S(1)}, u32[]{:S(2)}, u32[]{:S(2)}) collective-permute-start(bf16[64,1664]{1,0:T(8,128)(2,1)S(1)} %pad_maximum_fusion.3.refs_4_), channel_id=1, source_target_pairs={{0,2},{2,0},{4,6},{6,4},{8,10},{10,8},{12,14},{14,12},{16,18},{18,... | collective-permute-start | bytes 638984 | tf_op jit(solution)/shard_map/ppermute | solution.py:242
  30.0 33.8 %copy-start = (bf16[64,1664]{1,0:T(8,128)(2,1)}, bf16[64,1664]{1,0:T(8,128)(2,1)S(1)}, u32[]{:S(2)}) copy-start(bf16[64,1664]{1,0:T(8,128)(2,1)S(1)} %pad_maximum_fusion.4.refs_6_) | copy-start | bytes 638980
  30.0 7.1 %collective-permute-start.13 = (bf16[64,1664]{1,0:T(8,128)(2,1)S(1)}, bf16[64,1664]{1,0:T(8,128)(2,1)S(1)}, u32[]{:S(2)}, u32[]{:S(2)}) collective-permute-start(bf16[64,1664]{1,0:T(8,128)(2,1)S(1)} %pad_maximum_fusion.4.refs_6_), channel_id=1, source_target_pairs={{0,4},{2,6},{4,0},{6,2},{8,12},{10,14},{12,8},{14,10},{16,20},{18,... | collective-permute-start | bytes 638984 | tf_op jit(solution)/shard_map/ppermute | solution.py:242
  31.8 32.0 %copy-start.3 = (bf16[64,1664]{1,0:T(8,128)(2,1)}, bf16[64,1664]{1,0:T(8,128)(2,1)S(1)}, u32[]{:S(2)}) copy-start(bf16[64,1664]{1,0:T(8,128)(2,1)S(1)} %pad_maximum_fusion.1.refs_4_) | copy-start | bytes 638980
  31.8 8.3 %collective-permute-start.3 = (bf16[64,1664]{1,0:T(8,128)(2,1)S(1)}, bf16[64,1664]{1,0:T(8,128)(2,1)S(1)}, u32[]{:S(2)}, u32[]{:S(2)}) collective-permute-start(bf16[64,1664]{1,0:T(8,128)(2,1)S(1)} %pad_maximum_fusion.1.refs_4_), channel_id=1, source_target_pairs={{0,2},{2,0},{4,6},{6,4},{8,10},{10,8},{12,14},{14,12},{16,18},{18,... | collective-permute-start | bytes 638984 | tf_op jit(solution)/shard_map/ppermute | solution.py:242
  33.5 8.3 %collective-permute-start.6 = (bf16[64,1664]{1,0:T(8,128)(2,1)S(1)}, bf16[64,1664]{1,0:T(8,128)(2,1)S(1)}, u32[]{:S(2)}, u32[]{:S(2)}) collective-permute-start(bf16[64,1664]{1,0:T(8,128)(2,1)S(1)} %pad_maximum_fusion.2.refs_6_), channel_id=1, source_target_pairs={{0,4},{2,6},{4,0},{6,2},{8,12},{10,14},{12,8},{14,10},{16,20},{18,... | collective-permute-start | bytes 638984 | tf_op jit(solution)/shard_map/ppermute | solution.py:242
  35.1 8.1 %collective-permute-start.12 = (bf16[64,1664]{1,0:T(8,128)(2,1)S(1)}, bf16[64,1664]{1,0:T(8,128)(2,1)S(1)}, u32[]{:S(2)}, u32[]{:S(2)}) collective-permute-start(bf16[64,1664]{1,0:T(8,128)(2,1)S(1)} %pad_maximum_fusion.4.refs_6_), channel_id=1, source_target_pairs={{0,2},{2,0},{4,6},{6,4},{8,10},{10,8},{12,14},{14,12},{16,18},{18,... | collective-permute-start | bytes 638984 | tf_op jit(solution)/shard_map/ppermute | solution.py:242
  37.1 8.7 %collective-permute-start.2 = (bf16[64,1664]{1,0:T(8,128)(2,1)S(1)}, bf16[64,1664]{1,0:T(8,128)(2,1)S(1)}, u32[]{:S(2)}, u32[]{:S(2)}) collective-permute-start(bf16[64,1664]{1,0:T(8,128)(2,1)S(1)} %pad_maximum_fusion.1.refs_4_), channel_id=1, source_target_pairs={{0,4},{2,6},{4,0},{6,2},{8,12},{10,14},{12,8},{14,10},{16,20},{18,... | collective-permute-start | bytes 638984 | tf_op jit(solution)/shard_map/ppermute | solution.py:242
  40.1 28.6 %collective-permute-start.16 = (bf16[768,1024]{1,0:T(8,128)(2,1)S(1)}, bf16[768,1024]{1,0:T(8,128)(2,1)S(1)}, u32[]{:S(2)}, u32[]{:S(2)}) collective-permute-start(bf16[768,1024]{1,0:T(8,128)(2,1)S(1)} %pad_maximum_fusion.refs_8_), channel_id=1, source_target_pairs={{0,1},{1,0},{2,3},{3,2},{4,5},{5,4},{6,7},{7,6},{8,9},{9,8},{10,11... | collective-permute-start | bytes 4718600 | tf_op jit(solution)/shard_map/ppermute | solution.py:246
  41.7 6.2 %collective-permute-start.5 = (bf16[64,1664]{1,0:T(8,128)(2,1)S(1)}, bf16[64,1664]{1,0:T(8,128)(2,1)S(1)}, u32[]{:S(2)}, u32[]{:S(2)}) collective-permute-start(bf16[64,1664]{1,0:T(8,128)(2,1)S(1)} %pad_maximum_fusion.2.refs_6_), channel_id=1, source_target_pairs={{0,2},{2,0},{4,6},{6,4},{8,10},{10,8},{12,14},{14,12},{16,18},{18,... | collective-permute-start | bytes 638984 | tf_op jit(solution)/shard_map/ppermute | solution.py:242
  43.8 8.2 %collective-permute-start.9 = (bf16[64,1664]{1,0:T(8,128)(2,1)S(1)}, bf16[64,1664]{1,0:T(8,128)(2,1)S(1)}, u32[]{:S(2)}, u32[]{:S(2)}) collective-permute-start(bf16[64,1664]{1,0:T(8,128)(2,1)S(1)} %pad_maximum_fusion.3.refs_4_), channel_id=1, source_target_pairs={{0,4},{2,6},{4,0},{6,2},{8,12},{10,14},{12,8},{14,10},{16,20},{18,... | collective-permute-start | bytes 638984 | tf_op jit(solution)/shard_map/ppermute | solution.py:242
  46.5 10.0 %collective-permute-start.11 = (bf16[64,1664]{1,0:T(8,128)(2,1)S(1)}, bf16[64,1664]{1,0:T(8,128)(2,1)S(1)}, u32[]{:S(2)}, u32[]{:S(2)}) collective-permute-start(bf16[64,1664]{1,0:T(8,128)(2,1)S(1)} %collective-permute-done.10.refs_5_), channel_id=1, source_target_pairs={{0,4},{2,6},{4,0},{6,2},{8,12},{10,14},{12,8},{14,10},{16,20},{18,... | collective-permute-start | bytes 638984 | tf_op jit(solution)/shard_map/ppermute | solution.py:242
  48.7 11.3 %collective-permute-start.14 = (bf16[64,1664]{1,0:T(8,128)(2,1)S(1)}, bf16[64,1664]{1,0:T(8,128)(2,1)S(1)}, u32[]{:S(2)}, u32[]{:S(2)}) collective-permute-start(bf16[64,1664]{1,0:T(8,128)(2,1)S(1)} %collective-permute-done.13.refs_7_), channel_id=1, source_target_pairs={{0,2},{2,0},{4,6},{6,4},{8,10},{10,8},{12,14},{14,12},{16,18},{18,... | collective-permute-start | bytes 638984 | tf_op jit(solution)/shard_map/ppermute | solution.py:242
  52.7 7.9 %collective-permute-start.4 = (bf16[64,1664]{1,0:T(8,128)(2,1)S(1)}, bf16[64,1664]{1,0:T(8,128)(2,1)S(1)}, u32[]{:S(2)}, u32[]{:S(2)}) collective-permute-start(bf16[64,1664]{1,0:T(8,128)(2,1)S(1)} %collective-permute-done.3.refs_5_), channel_id=1, source_target_pairs={{0,4},{2,6},{4,0},{6,2},{8,12},{10,14},{12,8},{14,10},{16,20},{18,... | collective-permute-start | bytes 638984 | tf_op jit(solution)/shard_map/ppermute | solution.py:242
  57.2 5.8 %collective-permute-start.7 = (bf16[64,1664]{1,0:T(8,128)(2,1)S(1)}, bf16[64,1664]{1,0:T(8,128)(2,1)S(1)}, u32[]{:S(2)}, u32[]{:S(2)}) collective-permute-start(bf16[64,1664]{1,0:T(8,128)(2,1)S(1)} %collective-permute-done.6.refs_7_), channel_id=1, source_target_pairs={{0,2},{2,0},{4,6},{6,4},{8,10},{10,8},{12,14},{14,12},{16,18},{18,... | collective-permute-start | bytes 638984 | tf_op jit(solution)/shard_map/ppermute | solution.py:242
  63.8 20.9 %collective-permute-start.18 = (bf16[768,1024]{1,0:T(8,128)(2,1)}, bf16[768,1024]{1,0:T(8,128)(2,1)}, u32[]{:S(2)}, u32[]{:S(2)}) collective-permute-start(bf16[768,1024]{1,0:T(8,128)(2,1)} %collective-permute-done.refs_8_), channel_id=1, source_target_pairs={{0,1},{1,0},{2,3},{3,2},{4,5},{5,4},{6,7},{7,6},{8,9},{9,8},{10,11... | collective-permute-start | bytes 4718600 | tf_op jit(solution)/shard_map/ppermute | solution.py:246
  63.9 4.9 %collective-permute-start.17 = (bf16[512,768]{1,0:T(8,128)(2,1)}, bf16[512,768]{1,0:T(8,128)(2,1)}, u32[]{:S(2)}, u32[]{:S(2)}) collective-permute-start(bf16[512,768]{1,0:T(8,128)(2,1)} %bitcast.2.refs_10_), channel_id=1, source_target_pairs={{0,1},{1,0},{2,3},{3,2},{4,5},{5,4},{6,7},{7,6},{8,9},{9,8},{10,11... | collective-permute-start | bytes 2359304 | tf_op jit(solution)/shard_map/ppermute | solution.py:246
  64.4 24.5 %collective-permute-start.15 = (bf16[512,768]{1,0:T(8,128)(2,1)}, bf16[512,768]{1,0:T(8,128)(2,1)}, u32[]{:S(2)}, u32[]{:S(2)}) collective-permute-start(bf16[512,768]{1,0:T(8,128)(2,1)} %bitcast.2.refs_10_), channel_id=1, source_target_pairs={{0,8},{2,10},{4,12},{6,14},{8,0},{10,2},{12,4},{14,6},{16,24},{18,... | collective-permute-start | bytes 2359304 | tf_op jit(solution)/shard_map/ppermute | solution.py:242
  88.8 4.3 %collective-permute-start.19 = (bf16[512,768]{1,0:T(8,128)(2,1)}, bf16[512,768]{1,0:T(8,128)(2,1)S(1)}, u32[]{:S(2)}, u32[]{:S(2)}) collective-permute-start(bf16[512,768]{1,0:T(8,128)(2,1)} %collective-permute-done.15.down_a), channel_id=1, source_target_pairs={{0,1},{1,0},{2,3},{3,2},{4,5},{5,4},{6,7},{7,6},{8,9},{9,8},{10,11... | collective-permute-start | bytes 2359304 | tf_op jit(solution)/shard_map/ppermute | solution.py:246
  95.3 12.1 %collective-permute-start.27 = (bf16[128,1536]{1,0:T(8,128)(2,1)S(1)}, bf16[128,1536]{1,0:T(8,128)(2,1)S(1)}, u32[]{:S(2)}, u32[]{:S(2)}) collective-permute-start(bf16[128,1536]{1,0:T(8,128)(2,1)S(1)} %get-tuple-element.95), channel_id=1, source_target_pairs={{0,2},{2,0},{4,6},{6,4},{8,10},{10,8},{12,14},{14,12},{16,18},{18,... | collective-permute-start | bytes 1179656 | tf_op jit(solution)/shard_map/ppermute | solution.py:242
  97.3 12.0 %collective-permute-start.25 = (bf16[128,1536]{1,0:T(8,128)(2,1)S(1)}, bf16[128,1536]{1,0:T(8,128)(2,1)S(1)}, u32[]{:S(2)}, u32[]{:S(2)}) collective-permute-start(bf16[128,1536]{1,0:T(8,128)(2,1)S(1)} %get-tuple-element.91), channel_id=1, source_target_pairs={{0,4},{2,6},{4,0},{6,2},{8,12},{10,14},{12,8},{14,10},{16,20},{18,... | collective-permute-start | bytes 1179656 | tf_op jit(solution)/shard_map/ppermute | solution.py:242
  101.0 14.7 %collective-permute-start.22 = (bf16[128,1536]{1,0:T(8,128)(2,1)S(1)}, bf16[128,1536]{1,0:T(8,128)(2,1)S(1)}, u32[]{:S(2)}, u32[]{:S(2)}) collective-permute-start(bf16[128,1536]{1,0:T(8,128)(2,1)S(1)} %get-tuple-element.82), channel_id=1, source_target_pairs={{0,2},{2,0},{4,6},{6,4},{8,10},{10,8},{12,14},{14,12},{16,18},{18,... | collective-permute-start | bytes 1179656 | tf_op jit(solution)/shard_map/ppermute | solution.py:242
  101.2 16.5 %collective-permute-start.20 = (bf16[128,1536]{1,0:T(8,128)(2,1)S(1)}, bf16[128,1536]{1,0:T(8,128)(2,1)S(1)}, u32[]{:S(2)}, u32[]{:S(2)}) collective-permute-start(bf16[128,1536]{1,0:T(8,128)(2,1)S(1)} %get-tuple-element.78), channel_id=1, source_target_pairs={{0,4},{2,6},{4,0},{6,2},{8,12},{10,14},{12,8},{14,10},{16,20},{18,... | collective-permute-start | bytes 1179656 | tf_op jit(solution)/shard_map/ppermute | solution.py:242
  107.4 14.5 %collective-permute-start.28 = (bf16[64,1536]{1,0:T(8,128)(2,1)S(1)}, bf16[64,1536]{1,0:T(8,128)(2,1)S(1)}, u32[]{:S(2)}, u32[]{:S(2)}) collective-permute-start(bf16[64,1536]{1,0:T(8,128)(2,1)S(1)} %get-tuple-element.97), channel_id=1, source_target_pairs={{0,4},{2,6},{4,0},{6,2},{8,12},{10,14},{12,8},{14,10},{16,20},{18,... | collective-permute-start | bytes 589832 | tf_op jit(solution)/shard_map/ppermute | solution.py:242
  109.3 12.6 %collective-permute-start.26 = (bf16[64,1536]{1,0:T(8,128)(2,1)S(1)}, bf16[64,1536]{1,0:T(8,128)(2,1)S(1)}, u32[]{:S(2)}, u32[]{:S(2)}) collective-permute-start(bf16[64,1536]{1,0:T(8,128)(2,1)S(1)} %get-tuple-element.93), channel_id=1, source_target_pairs={{0,2},{2,0},{4,6},{6,4},{8,10},{10,8},{12,14},{14,12},{16,18},{18,... | collective-permute-start | bytes 589832 | tf_op jit(solution)/shard_map/ppermute | solution.py:242
  115.8 9.5 %collective-permute-start.23 = (bf16[64,1536]{1,0:T(8,128)(2,1)S(1)}, bf16[64,1536]{1,0:T(8,128)(2,1)S(1)}, u32[]{:S(2)}, u32[]{:S(2)}) collective-permute-start(bf16[64,1536]{1,0:T(8,128)(2,1)S(1)} %get-tuple-element.84), channel_id=1, source_target_pairs={{0,4},{2,6},{4,0},{6,2},{8,12},{10,14},{12,8},{14,10},{16,20},{18,... | collective-permute-start | bytes 589832 | tf_op jit(solution)/shard_map/ppermute | solution.py:242
  117.8 7.6 %collective-permute-start.21 = (bf16[64,1536]{1,0:T(8,128)(2,1)S(1)}, bf16[64,1536]{1,0:T(8,128)(2,1)S(1)}, u32[]{:S(2)}, u32[]{:S(2)}) collective-permute-start(bf16[64,1536]{1,0:T(8,128)(2,1)S(1)} %get-tuple-element.80), channel_id=1, source_target_pairs={{0,2},{2,0},{4,6},{6,4},{8,10},{10,8},{12,14},{14,12},{16,18},{18,... | collective-permute-start | bytes 589832 | tf_op jit(solution)/shard_map/ppermute | solution.py:242
  122.0 16.1 %collective-permute-start.29 = (bf16[64,1536]{1,0:T(8,128)(2,1)S(1)}, bf16[64,1536]{1,0:T(8,128)(2,1)S(1)}, u32[]{:S(2)}, u32[]{:S(2)}) collective-permute-start(bf16[64,1536]{1,0:T(8,128)(2,1)S(1)} %get-tuple-element.99), channel_id=1, source_target_pairs={{0,16},{2,18},{4,20},{6,22},{8,24},{10,26},{12,28},{14,30},{16,0},... | collective-permute-start | bytes 589832 | tf_op jit(solution)/shard_map/ppermute | solution.py:242
  125.4 15.5 %collective-permute-start.24 = (bf16[64,1536]{1,0:T(8,128)(2,1)S(1)}, bf16[64,1536]{1,0:T(8,128)(2,1)S(1)}, u32[]{:S(2)}, u32[]{:S(2)}) collective-permute-start(bf16[64,1536]{1,0:T(8,128)(2,1)S(1)} %get-tuple-element.86), channel_id=1, source_target_pairs={{0,16},{2,18},{4,20},{6,22},{8,24},{10,26},{12,28},{14,30},{16,0},... | collective-permute-start | bytes 589832 | tf_op jit(solution)/shard_map/ppermute | solution.py:242
  (44 other events, 90.8 us)

commit v4 on v3

--- a/solution.py
+++ b/solution.py
@@ -96,8 +96,10 @@
 
 
 def prepare_kernel(old_ref, new_ref, *refs):
-    hbm, outs, held, sems = refs[:7], refs[7:9], refs[9:16], refs[16]
-    copies = [pltpu.make_async_copy(a, b, sems.at[i]) for i, (a, b) in enumerate(zip(hbm, held))]
+    hbm, outs, both_ref, held, sems = refs[:9], refs[9:11], refs[11], refs[12:19], refs[19]
+    ff = both_ref.shape[1] // 2
+    places = list(held) + [both_ref.at[:, :ff], both_ref.at[:, ff:]]
+    copies = [pltpu.make_async_copy(a, b, sems.at[i]) for i, (a, b) in enumerate(zip(hbm, places))]
     for copy in copies:
         copy.start()
     group = old_ref.shape[0]
@@ -107,7 +109,7 @@
         wanted = new_ref[s]
         other = jnp.where(wanted == old_ref[left], left, right)
         sources.append(jnp.where(wanted == old_ref[s], s, other))
-    for copy in copies:
+    for copy in copies[: len(held)]:
         copy.wait()
     gain = held[0][...].astype(jnp.float32).reshape(1, -1)
     for b in range(2):
@@ -141,6 +143,8 @@
             preferred_element_type=jnp.float32,
         )
         out_ref[:, width:] = turned.astype(jnp.bfloat16)
+    for copy in copies[len(held) :]:
+        copy.wait()
 
 
 def hidden_of(place, rows_ref, both_refs, begin, count):
@@ -149,9 +153,8 @@
     for which, ref in enumerate(both_refs):
         half = place if which == 0 else 1 - place
         columns = pl.ds(pl.multiple_of(half * depth, depth), depth)
-        term = jnp.dot(
-            rows_ref[pl.ds(begin, count), columns], ref[...], preferred_element_type=jnp.float32
-        )
+        rows = rows_ref[pl.ds(begin, count), columns]
+        term = jnp.dot(rows, ref[...], preferred_element_type=jnp.float32)
         acts = term if acts is None else acts + term
     gate_act, up_act = acts[:, :ff], acts[:, ff:]
     return (gate_act / (1.0 + jnp.exp(-gate_act)) * up_act).astype(jnp.bfloat16)
@@ -163,21 +166,21 @@
     return jnp.sum(jnp.where(chosen, packed.astype(jnp.float32), 0.0), axis=1, keepdims=True)
 
 
-def own_kernel(pieces, group, place_ref, *refs):
+def own_kernel(pieces, group, *refs):
     piece_refs, refs = refs[:pieces], refs[pieces:]
     both_a, both_b, down_a, down_b, total_ref, rows_ref = refs
     tok = piece_refs[0].shape[0]
     width = total_ref.shape[1]
     for i, ref in enumerate(piece_refs):
         rows_ref[i * tok : (i + 1) * tok, :] = ref[...]
-    place = place_ref[0]
+    place, expert = lax.axis_index("tensor"), lax.axis_index("expert")
     block = 256
 
     @pl.loop(0, rows_ref.shape[0] // block)
     def _(step):
         begin = pl.multiple_of(step * block, block)
         hidden = hidden_of(place, rows_ref, (both_a, both_b), begin, block)
-        weight = weight_of(place_ref[1], group, rows_ref[pl.ds(begin, block), width:])
+        weight = weight_of(expert, group, rows_ref[pl.ds(begin, block), width:])
         for which, ref in enumerate((down_a, down_b)):
             half = place if which == 0 else 1 - place
             columns = pl.ds(pl.multiple_of(half * ref.shape[1], ref.shape[1]), ref.shape[1])
@@ -185,27 +188,28 @@
             total_ref[pl.ds(begin, block), columns] = part * weight
 
 
-def beside_kernel(pieces, group, place_ref, *refs):
+def beside_kernel(pieces, group, *refs):
     piece_refs, refs = refs[:pieces], refs[pieces:]
     both_a, both_b, hidden_ref, weight_ref, rows_ref = refs
     tok = piece_refs[0].shape[0]
     width = rows_ref.shape[1] - PACK
     for i, ref in enumerate(piece_refs):
         rows_ref[i * tok : (i + 1) * tok, :] = ref[...]
+    place, expert = lax.axis_index("tensor"), lax.axis_index("expert") ^ Z_LOW
     block = 256
 
     @pl.loop(0, rows_ref.shape[0] // block)
     def _(step):
         begin = pl.multiple_of(step * block, block)
         hidden_ref[pl.ds(begin, block), :] = hidden_of(
-            place_ref[0], rows_ref, (both_a, both_b), begin, block
+            place, rows_ref, (both_a, both_b), begin, block
         )
-        weight = weight_of(place_ref[1] ^ Z_LOW, group, rows_ref[pl.ds(begin, block), width:])
+        weight = weight_of(expert, group, rows_ref[pl.ds(begin, block), width:])
         weight_ref[pl.ds(begin, block), :] = jnp.broadcast_to(weight, (block, PACK))
 
 
-def join_kernel(place_ref, hidden_ref, weight_ref, total_ref, down_a, down_b, send_a, send_b, keep_a, keep_b):
-    place = place_ref[0]
+def join_kernel(hidden_ref, weight_ref, total_ref, down_a, down_b, send_a, send_b, keep_a, keep_b):
+    place = lax.axis_index("tensor")
     count = send_a.shape[0]
     for pair, outs in ((0, (send_a, send_b)), (1, (keep_a, keep_b))):
         rows = slice(pair * 2 * count, (pair + 1) * 2 * count)
@@ -246,31 +250,42 @@
     return lax.ppermute(block, "tensor", [(0, 1), (1, 0)])
 
 
-def spread(own):
+def halves(own, far):
     half = own.shape[0] // 2
-    far = swap(own, Z_HIGH)
-    a1 = jnp.concatenate([own[:half], far[:half]])
-    b1 = jnp.concatenate([own[half:], far[half:]])
-    a2, b2 = swap(a1, X), swap(b1, Y)
+    return [jnp.concatenate([own[i : i + half], far[i : i + half]]) for i in (0, half)]
+
+
+def spread(a1, b1, a2, b2):
     a3, b3 = swap(a1, Y), swap(b1, X)
     a4, b4 = swap(a2, Y), swap(b2, X)
     return [a3, a4, b3, b4, a1, a2, b1, b2]
 
 
-def send_back(send_a, send_b, keep_a, keep_b):
+def first_return(send_a, send_b, keep_a, keep_b):
     quarter, width = keep_a.shape[0] // 2, keep_a.shape[1]
-    bf = jax.ShapeDtypeStruct((quarter, width), jnp.bfloat16)
-    f32 = jax.ShapeDtypeStruct((quarter, width), jnp.float32)
+    outs = (
+        jax.ShapeDtypeStruct((quarter, width), jnp.bfloat16),
+        jax.ShapeDtypeStruct((quarter, width), jnp.float32),
+    )
     size = quarter * width
     got_a, got_b = swap(send_a, Y), swap(send_b, X)
-    next_a, held_a = call(first_sum_kernel, (bf, f32), (keep_a, got_a), 8, size, 18 * size)
-    next_b, held_b = call(first_sum_kernel, (bf, f32), (keep_b, got_b), 8, size, 18 * size)
+    next_a, held_a = call(first_sum_kernel, outs, (keep_a, got_a), 8, size, 18 * size)
+    next_b, held_b = call(first_sum_kernel, outs, (keep_b, got_b), 8, size, 18 * size)
+    return next_a, next_b, held_a, held_b
+
+
+def last_returns(next_a, next_b, held_a, held_b):
+    outs = (
+        jax.ShapeDtypeStruct(held_a.shape, jnp.bfloat16),
+        jax.ShapeDtypeStruct(held_a.shape, jnp.float32),
+    )
+    size = held_a.size
     got_a, got_b = swap(next_a, X), swap(next_b, Y)
     next_z, held_z = call(
-        second_sum_kernel, (bf, f32), (held_a, got_a, held_b, got_b), 8, size, 18 * size
+        second_sum_kernel, outs, (held_a, got_a, held_b, got_b), 8, size, 18 * size
     )
     got_z = swap(next_z, Z_HIGH)
-    return call(last_sum_kernel, bf, (held_z, got_z), 8, size, 8 * size)
+    return call(last_sum_kernel, outs[0], (held_z, got_z), 8, size, 8 * size)
 
 
 def local_pairs(
@@ -289,74 +304,89 @@
 ):
     group = table_old.shape[0]
     tok, width = batch_one.shape
-    place = jnp.stack([lax.axis_index("tensor"), lax.axis_index("expert")]).astype(jnp.int32)
-    tables = [pl.BlockSpec(memory_space=pltpu.SMEM)] * 2
-    ins = (
-        norm_gain, batch_one, batch_two, slots_one.T, slots_two.T, gates_one.T, gates_two.T
-    )
-    own = call(
+    ff = gate_old.shape[2]
+    gate, up, down = gate_old[0], up_old[0], down_old[0]
+    held = (norm_gain, batch_one, batch_two, slots_one.T, slots_two.T, gates_one.T, gates_two.T)
+    specs = [pl.BlockSpec(memory_space=pltpu.SMEM)] * 2
+    specs += [pl.BlockSpec(memory_space=pl.ANY)] * (len(held) + 2)
+    own_one, own_two, both = call(
         prepare_kernel,
-        (jax.ShapeDtypeStruct((tok, width + PACK), jnp.bfloat16),) * 2,
-        (table_old, table_new, *ins),
+        (jax.ShapeDtypeStruct((tok, width + PACK), jnp.bfloat16),) * 2
+        + (jax.ShapeDtypeStruct((gate.shape[0], 2 * ff), jnp.bfloat16),),
+        (table_old, table_new, *held, gate, up),
         8,
         10 * tok * width,
         8 * tok * width,
-        [pltpu.VMEM(x.shape, x.dtype) for x in ins] + [pltpu.SemaphoreType.DMA((len(ins),))],
-        tables + [pl.BlockSpec(memory_space=pl.ANY)] * len(ins),
-    )
-    both = jnp.concatenate([gate_old[0], up_old[0]], axis=1)
-    down = down_old[0]
-    beside_both = swap(both, Z_LOW)
-    twin_both, twin_down = swap_core(both), swap_core(down)
-    pieces = [spread(x) for x in own]
-    down_later, beside_both, pieces = lax.optimization_barrier((down, beside_both, pieces))
-    beside_down = swap(down_later, Z_LOW)
-    beside_twin_both = swap_core(beside_both)
-    ff = gate_old.shape[2]
+        [pltpu.VMEM(x.shape, x.dtype) for x in held]
+        + [pltpu.SemaphoreType.DMA((len(held) + 2,))],
+        specs,
+    )
+    own = (own_one, own_two)
+    both_by = swap(both, Z_LOW)
+    twins = (swap_core(both), swap_core(down))
+    far = [swap(x, Z_HIGH) for x in own]
+    far[0], twins = lax.optimization_barrier((far[0], twins))
+    first = [halves(x, y) for x, y in zip(own, far)]
+    second = [(swap(a1, X), swap(b1, Y)) for a1, b1 in first]
+    pieces = [spread(*f, *s) for f, s in zip(first, second)]
+
     rows = 8 * tok
     scratch = (pltpu.VMEM((rows, width + PACK), jnp.bfloat16),)
-    totals = [
-        call(
+
+    def own_total(p):
+        return call(
             functools.partial(own_kernel, 8, group),
             jax.ShapeDtypeStruct((rows, width), jnp.float32),
-            (place, *p, both, twin_both, down, twin_down),
+            (*p, both, twins[0], down, twins[1]),
             20,
             6 * rows * width * ff,
             6 * width * ff + 6 * rows * width,
             scratch,
         )
-        for p in pieces
-    ]
-    hidden = [
-        call(
+
+    def beside_hidden(p):
+        return call(
             functools.partial(beside_kernel, 8, group),
             (
                 jax.ShapeDtypeStruct((rows, ff), jnp.bfloat16),
                 jax.ShapeDtypeStruct((rows, PACK), jnp.float32),
             ),
-            (place, *p, beside_both, beside_twin_both),
+            (*p, both_by, both_twin),
             16,
             4 * rows * width * ff,
             4 * width * ff + 2 * rows * width,
             scratch,
         )
-        for p in pieces
-    ]
-    beside_down, totals, hidden[0] = lax.optimization_barrier((beside_down, totals, hidden[0]))
-    beside_twin_down = swap_core(beside_down)
-    outs = []
-    for total, (hid, weight) in zip(totals, hidden):
-        parts = call(
+
+    def join(total, hid, weight):
+        return call(
             join_kernel,
             (jax.ShapeDtypeStruct((2 * tok, width), jnp.bfloat16),) * 2
             + (jax.ShapeDtypeStruct((2 * tok, width), jnp.float32),) * 2,
-            (place, hid, weight, total, beside_down, beside_twin_down),
+            (hid, weight, total, down_by, down_twin),
             14,
             2 * rows * width * ff,
             2 * width * ff + 8 * rows * width,
         )
-        outs.append(send_back(*parts))
-    return tuple(outs)
+
+    pieces[0], second[1] = lax.optimization_barrier((pieces[0], second[1]))
+    total_one = own_total(pieces[0])
+    down_later, both_by, total_one, pieces = lax.optimization_barrier(
+        (down, both_by, total_one, pieces)
+    )
+    down_by = swap(down_later, Z_LOW)
+    both_twin = swap_core(both_by)
+    total_two = own_total(pieces[1])
+    hidden_one, hidden_two = beside_hidden(pieces[0]), beside_hidden(pieces[1])
+    down_by, total_two, hidden_one, hidden_two = lax.optimization_barrier(
+        (down_by, total_two, hidden_one, hidden_two)
+    )
+    down_twin = swap_core(down_by)
+    back_one = first_return(*join(total_one, *hidden_one))
+    sums_two = join(total_two, *hidden_two)
+    back_one, sums_two = lax.optimization_barrier((back_one, sums_two))
+    back_two = first_return(*sums_two)
+    return last_returns(*back_one), last_returns(*back_two)
 
 
 def solution(mesh):

time: 142 us -> 161 us (1.13)
  waiting for transfers between devices: 54.1 us -> 98.6 us
  local copies, waits for them, and re-layouts: 22.2 us -> 9 us
  Pallas kernels: 24.9 us -> 16 us
  starting transfers between devices: 37.6 us -> 35.8 us
  other arithmetic: 1.7 us -> 0.07 us
    ppermute x26, waiting for transfers between devices: 50.9 us -> 96.3 us  [swap(): lax.ppermute(block, 'expert', [(i, i ^ distance) for i in range(count)])]
    unnamed x92 -> x24, local copies, waits for them, and re-layouts: 22.1 us -> 8.93 us
    pallas_call x15, Pallas kernels: 24.9 us -> 16 us  [call(): pl.pallas_call(body, out_shape=outs, in_specs=specs or [smem if x.ndim ==...]
    ppermute x26, starting transfers between devices: 36.9 us -> 35.1 us  [swap(): lax.ppermute(block, 'expert', [(i, i ^ distance) for i in range(count)])]
  transfers between devices with their start and end apart: 30 -> 30, of which waited for: 18 -> 17; matrix products, arithmetic and copies ran while one was open for 1% -> 0% of each run, Pallas kernels for 15% -> 8%
where the time goes in v4:
time: 161 us; the launch traced here: 160 us
  waiting for transfers between devices  98.6 us (61%)
  starting transfers between devices  35.8 us (22%)
  Pallas kernels  16 us (10%)
  local copies, waits for them, and re-layouts  9 us (6%)
    ppermute x26, waiting for transfers between devices, swap(): lax.ppermute(block, 'expert', [(i, i ^ distance) for i in range(count)])  96.3 us
    ppermute x26, starting transfers between devices, swap(): lax.ppermute(block, 'expert', [(i, i ^ distance) for i in range(count)])  35.1 us
    pallas_call x15, Pallas kernels, call(): pl.pallas_call(body, out_shape=outs, in_specs=specs or [smem if x.ndim ==...  16 us
    unnamed x24, local copies, waits for them, and re-layouts  8.93 us
  transfers between devices with their start and end apart: 30, of which 17 were waited for; matrix products, arithmetic and copies ran while one was open for 0% of the time, Pallas kernels for 8%

profile of v4, /device:TPU:0, one launch (start us, length us, event | category | flops | bytes accessed | tf_op | source)
XLA Modules:
  0.0 160.2 jit_solution(1907528186293206304)
XLA Ops:
  9.6 1.6 shard_map.131
  11.7 2.6 %collective-permute-start = (bf16[768,1024]{1,0:T(8,128)(2,1)S(1)}, bf16[768,1024]{1,0:T(8,128)(2,1)S(1)}, u32[]{:S(2)}, u32[]{:S(2)}) collective-permute-start(bf16[768,1024]{1,0:T(8,128)(2,1)S(1)} %get-tuple-element.73.refs_8_), channel_id=1, source_target_pairs={{0,8},{2,10},{4,12},{6,14},{8,0},{10,2},{12,4},{14,6},{16,24},{18,... | collective-permute-start | bytes 4718600 | tf_op jit(solution)/shard_map/ppermute | solution.py:246
  14.5 2.6 %collective-permute-start.1 = (bf16[64,1664]{1,0:T(8,128)(2,1)S(1)}, bf16[64,1664]{1,0:T(8,128)(2,1)S(1)}, u32[]{:S(2)}, u32[]{:S(2)}) collective-permute-start(bf16[64,1664]{1,0:T(8,128)(2,1)S(1)} %get-tuple-element.74), channel_id=1, source_target_pairs={{0,16},{2,18},{4,20},{6,22},{8,24},{10,26},{12,28},{14,30},{16,0},... | collective-permute-start | bytes 638984 | tf_op jit(solution)/shard_map/ppermute | solution.py:246
  17.5 40.3 %collective-permute-done.10 = bf16[64,1664]{1,0:T(8,128)(2,1)S(1)} collective-permute-done((bf16[64,1664]{1,0:T(8,128)(2,1)S(1)}, bf16[64,1664]{1,0:T(8,128)(2,1)S(1)}, u32[]{:S(2)}, u32[]{:S(2)}) %collective-permute-start.10) | collective-permute-done | bytes 213024 | tf_op jit(solution)/shard_map/ppermute | solution.py:246
  57.8 1.6 collective-permute-start.11
  59.4 1.6 collective-permute-start.12
  62.2 3.8 %collective-permute-done.11.refs_5_ = bf16[64,1664]{1,0:T(8,128)(2,1)S(1)} collective-permute-done((bf16[64,1664]{1,0:T(8,128)(2,1)S(1)}, bf16[64,1664]{1,0:T(8,128)(2,1)S(1)}, u32[]{:S(2)}, u32[]{:S(2)}) %collective-permute-start.11) | collective-permute-done | bytes 213024 | tf_op jit(solution)/shard_map/ppermute | solution.py:246
  66.0 1.5 collective-permute-start.4
  67.6 1.4 collective-permute-start.7
  69.1 1.5 collective-permute-done.5.refs_5_
  70.6 1.5 collective-permute-start.6
  73.6 3.1 %collective-permute-done.4.refs_0_ = bf16[64,1664]{1,0:T(8,128)(2,1)S(1)} collective-permute-done((bf16[64,1664]{1,0:T(8,128)(2,1)S(1)}, bf16[64,1664]{1,0:T(8,128)(2,1)S(1)}, u32[]{:S(2)}, u32[]{:S(2)}) %collective-permute-start.4) | collective-permute-done | bytes 213024 | tf_op jit(solution)/shard_map/ppermute | solution.py:246
  76.8 1.5 collective-permute-start.13
  78.8 2.5 %collective-permute-done.6.refs_1_ = bf16[64,1664]{1,0:T(8,128)(2,1)S(1)} collective-permute-done((bf16[64,1664]{1,0:T(8,128)(2,1)S(1)}, bf16[64,1664]{1,0:T(8,128)(2,1)S(1)}, u32[]{:S(2)}, u32[]{:S(2)}) %collective-permute-start.6) | collective-permute-done | bytes 213024 | tf_op jit(solution)/shard_map/ppermute | solution.py:246
  81.3 1.5 collective-permute-start.14
  83.4 3.1 %shard_map.132.total_ref = f32[512,1536]{1,0:T(8,128)S(1)} custom-call(bf16[64,1664]{1,0:T(8,128)(2,1)S(1)} %collective-permute-done.4.refs_0_, bf16[64,1664]{1,0:T(8,128)(2,1)S(1)} %collective-permute-done.6.refs_1_, bf16[64,1664]{1,0:T(8,128)(2,1)S(1)} %collective-permute-done.7.refs_2_, bf16[64,1664]{1,0:T(8,128)(2,1)S(1)} %collective-permute-done.9.refs_3_, ...), custom_call_target="tpu_custom_call" | custom-call | flops 2415919104 | bytes 9437184 | tf_op jit(solution)/shard_map/pallas_call | solution.py:86
  86.6 2.2 %collective-permute-done.14.refs_1_ = bf16[64,1664]{1,0:T(8,128)(2,1)S(1)} collective-permute-done((bf16[64,1664]{1,0:T(8,128)(2,1)S(1)}, bf16[64,1664]{1,0:T(8,128)(2,1)S(1)}, u32[]{:S(2)}, u32[]{:S(2)}) %collective-permute-start.14) | collective-permute-done | bytes 213024 | tf_op jit(solution)/shard_map/ppermute | solution.py:246
  88.8 3.6 %collective-permute-start.17 = (bf16[512,768]{1,0:T(8,128)(2,1)S(1)}, bf16[512,768]{1,0:T(8,128)(2,1)S(1)}, u32[]{:S(2)}, u32[]{:S(2)}) collective-permute-start(bf16[512,768]{1,0:T(8,128)(2,1)S(1)} %bitcast.9), channel_id=1, source_target_pairs={{0,8},{2,10},{4,12},{6,14},{8,0},{10,2},{12,4},{14,6},{16,24},{18,... | collective-permute-start | bytes 2359304 | tf_op jit(solution)/shard_map/ppermute | solution.py:246
  92.4 3.1 %shard_map.133.total_ref = f32[512,1536]{1,0:T(8,128)S(1)} custom-call(bf16[64,1664]{1,0:T(8,128)(2,1)S(1)} %collective-permute-done.13.refs_0_, bf16[64,1664]{1,0:T(8,128)(2,1)S(1)} %collective-permute-done.14.refs_1_, bf16[64,1664]{1,0:T(8,128)(2,1)S(1)} %collective-permute-done.15.refs_2_, bf16[64,1664]{1,0:T(8,128)(2,1)S(1)} %collective-permute-done.16.refs_3_, ...), custom_call_target="tpu_custom_call" | custom-call | flops 2415919104 | bytes 9437184 | tf_op jit(solution)/shard_map/pallas_call | solution.py:86
  95.5 2.1 %shard_map.135 = (bf16[512,512]{1,0:T(8,128)(2,1)S(1)}, f32[512,128]{1,0:T(8,128)S(1)}) custom-call(bf16[64,1664]{1,0:T(8,128)(2,1)S(1)} %collective-permute-done.13.refs_0_, bf16[64,1664]{1,0:T(8,128)(2,1)S(1)} %collective-permute-done.14.refs_1_, bf16[64,1664]{1,0:T(8,128)(2,1)S(1)} %collective-permute-done.15.refs_2_, ...), custom_call_target="tpu_custom_call" | custom-call | flops 1610612736 | bytes 4718592 | tf_op jit(solution)/shard_map/pallas_call | solution.py:86
  97.7 2.2 %shard_map.134 = (bf16[512,512]{1,0:T(8,128)(2,1)S(1)}, f32[512,128]{1,0:T(8,128)S(1)}) custom-call(bf16[64,1664]{1,0:T(8,128)(2,1)S(1)} %collective-permute-done.4.refs_0_, bf16[64,1664]{1,0:T(8,128)(2,1)S(1)} %collective-permute-done.6.refs_1_, bf16[64,1664]{1,0:T(8,128)(2,1)S(1)} %collective-permute-done.7.refs_2_, ...), custom_call_target="tpu_custom_call" | custom-call | flops 1610612736 | bytes 4718592 | tf_op jit(solution)/shard_map/pallas_call | solution.py:86
  99.8 10.7 %collective-permute-done.17.down_a = bf16[512,768]{1,0:T(8,128)(2,1)S(1)} collective-permute-done((bf16[512,768]{1,0:T(8,128)(2,1)S(1)}, bf16[512,768]{1,0:T(8,128)(2,1)S(1)}, u32[]{:S(2)}, u32[]{:S(2)}) %collective-permute-start.17) | collective-permute-done | bytes 786464 | tf_op jit(solution)/shard_map/ppermute | solution.py:246
  110.5 2.3 %collective-permute-done.19.down_b = bf16[512,768]{1,0:T(8,128)(2,1)S(1)} collective-permute-done((bf16[512,768]{1,0:T(8,128)(2,1)S(1)}, bf16[512,768]{1,0:T(8,128)(2,1)S(1)}, u32[]{:S(2)}, u32[]{:S(2)}) %collective-permute-start.19) | collective-permute-done | bytes 786464 | tf_op jit(solution)/shard_map/ppermute | solution.py:250
  113.8 1.6 collective-permute-start.20
  117.0 8.1 %collective-permute-done.20.got_ref = bf16[128,1536]{1,0:T(8,128)(2,1)S(1)} collective-permute-done((bf16[128,1536]{1,0:T(8,128)(2,1)S(1)}, bf16[128,1536]{1,0:T(8,128)(2,1)S(1)}, u32[]{:S(2)}, u32[]{:S(2)}) %collective-permute-start.20) | collective-permute-done | bytes 393248 | tf_op jit(solution)/shard_map/ppermute | solution.py:246
  127.5 1.5 collective-permute-start.22
  129.0 1.5 collective-permute-start.23
  130.5 8.0 %collective-permute-done.25.got_ref = bf16[128,1536]{1,0:T(8,128)(2,1)S(1)} collective-permute-done((bf16[128,1536]{1,0:T(8,128)(2,1)S(1)}, bf16[128,1536]{1,0:T(8,128)(2,1)S(1)}, u32[]{:S(2)}, u32[]{:S(2)}) %collective-permute-start.25) | collective-permute-done | bytes 393248 | tf_op jit(solution)/shard_map/ppermute | solution.py:246
  140.6 2.5 %collective-permute-done.22.got_a = bf16[64,1536]{1,0:T(8,128)(2,1)S(1)} collective-permute-done((bf16[64,1536]{1,0:T(8,128)(2,1)S(1)}, bf16[64,1536]{1,0:T(8,128)(2,1)S(1)}, u32[]{:S(2)}, u32[]{:S(2)}) %collective-permute-start.22) | collective-permute-done | bytes 196640 | tf_op jit(solution)/shard_map/ppermute | solution.py:246
  143.2 1.7 %collective-permute-start.24 = (bf16[64,1536]{1,0:T(8,128)(2,1)S(1)}, bf16[64,1536]{1,0:T(8,128)(2,1)S(1)}, u32[]{:S(2)}, u32[]{:S(2)}) collective-permute-start(bf16[64,1536]{1,0:T(8,128)(2,1)S(1)} %get-tuple-element.133), channel_id=1, source_target_pairs={{0,16},{2,18},{4,20},{6,22},{8,24},{10,26},{12,28},{14,30},{16,0},... | collective-permute-start | bytes 589832 | tf_op jit(solution)/shard_map/ppermute | solution.py:246
  145.4 1.7 %collective-permute-start.29 = (bf16[64,1536]{1,0:T(8,128)(2,1)S(1)}, bf16[64,1536]{1,0:T(8,128)(2,1)S(1)}, u32[]{:S(2)}, u32[]{:S(2)}) collective-permute-start(bf16[64,1536]{1,0:T(8,128)(2,1)S(1)} %get-tuple-element.143), channel_id=1, source_target_pairs={{0,16},{2,18},{4,20},{6,22},{8,24},{10,26},{12,28},{14,30},{16,0},... | collective-permute-start | bytes 589832 | tf_op jit(solution)/shard_map/ppermute | solution.py:246
  147.0 10.4 %collective-permute-done.24.got_ref = bf16[64,1536]{1,0:T(8,128)(2,1)S(1)} collective-permute-done((bf16[64,1536]{1,0:T(8,128)(2,1)S(1)}, bf16[64,1536]{1,0:T(8,128)(2,1)S(1)}, u32[]{:S(2)}, u32[]{:S(2)}) %collective-permute-start.24) | collective-permute-done | bytes 196640 | tf_op jit(solution)/shard_map/ppermute | solution.py:246
  (74 shorter events, 24.3 us)
Async XLA Ops:
  0.6 13.7 %copy-start = (bf16[1,512,768]{2,1,0:T(8,128)(2,1)S(1)}, bf16[1,512,768]{2,1,0:T(8,128)(2,1)}, u32[]{:S(2)}) copy-start(bf16[1,512,768]{2,1,0:T(8,128)(2,1)} %param.23) | copy-start | bytes 2359300
  0.6 1.2 copy-start.1
  11.2 49.8 %collective-permute-start.2 = (bf16[768,1024]{1,0:T(8,128)(2,1)S(1)}, bf16[768,1024]{1,0:T(8,128)(2,1)S(1)}, u32[]{:S(2)}, u32[]{:S(2)}) collective-permute-start(bf16[768,1024]{1,0:T(8,128)(2,1)S(1)} %get-tuple-element.73.refs_8_), channel_id=1, source_target_pairs={{0,1},{1,0},{2,3},{3,2},{4,5},{5,4},{6,7},{7,6},{8,9},{9,8},{10,11... | collective-permute-start | bytes 4718600 | tf_op jit(solution)/shard_map/ppermute | solution.py:250
  11.7 77.1 %collective-permute-start = (bf16[768,1024]{1,0:T(8,128)(2,1)S(1)}, bf16[768,1024]{1,0:T(8,128)(2,1)S(1)}, u32[]{:S(2)}, u32[]{:S(2)}) collective-permute-start(bf16[768,1024]{1,0:T(8,128)(2,1)S(1)} %get-tuple-element.73.refs_8_), channel_id=1, source_target_pairs={{0,8},{2,10},{4,12},{6,14},{8,0},{10,2},{12,4},{14,6},{16,24},{18,... | collective-permute-start | bytes 4718600 | tf_op jit(solution)/shard_map/ppermute | solution.py:246
  14.4 46.6 %collective-permute-start.3 = (bf16[512,768]{1,0:T(8,128)(2,1)S(1)}, bf16[512,768]{1,0:T(8,128)(2,1)S(1)}, u32[]{:S(2)}, u32[]{:S(2)}) collective-permute-start(bf16[512,768]{1,0:T(8,128)(2,1)S(1)} %bitcast.7), channel_id=1, source_target_pairs={{0,1},{1,0},{2,3},{3,2},{4,5},{5,4},{6,7},{7,6},{8,9},{9,8},{10,11... | collective-permute-start | bytes 2359304 | tf_op jit(solution)/shard_map/ppermute | solution.py:250
  14.5 44.8 %collective-permute-start.1 = (bf16[64,1664]{1,0:T(8,128)(2,1)S(1)}, bf16[64,1664]{1,0:T(8,128)(2,1)S(1)}, u32[]{:S(2)}, u32[]{:S(2)}) collective-permute-start(bf16[64,1664]{1,0:T(8,128)(2,1)S(1)} %get-tuple-element.74), channel_id=1, source_target_pairs={{0,16},{2,18},{4,20},{6,22},{8,24},{10,26},{12,28},{14,30},{16,0},... | collective-permute-start | bytes 638984 | tf_op jit(solution)/shard_map/ppermute | solution.py:246
  17.1 40.6 %collective-permute-start.10 = (bf16[64,1664]{1,0:T(8,128)(2,1)S(1)}, bf16[64,1664]{1,0:T(8,128)(2,1)S(1)}, u32[]{:S(2)}, u32[]{:S(2)}) collective-permute-start(bf16[64,1664]{1,0:T(8,128)(2,1)S(1)} %get-tuple-element.76), channel_id=1, source_target_pairs={{0,16},{2,18},{4,20},{6,22},{8,24},{10,26},{12,28},{14,30},{16,0},... | collective-permute-start | bytes 638984 | tf_op jit(solution)/shard_map/ppermute | solution.py:246
  57.8 8.2 %collective-permute-start.11 = (bf16[64,1664]{1,0:T(8,128)(2,1)S(1)}, bf16[64,1664]{1,0:T(8,128)(2,1)S(1)}, u32[]{:S(2)}, u32[]{:S(2)}) collective-permute-start(bf16[64,1664]{1,0:T(8,128)(2,1)S(1)} %pad_maximum_fusion.2.refs_4_), channel_id=1, source_target_pairs={{0,2},{2,0},{4,6},{6,4},{8,10},{10,8},{12,14},{14,12},{16,18},{18,... | collective-permute-start | bytes 638984 | tf_op jit(solution)/shard_map/ppermute | solution.py:246
  59.4 8.3 %collective-permute-start.12 = (bf16[64,1664]{1,0:T(8,128)(2,1)S(1)}, bf16[64,1664]{1,0:T(8,128)(2,1)S(1)}, u32[]{:S(2)}, u32[]{:S(2)}) collective-permute-start(bf16[64,1664]{1,0:T(8,128)(2,1)S(1)} %pad_maximum_fusion.3.refs_6_), channel_id=1, source_target_pairs={{0,4},{2,6},{4,0},{6,2},{8,12},{10,14},{12,8},{14,10},{16,20},{18,... | collective-permute-start | bytes 638984 | tf_op jit(solution)/shard_map/ppermute | solution.py:246
  61.0 9.6 %collective-permute-start.5 = (bf16[64,1664]{1,0:T(8,128)(2,1)S(1)}, bf16[64,1664]{1,0:T(8,128)(2,1)S(1)}, u32[]{:S(2)}, u32[]{:S(2)}) collective-permute-start(bf16[64,1664]{1,0:T(8,128)(2,1)S(1)} %pad_maximum_fusion.refs_4_), channel_id=1, source_target_pairs={{0,2},{2,0},{4,6},{6,4},{8,10},{10,8},{12,14},{14,12},{16,18},{18,... | collective-permute-start | bytes 638984 | tf_op jit(solution)/shard_map/ppermute | solution.py:246
  61.6 10.6 %collective-permute-start.8 = (bf16[64,1664]{1,0:T(8,128)(2,1)S(1)}, bf16[64,1664]{1,0:T(8,128)(2,1)S(1)}, u32[]{:S(2)}, u32[]{:S(2)}) collective-permute-start(bf16[64,1664]{1,0:T(8,128)(2,1)S(1)} %pad_maximum_fusion.1.refs_6_), channel_id=1, source_target_pairs={{0,4},{2,6},{4,0},{6,2},{8,12},{10,14},{12,8},{14,10},{16,20},{18,... | collective-permute-start | bytes 638984 | tf_op jit(solution)/shard_map/ppermute | solution.py:246
  66.0 10.7 %collective-permute-start.4 = (bf16[64,1664]{1,0:T(8,128)(2,1)S(1)}, bf16[64,1664]{1,0:T(8,128)(2,1)S(1)}, u32[]{:S(2)}, u32[]{:S(2)}) collective-permute-start(bf16[64,1664]{1,0:T(8,128)(2,1)S(1)} %pad_maximum_fusion.refs_4_), channel_id=1, source_target_pairs={{0,4},{2,6},{4,0},{6,2},{8,12},{10,14},{12,8},{14,10},{16,20},{18,... | collective-permute-start | bytes 638984 | tf_op jit(solution)/shard_map/ppermute | solution.py:246
  67.6 10.7 %collective-permute-start.7 = (bf16[64,1664]{1,0:T(8,128)(2,1)S(1)}, bf16[64,1664]{1,0:T(8,128)(2,1)S(1)}, u32[]{:S(2)}, u32[]{:S(2)}) collective-permute-start(bf16[64,1664]{1,0:T(8,128)(2,1)S(1)} %pad_maximum_fusion.1.refs_6_), channel_id=1, source_target_pairs={{0,2},{2,0},{4,6},{6,4},{8,10},{10,8},{12,14},{14,12},{16,18},{18,... | collective-permute-start | bytes 638984 | tf_op jit(solution)/shard_map/ppermute | solution.py:246
  70.6 10.7 %collective-permute-start.6 = (bf16[64,1664]{1,0:T(8,128)(2,1)S(1)}, bf16[64,1664]{1,0:T(8,128)(2,1)S(1)}, u32[]{:S(2)}, u32[]{:S(2)}) collective-permute-start(bf16[64,1664]{1,0:T(8,128)(2,1)S(1)} %collective-permute-done.5.refs_5_), channel_id=1, source_target_pairs={{0,4},{2,6},{4,0},{6,2},{8,12},{10,14},{12,8},{14,10},{16,20},{18,... | collective-permute-start | bytes 638984 | tf_op jit(solution)/shard_map/ppermute | solution.py:246
  72.2 10.7 %collective-permute-start.9 = (bf16[64,1664]{1,0:T(8,128)(2,1)S(1)}, bf16[64,1664]{1,0:T(8,128)(2,1)S(1)}, u32[]{:S(2)}, u32[]{:S(2)}) collective-permute-start(bf16[64,1664]{1,0:T(8,128)(2,1)S(1)} %collective-permute-done.8.refs_7_), channel_id=1, source_target_pairs={{0,2},{2,0},{4,6},{6,4},{8,10},{10,8},{12,14},{14,12},{16,18},{18,... | collective-permute-start | bytes 638984 | tf_op jit(solution)/shard_map/ppermute | solution.py:246
  76.8 9.8 %collective-permute-start.13 = (bf16[64,1664]{1,0:T(8,128)(2,1)S(1)}, bf16[64,1664]{1,0:T(8,128)(2,1)S(1)}, u32[]{:S(2)}, u32[]{:S(2)}) collective-permute-start(bf16[64,1664]{1,0:T(8,128)(2,1)S(1)} %pad_maximum_fusion.2.refs_4_), channel_id=1, source_target_pairs={{0,4},{2,6},{4,0},{6,2},{8,12},{10,14},{12,8},{14,10},{16,20},{18,... | collective-permute-start | bytes 638984 | tf_op jit(solution)/shard_map/ppermute | solution.py:246
  78.3 8.2 %collective-permute-start.15 = (bf16[64,1664]{1,0:T(8,128)(2,1)S(1)}, bf16[64,1664]{1,0:T(8,128)(2,1)S(1)}, u32[]{:S(2)}, u32[]{:S(2)}) collective-permute-start(bf16[64,1664]{1,0:T(8,128)(2,1)S(1)} %pad_maximum_fusion.3.refs_6_), channel_id=1, source_target_pairs={{0,2},{2,0},{4,6},{6,4},{8,10},{10,8},{12,14},{14,12},{16,18},{18,... | collective-permute-start | bytes 638984 | tf_op jit(solution)/shard_map/ppermute | solution.py:246
  81.3 7.5 %collective-permute-start.14 = (bf16[64,1664]{1,0:T(8,128)(2,1)S(1)}, bf16[64,1664]{1,0:T(8,128)(2,1)S(1)}, u32[]{:S(2)}, u32[]{:S(2)}) collective-permute-start(bf16[64,1664]{1,0:T(8,128)(2,1)S(1)} %collective-permute-done.11.refs_5_), channel_id=1, source_target_pairs={{0,4},{2,6},{4,0},{6,2},{8,12},{10,14},{12,8},{14,10},{16,20},{18,... | collective-permute-start | bytes 638984 | tf_op jit(solution)/shard_map/ppermute | solution.py:246
  82.9 5.9 %collective-permute-start.16 = (bf16[64,1664]{1,0:T(8,128)(2,1)S(1)}, bf16[64,1664]{1,0:T(8,128)(2,1)S(1)}, u32[]{:S(2)}, u32[]{:S(2)}) collective-permute-start(bf16[64,1664]{1,0:T(8,128)(2,1)S(1)} %collective-permute-done.12.refs_7_), channel_id=1, source_target_pairs={{0,2},{2,0},{4,6},{6,4},{8,10},{10,8},{12,14},{14,12},{16,18},{18,... | collective-permute-start | bytes 638984 | tf_op jit(solution)/shard_map/ppermute | solution.py:246
  88.8 6.7 %collective-permute-start.18 = (bf16[768,1024]{1,0:T(8,128)(2,1)S(1)}, bf16[768,1024]{1,0:T(8,128)(2,1)S(1)}, u32[]{:S(2)}, u32[]{:S(2)}) collective-permute-start(bf16[768,1024]{1,0:T(8,128)(2,1)S(1)} %collective-permute-done.refs_8_), channel_id=1, source_target_pairs={{0,1},{1,0},{2,3},{3,2},{4,5},{5,4},{6,7},{7,6},{8,9},{9,8},{10,11... | collective-permute-start | bytes 4718600 | tf_op jit(solution)/shard_map/ppermute | solution.py:250
  88.8 21.7 %collective-permute-start.17 = (bf16[512,768]{1,0:T(8,128)(2,1)S(1)}, bf16[512,768]{1,0:T(8,128)(2,1)S(1)}, u32[]{:S(2)}, u32[]{:S(2)}) collective-permute-start(bf16[512,768]{1,0:T(8,128)(2,1)S(1)} %bitcast.9), channel_id=1, source_target_pairs={{0,8},{2,10},{4,12},{6,14},{8,0},{10,2},{12,4},{14,6},{16,24},{18,... | collective-permute-start | bytes 2359304 | tf_op jit(solution)/shard_map/ppermute | solution.py:246
  110.5 2.3 %collective-permute-start.19 = (bf16[512,768]{1,0:T(8,128)(2,1)S(1)}, bf16[512,768]{1,0:T(8,128)(2,1)S(1)}, u32[]{:S(2)}, u32[]{:S(2)}) collective-permute-start(bf16[512,768]{1,0:T(8,128)(2,1)S(1)} %collective-permute-done.17.down_a), channel_id=1, source_target_pairs={{0,1},{1,0},{2,3},{3,2},{4,5},{5,4},{6,7},{7,6},{8,9},{9,8},{10,11... | collective-permute-start | bytes 2359304 | tf_op jit(solution)/shard_map/ppermute | solution.py:250
  113.8 11.2 %collective-permute-start.20 = (bf16[128,1536]{1,0:T(8,128)(2,1)S(1)}, bf16[128,1536]{1,0:T(8,128)(2,1)S(1)}, u32[]{:S(2)}, u32[]{:S(2)}) collective-permute-start(bf16[128,1536]{1,0:T(8,128)(2,1)S(1)} %get-tuple-element.114), channel_id=1, source_target_pairs={{0,4},{2,6},{4,0},{6,2},{8,12},{10,14},{12,8},{14,10},{16,20},{18,... | collective-permute-start | bytes 1179656 | tf_op jit(solution)/shard_map/ppermute | solution.py:246
  115.4 10.9 %collective-permute-start.21 = (bf16[128,1536]{1,0:T(8,128)(2,1)S(1)}, bf16[128,1536]{1,0:T(8,128)(2,1)S(1)}, u32[]{:S(2)}, u32[]{:S(2)}) collective-permute-start(bf16[128,1536]{1,0:T(8,128)(2,1)S(1)} %get-tuple-element.117), channel_id=1, source_target_pairs={{0,2},{2,0},{4,6},{6,4},{8,10},{10,8},{12,14},{14,12},{16,18},{18,... | collective-permute-start | bytes 1179656 | tf_op jit(solution)/shard_map/ppermute | solution.py:246
  126.4 12.1 %collective-permute-start.25 = (bf16[128,1536]{1,0:T(8,128)(2,1)S(1)}, bf16[128,1536]{1,0:T(8,128)(2,1)S(1)}, u32[]{:S(2)}, u32[]{:S(2)}) collective-permute-start(bf16[128,1536]{1,0:T(8,128)(2,1)S(1)} %get-tuple-element.135), channel_id=1, source_target_pairs={{0,4},{2,6},{4,0},{6,2},{8,12},{10,14},{12,8},{14,10},{16,20},{18,... | collective-permute-start | bytes 1179656 | tf_op jit(solution)/shard_map/ppermute | solution.py:246
  126.9 12.2 %collective-permute-start.27 = (bf16[128,1536]{1,0:T(8,128)(2,1)S(1)}, bf16[128,1536]{1,0:T(8,128)(2,1)S(1)}, u32[]{:S(2)}, u32[]{:S(2)}) collective-permute-start(bf16[128,1536]{1,0:T(8,128)(2,1)S(1)} %get-tuple-element.139), channel_id=1, source_target_pairs={{0,2},{2,0},{4,6},{6,4},{8,10},{10,8},{12,14},{14,12},{16,18},{18,... | collective-permute-start | bytes 1179656 | tf_op jit(solution)/shard_map/ppermute | solution.py:246
  127.5 15.7 %collective-permute-start.22 = (bf16[64,1536]{1,0:T(8,128)(2,1)S(1)}, bf16[64,1536]{1,0:T(8,128)(2,1)S(1)}, u32[]{:S(2)}, u32[]{:S(2)}) collective-permute-start(bf16[64,1536]{1,0:T(8,128)(2,1)S(1)} %get-tuple-element.129), channel_id=1, source_target_pairs={{0,2},{2,0},{4,6},{6,4},{8,10},{10,8},{12,14},{14,12},{16,18},{18,... | collective-permute-start | bytes 589832 | tf_op jit(solution)/shard_map/ppermute | solution.py:246
  129.0 14.2 %collective-permute-start.23 = (bf16[64,1536]{1,0:T(8,128)(2,1)S(1)}, bf16[64,1536]{1,0:T(8,128)(2,1)S(1)}, u32[]{:S(2)}, u32[]{:S(2)}) collective-permute-start(bf16[64,1536]{1,0:T(8,128)(2,1)S(1)} %get-tuple-element.131), channel_id=1, source_target_pairs={{0,4},{2,6},{4,0},{6,2},{8,12},{10,14},{12,8},{14,10},{16,20},{18,... | collective-permute-start | bytes 589832 | tf_op jit(solution)/shard_map/ppermute | solution.py:246
  138.6 6.7 %collective-permute-start.26 = (bf16[64,1536]{1,0:T(8,128)(2,1)S(1)}, bf16[64,1536]{1,0:T(8,128)(2,1)S(1)}, u32[]{:S(2)}, u32[]{:S(2)}) collective-permute-start(bf16[64,1536]{1,0:T(8,128)(2,1)S(1)} %get-tuple-element.137), channel_id=1, source_target_pairs={{0,2},{2,0},{4,6},{6,4},{8,10},{10,8},{12,14},{14,12},{16,18},{18,... | collective-permute-start | bytes 589832 | tf_op jit(solution)/shard_map/ppermute | solution.py:246
  139.2 6.1 %collective-permute-start.28 = (bf16[64,1536]{1,0:T(8,128)(2,1)S(1)}, bf16[64,1536]{1,0:T(8,128)(2,1)S(1)}, u32[]{:S(2)}, u32[]{:S(2)}) collective-permute-start(bf16[64,1536]{1,0:T(8,128)(2,1)S(1)} %get-tuple-element.141), channel_id=1, source_target_pairs={{0,4},{2,6},{4,0},{6,2},{8,12},{10,14},{12,8},{14,10},{16,20},{18,... | collective-permute-start | bytes 589832 | tf_op jit(solution)/shard_map/ppermute | solution.py:246
  143.2 14.2 %collective-permute-start.24 = (bf16[64,1536]{1,0:T(8,128)(2,1)S(1)}, bf16[64,1536]{1,0:T(8,128)(2,1)S(1)}, u32[]{:S(2)}, u32[]{:S(2)}) collective-permute-start(bf16[64,1536]{1,0:T(8,128)(2,1)S(1)} %get-tuple-element.133), channel_id=1, source_target_pairs={{0,16},{2,18},{4,20},{6,22},{8,24},{10,26},{12,28},{14,30},{16,0},... | collective-permute-start | bytes 589832 | tf_op jit(solution)/shard_map/ppermute | solution.py:246
  145.4 14.2 %collective-permute-start.29 = (bf16[64,1536]{1,0:T(8,128)(2,1)S(1)}, bf16[64,1536]{1,0:T(8,128)(2,1)S(1)}, u32[]{:S(2)}, u32[]{:S(2)}) collective-permute-start(bf16[64,1536]{1,0:T(8,128)(2,1)S(1)} %get-tuple-element.143), channel_id=1, source_target_pairs={{0,16},{2,18},{4,20},{6,22},{8,24},{10,26},{12,28},{14,30},{16,0},... | collective-permute-start | bytes 589832 | tf_op jit(solution)/shard_map/ppermute | solution.py:246
  (10 other events, 7.7 us)

commit v5 on v4

--- a/solution.py
+++ b/solution.py
@@ -95,13 +95,14 @@
     )(*ins)
 
 
-def prepare_kernel(old_ref, new_ref, *refs):
-    hbm, outs, both_ref, held, sems = refs[:9], refs[9:11], refs[11], refs[12:19], refs[19]
-    ff = both_ref.shape[1] // 2
-    places = list(held) + [both_ref.at[:, :ff], both_ref.at[:, ff:]]
-    copies = [pltpu.make_async_copy(a, b, sems.at[i]) for i, (a, b) in enumerate(zip(hbm, places))]
+def prepare_kernel(*refs):
+    hbm, outs, held, sems = refs[:9], refs[9:11], refs[11:20], refs[20]
+    copies = [pltpu.make_async_copy(a, b, sems.at[i]) for i, (a, b) in enumerate(zip(hbm, held))]
     for copy in copies:
         copy.start()
+    for copy in copies:
+        copy.wait()
+    old_ref, new_ref = held[7:]
     group = old_ref.shape[0]
     sources = []
     for s in range(group):
@@ -109,8 +110,6 @@
         wanted = new_ref[s]
         other = jnp.where(wanted == old_ref[left], left, right)
         sources.append(jnp.where(wanted == old_ref[s], s, other))
-    for copy in copies[: len(held)]:
-        copy.wait()
     gain = held[0][...].astype(jnp.float32).reshape(1, -1)
     for b in range(2):
         tokens_ref, slots_ref, gates_ref = held[1 + b], held[3 + b], held[5 + b]
@@ -143,7 +142,17 @@
             preferred_element_type=jnp.float32,
         )
         out_ref[:, width:] = turned.astype(jnp.bfloat16)
-    for copy in copies[len(held) :]:
+
+
+def pack_kernel(gate_ref, up_ref, both_ref, sems):
+    ff = gate_ref.shape[1]
+    copies = [
+        pltpu.make_async_copy(gate_ref, both_ref.at[:, :ff], sems.at[0]),
+        pltpu.make_async_copy(up_ref, both_ref.at[:, ff:], sems.at[1]),
+    ]
+    for copy in copies:
+        copy.start()
+    for copy in copies:
         copy.wait()
 
 
@@ -306,29 +315,42 @@
     tok, width = batch_one.shape
     ff = gate_old.shape[2]
     gate, up, down = gate_old[0], up_old[0], down_old[0]
-    held = (norm_gain, batch_one, batch_two, slots_one.T, slots_two.T, gates_one.T, gates_two.T)
-    specs = [pl.BlockSpec(memory_space=pltpu.SMEM)] * 2
-    specs += [pl.BlockSpec(memory_space=pl.ANY)] * (len(held) + 2)
-    own_one, own_two, both = call(
+    held = (
+        norm_gain, batch_one, batch_two, slots_one.T, slots_two.T, gates_one.T, gates_two.T,
+        table_old, table_new,
+    )
+    hbm = pl.BlockSpec(memory_space=pltpu.HBM)
+    own = call(
         prepare_kernel,
-        (jax.ShapeDtypeStruct((tok, width + PACK), jnp.bfloat16),) * 2
-        + (jax.ShapeDtypeStruct((gate.shape[0], 2 * ff), jnp.bfloat16),),
-        (table_old, table_new, *held, gate, up),
+        (jax.ShapeDtypeStruct((tok, width + PACK), jnp.bfloat16),) * 2,
+        held,
         8,
         10 * tok * width,
         8 * tok * width,
-        [pltpu.VMEM(x.shape, x.dtype) for x in held]
-        + [pltpu.SemaphoreType.DMA((len(held) + 2,))],
-        specs,
-    )
-    own = (own_one, own_two)
-    both_by = swap(both, Z_LOW)
+        [(pltpu.SMEM if x.ndim == 1 and x.dtype == jnp.int32 else pltpu.VMEM)(x.shape, x.dtype) for x in held]
+        + [pltpu.SemaphoreType.DMA((len(held),))],
+        [hbm] * len(held),
+    )
+    both = call(
+        pack_kernel,
+        jax.ShapeDtypeStruct((gate.shape[0], 2 * ff), jnp.bfloat16),
+        (gate, up),
+        8,
+        0,
+        8 * gate.size,
+        [pltpu.SemaphoreType.DMA((2,))],
+        [hbm] * 2,
+    )
     twins = (swap_core(both), swap_core(down))
     far = [swap(x, Z_HIGH) for x in own]
-    far[0], twins = lax.optimization_barrier((far[0], twins))
-    first = [halves(x, y) for x, y in zip(own, far)]
-    second = [(swap(a1, X), swap(b1, Y)) for a1, b1 in first]
-    pieces = [spread(*f, *s) for f, s in zip(first, second)]
+    far[0], twins, both_later = lax.optimization_barrier((far[0], twins, both))
+    both_by = swap(both_later, Z_LOW)
+    first_one = halves(own[0], far[0])
+    second_one = swap(first_one[0], X), swap(first_one[1], Y)
+    far[1], second_one = lax.optimization_barrier((far[1], second_one))
+    first_two = halves(own[1], far[1])
+    second_two = swap(first_two[0], X), swap(first_two[1], Y)
+    pieces = [spread(*first_one, *second_one), spread(*first_two, *second_two)]
 
     rows = 8 * tok
     scratch = (pltpu.VMEM((rows, width + PACK), jnp.bfloat16),)
@@ -369,7 +391,6 @@
             2 * width * ff + 8 * rows * width,
         )
 
-    pieces[0], second[1] = lax.optimization_barrier((pieces[0], second[1]))
     total_one = own_total(pieces[0])
     down_later, both_by, total_one, pieces = lax.optimization_barrier(
         (down, both_by, total_one, pieces)
@@ -383,9 +404,7 @@
     )
     down_twin = swap_core(down_by)
     back_one = first_return(*join(total_one, *hidden_one))
-    sums_two = join(total_two, *hidden_two)
-    back_one, sums_two = lax.optimization_barrier((back_one, sums_two))
-    back_two = first_return(*sums_two)
+    back_two = first_return(*join(total_two, *hidden_two))
     return last_returns(*back_one), last_returns(*back_two)
 
 

time: 161 us -> 132 us (0.82)
  waiting for transfers between devices: 98.6 us -> 76 us
  local copies, waits for them, and re-layouts: 9 us -> 2.63 us
    ppermute x26, waiting for transfers between devices: 96.3 us -> 73.7 us  [swap(): lax.ppermute(block, 'expert', [(i, i ^ distance) for i in range(count)])]
    unnamed x24, local copies, waits for them, and re-layouts: 8.93 us -> 2.57 us
    pallas_call x15 -> x16, Pallas kernels: 16 us -> 16 us  [call(): pl.pallas_call(body, out_shape=outs, in_specs=specs or [smem if x.ndim ==...]
  transfers between devices with their start and end apart: 30 -> 30, of which waited for: 17 -> 18; matrix products, arithmetic and copies ran while one was open for 0% -> 0% of each run, Pallas kernels for 8% -> 11%
where the time goes in v5:
time: 132 us
  waiting for transfers between devices  76 us (58%)
  starting transfers between devices  35.9 us (27%)
  Pallas kernels  16 us (12%)
  local copies, waits for them, and re-layouts  2.63 us (2%)
    ppermute x26, waiting for transfers between devices, swap(): lax.ppermute(block, 'expert', [(i, i ^ distance) for i in range(count)])  73.7 us
    ppermute x26, starting transfers between devices, swap(): lax.ppermute(block, 'expert', [(i, i ^ distance) for i in range(count)])  35 us
    pallas_call x16, Pallas kernels, call(): pl.pallas_call(body, out_shape=outs, in_specs=specs or [smem if x.ndim ==...  16 us
  transfers between devices with their start and end apart: 30, of which 18 were waited for; matrix products, arithmetic and copies ran while one was open for 0% of the time, Pallas kernels for 11%

profile of v5, /device:TPU:0, one launch (start us, length us, event | category | flops | bytes accessed | tf_op | source)
XLA Modules:
  0.0 131.5 jit_solution(10481275514274840644)
XLA Ops:
  4.6 1.4 %shard_map.131 = (bf16[64,1664]{1,0:T(8,128)(2,1)S(1)}, bf16[64,1664]{1,0:T(8,128)(2,1)S(1)}) custom-call(bf16[1536]{0:T(1024)(128)(2,1)S(1)} %copy-done.5, bf16[64,1536]{1,0:T(8,128)(2,1)S(1)} %copy-done.3, bf16[64,1536]{1,0:T(8,128)(2,1)S(1)} %copy-done.4, s32[8,64]{1,0:T(8,128)S(1)} %bitcast.13, s32[8,64]{1,0:T(8,128)S(1)} %bitcast.14, ...), custom_call_target="tpu_custom_call" | custom-call | flops 983040 | bytes 786432 | tf_op jit(solution)/shard_map/pallas_call | solution.py:86
  6.0 3.7 %collective-permute-start = (bf16[64,1664]{1,0:T(8,128)(2,1)S(1)}, bf16[64,1664]{1,0:T(8,128)(2,1)S(1)}, u32[]{:S(2)}, u32[]{:S(2)}) collective-permute-start(bf16[64,1664]{1,0:T(8,128)(2,1)S(1)} %get-tuple-element.60), channel_id=1, source_target_pairs={{0,16},{2,18},{4,20},{6,22},{8,24},{10,26},{12,28},{14,30},{16,0},... | collective-permute-start | bytes 638984 | tf_op jit(solution)/shard_map/ppermute | solution.py:255
  9.8 15.1 %collective-permute-done = bf16[64,1664]{1,0:T(8,128)(2,1)S(1)} collective-permute-done((bf16[64,1664]{1,0:T(8,128)(2,1)S(1)}, bf16[64,1664]{1,0:T(8,128)(2,1)S(1)}, u32[]{:S(2)}, u32[]{:S(2)}) %collective-permute-start) | collective-permute-done | bytes 213024 | tf_op jit(solution)/shard_map/ppermute | solution.py:255
  25.0 1.8 %collective-permute-start.6 = (bf16[64,1664]{1,0:T(8,128)(2,1)S(1)}, bf16[64,1664]{1,0:T(8,128)(2,1)S(1)}, u32[]{:S(2)}, u32[]{:S(2)}) collective-permute-start(bf16[64,1664]{1,0:T(8,128)(2,1)S(1)} %pad_maximum_fusion.refs_4_), channel_id=1, source_target_pairs={{0,2},{2,0},{4,6},{6,4},{8,10},{10,8},{12,14},{14,12},{16,18},{18,... | collective-permute-start | bytes 638984 | tf_op jit(solution)/shard_map/ppermute | solution.py:255
  26.8 1.6 %collective-permute-start.7 = (bf16[64,1664]{1,0:T(8,128)(2,1)S(1)}, bf16[64,1664]{1,0:T(8,128)(2,1)S(1)}, u32[]{:S(2)}, u32[]{:S(2)}) collective-permute-start(bf16[64,1664]{1,0:T(8,128)(2,1)S(1)} %pad_maximum_fusion.1.refs_6_), channel_id=1, source_target_pairs={{0,4},{2,6},{4,0},{6,2},{8,12},{10,14},{12,8},{14,10},{16,20},{18,... | collective-permute-start | bytes 638984 | tf_op jit(solution)/shard_map/ppermute | solution.py:255
  29.2 1.6 %collective-permute-start.9 = (bf16[64,1664]{1,0:T(8,128)(2,1)S(1)}, bf16[64,1664]{1,0:T(8,128)(2,1)S(1)}, u32[]{:S(2)}, u32[]{:S(2)}) collective-permute-start(bf16[64,1664]{1,0:T(8,128)(2,1)S(1)} %pad_maximum_fusion.1.refs_6_), channel_id=1, source_target_pairs={{0,2},{2,0},{4,6},{6,4},{8,10},{10,8},{12,14},{14,12},{16,18},{18,... | collective-permute-start | bytes 638984 | tf_op jit(solution)/shard_map/ppermute | solution.py:255
  31.8 3.2 %collective-permute-done.7.refs_7_ = bf16[64,1664]{1,0:T(8,128)(2,1)S(1)} collective-permute-done((bf16[64,1664]{1,0:T(8,128)(2,1)S(1)}, bf16[64,1664]{1,0:T(8,128)(2,1)S(1)}, u32[]{:S(2)}, u32[]{:S(2)}) %collective-permute-start.7) | collective-permute-done | bytes 213024 | tf_op jit(solution)/shard_map/ppermute | solution.py:255
  35.5 1.8 %collective-permute-start.15 = (bf16[64,1664]{1,0:T(8,128)(2,1)S(1)}, bf16[64,1664]{1,0:T(8,128)(2,1)S(1)}, u32[]{:S(2)}, u32[]{:S(2)}) collective-permute-start(bf16[64,1664]{1,0:T(8,128)(2,1)S(1)} %pad_maximum_fusion.3.refs_6_), channel_id=1, source_target_pairs={{0,4},{2,6},{4,0},{6,2},{8,12},{10,14},{12,8},{14,10},{16,20},{18,... | collective-permute-start | bytes 638984 | tf_op jit(solution)/shard_map/ppermute | solution.py:255
  37.3 2.3 %collective-permute-done.4.refs_0_ = bf16[64,1664]{1,0:T(8,128)(2,1)S(1)} collective-permute-done((bf16[64,1664]{1,0:T(8,128)(2,1)S(1)}, bf16[64,1664]{1,0:T(8,128)(2,1)S(1)}, u32[]{:S(2)}, u32[]{:S(2)}) %collective-permute-start.4) | collective-permute-done | bytes 213024 | tf_op jit(solution)/shard_map/ppermute | solution.py:255
  39.6 1.5 %collective-permute-start.8 = (bf16[64,1664]{1,0:T(8,128)(2,1)S(1)}, bf16[64,1664]{1,0:T(8,128)(2,1)S(1)}, u32[]{:S(2)}, u32[]{:S(2)}) collective-permute-start(bf16[64,1664]{1,0:T(8,128)(2,1)S(1)} %collective-permute-done.6.refs_5_), channel_id=1, source_target_pairs={{0,4},{2,6},{4,0},{6,2},{8,12},{10,14},{12,8},{14,10},{16,20},{18,... | collective-permute-start | bytes 638984 | tf_op jit(solution)/shard_map/ppermute | solution.py:255
  42.8 2.1 %collective-permute-start.11 = (bf16[64,1664]{1,0:T(8,128)(2,1)S(1)}, bf16[64,1664]{1,0:T(8,128)(2,1)S(1)}, u32[]{:S(2)}, u32[]{:S(2)}) collective-permute-start(bf16[64,1664]{1,0:T(8,128)(2,1)S(1)} %pad_maximum_fusion.2.refs_4_), channel_id=1, source_target_pairs={{0,4},{2,6},{4,0},{6,2},{8,12},{10,14},{12,8},{14,10},{16,20},{18,... | collective-permute-start | bytes 638984 | tf_op jit(solution)/shard_map/ppermute | solution.py:255
  45.5 3.3 %collective-permute-done.8.refs_1_ = bf16[64,1664]{1,0:T(8,128)(2,1)S(1)} collective-permute-done((bf16[64,1664]{1,0:T(8,128)(2,1)S(1)}, bf16[64,1664]{1,0:T(8,128)(2,1)S(1)}, u32[]{:S(2)}, u32[]{:S(2)}) %collective-permute-start.8) | collective-permute-done | bytes 213024 | tf_op jit(solution)/shard_map/ppermute | solution.py:255
  48.7 1.5 %collective-permute-start.13 = (bf16[64,1664]{1,0:T(8,128)(2,1)S(1)}, bf16[64,1664]{1,0:T(8,128)(2,1)S(1)}, u32[]{:S(2)}, u32[]{:S(2)}) collective-permute-start(bf16[64,1664]{1,0:T(8,128)(2,1)S(1)} %collective-permute-done.12.refs_5_), channel_id=1, source_target_pairs={{0,4},{2,6},{4,0},{6,2},{8,12},{10,14},{12,8},{14,10},{16,20},{18,... | collective-permute-start | bytes 638984 | tf_op jit(solution)/shard_map/ppermute | solution.py:255
  50.3 1.3 collective-permute-start.16
  51.6 3.1 %shard_map.133.total_ref = f32[512,1536]{1,0:T(8,128)S(1)} custom-call(bf16[64,1664]{1,0:T(8,128)(2,1)S(1)} %collective-permute-done.4.refs_0_, bf16[64,1664]{1,0:T(8,128)(2,1)S(1)} %collective-permute-done.8.refs_1_, bf16[64,1664]{1,0:T(8,128)(2,1)S(1)} %collective-permute-done.9.refs_2_, bf16[64,1664]{1,0:T(8,128)(2,1)S(1)} %collective-permute-done.10.refs_3_, ...), custom_call_target="tpu_custom_call" | custom-call | flops 2415919104 | bytes 9437184 | tf_op jit(solution)/shard_map/pallas_call | solution.py:86
  56.1 7.2 %collective-permute-done.3.refs_8_ = bf16[768,1024]{1,0:T(8,128)(2,1)S(1)} collective-permute-done((bf16[768,1024]{1,0:T(8,128)(2,1)S(1)}, bf16[768,1024]{1,0:T(8,128)(2,1)S(1)}, u32[]{:S(2)}, u32[]{:S(2)}) %collective-permute-start.3) | collective-permute-done | bytes 1572896 | tf_op jit(solution)/shard_map/ppermute | solution.py:255
  64.4 3.1 %shard_map.134.total_ref = f32[512,1536]{1,0:T(8,128)S(1)} custom-call(bf16[64,1664]{1,0:T(8,128)(2,1)S(1)} %collective-permute-done.11.refs_0_, bf16[64,1664]{1,0:T(8,128)(2,1)S(1)} %collective-permute-done.13.refs_1_, bf16[64,1664]{1,0:T(8,128)(2,1)S(1)} %collective-permute-done.14.refs_2_, bf16[64,1664]{1,0:T(8,128)(2,1)S(1)} %collective-permute-done.16.refs_3_, ...), custom_call_target="tpu_custom_call" | custom-call | flops 2415919104 | bytes 9437184 | tf_op jit(solution)/shard_map/pallas_call | solution.py:86
  67.5 2.1 %shard_map.136 = (bf16[512,512]{1,0:T(8,128)(2,1)S(1)}, f32[512,128]{1,0:T(8,128)S(1)}) custom-call(bf16[64,1664]{1,0:T(8,128)(2,1)S(1)} %collective-permute-done.11.refs_0_, bf16[64,1664]{1,0:T(8,128)(2,1)S(1)} %collective-permute-done.13.refs_1_, bf16[64,1664]{1,0:T(8,128)(2,1)S(1)} %collective-permute-done.14.refs_2_, ...), custom_call_target="tpu_custom_call" | custom-call | flops 1610612736 | bytes 4718592 | tf_op jit(solution)/shard_map/pallas_call | solution.py:86
  69.7 2.2 %shard_map.135 = (bf16[512,512]{1,0:T(8,128)(2,1)S(1)}, f32[512,128]{1,0:T(8,128)S(1)}) custom-call(bf16[64,1664]{1,0:T(8,128)(2,1)S(1)} %collective-permute-done.4.refs_0_, bf16[64,1664]{1,0:T(8,128)(2,1)S(1)} %collective-permute-done.8.refs_1_, bf16[64,1664]{1,0:T(8,128)(2,1)S(1)} %collective-permute-done.9.refs_2_, ...), custom_call_target="tpu_custom_call" | custom-call | flops 1610612736 | bytes 4718592 | tf_op jit(solution)/shard_map/pallas_call | solution.py:86
  71.8 11.4 %collective-permute-done.17.down_a = bf16[512,768]{1,0:T(8,128)(2,1)S(1)} collective-permute-done((bf16[512,768]{1,0:T(8,128)(2,1)S(1)}, bf16[512,768]{1,0:T(8,128)(2,1)S(1)}, u32[]{:S(2)}, u32[]{:S(2)}) %collective-permute-start.17) | collective-permute-done | bytes 786464 | tf_op jit(solution)/shard_map/ppermute | solution.py:255
  83.3 2.3 %collective-permute-done.19.down_b = bf16[512,768]{1,0:T(8,128)(2,1)S(1)} collective-permute-done((bf16[512,768]{1,0:T(8,128)(2,1)S(1)}, bf16[512,768]{1,0:T(8,128)(2,1)S(1)}, u32[]{:S(2)}, u32[]{:S(2)}) %collective-permute-start.19) | collective-permute-done | bytes 786464 | tf_op jit(solution)/shard_map/ppermute | solution.py:259
  86.6 1.3 collective-permute-start.25
  87.8 1.5 %collective-permute-start.27 = (bf16[128,1536]{1,0:T(8,128)(2,1)S(1)}, bf16[128,1536]{1,0:T(8,128)(2,1)S(1)}, u32[]{:S(2)}, u32[]{:S(2)}) collective-permute-start(bf16[128,1536]{1,0:T(8,128)(2,1)S(1)} %get-tuple-element.113), channel_id=1, source_target_pairs={{0,2},{2,0},{4,6},{6,4},{8,10},{10,8},{12,14},{14,12},{16,18},{18,... | collective-permute-start | bytes 1179656 | tf_op jit(solution)/shard_map/ppermute | solution.py:255
  91.8 6.8 %collective-permute-done.25.got_ref = bf16[128,1536]{1,0:T(8,128)(2,1)S(1)} collective-permute-done((bf16[128,1536]{1,0:T(8,128)(2,1)S(1)}, bf16[128,1536]{1,0:T(8,128)(2,1)S(1)}, u32[]{:S(2)}, u32[]{:S(2)}) %collective-permute-start.25) | collective-permute-done | bytes 393248 | tf_op jit(solution)/shard_map/ppermute | solution.py:255
  100.0 1.6 %collective-permute-start.28 = (bf16[64,1536]{1,0:T(8,128)(2,1)S(1)}, bf16[64,1536]{1,0:T(8,128)(2,1)S(1)}, u32[]{:S(2)}, u32[]{:S(2)}) collective-permute-start(bf16[64,1536]{1,0:T(8,128)(2,1)S(1)} %get-tuple-element.115), channel_id=1, source_target_pairs={{0,4},{2,6},{4,0},{6,2},{8,12},{10,14},{12,8},{14,10},{16,20},{18,... | collective-permute-start | bytes 589832 | tf_op jit(solution)/shard_map/ppermute | solution.py:255
  101.5 5.5 %collective-permute-done.20.got_ref = bf16[128,1536]{1,0:T(8,128)(2,1)S(1)} collective-permute-done((bf16[128,1536]{1,0:T(8,128)(2,1)S(1)}, bf16[128,1536]{1,0:T(8,128)(2,1)S(1)}, u32[]{:S(2)}, u32[]{:S(2)}) %collective-permute-start.20) | collective-permute-done | bytes 393248 | tf_op jit(solution)/shard_map/ppermute | solution.py:255
  108.4 1.6 %collective-permute-start.23 = (bf16[64,1536]{1,0:T(8,128)(2,1)S(1)}, bf16[64,1536]{1,0:T(8,128)(2,1)S(1)}, u32[]{:S(2)}, u32[]{:S(2)}) collective-permute-start(bf16[64,1536]{1,0:T(8,128)(2,1)S(1)} %get-tuple-element.102), channel_id=1, source_target_pairs={{0,4},{2,6},{4,0},{6,2},{8,12},{10,14},{12,8},{14,10},{16,20},{18,... | collective-permute-start | bytes 589832 | tf_op jit(solution)/shard_map/ppermute | solution.py:255
  110.0 2.5 %collective-permute-done.26.got_a = bf16[64,1536]{1,0:T(8,128)(2,1)S(1)} collective-permute-done((bf16[64,1536]{1,0:T(8,128)(2,1)S(1)}, bf16[64,1536]{1,0:T(8,128)(2,1)S(1)}, u32[]{:S(2)}, u32[]{:S(2)}) %collective-permute-start.26) | collective-permute-done | bytes 196640 | tf_op jit(solution)/shard_map/ppermute | solution.py:255
  112.5 2.4 %collective-permute-start.29 = (bf16[64,1536]{1,0:T(8,128)(2,1)S(1)}, bf16[64,1536]{1,0:T(8,128)(2,1)S(1)}, u32[]{:S(2)}, u32[]{:S(2)}) collective-permute-start(bf16[64,1536]{1,0:T(8,128)(2,1)S(1)} %get-tuple-element.117), channel_id=1, source_target_pairs={{0,16},{2,18},{4,20},{6,22},{8,24},{10,26},{12,28},{14,30},{16,0},... | collective-permute-start | bytes 589832 | tf_op jit(solution)/shard_map/ppermute | solution.py:255
  115.6 2.4 %collective-permute-start.24 = (bf16[64,1536]{1,0:T(8,128)(2,1)S(1)}, bf16[64,1536]{1,0:T(8,128)(2,1)S(1)}, u32[]{:S(2)}, u32[]{:S(2)}) collective-permute-start(bf16[64,1536]{1,0:T(8,128)(2,1)S(1)} %get-tuple-element.104), channel_id=1, source_target_pairs={{0,16},{2,18},{4,20},{6,22},{8,24},{10,26},{12,28},{14,30},{16,0},... | collective-permute-start | bytes 589832 | tf_op jit(solution)/shard_map/ppermute | solution.py:255
  118.0 9.6 %collective-permute-done.29.got_ref = bf16[64,1536]{1,0:T(8,128)(2,1)S(1)} collective-permute-done((bf16[64,1536]{1,0:T(8,128)(2,1)S(1)}, bf16[64,1536]{1,0:T(8,128)(2,1)S(1)}, u32[]{:S(2)}, u32[]{:S(2)}) %collective-permute-start.29) | collective-permute-done | bytes 196640 | tf_op jit(solution)/shard_map/ppermute | solution.py:255
  128.4 2.5 %collective-permute-done.24.got_ref = bf16[64,1536]{1,0:T(8,128)(2,1)S(1)} collective-permute-done((bf16[64,1536]{1,0:T(8,128)(2,1)S(1)}, bf16[64,1536]{1,0:T(8,128)(2,1)S(1)}, u32[]{:S(2)}, u32[]{:S(2)}) %collective-permute-start.24) | collective-permute-done | bytes 196640 | tf_op jit(solution)/shard_map/ppermute | solution.py:255
  (75 shorter events, 19.3 us)
Async XLA Ops:
  2.9 1.6 %copy-start.4 = (bf16[64,1536]{1,0:T(8,128)(2,1)S(1)}, bf16[64,1536]{1,0:T(8,128)(2,1)}, u32[]{:S(2)}) copy-start(bf16[64,1536]{1,0:T(8,128)(2,1)} %refs_2_.1) | copy-start | bytes 589828
  2.9 1.6 %copy-start.5 = (bf16[1536]{0:T(1024)(128)(2,1)S(1)}, bf16[1536]{0:T(1024)(128)(2,1)}, u32[]{:S(2)}) copy-start(bf16[1536]{0:T(1024)(128)(2,1)} %refs_0_.1) | copy-start | bytes 9220
  3.2 21.7 %collective-permute-start.1 = (bf16[768,1024]{1,0:T(8,128)(2,1)S(1)}, bf16[768,1024]{1,0:T(8,128)(2,1)S(1)}, u32[]{:S(2)}, u32[]{:S(2)}) collective-permute-start(bf16[768,1024]{1,0:T(8,128)(2,1)S(1)} %shard_map.132.refs_8_), channel_id=1, source_target_pairs={{0,1},{1,0},{2,3},{3,2},{4,5},{5,4},{6,7},{7,6},{8,9},{9,8},{10,11... | collective-permute-start | bytes 4718600 | tf_op jit(solution)/shard_map/ppermute | solution.py:259
  4.0 20.9 %collective-permute-start.2 = (bf16[512,768]{1,0:T(8,128)(2,1)S(1)}, bf16[512,768]{1,0:T(8,128)(2,1)S(1)}, u32[]{:S(2)}, u32[]{:S(2)}) collective-permute-start(bf16[512,768]{1,0:T(8,128)(2,1)S(1)} %bitcast.7), channel_id=1, source_target_pairs={{0,1},{1,0},{2,3},{3,2},{4,5},{5,4},{6,7},{7,6},{8,9},{9,8},{10,11... | collective-permute-start | bytes 2359304 | tf_op jit(solution)/shard_map/ppermute | solution.py:259
  6.0 19.0 %collective-permute-start = (bf16[64,1664]{1,0:T(8,128)(2,1)S(1)}, bf16[64,1664]{1,0:T(8,128)(2,1)S(1)}, u32[]{:S(2)}, u32[]{:S(2)}) collective-permute-start(bf16[64,1664]{1,0:T(8,128)(2,1)S(1)} %get-tuple-element.60), channel_id=1, source_target_pairs={{0,16},{2,18},{4,20},{6,22},{8,24},{10,26},{12,28},{14,30},{16,0},... | collective-permute-start | bytes 638984 | tf_op jit(solution)/shard_map/ppermute | solution.py:255
  9.7 19.6 %collective-permute-start.5 = (bf16[64,1664]{1,0:T(8,128)(2,1)S(1)}, bf16[64,1664]{1,0:T(8,128)(2,1)S(1)}, u32[]{:S(2)}, u32[]{:S(2)}) collective-permute-start(bf16[64,1664]{1,0:T(8,128)(2,1)S(1)} %get-tuple-element.63), channel_id=1, source_target_pairs={{0,16},{2,18},{4,20},{6,22},{8,24},{10,26},{12,28},{14,30},{16,0},... | collective-permute-start | bytes 638984 | tf_op jit(solution)/shard_map/ppermute | solution.py:255
  25.0 6.9 %collective-permute-start.6 = (bf16[64,1664]{1,0:T(8,128)(2,1)S(1)}, bf16[64,1664]{1,0:T(8,128)(2,1)S(1)}, u32[]{:S(2)}, u32[]{:S(2)}) collective-permute-start(bf16[64,1664]{1,0:T(8,128)(2,1)S(1)} %pad_maximum_fusion.refs_4_), channel_id=1, source_target_pairs={{0,2},{2,0},{4,6},{6,4},{8,10},{10,8},{12,14},{14,12},{16,18},{18,... | collective-permute-start | bytes 638984 | tf_op jit(solution)/shard_map/ppermute | solution.py:255
  26.8 8.3 %collective-permute-start.7 = (bf16[64,1664]{1,0:T(8,128)(2,1)S(1)}, bf16[64,1664]{1,0:T(8,128)(2,1)S(1)}, u32[]{:S(2)}, u32[]{:S(2)}) collective-permute-start(bf16[64,1664]{1,0:T(8,128)(2,1)S(1)} %pad_maximum_fusion.1.refs_6_), channel_id=1, source_target_pairs={{0,4},{2,6},{4,0},{6,2},{8,12},{10,14},{12,8},{14,10},{16,20},{18,... | collective-permute-start | bytes 638984 | tf_op jit(solution)/shard_map/ppermute | solution.py:255
  28.4 34.9 %collective-permute-start.3 = (bf16[768,1024]{1,0:T(8,128)(2,1)S(1)}, bf16[768,1024]{1,0:T(8,128)(2,1)S(1)}, u32[]{:S(2)}, u32[]{:S(2)}) collective-permute-start(bf16[768,1024]{1,0:T(8,128)(2,1)S(1)} %shard_map.132.refs_8_), channel_id=1, source_target_pairs={{0,8},{2,10},{4,12},{6,14},{8,0},{10,2},{12,4},{14,6},{16,24},{18,... | collective-permute-start | bytes 4718600 | tf_op jit(solution)/shard_map/ppermute | solution.py:255
  28.6 11.0 %collective-permute-start.4 = (bf16[64,1664]{1,0:T(8,128)(2,1)S(1)}, bf16[64,1664]{1,0:T(8,128)(2,1)S(1)}, u32[]{:S(2)}, u32[]{:S(2)}) collective-permute-start(bf16[64,1664]{1,0:T(8,128)(2,1)S(1)} %pad_maximum_fusion.refs_4_), channel_id=1, source_target_pairs={{0,4},{2,6},{4,0},{6,2},{8,12},{10,14},{12,8},{14,10},{16,20},{18,... | collective-permute-start | bytes 638984 | tf_op jit(solution)/shard_map/ppermute | solution.py:255
  29.2 11.9 %collective-permute-start.9 = (bf16[64,1664]{1,0:T(8,128)(2,1)S(1)}, bf16[64,1664]{1,0:T(8,128)(2,1)S(1)}, u32[]{:S(2)}, u32[]{:S(2)}) collective-permute-start(bf16[64,1664]{1,0:T(8,128)(2,1)S(1)} %pad_maximum_fusion.1.refs_6_), channel_id=1, source_target_pairs={{0,2},{2,0},{4,6},{6,4},{8,10},{10,8},{12,14},{14,12},{16,18},{18,... | collective-permute-start | bytes 638984 | tf_op jit(solution)/shard_map/ppermute | solution.py:255
  35.1 7.7 %collective-permute-start.12 = (bf16[64,1664]{1,0:T(8,128)(2,1)S(1)}, bf16[64,1664]{1,0:T(8,128)(2,1)S(1)}, u32[]{:S(2)}, u32[]{:S(2)}) collective-permute-start(bf16[64,1664]{1,0:T(8,128)(2,1)S(1)} %pad_maximum_fusion.2.refs_4_), channel_id=1, source_target_pairs={{0,2},{2,0},{4,6},{6,4},{8,10},{10,8},{12,14},{14,12},{16,18},{18,... | collective-permute-start | bytes 638984 | tf_op jit(solution)/shard_map/ppermute | solution.py:255
  35.5 9.4 %collective-permute-start.15 = (bf16[64,1664]{1,0:T(8,128)(2,1)S(1)}, bf16[64,1664]{1,0:T(8,128)(2,1)S(1)}, u32[]{:S(2)}, u32[]{:S(2)}) collective-permute-start(bf16[64,1664]{1,0:T(8,128)(2,1)S(1)} %pad_maximum_fusion.3.refs_6_), channel_id=1, source_target_pairs={{0,4},{2,6},{4,0},{6,2},{8,12},{10,14},{12,8},{14,10},{16,20},{18,... | collective-permute-start | bytes 638984 | tf_op jit(solution)/shard_map/ppermute | solution.py:255
  39.6 9.1 %collective-permute-start.8 = (bf16[64,1664]{1,0:T(8,128)(2,1)S(1)}, bf16[64,1664]{1,0:T(8,128)(2,1)S(1)}, u32[]{:S(2)}, u32[]{:S(2)}) collective-permute-start(bf16[64,1664]{1,0:T(8,128)(2,1)S(1)} %collective-permute-done.6.refs_5_), channel_id=1, source_target_pairs={{0,4},{2,6},{4,0},{6,2},{8,12},{10,14},{12,8},{14,10},{16,20},{18,... | collective-permute-start | bytes 638984 | tf_op jit(solution)/shard_map/ppermute | solution.py:255
  41.1 9.1 %collective-permute-start.10 = (bf16[64,1664]{1,0:T(8,128)(2,1)S(1)}, bf16[64,1664]{1,0:T(8,128)(2,1)S(1)}, u32[]{:S(2)}, u32[]{:S(2)}) collective-permute-start(bf16[64,1664]{1,0:T(8,128)(2,1)S(1)} %collective-permute-done.7.refs_7_), channel_id=1, source_target_pairs={{0,2},{2,0},{4,6},{6,4},{8,10},{10,8},{12,14},{14,12},{16,18},{18,... | collective-permute-start | bytes 638984 | tf_op jit(solution)/shard_map/ppermute | solution.py:255
  42.8 11.9 %collective-permute-start.11 = (bf16[64,1664]{1,0:T(8,128)(2,1)S(1)}, bf16[64,1664]{1,0:T(8,128)(2,1)S(1)}, u32[]{:S(2)}, u32[]{:S(2)}) collective-permute-start(bf16[64,1664]{1,0:T(8,128)(2,1)S(1)} %pad_maximum_fusion.2.refs_4_), channel_id=1, source_target_pairs={{0,4},{2,6},{4,0},{6,2},{8,12},{10,14},{12,8},{14,10},{16,20},{18,... | collective-permute-start | bytes 638984 | tf_op jit(solution)/shard_map/ppermute | solution.py:255
  44.9 9.8 %collective-permute-start.14 = (bf16[64,1664]{1,0:T(8,128)(2,1)S(1)}, bf16[64,1664]{1,0:T(8,128)(2,1)S(1)}, u32[]{:S(2)}, u32[]{:S(2)}) collective-permute-start(bf16[64,1664]{1,0:T(8,128)(2,1)S(1)} %pad_maximum_fusion.3.refs_6_), channel_id=1, source_target_pairs={{0,2},{2,0},{4,6},{6,4},{8,10},{10,8},{12,14},{14,12},{16,18},{18,... | collective-permute-start | bytes 638984 | tf_op jit(solution)/shard_map/ppermute | solution.py:255
  48.7 7.0 %collective-permute-start.13 = (bf16[64,1664]{1,0:T(8,128)(2,1)S(1)}, bf16[64,1664]{1,0:T(8,128)(2,1)S(1)}, u32[]{:S(2)}, u32[]{:S(2)}) collective-permute-start(bf16[64,1664]{1,0:T(8,128)(2,1)S(1)} %collective-permute-done.12.refs_5_), channel_id=1, source_target_pairs={{0,4},{2,6},{4,0},{6,2},{8,12},{10,14},{12,8},{14,10},{16,20},{18,... | collective-permute-start | bytes 638984 | tf_op jit(solution)/shard_map/ppermute | solution.py:255
  50.3 5.8 %collective-permute-start.16 = (bf16[64,1664]{1,0:T(8,128)(2,1)S(1)}, bf16[64,1664]{1,0:T(8,128)(2,1)S(1)}, u32[]{:S(2)}, u32[]{:S(2)}) collective-permute-start(bf16[64,1664]{1,0:T(8,128)(2,1)S(1)} %collective-permute-done.15.refs_7_), channel_id=1, source_target_pairs={{0,2},{2,0},{4,6},{6,4},{8,10},{10,8},{12,14},{14,12},{16,18},{18,... | collective-permute-start | bytes 638984 | tf_op jit(solution)/shard_map/ppermute | solution.py:255
  63.3 4.2 %collective-permute-start.18 = (bf16[768,1024]{1,0:T(8,128)(2,1)S(1)}, bf16[768,1024]{1,0:T(8,128)(2,1)S(1)}, u32[]{:S(2)}, u32[]{:S(2)}) collective-permute-start(bf16[768,1024]{1,0:T(8,128)(2,1)S(1)} %collective-permute-done.3.refs_8_), channel_id=1, source_target_pairs={{0,1},{1,0},{2,3},{3,2},{4,5},{5,4},{6,7},{7,6},{8,9},{9,8},{10,11... | collective-permute-start | bytes 4718600 | tf_op jit(solution)/shard_map/ppermute | solution.py:259
  63.3 20.0 %collective-permute-start.17 = (bf16[512,768]{1,0:T(8,128)(2,1)S(1)}, bf16[512,768]{1,0:T(8,128)(2,1)S(1)}, u32[]{:S(2)}, u32[]{:S(2)}) collective-permute-start(bf16[512,768]{1,0:T(8,128)(2,1)S(1)} %bitcast.9), channel_id=1, source_target_pairs={{0,8},{2,10},{4,12},{6,14},{8,0},{10,2},{12,4},{14,6},{16,24},{18,... | collective-permute-start | bytes 2359304 | tf_op jit(solution)/shard_map/ppermute | solution.py:255
  83.3 2.3 %collective-permute-start.19 = (bf16[512,768]{1,0:T(8,128)(2,1)S(1)}, bf16[512,768]{1,0:T(8,128)(2,1)S(1)}, u32[]{:S(2)}, u32[]{:S(2)}) collective-permute-start(bf16[512,768]{1,0:T(8,128)(2,1)S(1)} %collective-permute-done.17.down_a), channel_id=1, source_target_pairs={{0,1},{1,0},{2,3},{3,2},{4,5},{5,4},{6,7},{7,6},{8,9},{9,8},{10,11... | collective-permute-start | bytes 2359304 | tf_op jit(solution)/shard_map/ppermute | solution.py:259
  86.6 12.0 %collective-permute-start.25 = (bf16[128,1536]{1,0:T(8,128)(2,1)S(1)}, bf16[128,1536]{1,0:T(8,128)(2,1)S(1)}, u32[]{:S(2)}, u32[]{:S(2)}) collective-permute-start(bf16[128,1536]{1,0:T(8,128)(2,1)S(1)} %get-tuple-element.109), channel_id=1, source_target_pairs={{0,4},{2,6},{4,0},{6,2},{8,12},{10,14},{12,8},{14,10},{16,20},{18,... | collective-permute-start | bytes 1179656 | tf_op jit(solution)/shard_map/ppermute | solution.py:255
  87.8 12.1 %collective-permute-start.27 = (bf16[128,1536]{1,0:T(8,128)(2,1)S(1)}, bf16[128,1536]{1,0:T(8,128)(2,1)S(1)}, u32[]{:S(2)}, u32[]{:S(2)}) collective-permute-start(bf16[128,1536]{1,0:T(8,128)(2,1)S(1)} %get-tuple-element.113), channel_id=1, source_target_pairs={{0,2},{2,0},{4,6},{6,4},{8,10},{10,8},{12,14},{14,12},{16,18},{18,... | collective-permute-start | bytes 1179656 | tf_op jit(solution)/shard_map/ppermute | solution.py:255
  90.3 16.7 %collective-permute-start.20 = (bf16[128,1536]{1,0:T(8,128)(2,1)S(1)}, bf16[128,1536]{1,0:T(8,128)(2,1)S(1)}, u32[]{:S(2)}, u32[]{:S(2)}) collective-permute-start(bf16[128,1536]{1,0:T(8,128)(2,1)S(1)} %get-tuple-element.96), channel_id=1, source_target_pairs={{0,4},{2,6},{4,0},{6,2},{8,12},{10,14},{12,8},{14,10},{16,20},{18,... | collective-permute-start | bytes 1179656 | tf_op jit(solution)/shard_map/ppermute | solution.py:255
  90.9 17.4 %collective-permute-start.22 = (bf16[128,1536]{1,0:T(8,128)(2,1)S(1)}, bf16[128,1536]{1,0:T(8,128)(2,1)S(1)}, u32[]{:S(2)}, u32[]{:S(2)}) collective-permute-start(bf16[128,1536]{1,0:T(8,128)(2,1)S(1)} %get-tuple-element.100), channel_id=1, source_target_pairs={{0,2},{2,0},{4,6},{6,4},{8,10},{10,8},{12,14},{14,12},{16,18},{18,... | collective-permute-start | bytes 1179656 | tf_op jit(solution)/shard_map/ppermute | solution.py:255
  98.7 13.8 %collective-permute-start.26 = (bf16[64,1536]{1,0:T(8,128)(2,1)S(1)}, bf16[64,1536]{1,0:T(8,128)(2,1)S(1)}, u32[]{:S(2)}, u32[]{:S(2)}) collective-permute-start(bf16[64,1536]{1,0:T(8,128)(2,1)S(1)} %get-tuple-element.111), channel_id=1, source_target_pairs={{0,2},{2,0},{4,6},{6,4},{8,10},{10,8},{12,14},{14,12},{16,18},{18,... | collective-permute-start | bytes 589832 | tf_op jit(solution)/shard_map/ppermute | solution.py:255
  100.0 12.5 %collective-permute-start.28 = (bf16[64,1536]{1,0:T(8,128)(2,1)S(1)}, bf16[64,1536]{1,0:T(8,128)(2,1)S(1)}, u32[]{:S(2)}, u32[]{:S(2)}) collective-permute-start(bf16[64,1536]{1,0:T(8,128)(2,1)S(1)} %get-tuple-element.115), channel_id=1, source_target_pairs={{0,4},{2,6},{4,0},{6,2},{8,12},{10,14},{12,8},{14,10},{16,20},{18,... | collective-permute-start | bytes 589832 | tf_op jit(solution)/shard_map/ppermute | solution.py:255
  107.1 8.5 %collective-permute-start.21 = (bf16[64,1536]{1,0:T(8,128)(2,1)S(1)}, bf16[64,1536]{1,0:T(8,128)(2,1)S(1)}, u32[]{:S(2)}, u32[]{:S(2)}) collective-permute-start(bf16[64,1536]{1,0:T(8,128)(2,1)S(1)} %get-tuple-element.98), channel_id=1, source_target_pairs={{0,2},{2,0},{4,6},{6,4},{8,10},{10,8},{12,14},{14,12},{16,18},{18,... | collective-permute-start | bytes 589832 | tf_op jit(solution)/shard_map/ppermute | solution.py:255
  108.4 7.2 %collective-permute-start.23 = (bf16[64,1536]{1,0:T(8,128)(2,1)S(1)}, bf16[64,1536]{1,0:T(8,128)(2,1)S(1)}, u32[]{:S(2)}, u32[]{:S(2)}) collective-permute-start(bf16[64,1536]{1,0:T(8,128)(2,1)S(1)} %get-tuple-element.102), channel_id=1, source_target_pairs={{0,4},{2,6},{4,0},{6,2},{8,12},{10,14},{12,8},{14,10},{16,20},{18,... | collective-permute-start | bytes 589832 | tf_op jit(solution)/shard_map/ppermute | solution.py:255
  112.5 15.1 %collective-permute-start.29 = (bf16[64,1536]{1,0:T(8,128)(2,1)S(1)}, bf16[64,1536]{1,0:T(8,128)(2,1)S(1)}, u32[]{:S(2)}, u32[]{:S(2)}) collective-permute-start(bf16[64,1536]{1,0:T(8,128)(2,1)S(1)} %get-tuple-element.117), channel_id=1, source_target_pairs={{0,16},{2,18},{4,20},{6,22},{8,24},{10,26},{12,28},{14,30},{16,0},... | collective-permute-start | bytes 589832 | tf_op jit(solution)/shard_map/ppermute | solution.py:255
  115.6 15.2 %collective-permute-start.24 = (bf16[64,1536]{1,0:T(8,128)(2,1)S(1)}, bf16[64,1536]{1,0:T(8,128)(2,1)S(1)}, u32[]{:S(2)}, u32[]{:S(2)}) collective-permute-start(bf16[64,1536]{1,0:T(8,128)(2,1)S(1)} %get-tuple-element.104), channel_id=1, source_target_pairs={{0,16},{2,18},{4,20},{6,22},{8,24},{10,26},{12,28},{14,30},{16,0},... | collective-permute-start | bytes 589832 | tf_op jit(solution)/shard_map/ppermute | solution.py:255
  (10 other events, 14.5 us)

commit v6 on v5

--- a/solution.py
+++ b/solution.py
@@ -9,7 +9,7 @@
 
 EPS = 1e-05
 PACK = 128
-X, Y, Z_LOW, Z_HIGH = 1, 2, 4, 8
+X, Y, Z_LOW, Z_HIGH = 1, 2, 4, 8 | 1
 
 
 def rms_rows(tokens, norm_gain):
@@ -331,6 +331,7 @@
         + [pltpu.SemaphoreType.DMA((len(held),))],
         [hbm] * len(held),
     )
+    own, gate, up = lax.optimization_barrier((own, gate, up))
     both = call(
         pack_kernel,
         jax.ShapeDtypeStruct((gate.shape[0], 2 * ff), jnp.bfloat16),
@@ -343,8 +344,7 @@
     )
     twins = (swap_core(both), swap_core(down))
     far = [swap(x, Z_HIGH) for x in own]
-    far[0], twins, both_later = lax.optimization_barrier((far[0], twins, both))
-    both_by = swap(both_later, Z_LOW)
+    both_by = swap(both, Z_LOW)
     first_one = halves(own[0], far[0])
     second_one = swap(first_one[0], X), swap(first_one[1], Y)
     far[1], second_one = lax.optimization_barrier((far[1], second_one))
@@ -392,8 +392,8 @@
         )
 
     total_one = own_total(pieces[0])
-    down_later, both_by, total_one, pieces = lax.optimization_barrier(
-        (down, both_by, total_one, pieces)
+    down_later, both_by, total_one, second_two = lax.optimization_barrier(
+        (down, both_by, total_one, second_two)
     )
     down_by = swap(down_later, Z_LOW)
     both_twin = swap_core(both_by)

time: 132 us -> 157 us (1.19)
  waiting for transfers between devices: 76 us -> 90.4 us
  local copies, waits for them, and re-layouts: 2.63 us -> 8.92 us
  starting transfers between devices: 35.9 us -> 40.7 us
    ppermute x26, waiting for transfers between devices: 73.7 us -> 88.1 us  [swap(): lax.ppermute(block, 'expert', [(i, i ^ distance) for i in range(count)])]
    unnamed x24, local copies, waits for them, and re-layouts: 2.57 us -> 8.85 us
    ppermute x26, starting transfers between devices: 35 us -> 40.1 us  [swap(): lax.ppermute(block, 'expert', [(i, i ^ distance) for i in range(count)])]
  transfers between devices with their start and end apart: 30 -> 30, of which waited for: 18 -> 19; matrix products, arithmetic and copies ran while one was open for 0% -> 0% of each run, Pallas kernels for 11% -> 8%
where the time goes in v6:
time: 157 us
  waiting for transfers between devices  90.4 us (58%)
  starting transfers between devices  40.7 us (26%)
  Pallas kernels  16 us (10%)
  local copies, waits for them, and re-layouts  8.92 us (6%)
    ppermute x26, waiting for transfers between devices, swap(): lax.ppermute(block, 'expert', [(i, i ^ distance) for i in range(count)])  88.1 us
    ppermute x26, starting transfers between devices, swap(): lax.ppermute(block, 'expert', [(i, i ^ distance) for i in range(count)])  40.1 us
    pallas_call x16, Pallas kernels, call(): pl.pallas_call(body, out_shape=outs, in_specs=specs or [smem if x.ndim ==...  16 us
    unnamed x24, local copies, waits for them, and re-layouts  8.85 us
  transfers between devices with their start and end apart: 30, of which 19 were waited for; matrix products, arithmetic and copies ran while one was open for 0% of the time, Pallas kernels for 8%

profile of v6, /device:TPU:0, one launch (start us, length us, event | category | flops | bytes accessed | tf_op | source)
XLA Modules:
  0.0 156.9 jit_solution(14085812814470694641)
XLA Ops:
  11.7 2.6 %collective-permute-start = (bf16[768,1024]{1,0:T(8,128)(2,1)S(1)}, bf16[768,1024]{1,0:T(8,128)(2,1)S(1)}, u32[]{:S(2)}, u32[]{:S(2)}) collective-permute-start(bf16[768,1024]{1,0:T(8,128)(2,1)S(1)} %shard_map.132.refs_8_), channel_id=1, source_target_pairs={{0,8},{2,10},{4,12},{6,14},{8,0},{10,2},{12,4},{14,6},{16,24},{18,... | collective-permute-start | bytes 4718600 | tf_op jit(solution)/shard_map/ppermute | solution.py:255
  14.3 3.5 %collective-permute-start.1 = (bf16[64,1664]{1,0:T(8,128)(2,1)S(1)}, bf16[64,1664]{1,0:T(8,128)(2,1)S(1)}, u32[]{:S(2)}, u32[]{:S(2)}) collective-permute-start(bf16[64,1664]{1,0:T(8,128)(2,1)S(1)} %get-tuple-element.48), channel_id=1, source_target_pairs={{0,18},{2,16},{4,22},{6,20},{8,26},{10,24},{12,30},{14,28},{16,2},... | collective-permute-start | bytes 638984 | tf_op jit(solution)/shard_map/ppermute | solution.py:255
  18.2 35.4 %collective-permute-done.1 = bf16[64,1664]{1,0:T(8,128)(2,1)S(1)} collective-permute-done((bf16[64,1664]{1,0:T(8,128)(2,1)S(1)}, bf16[64,1664]{1,0:T(8,128)(2,1)S(1)}, u32[]{:S(2)}, u32[]{:S(2)}) %collective-permute-start.1) | collective-permute-done | bytes 213024 | tf_op jit(solution)/shard_map/ppermute | solution.py:255
  53.7 1.6 %collective-permute-start.5 = (bf16[64,1664]{1,0:T(8,128)(2,1)S(1)}, bf16[64,1664]{1,0:T(8,128)(2,1)S(1)}, u32[]{:S(2)}, u32[]{:S(2)}) collective-permute-start(bf16[64,1664]{1,0:T(8,128)(2,1)S(1)} %pad_maximum_fusion.1.refs_6_), channel_id=1, source_target_pairs={{0,4},{2,6},{4,0},{6,2},{8,12},{10,14},{12,8},{14,10},{16,20},{18,... | collective-permute-start | bytes 638984 | tf_op jit(solution)/shard_map/ppermute | solution.py:255
  55.3 1.6 collective-permute-start.4
  57.7 2.4 %collective-permute-done.5.refs_7_ = bf16[64,1664]{1,0:T(8,128)(2,1)S(1)} collective-permute-done((bf16[64,1664]{1,0:T(8,128)(2,1)S(1)}, bf16[64,1664]{1,0:T(8,128)(2,1)S(1)}, u32[]{:S(2)}, u32[]{:S(2)}) %collective-permute-start.5) | collective-permute-done | bytes 213024 | tf_op jit(solution)/shard_map/ppermute | solution.py:255
  60.1 1.5 collective-permute-start.7
  63.1 2.8 %collective-permute-done.7.refs_2_ = bf16[64,1664]{1,0:T(8,128)(2,1)S(1)} collective-permute-done((bf16[64,1664]{1,0:T(8,128)(2,1)S(1)}, bf16[64,1664]{1,0:T(8,128)(2,1)S(1)}, u32[]{:S(2)}, u32[]{:S(2)}) %collective-permute-start.7) | collective-permute-done | bytes 213024 | tf_op jit(solution)/shard_map/ppermute | solution.py:255
  67.5 1.7 %collective-permute-done.2.refs_0_ = bf16[64,1664]{1,0:T(8,128)(2,1)S(1)} collective-permute-done((bf16[64,1664]{1,0:T(8,128)(2,1)S(1)}, bf16[64,1664]{1,0:T(8,128)(2,1)S(1)}, u32[]{:S(2)}, u32[]{:S(2)}) %collective-permute-start.2) | collective-permute-done | bytes 213024 | tf_op jit(solution)/shard_map/ppermute | solution.py:255
  69.2 1.5 collective-permute-start.8
  70.7 1.5 collective-permute-done.6.refs_1_
  73.7 3.4 %collective-permute-done.8.refs_3_ = bf16[64,1664]{1,0:T(8,128)(2,1)S(1)} collective-permute-done((bf16[64,1664]{1,0:T(8,128)(2,1)S(1)}, bf16[64,1664]{1,0:T(8,128)(2,1)S(1)}, u32[]{:S(2)}, u32[]{:S(2)}) %collective-permute-start.8) | collective-permute-done | bytes 213024 | tf_op jit(solution)/shard_map/ppermute | solution.py:255
  77.1 1.5 collective-permute-start.12
  78.7 3.1 %shard_map.133.total_ref = f32[512,1536]{1,0:T(8,128)S(1)} custom-call(bf16[64,1664]{1,0:T(8,128)(2,1)S(1)} %collective-permute-done.2.refs_0_, bf16[64,1664]{1,0:T(8,128)(2,1)S(1)} %collective-permute-done.6.refs_1_, bf16[64,1664]{1,0:T(8,128)(2,1)S(1)} %collective-permute-done.7.refs_2_, bf16[64,1664]{1,0:T(8,128)(2,1)S(1)} %collective-permute-done.8.refs_3_, ...), custom_call_target="tpu_custom_call" | custom-call | flops 2415919104 | bytes 9437184 | tf_op jit(solution)/shard_map/pallas_call | solution.py:86
  83.0 1.5 collective-permute-start.14
  84.5 4.6 %collective-permute-start.13 = (bf16[512,768]{1,0:T(8,128)(2,1)S(1)}, bf16[512,768]{1,0:T(8,128)(2,1)S(1)}, u32[]{:S(2)}, u32[]{:S(2)}) collective-permute-start(bf16[512,768]{1,0:T(8,128)(2,1)S(1)} %bitcast.9), channel_id=1, source_target_pairs={{0,8},{2,10},{4,12},{6,14},{8,0},{10,2},{12,4},{14,6},{16,24},{18,... | collective-permute-start | bytes 2359304 | tf_op jit(solution)/shard_map/ppermute | solution.py:255
  90.7 1.5 collective-permute-start.17
  92.1 5.1 %collective-permute-done.16.refs_2_ = bf16[64,1664]{1,0:T(8,128)(2,1)S(1)} collective-permute-done((bf16[64,1664]{1,0:T(8,128)(2,1)S(1)}, bf16[64,1664]{1,0:T(8,128)(2,1)S(1)}, u32[]{:S(2)}, u32[]{:S(2)}) %collective-permute-start.16) | collective-permute-done | bytes 213024 | tf_op jit(solution)/shard_map/ppermute | solution.py:255
  97.2 3.5 %collective-permute-done.17.refs_3_ = bf16[64,1664]{1,0:T(8,128)(2,1)S(1)} collective-permute-done((bf16[64,1664]{1,0:T(8,128)(2,1)S(1)}, bf16[64,1664]{1,0:T(8,128)(2,1)S(1)}, u32[]{:S(2)}, u32[]{:S(2)}) %collective-permute-start.17) | collective-permute-done | bytes 213024 | tf_op jit(solution)/shard_map/ppermute | solution.py:255
  100.8 3.1 %shard_map.134.total_ref = f32[512,1536]{1,0:T(8,128)S(1)} custom-call(bf16[64,1664]{1,0:T(8,128)(2,1)S(1)} %collective-permute-done.14.refs_0_, bf16[64,1664]{1,0:T(8,128)(2,1)S(1)} %collective-permute-done.15.refs_1_, bf16[64,1664]{1,0:T(8,128)(2,1)S(1)} %collective-permute-done.16.refs_2_, bf16[64,1664]{1,0:T(8,128)(2,1)S(1)} %collective-permute-done.17.refs_3_, ...), custom_call_target="tpu_custom_call" | custom-call | flops 2415919104 | bytes 9437184 | tf_op jit(solution)/shard_map/pallas_call | solution.py:86
  103.9 2.1 %shard_map.136 = (bf16[512,512]{1,0:T(8,128)(2,1)S(1)}, f32[512,128]{1,0:T(8,128)S(1)}) custom-call(bf16[64,1664]{1,0:T(8,128)(2,1)S(1)} %collective-permute-done.14.refs_0_, bf16[64,1664]{1,0:T(8,128)(2,1)S(1)} %collective-permute-done.15.refs_1_, bf16[64,1664]{1,0:T(8,128)(2,1)S(1)} %collective-permute-done.16.refs_2_, ...), custom_call_target="tpu_custom_call" | custom-call | flops 1610612736 | bytes 4718592 | tf_op jit(solution)/shard_map/pallas_call | solution.py:86
  106.1 2.1 %shard_map.135 = (bf16[512,512]{1,0:T(8,128)(2,1)S(1)}, f32[512,128]{1,0:T(8,128)S(1)}) custom-call(bf16[64,1664]{1,0:T(8,128)(2,1)S(1)} %collective-permute-done.2.refs_0_, bf16[64,1664]{1,0:T(8,128)(2,1)S(1)} %collective-permute-done.6.refs_1_, bf16[64,1664]{1,0:T(8,128)(2,1)S(1)} %collective-permute-done.7.refs_2_, ...), custom_call_target="tpu_custom_call" | custom-call | flops 1610612736 | bytes 4718592 | tf_op jit(solution)/shard_map/pallas_call | solution.py:86
  108.3 2.3 %collective-permute-done.19.down_b = bf16[512,768]{1,0:T(8,128)(2,1)S(1)} collective-permute-done((bf16[512,768]{1,0:T(8,128)(2,1)S(1)}, bf16[512,768]{1,0:T(8,128)(2,1)S(1)}, u32[]{:S(2)}, u32[]{:S(2)}) %collective-permute-start.19) | collective-permute-done | bytes 786464 | tf_op jit(solution)/shard_map/ppermute | solution.py:259
  115.3 1.5 collective-permute-start.22
  116.8 6.8 %collective-permute-done.25.got_ref = bf16[128,1536]{1,0:T(8,128)(2,1)S(1)} collective-permute-done((bf16[128,1536]{1,0:T(8,128)(2,1)S(1)}, bf16[128,1536]{1,0:T(8,128)(2,1)S(1)}, u32[]{:S(2)}, u32[]{:S(2)}) %collective-permute-start.25) | collective-permute-done | bytes 393248 | tf_op jit(solution)/shard_map/ppermute | solution.py:255
  125.8 6.2 %collective-permute-done.20.got_ref = bf16[128,1536]{1,0:T(8,128)(2,1)S(1)} collective-permute-done((bf16[128,1536]{1,0:T(8,128)(2,1)S(1)}, bf16[128,1536]{1,0:T(8,128)(2,1)S(1)}, u32[]{:S(2)}, u32[]{:S(2)}) %collective-permute-start.20) | collective-permute-done | bytes 393248 | tf_op jit(solution)/shard_map/ppermute | solution.py:255
  134.3 2.7 %collective-permute-done.26.got_a = bf16[64,1536]{1,0:T(8,128)(2,1)S(1)} collective-permute-done((bf16[64,1536]{1,0:T(8,128)(2,1)S(1)}, bf16[64,1536]{1,0:T(8,128)(2,1)S(1)}, u32[]{:S(2)}, u32[]{:S(2)}) %collective-permute-start.26) | collective-permute-done | bytes 196640 | tf_op jit(solution)/shard_map/ppermute | solution.py:255
  137.0 2.2 %collective-permute-start.29 = (bf16[64,1536]{1,0:T(8,128)(2,1)S(1)}, bf16[64,1536]{1,0:T(8,128)(2,1)S(1)}, u32[]{:S(2)}, u32[]{:S(2)}) collective-permute-start(bf16[64,1536]{1,0:T(8,128)(2,1)S(1)} %get-tuple-element.85), channel_id=1, source_target_pairs={{0,18},{2,16},{4,22},{6,20},{8,26},{10,24},{12,30},{14,28},{16,2},... | collective-permute-start | bytes 589832 | tf_op jit(solution)/shard_map/ppermute | solution.py:255
  139.2 2.6 %collective-permute-done.21.got_a = bf16[64,1536]{1,0:T(8,128)(2,1)S(1)} collective-permute-done((bf16[64,1536]{1,0:T(8,128)(2,1)S(1)}, bf16[64,1536]{1,0:T(8,128)(2,1)S(1)}, u32[]{:S(2)}, u32[]{:S(2)}) %collective-permute-start.21) | collective-permute-done | bytes 196640 | tf_op jit(solution)/shard_map/ppermute | solution.py:255
  141.9 2.5 %collective-permute-start.24 = (bf16[64,1536]{1,0:T(8,128)(2,1)S(1)}, bf16[64,1536]{1,0:T(8,128)(2,1)S(1)}, u32[]{:S(2)}, u32[]{:S(2)}) collective-permute-start(bf16[64,1536]{1,0:T(8,128)(2,1)S(1)} %get-tuple-element.72), channel_id=1, source_target_pairs={{0,18},{2,16},{4,22},{6,20},{8,26},{10,24},{12,30},{14,28},{16,2},... | collective-permute-start | bytes 589832 | tf_op jit(solution)/shard_map/ppermute | solution.py:255
  144.4 9.4 %collective-permute-done.29.got_ref = bf16[64,1536]{1,0:T(8,128)(2,1)S(1)} collective-permute-done((bf16[64,1536]{1,0:T(8,128)(2,1)S(1)}, bf16[64,1536]{1,0:T(8,128)(2,1)S(1)}, u32[]{:S(2)}, u32[]{:S(2)}) %collective-permute-start.29) | collective-permute-done | bytes 196640 | tf_op jit(solution)/shard_map/ppermute | solution.py:255
  154.5 1.7 %collective-permute-done.24.got_ref = bf16[64,1536]{1,0:T(8,128)(2,1)S(1)} collective-permute-done((bf16[64,1536]{1,0:T(8,128)(2,1)S(1)}, bf16[64,1536]{1,0:T(8,128)(2,1)S(1)}, u32[]{:S(2)}, u32[]{:S(2)}) %collective-permute-start.24) | collective-permute-done | bytes 196640 | tf_op jit(solution)/shard_map/ppermute | solution.py:255
  (75 shorter events, 30.3 us)
Async XLA Ops:
  8.6 1.1 copy-start.1
  11.1 46.6 %copy-start = (bf16[1,512,768]{2,1,0:T(8,128)(2,1)S(1)}, bf16[1,512,768]{2,1,0:T(8,128)(2,1)}, u32[]{:S(2)}) copy-start(bf16[1,512,768]{2,1,0:T(8,128)(2,1)} %param.23) | copy-start | bytes 2359300
  11.2 67.5 %collective-permute-start.9 = (bf16[768,1024]{1,0:T(8,128)(2,1)S(1)}, bf16[768,1024]{1,0:T(8,128)(2,1)S(1)}, u32[]{:S(2)}, u32[]{:S(2)}) collective-permute-start(bf16[768,1024]{1,0:T(8,128)(2,1)S(1)} %shard_map.132.refs_8_), channel_id=1, source_target_pairs={{0,1},{1,0},{2,3},{3,2},{4,5},{5,4},{6,7},{7,6},{8,9},{9,8},{10,11... | collective-permute-start | bytes 4718600 | tf_op jit(solution)/shard_map/ppermute | solution.py:259
  11.7 71.3 %collective-permute-start = (bf16[768,1024]{1,0:T(8,128)(2,1)S(1)}, bf16[768,1024]{1,0:T(8,128)(2,1)S(1)}, u32[]{:S(2)}, u32[]{:S(2)}) collective-permute-start(bf16[768,1024]{1,0:T(8,128)(2,1)S(1)} %shard_map.132.refs_8_), channel_id=1, source_target_pairs={{0,8},{2,10},{4,12},{6,14},{8,0},{10,2},{12,4},{14,6},{16,24},{18,... | collective-permute-start | bytes 4718600 | tf_op jit(solution)/shard_map/ppermute | solution.py:255
  14.3 39.3 %collective-permute-start.1 = (bf16[64,1664]{1,0:T(8,128)(2,1)S(1)}, bf16[64,1664]{1,0:T(8,128)(2,1)S(1)}, u32[]{:S(2)}, u32[]{:S(2)}) collective-permute-start(bf16[64,1664]{1,0:T(8,128)(2,1)S(1)} %get-tuple-element.48), channel_id=1, source_target_pairs={{0,18},{2,16},{4,22},{6,20},{8,26},{10,24},{12,30},{14,28},{16,2},... | collective-permute-start | bytes 638984 | tf_op jit(solution)/shard_map/ppermute | solution.py:255
  17.8 39.9 %collective-permute-start.3 = (bf16[64,1664]{1,0:T(8,128)(2,1)S(1)}, bf16[64,1664]{1,0:T(8,128)(2,1)S(1)}, u32[]{:S(2)}, u32[]{:S(2)}) collective-permute-start(bf16[64,1664]{1,0:T(8,128)(2,1)S(1)} %get-tuple-element.49), channel_id=1, source_target_pairs={{0,18},{2,16},{4,22},{6,20},{8,26},{10,24},{12,30},{14,28},{16,2},... | collective-permute-start | bytes 638984 | tf_op jit(solution)/shard_map/ppermute | solution.py:255
  53.7 6.4 %collective-permute-start.5 = (bf16[64,1664]{1,0:T(8,128)(2,1)S(1)}, bf16[64,1664]{1,0:T(8,128)(2,1)S(1)}, u32[]{:S(2)}, u32[]{:S(2)}) collective-permute-start(bf16[64,1664]{1,0:T(8,128)(2,1)S(1)} %pad_maximum_fusion.1.refs_6_), channel_id=1, source_target_pairs={{0,4},{2,6},{4,0},{6,2},{8,12},{10,14},{12,8},{14,10},{16,20},{18,... | collective-permute-start | bytes 638984 | tf_op jit(solution)/shard_map/ppermute | solution.py:255
  55.3 6.5 %collective-permute-start.4 = (bf16[64,1664]{1,0:T(8,128)(2,1)S(1)}, bf16[64,1664]{1,0:T(8,128)(2,1)S(1)}, u32[]{:S(2)}, u32[]{:S(2)}) collective-permute-start(bf16[64,1664]{1,0:T(8,128)(2,1)S(1)} %pad_maximum_fusion.refs_4_), channel_id=1, source_target_pairs={{0,2},{2,0},{4,6},{6,4},{8,10},{10,8},{12,14},{14,12},{16,18},{18,... | collective-permute-start | bytes 638984 | tf_op jit(solution)/shard_map/ppermute | solution.py:255
  57.7 20.9 %collective-permute-start.10 = (bf16[512,768]{1,0:T(8,128)(2,1)S(1)}, bf16[512,768]{1,0:T(8,128)(2,1)S(1)}, u32[]{:S(2)}, u32[]{:S(2)}) collective-permute-start(bf16[512,768]{1,0:T(8,128)(2,1)S(1)} %bitcast.7), channel_id=1, source_target_pairs={{0,1},{1,0},{2,3},{3,2},{4,5},{5,4},{6,7},{7,6},{8,9},{9,8},{10,11... | collective-permute-start | bytes 2359304 | tf_op jit(solution)/shard_map/ppermute | solution.py:259
  60.1 5.9 %collective-permute-start.7 = (bf16[64,1664]{1,0:T(8,128)(2,1)S(1)}, bf16[64,1664]{1,0:T(8,128)(2,1)S(1)}, u32[]{:S(2)}, u32[]{:S(2)}) collective-permute-start(bf16[64,1664]{1,0:T(8,128)(2,1)S(1)} %pad_maximum_fusion.1.refs_6_), channel_id=1, source_target_pairs={{0,2},{2,0},{4,6},{6,4},{8,10},{10,8},{12,14},{14,12},{16,18},{18,... | collective-permute-start | bytes 638984 | tf_op jit(solution)/shard_map/ppermute | solution.py:255
  61.8 7.4 %collective-permute-start.2 = (bf16[64,1664]{1,0:T(8,128)(2,1)S(1)}, bf16[64,1664]{1,0:T(8,128)(2,1)S(1)}, u32[]{:S(2)}, u32[]{:S(2)}) collective-permute-start(bf16[64,1664]{1,0:T(8,128)(2,1)S(1)} %pad_maximum_fusion.refs_4_), channel_id=1, source_target_pairs={{0,4},{2,6},{4,0},{6,2},{8,12},{10,14},{12,8},{14,10},{16,20},{18,... | collective-permute-start | bytes 638984 | tf_op jit(solution)/shard_map/ppermute | solution.py:255
  66.0 6.2 %collective-permute-start.6 = (bf16[64,1664]{1,0:T(8,128)(2,1)S(1)}, bf16[64,1664]{1,0:T(8,128)(2,1)S(1)}, u32[]{:S(2)}, u32[]{:S(2)}) collective-permute-start(bf16[64,1664]{1,0:T(8,128)(2,1)S(1)} %collective-permute-done.4.refs_5_), channel_id=1, source_target_pairs={{0,4},{2,6},{4,0},{6,2},{8,12},{10,14},{12,8},{14,10},{16,20},{18,... | collective-permute-start | bytes 638984 | tf_op jit(solution)/shard_map/ppermute | solution.py:255
  69.2 7.9 %collective-permute-start.8 = (bf16[64,1664]{1,0:T(8,128)(2,1)S(1)}, bf16[64,1664]{1,0:T(8,128)(2,1)S(1)}, u32[]{:S(2)}, u32[]{:S(2)}) collective-permute-start(bf16[64,1664]{1,0:T(8,128)(2,1)S(1)} %collective-permute-done.5.refs_7_), channel_id=1, source_target_pairs={{0,2},{2,0},{4,6},{6,4},{8,10},{10,8},{12,14},{14,12},{16,18},{18,... | collective-permute-start | bytes 638984 | tf_op jit(solution)/shard_map/ppermute | solution.py:255
  72.2 9.6 %collective-permute-start.11 = (bf16[64,1664]{1,0:T(8,128)(2,1)S(1)}, bf16[64,1664]{1,0:T(8,128)(2,1)S(1)}, u32[]{:S(2)}, u32[]{:S(2)}) collective-permute-start(bf16[64,1664]{1,0:T(8,128)(2,1)S(1)} %pad_maximum_fusion.2.refs_4_), channel_id=1, source_target_pairs={{0,2},{2,0},{4,6},{6,4},{8,10},{10,8},{12,14},{14,12},{16,18},{18,... | collective-permute-start | bytes 638984 | tf_op jit(solution)/shard_map/ppermute | solution.py:255
  77.1 5.8 %collective-permute-start.12 = (bf16[64,1664]{1,0:T(8,128)(2,1)S(1)}, bf16[64,1664]{1,0:T(8,128)(2,1)S(1)}, u32[]{:S(2)}, u32[]{:S(2)}) collective-permute-start(bf16[64,1664]{1,0:T(8,128)(2,1)S(1)} %pad_maximum_fusion.3.refs_6_), channel_id=1, source_target_pairs={{0,4},{2,6},{4,0},{6,2},{8,12},{10,14},{12,8},{14,10},{16,20},{18,... | collective-permute-start | bytes 638984 | tf_op jit(solution)/shard_map/ppermute | solution.py:255
  83.0 20.9 %collective-permute-start.18 = (bf16[768,1024]{1,0:T(8,128)(2,1)S(1)}, bf16[768,1024]{1,0:T(8,128)(2,1)S(1)}, u32[]{:S(2)}, u32[]{:S(2)}) collective-permute-start(bf16[768,1024]{1,0:T(8,128)(2,1)S(1)} %collective-permute-done.refs_8_), channel_id=1, source_target_pairs={{0,1},{1,0},{2,3},{3,2},{4,5},{5,4},{6,7},{7,6},{8,9},{9,8},{10,11... | collective-permute-start | bytes 4718600 | tf_op jit(solution)/shard_map/ppermute | solution.py:259
  83.0 7.7 %collective-permute-start.14 = (bf16[64,1664]{1,0:T(8,128)(2,1)S(1)}, bf16[64,1664]{1,0:T(8,128)(2,1)S(1)}, u32[]{:S(2)}, u32[]{:S(2)}) collective-permute-start(bf16[64,1664]{1,0:T(8,128)(2,1)S(1)} %pad_maximum_fusion.2.refs_4_), channel_id=1, source_target_pairs={{0,4},{2,6},{4,0},{6,2},{8,12},{10,14},{12,8},{14,10},{16,20},{18,... | collective-permute-start | bytes 638984 | tf_op jit(solution)/shard_map/ppermute | solution.py:255
  84.5 23.7 %collective-permute-start.13 = (bf16[512,768]{1,0:T(8,128)(2,1)S(1)}, bf16[512,768]{1,0:T(8,128)(2,1)S(1)}, u32[]{:S(2)}, u32[]{:S(2)}) collective-permute-start(bf16[512,768]{1,0:T(8,128)(2,1)S(1)} %bitcast.9), channel_id=1, source_target_pairs={{0,8},{2,10},{4,12},{6,14},{8,0},{10,2},{12,4},{14,6},{16,24},{18,... | collective-permute-start | bytes 2359304 | tf_op jit(solution)/shard_map/ppermute | solution.py:255
  89.1 8.1 %collective-permute-start.16 = (bf16[64,1664]{1,0:T(8,128)(2,1)S(1)}, bf16[64,1664]{1,0:T(8,128)(2,1)S(1)}, u32[]{:S(2)}, u32[]{:S(2)}) collective-permute-start(bf16[64,1664]{1,0:T(8,128)(2,1)S(1)} %pad_maximum_fusion.3.refs_6_), channel_id=1, source_target_pairs={{0,2},{2,0},{4,6},{6,4},{8,10},{10,8},{12,14},{14,12},{16,18},{18,... | collective-permute-start | bytes 638984 | tf_op jit(solution)/shard_map/ppermute | solution.py:255
  89.6 7.6 %collective-permute-start.15 = (bf16[64,1664]{1,0:T(8,128)(2,1)S(1)}, bf16[64,1664]{1,0:T(8,128)(2,1)S(1)}, u32[]{:S(2)}, u32[]{:S(2)}) collective-permute-start(bf16[64,1664]{1,0:T(8,128)(2,1)S(1)} %collective-permute-done.11.refs_5_), channel_id=1, source_target_pairs={{0,4},{2,6},{4,0},{6,2},{8,12},{10,14},{12,8},{14,10},{16,20},{18,... | collective-permute-start | bytes 638984 | tf_op jit(solution)/shard_map/ppermute | solution.py:255
  90.7 10.1 %collective-permute-start.17 = (bf16[64,1664]{1,0:T(8,128)(2,1)S(1)}, bf16[64,1664]{1,0:T(8,128)(2,1)S(1)}, u32[]{:S(2)}, u32[]{:S(2)}) collective-permute-start(bf16[64,1664]{1,0:T(8,128)(2,1)S(1)} %collective-permute-done.12.refs_7_), channel_id=1, source_target_pairs={{0,2},{2,0},{4,6},{6,4},{8,10},{10,8},{12,14},{14,12},{16,18},{18,... | collective-permute-start | bytes 638984 | tf_op jit(solution)/shard_map/ppermute | solution.py:255
  108.2 2.4 %collective-permute-start.19 = (bf16[512,768]{1,0:T(8,128)(2,1)S(1)}, bf16[512,768]{1,0:T(8,128)(2,1)S(1)}, u32[]{:S(2)}, u32[]{:S(2)}) collective-permute-start(bf16[512,768]{1,0:T(8,128)(2,1)S(1)} %collective-permute-done.13.down_a), channel_id=1, source_target_pairs={{0,1},{1,0},{2,3},{3,2},{4,5},{5,4},{6,7},{7,6},{8,9},{9,8},{10,11... | collective-permute-start | bytes 2359304 | tf_op jit(solution)/shard_map/ppermute | solution.py:259
  111.6 12.0 %collective-permute-start.25 = (bf16[128,1536]{1,0:T(8,128)(2,1)S(1)}, bf16[128,1536]{1,0:T(8,128)(2,1)S(1)}, u32[]{:S(2)}, u32[]{:S(2)}) collective-permute-start(bf16[128,1536]{1,0:T(8,128)(2,1)S(1)} %get-tuple-element.77), channel_id=1, source_target_pairs={{0,4},{2,6},{4,0},{6,2},{8,12},{10,14},{12,8},{14,10},{16,20},{18,... | collective-permute-start | bytes 1179656 | tf_op jit(solution)/shard_map/ppermute | solution.py:255
  112.3 12.0 %collective-permute-start.27 = (bf16[128,1536]{1,0:T(8,128)(2,1)S(1)}, bf16[128,1536]{1,0:T(8,128)(2,1)S(1)}, u32[]{:S(2)}, u32[]{:S(2)}) collective-permute-start(bf16[128,1536]{1,0:T(8,128)(2,1)S(1)} %get-tuple-element.81), channel_id=1, source_target_pairs={{0,2},{2,0},{4,6},{6,4},{8,10},{10,8},{12,14},{14,12},{16,18},{18,... | collective-permute-start | bytes 1179656 | tf_op jit(solution)/shard_map/ppermute | solution.py:255
  113.8 18.2 %collective-permute-start.20 = (bf16[128,1536]{1,0:T(8,128)(2,1)S(1)}, bf16[128,1536]{1,0:T(8,128)(2,1)S(1)}, u32[]{:S(2)}, u32[]{:S(2)}) collective-permute-start(bf16[128,1536]{1,0:T(8,128)(2,1)S(1)} %get-tuple-element.64), channel_id=1, source_target_pairs={{0,4},{2,6},{4,0},{6,2},{8,12},{10,14},{12,8},{14,10},{16,20},{18,... | collective-permute-start | bytes 1179656 | tf_op jit(solution)/shard_map/ppermute | solution.py:255
  115.3 17.4 %collective-permute-start.22 = (bf16[128,1536]{1,0:T(8,128)(2,1)S(1)}, bf16[128,1536]{1,0:T(8,128)(2,1)S(1)}, u32[]{:S(2)}, u32[]{:S(2)}) collective-permute-start(bf16[128,1536]{1,0:T(8,128)(2,1)S(1)} %get-tuple-element.68), channel_id=1, source_target_pairs={{0,2},{2,0},{4,6},{6,4},{8,10},{10,8},{12,14},{14,12},{16,18},{18,... | collective-permute-start | bytes 1179656 | tf_op jit(solution)/shard_map/ppermute | solution.py:255
  123.7 13.2 %collective-permute-start.26 = (bf16[64,1536]{1,0:T(8,128)(2,1)S(1)}, bf16[64,1536]{1,0:T(8,128)(2,1)S(1)}, u32[]{:S(2)}, u32[]{:S(2)}) collective-permute-start(bf16[64,1536]{1,0:T(8,128)(2,1)S(1)} %get-tuple-element.79), channel_id=1, source_target_pairs={{0,2},{2,0},{4,6},{6,4},{8,10},{10,8},{12,14},{14,12},{16,18},{18,... | collective-permute-start | bytes 589832 | tf_op jit(solution)/shard_map/ppermute | solution.py:255
  124.4 12.6 %collective-permute-start.28 = (bf16[64,1536]{1,0:T(8,128)(2,1)S(1)}, bf16[64,1536]{1,0:T(8,128)(2,1)S(1)}, u32[]{:S(2)}, u32[]{:S(2)}) collective-permute-start(bf16[64,1536]{1,0:T(8,128)(2,1)S(1)} %get-tuple-element.83), channel_id=1, source_target_pairs={{0,4},{2,6},{4,0},{6,2},{8,12},{10,14},{12,8},{14,10},{16,20},{18,... | collective-permute-start | bytes 589832 | tf_op jit(solution)/shard_map/ppermute | solution.py:255
  132.1 9.7 %collective-permute-start.21 = (bf16[64,1536]{1,0:T(8,128)(2,1)S(1)}, bf16[64,1536]{1,0:T(8,128)(2,1)S(1)}, u32[]{:S(2)}, u32[]{:S(2)}) collective-permute-start(bf16[64,1536]{1,0:T(8,128)(2,1)S(1)} %get-tuple-element.66), channel_id=1, source_target_pairs={{0,2},{2,0},{4,6},{6,4},{8,10},{10,8},{12,14},{14,12},{16,18},{18,... | collective-permute-start | bytes 589832 | tf_op jit(solution)/shard_map/ppermute | solution.py:255
  132.8 9.0 %collective-permute-start.23 = (bf16[64,1536]{1,0:T(8,128)(2,1)S(1)}, bf16[64,1536]{1,0:T(8,128)(2,1)S(1)}, u32[]{:S(2)}, u32[]{:S(2)}) collective-permute-start(bf16[64,1536]{1,0:T(8,128)(2,1)S(1)} %get-tuple-element.70), channel_id=1, source_target_pairs={{0,4},{2,6},{4,0},{6,2},{8,12},{10,14},{12,8},{14,10},{16,20},{18,... | collective-permute-start | bytes 589832 | tf_op jit(solution)/shard_map/ppermute | solution.py:255
  137.0 16.8 %collective-permute-start.29 = (bf16[64,1536]{1,0:T(8,128)(2,1)S(1)}, bf16[64,1536]{1,0:T(8,128)(2,1)S(1)}, u32[]{:S(2)}, u32[]{:S(2)}) collective-permute-start(bf16[64,1536]{1,0:T(8,128)(2,1)S(1)} %get-tuple-element.85), channel_id=1, source_target_pairs={{0,18},{2,16},{4,22},{6,20},{8,26},{10,24},{12,30},{14,28},{16,2},... | collective-permute-start | bytes 589832 | tf_op jit(solution)/shard_map/ppermute | solution.py:255
  141.9 14.3 %collective-permute-start.24 = (bf16[64,1536]{1,0:T(8,128)(2,1)S(1)}, bf16[64,1536]{1,0:T(8,128)(2,1)S(1)}, u32[]{:S(2)}, u32[]{:S(2)}) collective-permute-start(bf16[64,1536]{1,0:T(8,128)(2,1)S(1)} %get-tuple-element.72), channel_id=1, source_target_pairs={{0,18},{2,16},{4,22},{6,20},{8,26},{10,24},{12,30},{14,28},{16,2},... | collective-permute-start | bytes 589832 | tf_op jit(solution)/shard_map/ppermute | solution.py:255
  (10 other events, 7.7 us)

commit v7 on v5

--- a/solution.py
+++ b/solution.py
@@ -331,6 +331,7 @@
         + [pltpu.SemaphoreType.DMA((len(held),))],
         [hbm] * len(held),
     )
+    own, gate, up = lax.optimization_barrier((own, gate, up))
     both = call(
         pack_kernel,
         jax.ShapeDtypeStruct((gate.shape[0], 2 * ff), jnp.bfloat16),
@@ -342,15 +343,14 @@
         [hbm] * 2,
     )
     twins = (swap_core(both), swap_core(down))
-    far = [swap(x, Z_HIGH) for x in own]
-    far[0], twins, both_later = lax.optimization_barrier((far[0], twins, both))
+    far_one = swap(own[0], Z_HIGH)
+    far_one, both_later = lax.optimization_barrier((far_one, both))
     both_by = swap(both_later, Z_LOW)
-    first_one = halves(own[0], far[0])
+    first_one = halves(own[0], far_one)
     second_one = swap(first_one[0], X), swap(first_one[1], Y)
-    far[1], second_one = lax.optimization_barrier((far[1], second_one))
-    first_two = halves(own[1], far[1])
-    second_two = swap(first_two[0], X), swap(first_two[1], Y)
-    pieces = [spread(*first_one, *second_one), spread(*first_two, *second_two)]
+    second_one, own_two = lax.optimization_barrier((second_one, own[1]))
+    far_two = swap(own_two, Z_HIGH)
+    pieces_one = spread(*first_one, *second_one)
 
     rows = 8 * tok
     scratch = (pltpu.VMEM((rows, width + PACK), jnp.bfloat16),)
@@ -391,19 +391,20 @@
             2 * width * ff + 8 * rows * width,
         )
 
-    total_one = own_total(pieces[0])
-    down_later, both_by, total_one, pieces = lax.optimization_barrier(
-        (down, both_by, total_one, pieces)
-    )
+    total_one = own_total(pieces_one)
+    down_later, both_by, total_one = lax.optimization_barrier((down, both_by, total_one))
     down_by = swap(down_later, Z_LOW)
     both_twin = swap_core(both_by)
-    total_two = own_total(pieces[1])
-    hidden_one, hidden_two = beside_hidden(pieces[0]), beside_hidden(pieces[1])
-    down_by, total_two, hidden_one, hidden_two = lax.optimization_barrier(
-        (down_by, total_two, hidden_one, hidden_two)
-    )
+    hidden_one = beside_hidden(pieces_one)
+    hidden_one, far_two = lax.optimization_barrier((hidden_one, far_two))
+    first_two = halves(own[1], far_two)
+    second_two = swap(first_two[0], X), swap(first_two[1], Y)
+    pieces_two = spread(*first_two, *second_two)
+    down_by, hidden_one, pieces_two = lax.optimization_barrier((down_by, hidden_one, pieces_two))
     down_twin = swap_core(down_by)
-    back_one = first_return(*join(total_one, *hidden_one))
+    sums_one, pieces_two = lax.optimization_barrier((join(total_one, *hidden_one), pieces_two))
+    back_one = first_return(*sums_one)
+    total_two, hidden_two = own_total(pieces_two), beside_hidden(pieces_two)
     back_two = first_return(*join(total_two, *hidden_two))
     return last_returns(*back_one), last_returns(*back_two)
 

time: 132 us -> 138 us (1.045)
  local copies, waits for them, and re-layouts: 2.63 us -> 8.92 us
  waiting for transfers between devices: 76 us -> 78.6 us
  starting transfers between devices: 35.9 us -> 33.6 us
    unnamed x24, local copies, waits for them, and re-layouts: 2.57 us -> 8.86 us
    ppermute x26, waiting for transfers between devices: 73.7 us -> 76.3 us  [swap(): lax.ppermute(block, 'expert', [(i, i ^ distance) for i in range(count)])]
    ppermute x26, starting transfers between devices: 35 us -> 33 us  [swap(): lax.ppermute(block, 'expert', [(i, i ^ distance) for i in range(count)])]
  transfers between devices with their start and end apart: 30 -> 30, of which waited for: 18 -> 20; matrix products, arithmetic and copies ran while one was open for 0% -> 0% of each run, Pallas kernels for 11% -> 9%
where the time goes in v7:
time: 138 us
  waiting for transfers between devices  78.6 us (57%)
  starting transfers between devices  33.6 us (24%)
  Pallas kernels  16 us (12%)
  local copies, waits for them, and re-layouts  8.92 us (6%)
    ppermute x26, waiting for transfers between devices, swap(): lax.ppermute(block, 'expert', [(i, i ^ distance) for i in range(count)])  76.3 us
    ppermute x26, starting transfers between devices, swap(): lax.ppermute(block, 'expert', [(i, i ^ distance) for i in range(count)])  33 us
    pallas_call x16, Pallas kernels, call(): pl.pallas_call(body, out_shape=outs, in_specs=specs or [smem if x.ndim ==...  16 us
    unnamed x24, local copies, waits for them, and re-layouts  8.86 us
  transfers between devices with their start and end apart: 30, of which 20 were waited for; matrix products, arithmetic and copies ran while one was open for 0% of the time, Pallas kernels for 9%

profile of v7, /device:TPU:0, one launch (start us, length us, event | category | flops | bytes accessed | tf_op | source)
XLA Modules:
  0.0 138.0 jit_solution(17880895348309077425)
XLA Ops:
  8.6 4.1 %collective-permute-start = (bf16[64,1664]{1,0:T(8,128)(2,1)S(1)}, bf16[64,1664]{1,0:T(8,128)(2,1)S(1)}, u32[]{:S(2)}, u32[]{:S(2)}) collective-permute-start(bf16[64,1664]{1,0:T(8,128)(2,1)S(1)} %get-tuple-element.68), channel_id=1, source_target_pairs={{0,16},{2,18},{4,20},{6,22},{8,24},{10,26},{12,28},{14,30},{16,0},... | collective-permute-start | bytes 638984 | tf_op jit(solution)/shard_map/ppermute | solution.py:255
  15.9 6.7 %collective-permute-done = bf16[64,1664]{1,0:T(8,128)(2,1)S(1)} collective-permute-done((bf16[64,1664]{1,0:T(8,128)(2,1)S(1)}, bf16[64,1664]{1,0:T(8,128)(2,1)S(1)}, u32[]{:S(2)}, u32[]{:S(2)}) %collective-permute-start) | collective-permute-done | bytes 213024 | tf_op jit(solution)/shard_map/ppermute | solution.py:255
  23.3 1.6 %collective-permute-start.3 = (bf16[64,1664]{1,0:T(8,128)(2,1)S(1)}, bf16[64,1664]{1,0:T(8,128)(2,1)S(1)}, u32[]{:S(2)}, u32[]{:S(2)}) collective-permute-start(bf16[64,1664]{1,0:T(8,128)(2,1)S(1)} %pad_maximum_fusion.refs_4_), channel_id=1, source_target_pairs={{0,2},{2,0},{4,6},{6,4},{8,10},{10,8},{12,14},{14,12},{16,18},{18,... | collective-permute-start | bytes 638984 | tf_op jit(solution)/shard_map/ppermute | solution.py:255
  24.9 1.6 %collective-permute-start.4 = (bf16[64,1664]{1,0:T(8,128)(2,1)S(1)}, bf16[64,1664]{1,0:T(8,128)(2,1)S(1)}, u32[]{:S(2)}, u32[]{:S(2)}) collective-permute-start(bf16[64,1664]{1,0:T(8,128)(2,1)S(1)} %pad_maximum_fusion.1.refs_6_), channel_id=1, source_target_pairs={{0,4},{2,6},{4,0},{6,2},{8,12},{10,14},{12,8},{14,10},{16,20},{18,... | collective-permute-start | bytes 638984 | tf_op jit(solution)/shard_map/ppermute | solution.py:255
  26.5 3.8 %collective-permute-done.3.refs_5_ = bf16[64,1664]{1,0:T(8,128)(2,1)S(1)} collective-permute-done((bf16[64,1664]{1,0:T(8,128)(2,1)S(1)}, bf16[64,1664]{1,0:T(8,128)(2,1)S(1)}, u32[]{:S(2)}, u32[]{:S(2)}) %collective-permute-start.3) | collective-permute-done | bytes 213024 | tf_op jit(solution)/shard_map/ppermute | solution.py:255
  30.3 1.5 %collective-permute-start.2 = (bf16[64,1664]{1,0:T(8,128)(2,1)S(1)}, bf16[64,1664]{1,0:T(8,128)(2,1)S(1)}, u32[]{:S(2)}, u32[]{:S(2)}) collective-permute-start(bf16[64,1664]{1,0:T(8,128)(2,1)S(1)} %pad_maximum_fusion.refs_4_), channel_id=1, source_target_pairs={{0,4},{2,6},{4,0},{6,2},{8,12},{10,14},{12,8},{14,10},{16,20},{18,... | collective-permute-start | bytes 638984 | tf_op jit(solution)/shard_map/ppermute | solution.py:255
  33.3 3.0 %collective-permute-done.2.refs_0_ = bf16[64,1664]{1,0:T(8,128)(2,1)S(1)} collective-permute-done((bf16[64,1664]{1,0:T(8,128)(2,1)S(1)}, bf16[64,1664]{1,0:T(8,128)(2,1)S(1)}, u32[]{:S(2)}, u32[]{:S(2)}) %collective-permute-start.2) | collective-permute-done | bytes 213024 | tf_op jit(solution)/shard_map/ppermute | solution.py:255
  39.3 2.8 %collective-permute-done.5.refs_1_ = bf16[64,1664]{1,0:T(8,128)(2,1)S(1)} collective-permute-done((bf16[64,1664]{1,0:T(8,128)(2,1)S(1)}, bf16[64,1664]{1,0:T(8,128)(2,1)S(1)}, u32[]{:S(2)}, u32[]{:S(2)}) %collective-permute-start.5) | collective-permute-done | bytes 213024 | tf_op jit(solution)/shard_map/ppermute | solution.py:255
  42.1 1.5 %collective-permute-done.7.refs_3_ = bf16[64,1664]{1,0:T(8,128)(2,1)S(1)} collective-permute-done((bf16[64,1664]{1,0:T(8,128)(2,1)S(1)}, bf16[64,1664]{1,0:T(8,128)(2,1)S(1)}, u32[]{:S(2)}, u32[]{:S(2)}) %collective-permute-start.7) | collective-permute-done | bytes 213024 | tf_op jit(solution)/shard_map/ppermute | solution.py:255
  43.6 3.1 %shard_map.133.total_ref = f32[512,1536]{1,0:T(8,128)S(1)} custom-call(bf16[64,1664]{1,0:T(8,128)(2,1)S(1)} %collective-permute-done.2.refs_0_, bf16[64,1664]{1,0:T(8,128)(2,1)S(1)} %collective-permute-done.5.refs_1_, bf16[64,1664]{1,0:T(8,128)(2,1)S(1)} %collective-permute-done.6.refs_2_, bf16[64,1664]{1,0:T(8,128)(2,1)S(1)} %collective-permute-done.7.refs_3_, ...), custom_call_target="tpu_custom_call" | custom-call | flops 2415919104 | bytes 9437184 | tf_op jit(solution)/shard_map/pallas_call | solution.py:86
  46.8 11.3 %collective-permute-done.1.refs_8_ = bf16[768,1024]{1,0:T(8,128)(2,1)S(1)} collective-permute-done((bf16[768,1024]{1,0:T(8,128)(2,1)S(1)}, bf16[768,1024]{1,0:T(8,128)(2,1)S(1)}, u32[]{:S(2)}, u32[]{:S(2)}) %collective-permute-start.1) | collective-permute-done | bytes 1572896 | tf_op jit(solution)/shard_map/ppermute | solution.py:255
  58.1 3.1 %collective-permute-start.12 = (bf16[64,1664]{1,0:T(8,128)(2,1)S(1)}, bf16[64,1664]{1,0:T(8,128)(2,1)S(1)}, u32[]{:S(2)}, u32[]{:S(2)}) collective-permute-start(bf16[64,1664]{1,0:T(8,128)(2,1)S(1)} %get-tuple-element.80), channel_id=1, source_target_pairs={{0,16},{2,18},{4,20},{6,22},{8,24},{10,26},{12,28},{14,30},{16,0},... | collective-permute-start | bytes 638984 | tf_op jit(solution)/shard_map/ppermute | solution.py:255
  61.2 1.7 %collective-permute-start.10 = (bf16[512,768]{1,0:T(8,128)(2,1)S(1)}, bf16[512,768]{1,0:T(8,128)(2,1)S(1)}, u32[]{:S(2)}, u32[]{:S(2)}) collective-permute-start(bf16[512,768]{1,0:T(8,128)(2,1)S(1)} %bitcast.9), channel_id=1, source_target_pairs={{0,8},{2,10},{4,12},{6,14},{8,0},{10,2},{12,4},{14,6},{16,24},{18,... | collective-permute-start | bytes 2359304 | tf_op jit(solution)/shard_map/ppermute | solution.py:255
  63.0 2.1 %shard_map.134 = (bf16[512,512]{1,0:T(8,128)(2,1)S(1)}, f32[512,128]{1,0:T(8,128)S(1)}) custom-call(bf16[64,1664]{1,0:T(8,128)(2,1)S(1)} %collective-permute-done.2.refs_0_, bf16[64,1664]{1,0:T(8,128)(2,1)S(1)} %collective-permute-done.5.refs_1_, bf16[64,1664]{1,0:T(8,128)(2,1)S(1)} %collective-permute-done.6.refs_2_, ...), custom_call_target="tpu_custom_call" | custom-call | flops 1610612736 | bytes 4718592 | tf_op jit(solution)/shard_map/pallas_call | solution.py:86
  65.1 6.7 %collective-permute-done.12 = bf16[64,1664]{1,0:T(8,128)(2,1)S(1)} collective-permute-done((bf16[64,1664]{1,0:T(8,128)(2,1)S(1)}, bf16[64,1664]{1,0:T(8,128)(2,1)S(1)}, u32[]{:S(2)}, u32[]{:S(2)}) %collective-permute-start.12) | collective-permute-done | bytes 213024 | tf_op jit(solution)/shard_map/ppermute | solution.py:255
  71.8 1.6 %collective-permute-start.14 = (bf16[64,1664]{1,0:T(8,128)(2,1)S(1)}, bf16[64,1664]{1,0:T(8,128)(2,1)S(1)}, u32[]{:S(2)}, u32[]{:S(2)}) collective-permute-start(bf16[64,1664]{1,0:T(8,128)(2,1)S(1)} %pad_maximum_fusion.2.refs_4_), channel_id=1, source_target_pairs={{0,2},{2,0},{4,6},{6,4},{8,10},{10,8},{12,14},{14,12},{16,18},{18,... | collective-permute-start | bytes 638984 | tf_op jit(solution)/shard_map/ppermute | solution.py:255
  73.4 1.6 %collective-permute-start.17 = (bf16[64,1664]{1,0:T(8,128)(2,1)S(1)}, bf16[64,1664]{1,0:T(8,128)(2,1)S(1)}, u32[]{:S(2)}, u32[]{:S(2)}) collective-permute-start(bf16[64,1664]{1,0:T(8,128)(2,1)S(1)} %pad_maximum_fusion.3.refs_6_), channel_id=1, source_target_pairs={{0,4},{2,6},{4,0},{6,2},{8,12},{10,14},{12,8},{14,10},{16,20},{18,... | collective-permute-start | bytes 638984 | tf_op jit(solution)/shard_map/ppermute | solution.py:255
  76.1 4.0 %collective-permute-done.14.refs_5_ = bf16[64,1664]{1,0:T(8,128)(2,1)S(1)} collective-permute-done((bf16[64,1664]{1,0:T(8,128)(2,1)S(1)}, bf16[64,1664]{1,0:T(8,128)(2,1)S(1)}, u32[]{:S(2)}, u32[]{:S(2)}) %collective-permute-start.14) | collective-permute-done | bytes 213024 | tf_op jit(solution)/shard_map/ppermute | solution.py:255
  80.0 1.5 %collective-permute-start.15 = (bf16[64,1664]{1,0:T(8,128)(2,1)S(1)}, bf16[64,1664]{1,0:T(8,128)(2,1)S(1)}, u32[]{:S(2)}, u32[]{:S(2)}) collective-permute-start(bf16[64,1664]{1,0:T(8,128)(2,1)S(1)} %collective-permute-done.14.refs_5_), channel_id=1, source_target_pairs={{0,4},{2,6},{4,0},{6,2},{8,12},{10,14},{12,8},{14,10},{16,20},{18,... | collective-permute-start | bytes 638984 | tf_op jit(solution)/shard_map/ppermute | solution.py:255
  84.2 2.1 %collective-permute-done.13.refs_0_ = bf16[64,1664]{1,0:T(8,128)(2,1)S(1)} collective-permute-done((bf16[64,1664]{1,0:T(8,128)(2,1)S(1)}, bf16[64,1664]{1,0:T(8,128)(2,1)S(1)}, u32[]{:S(2)}, u32[]{:S(2)}) %collective-permute-start.13) | collective-permute-done | bytes 213024 | tf_op jit(solution)/shard_map/ppermute | solution.py:255
  86.2 3.1 %collective-permute-done.15.refs_1_ = bf16[64,1664]{1,0:T(8,128)(2,1)S(1)} collective-permute-done((bf16[64,1664]{1,0:T(8,128)(2,1)S(1)}, bf16[64,1664]{1,0:T(8,128)(2,1)S(1)}, u32[]{:S(2)}, u32[]{:S(2)}) %collective-permute-start.15) | collective-permute-done | bytes 213024 | tf_op jit(solution)/shard_map/ppermute | solution.py:255
  89.4 2.3 %collective-permute-done.19.down_b = bf16[512,768]{1,0:T(8,128)(2,1)S(1)} collective-permute-done((bf16[512,768]{1,0:T(8,128)(2,1)S(1)}, bf16[512,768]{1,0:T(8,128)(2,1)S(1)}, u32[]{:S(2)}, u32[]{:S(2)}) %collective-permute-start.19) | collective-permute-done | bytes 786464 | tf_op jit(solution)/shard_map/ppermute | solution.py:259
  92.7 1.6 %collective-permute-start.20 = (bf16[128,1536]{1,0:T(8,128)(2,1)S(1)}, bf16[128,1536]{1,0:T(8,128)(2,1)S(1)}, u32[]{:S(2)}, u32[]{:S(2)}) collective-permute-start(bf16[128,1536]{1,0:T(8,128)(2,1)S(1)} %get-tuple-element.101), channel_id=1, source_target_pairs={{0,4},{2,6},{4,0},{6,2},{8,12},{10,14},{12,8},{14,10},{16,20},{18,... | collective-permute-start | bytes 1179656 | tf_op jit(solution)/shard_map/ppermute | solution.py:255
  94.8 2.1 %shard_map.140 = (bf16[512,512]{1,0:T(8,128)(2,1)S(1)}, f32[512,128]{1,0:T(8,128)S(1)}) custom-call(bf16[64,1664]{1,0:T(8,128)(2,1)S(1)} %collective-permute-done.13.refs_0_, bf16[64,1664]{1,0:T(8,128)(2,1)S(1)} %collective-permute-done.15.refs_1_, bf16[64,1664]{1,0:T(8,128)(2,1)S(1)} %collective-permute-done.16.refs_2_, ...), custom_call_target="tpu_custom_call" | custom-call | flops 1610612736 | bytes 4718592 | tf_op jit(solution)/shard_map/pallas_call | solution.py:86
  96.9 3.1 %shard_map.141.total_ref = f32[512,1536]{1,0:T(8,128)S(1)} custom-call(bf16[64,1664]{1,0:T(8,128)(2,1)S(1)} %collective-permute-done.13.refs_0_, bf16[64,1664]{1,0:T(8,128)(2,1)S(1)} %collective-permute-done.15.refs_1_, bf16[64,1664]{1,0:T(8,128)(2,1)S(1)} %collective-permute-done.16.refs_2_, bf16[64,1664]{1,0:T(8,128)(2,1)S(1)} %collective-permute-done.18.refs_3_, ...), custom_call_target="tpu_custom_call" | custom-call | flops 2415919104 | bytes 9437184 | tf_op jit(solution)/shard_map/pallas_call | solution.py:86
  104.6 1.7 %collective-permute-done.22.got_ref = bf16[128,1536]{1,0:T(8,128)(2,1)S(1)} collective-permute-done((bf16[128,1536]{1,0:T(8,128)(2,1)S(1)}, bf16[128,1536]{1,0:T(8,128)(2,1)S(1)}, u32[]{:S(2)}, u32[]{:S(2)}) %collective-permute-start.22) | collective-permute-done | bytes 393248 | tf_op jit(solution)/shard_map/ppermute | solution.py:255
  106.8 6.4 %collective-permute-done.25.got_ref = bf16[128,1536]{1,0:T(8,128)(2,1)S(1)} collective-permute-done((bf16[128,1536]{1,0:T(8,128)(2,1)S(1)}, bf16[128,1536]{1,0:T(8,128)(2,1)S(1)}, u32[]{:S(2)}, u32[]{:S(2)}) %collective-permute-start.25) | collective-permute-done | bytes 393248 | tf_op jit(solution)/shard_map/ppermute | solution.py:255
  113.3 1.6 %collective-permute-start.26 = (bf16[64,1536]{1,0:T(8,128)(2,1)S(1)}, bf16[64,1536]{1,0:T(8,128)(2,1)S(1)}, u32[]{:S(2)}, u32[]{:S(2)}) collective-permute-start(bf16[64,1536]{1,0:T(8,128)(2,1)S(1)} %get-tuple-element.123), channel_id=1, source_target_pairs={{0,2},{2,0},{4,6},{6,4},{8,10},{10,8},{12,14},{14,12},{16,18},{18,... | collective-permute-start | bytes 589832 | tf_op jit(solution)/shard_map/ppermute | solution.py:255
  115.5 3.4 %collective-permute-done.21.got_a = bf16[64,1536]{1,0:T(8,128)(2,1)S(1)} collective-permute-done((bf16[64,1536]{1,0:T(8,128)(2,1)S(1)}, bf16[64,1536]{1,0:T(8,128)(2,1)S(1)}, u32[]{:S(2)}, u32[]{:S(2)}) %collective-permute-start.21) | collective-permute-done | bytes 196640 | tf_op jit(solution)/shard_map/ppermute | solution.py:255
  119.0 2.9 %collective-permute-done.26.got_a = bf16[64,1536]{1,0:T(8,128)(2,1)S(1)} collective-permute-done((bf16[64,1536]{1,0:T(8,128)(2,1)S(1)}, bf16[64,1536]{1,0:T(8,128)(2,1)S(1)}, u32[]{:S(2)}, u32[]{:S(2)}) %collective-permute-start.26) | collective-permute-done | bytes 196640 | tf_op jit(solution)/shard_map/ppermute | solution.py:255
  122.1 12.1 %collective-permute-done.24.got_ref = bf16[64,1536]{1,0:T(8,128)(2,1)S(1)} collective-permute-done((bf16[64,1536]{1,0:T(8,128)(2,1)S(1)}, bf16[64,1536]{1,0:T(8,128)(2,1)S(1)}, u32[]{:S(2)}, u32[]{:S(2)}) %collective-permute-start.24) | collective-permute-done | bytes 196640 | tf_op jit(solution)/shard_map/ppermute | solution.py:255
  135.0 2.3 %collective-permute-done.29.got_ref = bf16[64,1536]{1,0:T(8,128)(2,1)S(1)} collective-permute-done((bf16[64,1536]{1,0:T(8,128)(2,1)S(1)}, bf16[64,1536]{1,0:T(8,128)(2,1)S(1)}, u32[]{:S(2)}, u32[]{:S(2)}) %collective-permute-start.29) | collective-permute-done | bytes 196640 | tf_op jit(solution)/shard_map/ppermute | solution.py:255
  (75 shorter events, 29.1 us)
Async XLA Ops:
  8.6 13.9 %collective-permute-start = (bf16[64,1664]{1,0:T(8,128)(2,1)S(1)}, bf16[64,1664]{1,0:T(8,128)(2,1)S(1)}, u32[]{:S(2)}, u32[]{:S(2)}) collective-permute-start(bf16[64,1664]{1,0:T(8,128)(2,1)S(1)} %get-tuple-element.68), channel_id=1, source_target_pairs={{0,16},{2,18},{4,20},{6,22},{8,24},{10,26},{12,28},{14,30},{16,0},... | collective-permute-start | bytes 638984 | tf_op jit(solution)/shard_map/ppermute | solution.py:255
  12.7 30.9 %collective-permute-start.9 = (bf16[512,768]{1,0:T(8,128)(2,1)}, bf16[512,768]{1,0:T(8,128)(2,1)S(1)}, u32[]{:S(2)}, u32[]{:S(2)}) collective-permute-start(bf16[512,768]{1,0:T(8,128)(2,1)} %bitcast.7), channel_id=1, source_target_pairs={{0,1},{1,0},{2,3},{3,2},{4,5},{5,4},{6,7},{7,6},{8,9},{9,8},{10,11... | collective-permute-start | bytes 2359304 | tf_op jit(solution)/shard_map/ppermute | solution.py:259
  12.7 1.1 copy-start.1
  15.2 28.4 %copy-start = (bf16[1,512,768]{2,1,0:T(8,128)(2,1)S(1)}, bf16[1,512,768]{2,1,0:T(8,128)(2,1)}, u32[]{:S(2)}) copy-start(bf16[1,512,768]{2,1,0:T(8,128)(2,1)} %param.23) | copy-start | bytes 2359300
  15.3 28.4 %collective-permute-start.8 = (bf16[768,1024]{1,0:T(8,128)(2,1)S(1)}, bf16[768,1024]{1,0:T(8,128)(2,1)S(1)}, u32[]{:S(2)}, u32[]{:S(2)}) collective-permute-start(bf16[768,1024]{1,0:T(8,128)(2,1)S(1)} %shard_map.132.refs_8_), channel_id=1, source_target_pairs={{0,1},{1,0},{2,3},{3,2},{4,5},{5,4},{6,7},{7,6},{8,9},{9,8},{10,11... | collective-permute-start | bytes 4718600 | tf_op jit(solution)/shard_map/ppermute | solution.py:259
  22.5 35.6 %collective-permute-start.1 = (bf16[768,1024]{1,0:T(8,128)(2,1)S(1)}, bf16[768,1024]{1,0:T(8,128)(2,1)S(1)}, u32[]{:S(2)}, u32[]{:S(2)}) collective-permute-start(bf16[768,1024]{1,0:T(8,128)(2,1)S(1)} %shard_map.132.refs_8_), channel_id=1, source_target_pairs={{0,8},{2,10},{4,12},{6,14},{8,0},{10,2},{12,4},{14,6},{16,24},{18,... | collective-permute-start | bytes 4718600 | tf_op jit(solution)/shard_map/ppermute | solution.py:255
  23.3 7.0 %collective-permute-start.3 = (bf16[64,1664]{1,0:T(8,128)(2,1)S(1)}, bf16[64,1664]{1,0:T(8,128)(2,1)S(1)}, u32[]{:S(2)}, u32[]{:S(2)}) collective-permute-start(bf16[64,1664]{1,0:T(8,128)(2,1)S(1)} %pad_maximum_fusion.refs_4_), channel_id=1, source_target_pairs={{0,2},{2,0},{4,6},{6,4},{8,10},{10,8},{12,14},{14,12},{16,18},{18,... | collective-permute-start | bytes 638984 | tf_op jit(solution)/shard_map/ppermute | solution.py:255
  24.9 6.9 %collective-permute-start.4 = (bf16[64,1664]{1,0:T(8,128)(2,1)S(1)}, bf16[64,1664]{1,0:T(8,128)(2,1)S(1)}, u32[]{:S(2)}, u32[]{:S(2)}) collective-permute-start(bf16[64,1664]{1,0:T(8,128)(2,1)S(1)} %pad_maximum_fusion.1.refs_6_), channel_id=1, source_target_pairs={{0,4},{2,6},{4,0},{6,2},{8,12},{10,14},{12,8},{14,10},{16,20},{18,... | collective-permute-start | bytes 638984 | tf_op jit(solution)/shard_map/ppermute | solution.py:255
  30.3 6.0 %collective-permute-start.2 = (bf16[64,1664]{1,0:T(8,128)(2,1)S(1)}, bf16[64,1664]{1,0:T(8,128)(2,1)S(1)}, u32[]{:S(2)}, u32[]{:S(2)}) collective-permute-start(bf16[64,1664]{1,0:T(8,128)(2,1)S(1)} %pad_maximum_fusion.refs_4_), channel_id=1, source_target_pairs={{0,4},{2,6},{4,0},{6,2},{8,12},{10,14},{12,8},{14,10},{16,20},{18,... | collective-permute-start | bytes 638984 | tf_op jit(solution)/shard_map/ppermute | solution.py:255
  31.8 6.0 %collective-permute-start.6 = (bf16[64,1664]{1,0:T(8,128)(2,1)S(1)}, bf16[64,1664]{1,0:T(8,128)(2,1)S(1)}, u32[]{:S(2)}, u32[]{:S(2)}) collective-permute-start(bf16[64,1664]{1,0:T(8,128)(2,1)S(1)} %pad_maximum_fusion.1.refs_6_), channel_id=1, source_target_pairs={{0,2},{2,0},{4,6},{6,4},{8,10},{10,8},{12,14},{14,12},{16,18},{18,... | collective-permute-start | bytes 638984 | tf_op jit(solution)/shard_map/ppermute | solution.py:255
  36.3 5.8 %collective-permute-start.5 = (bf16[64,1664]{1,0:T(8,128)(2,1)S(1)}, bf16[64,1664]{1,0:T(8,128)(2,1)S(1)}, u32[]{:S(2)}, u32[]{:S(2)}) collective-permute-start(bf16[64,1664]{1,0:T(8,128)(2,1)S(1)} %collective-permute-done.3.refs_5_), channel_id=1, source_target_pairs={{0,4},{2,6},{4,0},{6,2},{8,12},{10,14},{12,8},{14,10},{16,20},{18,... | collective-permute-start | bytes 638984 | tf_op jit(solution)/shard_map/ppermute | solution.py:255
  37.8 5.8 %collective-permute-start.7 = (bf16[64,1664]{1,0:T(8,128)(2,1)S(1)}, bf16[64,1664]{1,0:T(8,128)(2,1)S(1)}, u32[]{:S(2)}, u32[]{:S(2)}) collective-permute-start(bf16[64,1664]{1,0:T(8,128)(2,1)S(1)} %collective-permute-done.4.refs_7_), channel_id=1, source_target_pairs={{0,2},{2,0},{4,6},{6,4},{8,10},{10,8},{12,14},{14,12},{16,18},{18,... | collective-permute-start | bytes 638984 | tf_op jit(solution)/shard_map/ppermute | solution.py:255
  58.1 4.8 %collective-permute-start.11 = (bf16[768,1024]{1,0:T(8,128)(2,1)S(1)}, bf16[768,1024]{1,0:T(8,128)(2,1)S(1)}, u32[]{:S(2)}, u32[]{:S(2)}) collective-permute-start(bf16[768,1024]{1,0:T(8,128)(2,1)S(1)} %collective-permute-done.1.refs_8_), channel_id=1, source_target_pairs={{0,1},{1,0},{2,3},{3,2},{4,5},{5,4},{6,7},{7,6},{8,9},{9,8},{10,11... | collective-permute-start | bytes 4718600 | tf_op jit(solution)/shard_map/ppermute | solution.py:259
  58.1 13.7 %collective-permute-start.12 = (bf16[64,1664]{1,0:T(8,128)(2,1)S(1)}, bf16[64,1664]{1,0:T(8,128)(2,1)S(1)}, u32[]{:S(2)}, u32[]{:S(2)}) collective-permute-start(bf16[64,1664]{1,0:T(8,128)(2,1)S(1)} %get-tuple-element.80), channel_id=1, source_target_pairs={{0,16},{2,18},{4,20},{6,22},{8,24},{10,26},{12,28},{14,30},{16,0},... | collective-permute-start | bytes 638984 | tf_op jit(solution)/shard_map/ppermute | solution.py:255
  61.2 23.0 %collective-permute-start.10 = (bf16[512,768]{1,0:T(8,128)(2,1)S(1)}, bf16[512,768]{1,0:T(8,128)(2,1)S(1)}, u32[]{:S(2)}, u32[]{:S(2)}) collective-permute-start(bf16[512,768]{1,0:T(8,128)(2,1)S(1)} %bitcast.9), channel_id=1, source_target_pairs={{0,8},{2,10},{4,12},{6,14},{8,0},{10,2},{12,4},{14,6},{16,24},{18,... | collective-permute-start | bytes 2359304 | tf_op jit(solution)/shard_map/ppermute | solution.py:255
  71.8 8.2 %collective-permute-start.14 = (bf16[64,1664]{1,0:T(8,128)(2,1)S(1)}, bf16[64,1664]{1,0:T(8,128)(2,1)S(1)}, u32[]{:S(2)}, u32[]{:S(2)}) collective-permute-start(bf16[64,1664]{1,0:T(8,128)(2,1)S(1)} %pad_maximum_fusion.2.refs_4_), channel_id=1, source_target_pairs={{0,2},{2,0},{4,6},{6,4},{8,10},{10,8},{12,14},{14,12},{16,18},{18,... | collective-permute-start | bytes 638984 | tf_op jit(solution)/shard_map/ppermute | solution.py:255
  73.4 8.2 %collective-permute-start.17 = (bf16[64,1664]{1,0:T(8,128)(2,1)S(1)}, bf16[64,1664]{1,0:T(8,128)(2,1)S(1)}, u32[]{:S(2)}, u32[]{:S(2)}) collective-permute-start(bf16[64,1664]{1,0:T(8,128)(2,1)S(1)} %pad_maximum_fusion.3.refs_6_), channel_id=1, source_target_pairs={{0,4},{2,6},{4,0},{6,2},{8,12},{10,14},{12,8},{14,10},{16,20},{18,... | collective-permute-start | bytes 638984 | tf_op jit(solution)/shard_map/ppermute | solution.py:255
  75.0 11.2 %collective-permute-start.13 = (bf16[64,1664]{1,0:T(8,128)(2,1)S(1)}, bf16[64,1664]{1,0:T(8,128)(2,1)S(1)}, u32[]{:S(2)}, u32[]{:S(2)}) collective-permute-start(bf16[64,1664]{1,0:T(8,128)(2,1)S(1)} %pad_maximum_fusion.2.refs_4_), channel_id=1, source_target_pairs={{0,4},{2,6},{4,0},{6,2},{8,12},{10,14},{12,8},{14,10},{16,20},{18,... | collective-permute-start | bytes 638984 | tf_op jit(solution)/shard_map/ppermute | solution.py:255
  75.5 10.7 %collective-permute-start.16 = (bf16[64,1664]{1,0:T(8,128)(2,1)S(1)}, bf16[64,1664]{1,0:T(8,128)(2,1)S(1)}, u32[]{:S(2)}, u32[]{:S(2)}) collective-permute-start(bf16[64,1664]{1,0:T(8,128)(2,1)S(1)} %pad_maximum_fusion.3.refs_6_), channel_id=1, source_target_pairs={{0,2},{2,0},{4,6},{6,4},{8,10},{10,8},{12,14},{14,12},{16,18},{18,... | collective-permute-start | bytes 638984 | tf_op jit(solution)/shard_map/ppermute | solution.py:255
  80.0 9.3 %collective-permute-start.15 = (bf16[64,1664]{1,0:T(8,128)(2,1)S(1)}, bf16[64,1664]{1,0:T(8,128)(2,1)S(1)}, u32[]{:S(2)}, u32[]{:S(2)}) collective-permute-start(bf16[64,1664]{1,0:T(8,128)(2,1)S(1)} %collective-permute-done.14.refs_5_), channel_id=1, source_target_pairs={{0,4},{2,6},{4,0},{6,2},{8,12},{10,14},{12,8},{14,10},{16,20},{18,... | collective-permute-start | bytes 638984 | tf_op jit(solution)/shard_map/ppermute | solution.py:255
  81.7 7.7 %collective-permute-start.18 = (bf16[64,1664]{1,0:T(8,128)(2,1)S(1)}, bf16[64,1664]{1,0:T(8,128)(2,1)S(1)}, u32[]{:S(2)}, u32[]{:S(2)}) collective-permute-start(bf16[64,1664]{1,0:T(8,128)(2,1)S(1)} %collective-permute-done.17.refs_7_), channel_id=1, source_target_pairs={{0,2},{2,0},{4,6},{6,4},{8,10},{10,8},{12,14},{14,12},{16,18},{18,... | collective-permute-start | bytes 638984 | tf_op jit(solution)/shard_map/ppermute | solution.py:255
  89.4 2.3 %collective-permute-start.19 = (bf16[512,768]{1,0:T(8,128)(2,1)S(1)}, bf16[512,768]{1,0:T(8,128)(2,1)S(1)}, u32[]{:S(2)}, u32[]{:S(2)}) collective-permute-start(bf16[512,768]{1,0:T(8,128)(2,1)S(1)} %collective-permute-done.10.down_a), channel_id=1, source_target_pairs={{0,1},{1,0},{2,3},{3,2},{4,5},{5,4},{6,7},{7,6},{8,9},{9,8},{10,11... | collective-permute-start | bytes 2359304 | tf_op jit(solution)/shard_map/ppermute | solution.py:259
  92.7 11.8 %collective-permute-start.20 = (bf16[128,1536]{1,0:T(8,128)(2,1)S(1)}, bf16[128,1536]{1,0:T(8,128)(2,1)S(1)}, u32[]{:S(2)}, u32[]{:S(2)}) collective-permute-start(bf16[128,1536]{1,0:T(8,128)(2,1)S(1)} %get-tuple-element.101), channel_id=1, source_target_pairs={{0,4},{2,6},{4,0},{6,2},{8,12},{10,14},{12,8},{14,10},{16,20},{18,... | collective-permute-start | bytes 1179656 | tf_op jit(solution)/shard_map/ppermute | solution.py:255
  94.3 12.0 %collective-permute-start.22 = (bf16[128,1536]{1,0:T(8,128)(2,1)S(1)}, bf16[128,1536]{1,0:T(8,128)(2,1)S(1)}, u32[]{:S(2)}, u32[]{:S(2)}) collective-permute-start(bf16[128,1536]{1,0:T(8,128)(2,1)S(1)} %get-tuple-element.105), channel_id=1, source_target_pairs={{0,2},{2,0},{4,6},{6,4},{8,10},{10,8},{12,14},{14,12},{16,18},{18,... | collective-permute-start | bytes 1179656 | tf_op jit(solution)/shard_map/ppermute | solution.py:255
  101.1 12.1 %collective-permute-start.25 = (bf16[128,1536]{1,0:T(8,128)(2,1)S(1)}, bf16[128,1536]{1,0:T(8,128)(2,1)S(1)}, u32[]{:S(2)}, u32[]{:S(2)}) collective-permute-start(bf16[128,1536]{1,0:T(8,128)(2,1)S(1)} %get-tuple-element.121), channel_id=1, source_target_pairs={{0,4},{2,6},{4,0},{6,2},{8,12},{10,14},{12,8},{14,10},{16,20},{18,... | collective-permute-start | bytes 1179656 | tf_op jit(solution)/shard_map/ppermute | solution.py:255
  101.7 13.2 %collective-permute-start.27 = (bf16[128,1536]{1,0:T(8,128)(2,1)S(1)}, bf16[128,1536]{1,0:T(8,128)(2,1)S(1)}, u32[]{:S(2)}, u32[]{:S(2)}) collective-permute-start(bf16[128,1536]{1,0:T(8,128)(2,1)S(1)} %get-tuple-element.125), channel_id=1, source_target_pairs={{0,2},{2,0},{4,6},{6,4},{8,10},{10,8},{12,14},{14,12},{16,18},{18,... | collective-permute-start | bytes 1179656 | tf_op jit(solution)/shard_map/ppermute | solution.py:255
  104.5 14.4 %collective-permute-start.21 = (bf16[64,1536]{1,0:T(8,128)(2,1)S(1)}, bf16[64,1536]{1,0:T(8,128)(2,1)S(1)}, u32[]{:S(2)}, u32[]{:S(2)}) collective-permute-start(bf16[64,1536]{1,0:T(8,128)(2,1)S(1)} %get-tuple-element.103), channel_id=1, source_target_pairs={{0,2},{2,0},{4,6},{6,4},{8,10},{10,8},{12,14},{14,12},{16,18},{18,... | collective-permute-start | bytes 589832 | tf_op jit(solution)/shard_map/ppermute | solution.py:255
  106.3 12.6 %collective-permute-start.23 = (bf16[64,1536]{1,0:T(8,128)(2,1)S(1)}, bf16[64,1536]{1,0:T(8,128)(2,1)S(1)}, u32[]{:S(2)}, u32[]{:S(2)}) collective-permute-start(bf16[64,1536]{1,0:T(8,128)(2,1)S(1)} %get-tuple-element.107), channel_id=1, source_target_pairs={{0,4},{2,6},{4,0},{6,2},{8,12},{10,14},{12,8},{14,10},{16,20},{18,... | collective-permute-start | bytes 589832 | tf_op jit(solution)/shard_map/ppermute | solution.py:255
  113.3 8.7 %collective-permute-start.26 = (bf16[64,1536]{1,0:T(8,128)(2,1)S(1)}, bf16[64,1536]{1,0:T(8,128)(2,1)S(1)}, u32[]{:S(2)}, u32[]{:S(2)}) collective-permute-start(bf16[64,1536]{1,0:T(8,128)(2,1)S(1)} %get-tuple-element.123), channel_id=1, source_target_pairs={{0,2},{2,0},{4,6},{6,4},{8,10},{10,8},{12,14},{14,12},{16,18},{18,... | collective-permute-start | bytes 589832 | tf_op jit(solution)/shard_map/ppermute | solution.py:255
  114.9 7.1 %collective-permute-start.28 = (bf16[64,1536]{1,0:T(8,128)(2,1)S(1)}, bf16[64,1536]{1,0:T(8,128)(2,1)S(1)}, u32[]{:S(2)}, u32[]{:S(2)}) collective-permute-start(bf16[64,1536]{1,0:T(8,128)(2,1)S(1)} %get-tuple-element.127), channel_id=1, source_target_pairs={{0,4},{2,6},{4,0},{6,2},{8,12},{10,14},{12,8},{14,10},{16,20},{18,... | collective-permute-start | bytes 589832 | tf_op jit(solution)/shard_map/ppermute | solution.py:255
  119.0 15.3 %collective-permute-start.24 = (bf16[64,1536]{1,0:T(8,128)(2,1)S(1)}, bf16[64,1536]{1,0:T(8,128)(2,1)S(1)}, u32[]{:S(2)}, u32[]{:S(2)}) collective-permute-start(bf16[64,1536]{1,0:T(8,128)(2,1)S(1)} %get-tuple-element.109), channel_id=1, source_target_pairs={{0,16},{2,18},{4,20},{6,22},{8,24},{10,26},{12,28},{14,30},{16,0},... | collective-permute-start | bytes 589832 | tf_op jit(solution)/shard_map/ppermute | solution.py:255
  122.1 15.2 %collective-permute-start.29 = (bf16[64,1536]{1,0:T(8,128)(2,1)S(1)}, bf16[64,1536]{1,0:T(8,128)(2,1)S(1)}, u32[]{:S(2)}, u32[]{:S(2)}) collective-permute-start(bf16[64,1536]{1,0:T(8,128)(2,1)S(1)} %get-tuple-element.129), channel_id=1, source_target_pairs={{0,16},{2,18},{4,20},{6,22},{8,24},{10,26},{12,28},{14,30},{16,0},... | collective-permute-start | bytes 589832 | tf_op jit(solution)/shard_map/ppermute | solution.py:255
  (10 other events, 7.7 us)

commit v8 on v5

--- a/solution.py
+++ b/solution.py
@@ -144,28 +144,17 @@
         out_ref[:, width:] = turned.astype(jnp.bfloat16)
 
 
-def pack_kernel(gate_ref, up_ref, both_ref, sems):
-    ff = gate_ref.shape[1]
-    copies = [
-        pltpu.make_async_copy(gate_ref, both_ref.at[:, :ff], sems.at[0]),
-        pltpu.make_async_copy(up_ref, both_ref.at[:, ff:], sems.at[1]),
-    ]
-    for copy in copies:
-        copy.start()
-    for copy in copies:
-        copy.wait()
-
-
-def hidden_of(place, rows_ref, both_refs, begin, count):
-    depth, ff = both_refs[0].shape[0], both_refs[0].shape[1] // 2
-    acts = None
-    for which, ref in enumerate(both_refs):
+def hidden_of(place, rows_ref, gate_refs, up_refs, begin, count):
+    depth = gate_refs[0].shape[0]
+    acts = [None, None]
+    for which in range(2):
         half = place if which == 0 else 1 - place
         columns = pl.ds(pl.multiple_of(half * depth, depth), depth)
         rows = rows_ref[pl.ds(begin, count), columns]
-        term = jnp.dot(rows, ref[...], preferred_element_type=jnp.float32)
-        acts = term if acts is None else acts + term
-    gate_act, up_act = acts[:, :ff], acts[:, ff:]
+        for i, refs in enumerate((gate_refs, up_refs)):
+            term = jnp.dot(rows, refs[which][...], preferred_element_type=jnp.float32)
+            acts[i] = term if acts[i] is None else acts[i] + term
+    gate_act, up_act = acts
     return (gate_act / (1.0 + jnp.exp(-gate_act)) * up_act).astype(jnp.bfloat16)
 
 
@@ -177,7 +166,7 @@
 
 def own_kernel(pieces, group, *refs):
     piece_refs, refs = refs[:pieces], refs[pieces:]
-    both_a, both_b, down_a, down_b, total_ref, rows_ref = refs
+    gate_a, gate_b, up_a, up_b, down_a, down_b, total_ref, rows_ref = refs
     tok = piece_refs[0].shape[0]
     width = total_ref.shape[1]
     for i, ref in enumerate(piece_refs):
@@ -188,7 +177,7 @@
     @pl.loop(0, rows_ref.shape[0] // block)
     def _(step):
         begin = pl.multiple_of(step * block, block)
-        hidden = hidden_of(place, rows_ref, (both_a, both_b), begin, block)
+        hidden = hidden_of(place, rows_ref, (gate_a, gate_b), (up_a, up_b), begin, block)
         weight = weight_of(expert, group, rows_ref[pl.ds(begin, block), width:])
         for which, ref in enumerate((down_a, down_b)):
             half = place if which == 0 else 1 - place
@@ -199,7 +188,7 @@
 
 def beside_kernel(pieces, group, *refs):
     piece_refs, refs = refs[:pieces], refs[pieces:]
-    both_a, both_b, hidden_ref, weight_ref, rows_ref = refs
+    gate_a, gate_b, up_a, up_b, hidden_ref, weight_ref, rows_ref = refs
     tok = piece_refs[0].shape[0]
     width = rows_ref.shape[1] - PACK
     for i, ref in enumerate(piece_refs):
@@ -211,7 +200,7 @@
     def _(step):
         begin = pl.multiple_of(step * block, block)
         hidden_ref[pl.ds(begin, block), :] = hidden_of(
-            place, rows_ref, (both_a, both_b), begin, block
+            place, rows_ref, (gate_a, gate_b), (up_a, up_b), begin, block
         )
         weight = weight_of(expert, group, rows_ref[pl.ds(begin, block), width:])
         weight_ref[pl.ds(begin, block), :] = jnp.broadcast_to(weight, (block, PACK))
@@ -253,6 +242,32 @@
 def swap(block, distance):
     count = lax.axis_size("expert")
     return lax.ppermute(block, "expert", [(i, i ^ distance) for i in range(count)])
+
+
+def pair_gather(block):
+    count = lax.axis_size("expert")
+    pairs = [[i, i | Z_LOW] for i in range(count) if not i & Z_LOW]
+    return lax.all_gather(block, "expert", axis_index_groups=pairs)
+
+
+def beside_copy_kernel(pair_ref, out_ref, sem):
+    other = 1 - lax.axis_index("expert") // Z_LOW % 2
+    copy = pltpu.make_async_copy(pair_ref.at[other], out_ref, sem)
+    copy.start()
+    copy.wait()
+
+
+def beside(pair):
+    return call(
+        beside_copy_kernel,
+        jax.ShapeDtypeStruct(pair.shape[1:], pair.dtype),
+        (pair,),
+        4,
+        0,
+        2 * pair.size,
+        [pltpu.SemaphoreType.DMA],
+        [pl.BlockSpec(memory_space=pltpu.HBM)],
+    )
 
 
 def swap_core(block):
@@ -331,20 +346,11 @@
         + [pltpu.SemaphoreType.DMA((len(held),))],
         [hbm] * len(held),
     )
-    both = call(
-        pack_kernel,
-        jax.ShapeDtypeStruct((gate.shape[0], 2 * ff), jnp.bfloat16),
-        (gate, up),
-        8,
-        0,
-        8 * gate.size,
-        [pltpu.SemaphoreType.DMA((2,))],
-        [hbm] * 2,
-    )
-    twins = (swap_core(both), swap_core(down))
+    mine = (gate, up, down)
+    gathered = [pair_gather(w) for w in mine]
+    twins = [swap_core(w) for w in mine]
     far = [swap(x, Z_HIGH) for x in own]
-    far[0], twins, both_later = lax.optimization_barrier((far[0], twins, both))
-    both_by = swap(both_later, Z_LOW)
+    far[0], twins = lax.optimization_barrier((far[0], twins))
     first_one = halves(own[0], far[0])
     second_one = swap(first_one[0], X), swap(first_one[1], Y)
     far[1], second_one = lax.optimization_barrier((far[1], second_one))
@@ -359,7 +365,7 @@
         return call(
             functools.partial(own_kernel, 8, group),
             jax.ShapeDtypeStruct((rows, width), jnp.float32),
-            (*p, both, twins[0], down, twins[1]),
+            (*p, gate, twins[0], up, twins[1], down, twins[2]),
             20,
             6 * rows * width * ff,
             6 * width * ff + 6 * rows * width,
@@ -373,7 +379,7 @@
                 jax.ShapeDtypeStruct((rows, ff), jnp.bfloat16),
                 jax.ShapeDtypeStruct((rows, PACK), jnp.float32),
             ),
-            (*p, both_by, both_twin),
+            (*p, gate_by, gate_twin, up_by, up_twin),
             16,
             4 * rows * width * ff,
             4 * width * ff + 2 * rows * width,
@@ -391,17 +397,17 @@
             2 * width * ff + 8 * rows * width,
         )
 
-    total_one = own_total(pieces[0])
-    down_later, both_by, total_one, pieces = lax.optimization_barrier(
-        (down, both_by, total_one, pieces)
-    )
-    down_by = swap(down_later, Z_LOW)
-    both_twin = swap_core(both_by)
-    total_two = own_total(pieces[1])
+    total_one, total_two = own_total(pieces[0]), own_total(pieces[1])
+    gate_pair, up_pair, total_one, total_two = lax.optimization_barrier(
+        (*gathered[:2], total_one, total_two)
+    )
+    gate_by, up_by = beside(gate_pair), beside(up_pair)
+    gate_twin, up_twin = swap_core(gate_by), swap_core(up_by)
     hidden_one, hidden_two = beside_hidden(pieces[0]), beside_hidden(pieces[1])
-    down_by, total_two, hidden_one, hidden_two = lax.optimization_barrier(
-        (down_by, total_two, hidden_one, hidden_two)
-    )
+    down_pair, hidden_one, hidden_two = lax.optimization_barrier(
+        (gathered[2], hidden_one, hidden_two)
+    )
+    down_by = beside(down_pair)
     down_twin = swap_core(down_by)
     back_one = first_return(*join(total_one, *hidden_one))
     back_two = first_return(*join(total_two, *hidden_two))

time: 132 us -> 166 us (1.26)
  local copies, waits for them, and re-layouts: 2.63 us -> 36.5 us
  waiting for transfers between devices: 76 us -> 58 us
  between operations: 0.92 us -> 14.2 us
  Pallas kernels: 16 us -> 20.7 us
  starting transfers between devices: 35.9 us -> 33.8 us
    unnamed x24 -> x114, local copies, waits for them, and re-layouts: 2.57 us -> 35.5 us
    ppermute x26 -> x24, waiting for transfers between devices: 73.7 us -> 47.3 us  [swap(): lax.ppermute(block, 'expert', [(i, i ^ distance) for i in range(count)])]
    all_gather x0 -> x3, waiting for transfers between devices: none -> 5.46 us  [pair_gather(): return lax.all_gather(block, 'expert', axis_index_groups=pairs)]
    pallas_call x16 -> x18, Pallas kernels: 16 us -> 20.7 us  [call(): pl.pallas_call(body, out_shape=outs, in_specs=specs or [smem if x.ndim ==...]
    ppermute x26 -> x24, starting transfers between devices: 35 us -> 32.4 us  [swap(): lax.ppermute(block, 'expert', [(i, i ^ distance) for i in range(count)])]
    ppermute x4 -> x6, waiting for transfers between devices: 2.29 us -> 4.55 us  [swap_core(): return lax.ppermute(block, 'tensor', [(0, 1), (1, 0)])]
  transfers between devices with their start and end apart: 30 -> 33, of which waited for: 18 -> 17; matrix products, arithmetic and copies ran while one was open for 0% -> 1% of each run, Pallas kernels for 11% -> 11%
where the time goes in v8:
time: 166 us; the launch traced here: 165 us
  waiting for transfers between devices  58 us (35%)
  local copies, waits for them, and re-layouts  36.5 us (22%)
  starting transfers between devices  33.8 us (20%)
  Pallas kernels  20.7 us (12%)
  between operations  14.2 us (9%)
    ppermute x24, waiting for transfers between devices, swap(): lax.ppermute(block, 'expert', [(i, i ^ distance) for i in range(count)])  47.3 us
    unnamed x114, local copies, waits for them, and re-layouts  35.5 us
    ppermute x24, starting transfers between devices, swap(): lax.ppermute(block, 'expert', [(i, i ^ distance) for i in range(count)])  32.4 us
    pallas_call x18, Pallas kernels, call(): pl.pallas_call(body, out_shape=outs, in_specs=specs or [smem if x.ndim ==...  20.7 us
    all_gather x3, waiting for transfers between devices, pair_gather(): return lax.all_gather(block, 'expert', axis_index_groups=pairs)  5.46 us
    ppermute x6, waiting for transfers between devices, swap_core(): return lax.ppermute(block, 'tensor', [(0, 1), (1, 0)])  4.55 us
  transfers between devices with their start and end apart: 33, of which 17 were waited for; matrix products, arithmetic and copies ran while one was open for 1% of the time, Pallas kernels for 11%

profile of v8, /device:TPU:0, one launch (start us, length us, event | category | flops | bytes accessed | tf_op | source)
XLA Modules:
  0.0 164.8 jit_solution(10377326138861213239)
XLA Ops:
  16.9 3.7 %collective-permute-start = (bf16[64,1664]{1,0:T(8,128)(2,1)S(1)}, bf16[64,1664]{1,0:T(8,128)(2,1)S(1)}, u32[]{:S(2)}, u32[]{:S(2)}) collective-permute-start(bf16[64,1664]{1,0:T(8,128)(2,1)S(1)} %get-tuple-element.44), channel_id=1, source_target_pairs={{0,16},{2,18},{4,20},{6,22},{8,24},{10,26},{12,28},{14,30},{16,0},... | collective-permute-start | bytes 638984 | tf_op jit(solution)/shard_map/ppermute | solution.py:244
  20.9 10.7 %collective-permute-done = bf16[64,1664]{1,0:T(8,128)(2,1)S(1)} collective-permute-done((bf16[64,1664]{1,0:T(8,128)(2,1)S(1)}, bf16[64,1664]{1,0:T(8,128)(2,1)S(1)}, u32[]{:S(2)}, u32[]{:S(2)}) %collective-permute-start) | collective-permute-done | bytes 213024 | tf_op jit(solution)/shard_map/ppermute | solution.py:244
  31.7 2.0 %collective-permute-start.7 = (bf16[64,1664]{1,0:T(8,128)(2,1)S(1)}, bf16[64,1664]{1,0:T(8,128)(2,1)S(1)}, u32[]{:S(2)}, u32[]{:S(2)}) collective-permute-start(bf16[64,1664]{1,0:T(8,128)(2,1)S(1)} %pad_maximum_fusion.1.refs_6_), channel_id=1, source_target_pairs={{0,4},{2,6},{4,0},{6,2},{8,12},{10,14},{12,8},{14,10},{16,20},{18,... | collective-permute-start | bytes 638984 | tf_op jit(solution)/shard_map/ppermute | solution.py:244
  33.8 1.6 collective-permute-start.6
  36.0 4.1 %collective-permute-done.5 = bf16[64,1664]{1,0:T(8,128)(2,1)} collective-permute-done((bf16[64,1664]{1,0:T(8,128)(2,1)S(1)}, bf16[64,1664]{1,0:T(8,128)(2,1)}, u32[]{:S(2)}, u32[]{:S(2)}) %collective-permute-start.5) | collective-permute-done | bytes 213024 | tf_op jit(solution)/shard_map/ppermute | solution.py:244
  43.1 1.6 collective-permute-start.12
  49.4 1.8 %collective-permute-done.12.refs_5_ = bf16[64,1664]{1,0:T(8,128)(2,1)} collective-permute-done((bf16[64,1664]{1,0:T(8,128)(2,1)}, bf16[64,1664]{1,0:T(8,128)(2,1)}, u32[]{:S(2)}, u32[]{:S(2)}) %collective-permute-start.12) | collective-permute-done | bytes 213024 | tf_op jit(solution)/shard_map/ppermute | solution.py:244
  51.3 1.9 %collective-permute-start.14 = (bf16[64,1664]{1,0:T(8,128)(2,1)}, bf16[64,1664]{1,0:T(8,128)(2,1)S(1)}, u32[]{:S(2)}, u32[]{:S(2)}) collective-permute-start(bf16[64,1664]{1,0:T(8,128)(2,1)} %pad_maximum_fusion.3.refs_6_), channel_id=1, source_target_pairs={{0,2},{2,0},{4,6},{6,4},{8,10},{10,8},{12,14},{14,12},{16,18},{18,... | collective-permute-start | bytes 638984 | tf_op jit(solution)/shard_map/ppermute | solution.py:244
  56.4 1.9 %collective-permute-start.16 = (bf16[64,1664]{1,0:T(8,128)(2,1)}, bf16[64,1664]{1,0:T(8,128)(2,1)S(1)}, u32[]{:S(2)}, u32[]{:S(2)}) collective-permute-start(bf16[64,1664]{1,0:T(8,128)(2,1)} %collective-permute-done.15.refs_7_), channel_id=1, source_target_pairs={{0,2},{2,0},{4,6},{6,4},{8,10},{10,8},{12,14},{14,12},{16,18},{18,... | collective-permute-start | bytes 638984 | tf_op jit(solution)/shard_map/ppermute | solution.py:244
  69.0 4.4 %shard_map.132.total_ref = f32[512,1536]{1,0:T(8,128)S(1)} custom-call(bf16[64,1664]{1,0:T(8,128)(2,1)} %collective-permute-done.4.refs_0_, bf16[64,1664]{1,0:T(8,128)(2,1)} %collective-permute-done.8.refs_1_, bf16[64,1664]{1,0:T(8,128)(2,1)S(1)} %copy-done.35, bf16[64,1664]{1,0:T(8,128)(2,1)S(1)} %copy-done.38, bf16[64,1664]{1,0:T(8,128)(2,1)S(1)} %copy-done.21, ...), custom_call_target="tpu_custom_call" | custom-call | flops 2415919104 | bytes 9437184 | tf_op jit(solution)/shard_map/pallas_call | solution.py:86
  76.9 4.3 %shard_map.133.total_ref = f32[512,1536]{1,0:T(8,128)S(1)} custom-call(bf16[64,1664]{1,0:T(8,128)(2,1)S(1)} %collective-permute-done.11.refs_0_, bf16[64,1664]{1,0:T(8,128)(2,1)S(1)} %collective-permute-done.13.refs_1_, bf16[64,1664]{1,0:T(8,128)(2,1)S(1)} %collective-permute-done.14.refs_2_, bf16[64,1664]{1,0:T(8,128)(2,1)S(1)} %collective-permute-done.16.refs_3_, ...), custom_call_target="tpu_custom_call" | custom-call | flops 2415919104 | bytes 9437184 | tf_op jit(solution)/shard_map/pallas_call | solution.py:86
  81.2 1.6 copy-done
  85.6 1.5 copy-done.17
  89.6 1.5 collective-permute-done.18.refs_11_
  91.2 3.4 %shard_map.137 = (bf16[512,512]{1,0:T(8,128)(2,1)S(1)}, f32[512,128]{1,0:T(8,128)S(1)}) custom-call(bf16[64,1664]{1,0:T(8,128)(2,1)S(1)} %copy-done.41, bf16[64,1664]{1,0:T(8,128)(2,1)S(1)} %copy-done.45, bf16[64,1664]{1,0:T(8,128)(2,1)S(1)} %copy-done.43, bf16[64,1664]{1,0:T(8,128)(2,1)S(1)} %copy-done.47, bf16[64,1664]{1,0:T(8,128)(2,1)} %pad_maximum_fusion.2.refs_4_, ...), custom_call_target="tpu_custom_call" | custom-call | flops 1610612736 | bytes 4718592 | tf_op jit(solution)/shard_map/pallas_call | solution.py:86
  96.0 3.3 %shard_map.136 = (bf16[512,512]{1,0:T(8,128)(2,1)S(1)}, f32[512,128]{1,0:T(8,128)S(1)}) custom-call(bf16[64,1664]{1,0:T(8,128)(2,1)} %collective-permute-done.4.refs_0_, bf16[64,1664]{1,0:T(8,128)(2,1)} %collective-permute-done.8.refs_1_, bf16[64,1664]{1,0:T(8,128)(2,1)S(1)} %copy-done.36, bf16[64,1664]{1,0:T(8,128)(2,1)S(1)} %copy-done.39, ...), custom_call_target="tpu_custom_call" | custom-call | flops 1610612736 | bytes 4718592 | tf_op jit(solution)/shard_map/pallas_call | solution.py:86
  100.8 5.5 %all-gather.4.cloned.1.call-done.pair_ref = bf16[2,512,768]{2,1,0:T(8,128)(2,1)} async-done(((bf16[1,512,768]{2,1,0:T(8,128)(2,1)}), bf16[2,512,768]{2,1,0:T(8,128)(2,1)}) %all-gather.4.cloned.1.call-update) | async-done | bytes 1572880 | tf_op jit(solution)/shard_map/all_gather | solution.py:250
  107.8 2.3 %collective-permute-done.19.down_b = bf16[512,768]{1,0:T(8,128)(2,1)S(1)} collective-permute-done((bf16[512,768]{1,0:T(8,128)(2,1)S(1)}, bf16[512,768]{1,0:T(8,128)(2,1)S(1)}, u32[]{:S(2)}, u32[]{:S(2)}) %collective-permute-start.19) | collective-permute-done | bytes 786464 | tf_op jit(solution)/shard_map/ppermute | solution.py:274
  110.1 1.9 %copy-done.1 = f32[512,1536]{1,0:T(8,128)S(1)} copy-done((f32[512,1536]{1,0:T(8,128)S(1)}, f32[512,1536]{1,0:T(8,128)}, u32[]{:S(2)}) %copy-start.1) | copy-done | bytes 3145752
  113.0 1.5 collective-permute-start.27
  114.6 1.5 collective-permute-start.25
  118.2 6.8 %collective-permute-done.27.got_ref = bf16[128,1536]{1,0:T(8,128)(2,1)S(1)} collective-permute-done((bf16[128,1536]{1,0:T(8,128)(2,1)S(1)}, bf16[128,1536]{1,0:T(8,128)(2,1)S(1)}, u32[]{:S(2)}, u32[]{:S(2)}) %collective-permute-start.27) | collective-permute-done | bytes 393248 | tf_op jit(solution)/shard_map/ppermute | solution.py:244
  125.1 1.5 collective-permute-start.28
  126.7 1.5 collective-permute-start.26
  128.3 5.2 %collective-permute-done.22.got_ref = bf16[128,1536]{1,0:T(8,128)(2,1)S(1)} collective-permute-done((bf16[128,1536]{1,0:T(8,128)(2,1)S(1)}, bf16[128,1536]{1,0:T(8,128)(2,1)S(1)}, u32[]{:S(2)}, u32[]{:S(2)}) %collective-permute-start.22) | collective-permute-done | bytes 393248 | tf_op jit(solution)/shard_map/ppermute | solution.py:244
  133.5 1.5 collective-permute-start.23
  135.2 1.5 collective-permute-start.21
  136.7 2.5 %collective-permute-done.28.got_b = bf16[64,1536]{1,0:T(8,128)(2,1)S(1)} collective-permute-done((bf16[64,1536]{1,0:T(8,128)(2,1)S(1)}, bf16[64,1536]{1,0:T(8,128)(2,1)S(1)}, u32[]{:S(2)}, u32[]{:S(2)}) %collective-permute-start.28) | collective-permute-done | bytes 196640 | tf_op jit(solution)/shard_map/ppermute | solution.py:244
  139.3 2.5 %collective-permute-start.29 = (bf16[64,1536]{1,0:T(8,128)(2,1)S(1)}, bf16[64,1536]{1,0:T(8,128)(2,1)S(1)}, u32[]{:S(2)}, u32[]{:S(2)}) collective-permute-start(bf16[64,1536]{1,0:T(8,128)(2,1)S(1)} %get-tuple-element.85), channel_id=1, source_target_pairs={{0,16},{2,18},{4,20},{6,22},{8,24},{10,26},{12,28},{14,30},{16,0},... | collective-permute-start | bytes 589832 | tf_op jit(solution)/shard_map/ppermute | solution.py:244
  142.4 2.5 %collective-permute-start.24 = (bf16[64,1536]{1,0:T(8,128)(2,1)S(1)}, bf16[64,1536]{1,0:T(8,128)(2,1)S(1)}, u32[]{:S(2)}, u32[]{:S(2)}) collective-permute-start(bf16[64,1536]{1,0:T(8,128)(2,1)S(1)} %get-tuple-element.72), channel_id=1, source_target_pairs={{0,16},{2,18},{4,20},{6,22},{8,24},{10,26},{12,28},{14,30},{16,0},... | collective-permute-start | bytes 589832 | tf_op jit(solution)/shard_map/ppermute | solution.py:244
  144.8 9.5 %collective-permute-done.29.got_ref = bf16[64,1536]{1,0:T(8,128)(2,1)S(1)} collective-permute-done((bf16[64,1536]{1,0:T(8,128)(2,1)S(1)}, bf16[64,1536]{1,0:T(8,128)(2,1)S(1)}, u32[]{:S(2)}, u32[]{:S(2)}) %collective-permute-start.29) | collective-permute-done | bytes 196640 | tf_op jit(solution)/shard_map/ppermute | solution.py:244
  155.1 2.4 %collective-permute-done.24.got_ref = bf16[64,1536]{1,0:T(8,128)(2,1)S(1)} collective-permute-done((bf16[64,1536]{1,0:T(8,128)(2,1)S(1)}, bf16[64,1536]{1,0:T(8,128)(2,1)S(1)}, u32[]{:S(2)}, u32[]{:S(2)}) %collective-permute-start.24) | collective-permute-done | bytes 196640 | tf_op jit(solution)/shard_map/ppermute | solution.py:244
  (176 shorter events, 50.8 us)
Async XLA Ops:
  7.2 78.4 %all-gather.6.cloned.1.call-start = ((), (), s32[]{:S(2)}) async-start(), calls=%async_computation.1 | async-start | bytes 2359296 | tf_op jit(solution)/shard_map/all_gather | solution.py:250
  7.9 77.7 %all-gather.8.cloned.1.call-start = ((), (), s32[]{:S(2)}) async-start(), calls=%async_computation.2 | async-start | bytes 2359296 | tf_op jit(solution)/shard_map/all_gather | solution.py:250
  7.9 23.7 %collective-permute-start.1 = (bf16[768,512]{1,0:T(8,128)(2,1)}, bf16[768,512]{1,0:T(8,128)(2,1)S(1)}, u32[]{:S(2)}, u32[]{:S(2)}) collective-permute-start(bf16[768,512]{1,0:T(8,128)(2,1)} %bitcast.7), channel_id=1, source_target_pairs={{0,1},{1,0},{2,3},{3,2},{4,5},{5,4},{6,7},{7,6},{8,9},{9,8},{10,11... | collective-permute-start | bytes 2359304 | tf_op jit(solution)/shard_map/ppermute | solution.py:274
  8.5 23.2 %collective-permute-start.2 = (bf16[768,512]{1,0:T(8,128)(2,1)}, bf16[768,512]{1,0:T(8,128)(2,1)S(1)}, u32[]{:S(2)}, u32[]{:S(2)}) collective-permute-start(bf16[768,512]{1,0:T(8,128)(2,1)} %bitcast.10), channel_id=1, source_target_pairs={{0,1},{1,0},{2,3},{3,2},{4,5},{5,4},{6,7},{7,6},{8,9},{9,8},{10,11... | collective-permute-start | bytes 2359304 | tf_op jit(solution)/shard_map/ppermute | solution.py:274
  8.5 23.1 %collective-permute-start.3 = (bf16[512,768]{1,0:T(8,128)(2,1)}, bf16[512,768]{1,0:T(8,128)(2,1)S(1)}, u32[]{:S(2)}, u32[]{:S(2)}) collective-permute-start(bf16[512,768]{1,0:T(8,128)(2,1)} %bitcast.13), channel_id=1, source_target_pairs={{0,1},{1,0},{2,3},{3,2},{4,5},{5,4},{6,7},{7,6},{8,9},{9,8},{10,11... | collective-permute-start | bytes 2359304 | tf_op jit(solution)/shard_map/ppermute | solution.py:274
  16.9 14.7 %collective-permute-start = (bf16[64,1664]{1,0:T(8,128)(2,1)S(1)}, bf16[64,1664]{1,0:T(8,128)(2,1)S(1)}, u32[]{:S(2)}, u32[]{:S(2)}) collective-permute-start(bf16[64,1664]{1,0:T(8,128)(2,1)S(1)} %get-tuple-element.44), channel_id=1, source_target_pairs={{0,16},{2,18},{4,20},{6,22},{8,24},{10,26},{12,28},{14,30},{16,0},... | collective-permute-start | bytes 638984 | tf_op jit(solution)/shard_map/ppermute | solution.py:244
  20.7 19.4 %collective-permute-start.5 = (bf16[64,1664]{1,0:T(8,128)(2,1)S(1)}, bf16[64,1664]{1,0:T(8,128)(2,1)}, u32[]{:S(2)}, u32[]{:S(2)}) collective-permute-start(bf16[64,1664]{1,0:T(8,128)(2,1)S(1)} %get-tuple-element.46), channel_id=1, source_target_pairs={{0,16},{2,18},{4,20},{6,22},{8,24},{10,26},{12,28},{14,30},{16,0},... | collective-permute-start | bytes 638984 | tf_op jit(solution)/shard_map/ppermute | solution.py:244
  20.8 85.5 %all-gather.4.cloned.1.call-start = ((), (), s32[]{:S(2)}) async-start(), calls=%async_computation | async-start | bytes 2359296 | tf_op jit(solution)/shard_map/all_gather | solution.py:250
  31.7 8.4 %collective-permute-start.7 = (bf16[64,1664]{1,0:T(8,128)(2,1)S(1)}, bf16[64,1664]{1,0:T(8,128)(2,1)S(1)}, u32[]{:S(2)}, u32[]{:S(2)}) collective-permute-start(bf16[64,1664]{1,0:T(8,128)(2,1)S(1)} %pad_maximum_fusion.1.refs_6_), channel_id=1, source_target_pairs={{0,4},{2,6},{4,0},{6,2},{8,12},{10,14},{12,8},{14,10},{16,20},{18,... | collective-permute-start | bytes 638984 | tf_op jit(solution)/shard_map/ppermute | solution.py:244
  33.8 7.6 %collective-permute-start.6 = (bf16[64,1664]{1,0:T(8,128)(2,1)S(1)}, bf16[64,1664]{1,0:T(8,128)(2,1)}, u32[]{:S(2)}, u32[]{:S(2)}) collective-permute-start(bf16[64,1664]{1,0:T(8,128)(2,1)S(1)} %pad_maximum_fusion.refs_4_), channel_id=1, source_target_pairs={{0,2},{2,0},{4,6},{6,4},{8,10},{10,8},{12,14},{14,12},{16,18},{18,... | collective-permute-start | bytes 638984 | tf_op jit(solution)/shard_map/ppermute | solution.py:244
  35.4 11.2 %collective-permute-start.9 = (bf16[64,1664]{1,0:T(8,128)(2,1)S(1)}, bf16[64,1664]{1,0:T(8,128)(2,1)S(1)}, u32[]{:S(2)}, u32[]{:S(2)}) collective-permute-start(bf16[64,1664]{1,0:T(8,128)(2,1)S(1)} %pad_maximum_fusion.1.refs_6_), channel_id=1, source_target_pairs={{0,2},{2,0},{4,6},{6,4},{8,10},{10,8},{12,14},{14,12},{16,18},{18,... | collective-permute-start | bytes 638984 | tf_op jit(solution)/shard_map/ppermute | solution.py:244
  35.9 12.7 %collective-permute-start.4 = (bf16[64,1664]{1,0:T(8,128)(2,1)S(1)}, bf16[64,1664]{1,0:T(8,128)(2,1)}, u32[]{:S(2)}, u32[]{:S(2)}) collective-permute-start(bf16[64,1664]{1,0:T(8,128)(2,1)S(1)} %pad_maximum_fusion.refs_4_), channel_id=1, source_target_pairs={{0,4},{2,6},{4,0},{6,2},{8,12},{10,14},{12,8},{14,10},{16,20},{18,... | collective-permute-start | bytes 638984 | tf_op jit(solution)/shard_map/ppermute | solution.py:244
  43.1 8.2 %collective-permute-start.12 = (bf16[64,1664]{1,0:T(8,128)(2,1)}, bf16[64,1664]{1,0:T(8,128)(2,1)}, u32[]{:S(2)}, u32[]{:S(2)}) collective-permute-start(bf16[64,1664]{1,0:T(8,128)(2,1)} %pad_maximum_fusion.2.refs_4_), channel_id=1, source_target_pairs={{0,2},{2,0},{4,6},{6,4},{8,10},{10,8},{12,14},{14,12},{16,18},{18,... | collective-permute-start | bytes 638984 | tf_op jit(solution)/shard_map/ppermute | solution.py:244
  45.3 8.5 %collective-permute-start.15 = (bf16[64,1664]{1,0:T(8,128)(2,1)}, bf16[64,1664]{1,0:T(8,128)(2,1)}, u32[]{:S(2)}, u32[]{:S(2)}) collective-permute-start(bf16[64,1664]{1,0:T(8,128)(2,1)} %pad_maximum_fusion.3.refs_6_), channel_id=1, source_target_pairs={{0,4},{2,6},{4,0},{6,2},{8,12},{10,14},{12,8},{14,10},{16,20},{18,... | collective-permute-start | bytes 638984 | tf_op jit(solution)/shard_map/ppermute | solution.py:244
  45.8 9.9 %collective-permute-start.10 = (bf16[64,1664]{1,0:T(8,128)(2,1)S(1)}, bf16[64,1664]{1,0:T(8,128)(2,1)S(1)}, u32[]{:S(2)}, u32[]{:S(2)}) collective-permute-start(bf16[64,1664]{1,0:T(8,128)(2,1)S(1)} %collective-permute-done.7.refs_7_), channel_id=1, source_target_pairs={{0,2},{2,0},{4,6},{6,4},{8,10},{10,8},{12,14},{14,12},{16,18},{18,... | collective-permute-start | bytes 638984 | tf_op jit(solution)/shard_map/ppermute | solution.py:244
  47.3 11.1 %collective-permute-start.8 = (bf16[64,1664]{1,0:T(8,128)(2,1)}, bf16[64,1664]{1,0:T(8,128)(2,1)}, u32[]{:S(2)}, u32[]{:S(2)}) collective-permute-start(bf16[64,1664]{1,0:T(8,128)(2,1)} %collective-permute-done.6.refs_5_), channel_id=1, source_target_pairs={{0,4},{2,6},{4,0},{6,2},{8,12},{10,14},{12,8},{14,10},{16,20},{18,... | collective-permute-start | bytes 638984 | tf_op jit(solution)/shard_map/ppermute | solution.py:244
  48.6 24.8 %collective-permute-start.11 = (bf16[64,1664]{1,0:T(8,128)(2,1)}, bf16[64,1664]{1,0:T(8,128)(2,1)S(1)}, u32[]{:S(2)}, u32[]{:S(2)}) collective-permute-start(bf16[64,1664]{1,0:T(8,128)(2,1)} %pad_maximum_fusion.2.refs_4_), channel_id=1, source_target_pairs={{0,4},{2,6},{4,0},{6,2},{8,12},{10,14},{12,8},{14,10},{16,20},{18,... | collective-permute-start | bytes 638984 | tf_op jit(solution)/shard_map/ppermute | solution.py:244
  51.3 22.2 %collective-permute-start.14 = (bf16[64,1664]{1,0:T(8,128)(2,1)}, bf16[64,1664]{1,0:T(8,128)(2,1)S(1)}, u32[]{:S(2)}, u32[]{:S(2)}) collective-permute-start(bf16[64,1664]{1,0:T(8,128)(2,1)} %pad_maximum_fusion.3.refs_6_), channel_id=1, source_target_pairs={{0,2},{2,0},{4,6},{6,4},{8,10},{10,8},{12,14},{14,12},{16,18},{18,... | collective-permute-start | bytes 638984 | tf_op jit(solution)/shard_map/ppermute | solution.py:244
  53.9 19.6 %collective-permute-start.13 = (bf16[64,1664]{1,0:T(8,128)(2,1)}, bf16[64,1664]{1,0:T(8,128)(2,1)S(1)}, u32[]{:S(2)}, u32[]{:S(2)}) collective-permute-start(bf16[64,1664]{1,0:T(8,128)(2,1)} %collective-permute-done.12.refs_5_), channel_id=1, source_target_pairs={{0,4},{2,6},{4,0},{6,2},{8,12},{10,14},{12,8},{14,10},{16,20},{18,... | collective-permute-start | bytes 638984 | tf_op jit(solution)/shard_map/ppermute | solution.py:244
  56.4 17.0 %collective-permute-start.16 = (bf16[64,1664]{1,0:T(8,128)(2,1)}, bf16[64,1664]{1,0:T(8,128)(2,1)S(1)}, u32[]{:S(2)}, u32[]{:S(2)}) collective-permute-start(bf16[64,1664]{1,0:T(8,128)(2,1)} %collective-permute-done.15.refs_7_), channel_id=1, source_target_pairs={{0,2},{2,0},{4,6},{6,4},{8,10},{10,8},{12,14},{14,12},{16,18},{18,... | collective-permute-start | bytes 638984 | tf_op jit(solution)/shard_map/ppermute | solution.py:244
  87.3 2.4 %collective-permute-start.17 = (bf16[768,512]{1,0:T(8,128)(2,1)S(1)}, bf16[768,512]{1,0:T(8,128)(2,1)S(1)}, u32[]{:S(2)}, u32[]{:S(2)}) collective-permute-start(bf16[768,512]{1,0:T(8,128)(2,1)S(1)} %shard_map.134.refs_8_), channel_id=1, source_target_pairs={{0,1},{1,0},{2,3},{3,2},{4,5},{5,4},{6,7},{7,6},{8,9},{9,8},{10,11... | collective-permute-start | bytes 2359304 | tf_op jit(solution)/shard_map/ppermute | solution.py:274
  88.8 2.4 %collective-permute-start.18 = (bf16[768,512]{1,0:T(8,128)(2,1)S(1)}, bf16[768,512]{1,0:T(8,128)(2,1)S(1)}, u32[]{:S(2)}, u32[]{:S(2)}) collective-permute-start(bf16[768,512]{1,0:T(8,128)(2,1)S(1)} %shard_map.135.refs_10_), channel_id=1, source_target_pairs={{0,1},{1,0},{2,3},{3,2},{4,5},{5,4},{6,7},{7,6},{8,9},{9,8},{10,11... | collective-permute-start | bytes 2359304 | tf_op jit(solution)/shard_map/ppermute | solution.py:274
  113.0 12.0 %collective-permute-start.27 = (bf16[128,1536]{1,0:T(8,128)(2,1)S(1)}, bf16[128,1536]{1,0:T(8,128)(2,1)S(1)}, u32[]{:S(2)}, u32[]{:S(2)}) collective-permute-start(bf16[128,1536]{1,0:T(8,128)(2,1)S(1)} %get-tuple-element.81), channel_id=1, source_target_pairs={{0,2},{2,0},{4,6},{6,4},{8,10},{10,8},{12,14},{14,12},{16,18},{18,... | collective-permute-start | bytes 1179656 | tf_op jit(solution)/shard_map/ppermute | solution.py:244
  114.6 12.1 %collective-permute-start.25 = (bf16[128,1536]{1,0:T(8,128)(2,1)S(1)}, bf16[128,1536]{1,0:T(8,128)(2,1)S(1)}, u32[]{:S(2)}, u32[]{:S(2)}) collective-permute-start(bf16[128,1536]{1,0:T(8,128)(2,1)S(1)} %get-tuple-element.77), channel_id=1, source_target_pairs={{0,4},{2,6},{4,0},{6,2},{8,12},{10,14},{12,8},{14,10},{16,20},{18,... | collective-permute-start | bytes 1179656 | tf_op jit(solution)/shard_map/ppermute | solution.py:244
  117.0 16.4 %collective-permute-start.22 = (bf16[128,1536]{1,0:T(8,128)(2,1)S(1)}, bf16[128,1536]{1,0:T(8,128)(2,1)S(1)}, u32[]{:S(2)}, u32[]{:S(2)}) collective-permute-start(bf16[128,1536]{1,0:T(8,128)(2,1)S(1)} %get-tuple-element.68), channel_id=1, source_target_pairs={{0,2},{2,0},{4,6},{6,4},{8,10},{10,8},{12,14},{14,12},{16,18},{18,... | collective-permute-start | bytes 1179656 | tf_op jit(solution)/shard_map/ppermute | solution.py:244
  117.7 17.4 %collective-permute-start.20 = (bf16[128,1536]{1,0:T(8,128)(2,1)S(1)}, bf16[128,1536]{1,0:T(8,128)(2,1)S(1)}, u32[]{:S(2)}, u32[]{:S(2)}) collective-permute-start(bf16[128,1536]{1,0:T(8,128)(2,1)S(1)} %get-tuple-element.64), channel_id=1, source_target_pairs={{0,4},{2,6},{4,0},{6,2},{8,12},{10,14},{12,8},{14,10},{16,20},{18,... | collective-permute-start | bytes 1179656 | tf_op jit(solution)/shard_map/ppermute | solution.py:244
  125.1 14.1 %collective-permute-start.28 = (bf16[64,1536]{1,0:T(8,128)(2,1)S(1)}, bf16[64,1536]{1,0:T(8,128)(2,1)S(1)}, u32[]{:S(2)}, u32[]{:S(2)}) collective-permute-start(bf16[64,1536]{1,0:T(8,128)(2,1)S(1)} %get-tuple-element.83), channel_id=1, source_target_pairs={{0,4},{2,6},{4,0},{6,2},{8,12},{10,14},{12,8},{14,10},{16,20},{18,... | collective-permute-start | bytes 589832 | tf_op jit(solution)/shard_map/ppermute | solution.py:244
  126.7 12.5 %collective-permute-start.26 = (bf16[64,1536]{1,0:T(8,128)(2,1)S(1)}, bf16[64,1536]{1,0:T(8,128)(2,1)S(1)}, u32[]{:S(2)}, u32[]{:S(2)}) collective-permute-start(bf16[64,1536]{1,0:T(8,128)(2,1)S(1)} %get-tuple-element.79), channel_id=1, source_target_pairs={{0,2},{2,0},{4,6},{6,4},{8,10},{10,8},{12,14},{14,12},{16,18},{18,... | collective-permute-start | bytes 589832 | tf_op jit(solution)/shard_map/ppermute | solution.py:244
  133.5 8.7 %collective-permute-start.23 = (bf16[64,1536]{1,0:T(8,128)(2,1)S(1)}, bf16[64,1536]{1,0:T(8,128)(2,1)S(1)}, u32[]{:S(2)}, u32[]{:S(2)}) collective-permute-start(bf16[64,1536]{1,0:T(8,128)(2,1)S(1)} %get-tuple-element.70), channel_id=1, source_target_pairs={{0,4},{2,6},{4,0},{6,2},{8,12},{10,14},{12,8},{14,10},{16,20},{18,... | collective-permute-start | bytes 589832 | tf_op jit(solution)/shard_map/ppermute | solution.py:244
  135.2 7.1 %collective-permute-start.21 = (bf16[64,1536]{1,0:T(8,128)(2,1)S(1)}, bf16[64,1536]{1,0:T(8,128)(2,1)S(1)}, u32[]{:S(2)}, u32[]{:S(2)}) collective-permute-start(bf16[64,1536]{1,0:T(8,128)(2,1)S(1)} %get-tuple-element.66), channel_id=1, source_target_pairs={{0,2},{2,0},{4,6},{6,4},{8,10},{10,8},{12,14},{14,12},{16,18},{18,... | collective-permute-start | bytes 589832 | tf_op jit(solution)/shard_map/ppermute | solution.py:244
  139.3 15.1 %collective-permute-start.29 = (bf16[64,1536]{1,0:T(8,128)(2,1)S(1)}, bf16[64,1536]{1,0:T(8,128)(2,1)S(1)}, u32[]{:S(2)}, u32[]{:S(2)}) collective-permute-start(bf16[64,1536]{1,0:T(8,128)(2,1)S(1)} %get-tuple-element.85), channel_id=1, source_target_pairs={{0,16},{2,18},{4,20},{6,22},{8,24},{10,26},{12,28},{14,30},{16,0},... | collective-permute-start | bytes 589832 | tf_op jit(solution)/shard_map/ppermute | solution.py:244
  142.4 15.2 %collective-permute-start.24 = (bf16[64,1536]{1,0:T(8,128)(2,1)S(1)}, bf16[64,1536]{1,0:T(8,128)(2,1)S(1)}, u32[]{:S(2)}, u32[]{:S(2)}) collective-permute-start(bf16[64,1536]{1,0:T(8,128)(2,1)S(1)} %get-tuple-element.72), channel_id=1, source_target_pairs={{0,16},{2,18},{4,20},{6,22},{8,24},{10,26},{12,28},{14,30},{16,0},... | collective-permute-start | bytes 589832 | tf_op jit(solution)/shard_map/ppermute | solution.py:244
  (58 other events, 211.3 us)
Sparse Core Ops, SparseCore 0:
  9.5 38.6 all-gather.5
  49.7 27.6 all-gather.7
  79.0 27.1 all-gather.3

commit v9 on v6

--- a/solution.py
+++ b/solution.py
@@ -9,7 +9,8 @@
 
 EPS = 1e-05
 PACK = 128
-X, Y, Z_LOW, Z_HIGH = 1, 2, 4, 8 | 1
+X, Y = 1, 2
+Z_WAYS = (12, 8, 4)
 
 
 def rms_rows(tokens, norm_gain):
@@ -204,7 +205,7 @@
     width = rows_ref.shape[1] - PACK
     for i, ref in enumerate(piece_refs):
         rows_ref[i * tok : (i + 1) * tok, :] = ref[...]
-    place, expert = lax.axis_index("tensor"), lax.axis_index("expert") ^ Z_LOW
+    place, expert = lax.axis_index("tensor"), lax.axis_index("expert") ^ X
     block = 256
 
     @pl.loop(0, rows_ref.shape[0] // block)
@@ -217,37 +218,27 @@
         weight_ref[pl.ds(begin, block), :] = jnp.broadcast_to(weight, (block, PACK))
 
 
-def join_kernel(hidden_ref, weight_ref, total_ref, down_a, down_b, send_a, send_b, keep_a, keep_b):
+def join_kernel(hidden_ref, weight_ref, total_ref, down_a, down_b, *outs):
     place = lax.axis_index("tensor")
-    count = send_a.shape[0]
-    for pair, outs in ((0, (send_a, send_b)), (1, (keep_a, keep_b))):
-        rows = slice(pair * 2 * count, (pair + 1) * 2 * count)
+    count = outs[0].shape[0]
+    block = 4 * count
+    for part in range(len(outs) // 4):
+        rows = slice(part * block, (part + 1) * block)
         weight = weight_ref[rows, :1]
         for which, ref in enumerate((down_a, down_b)):
             half = place if which == 0 else 1 - place
             columns = pl.ds(pl.multiple_of(half * ref.shape[1], ref.shape[1]), ref.shape[1])
-            part = jnp.dot(hidden_ref[rows, :], ref[...], preferred_element_type=jnp.float32)
-            part = part * weight + total_ref[rows, columns]
-            outs[0][:, columns] = part[:count].astype(outs[0].dtype)
-            outs[1][:, columns] = part[count:].astype(outs[1].dtype)
-
-
-def first_sum_kernel(keep_ref, got_ref, send_ref, held_ref):
-    half = held_ref.shape[0]
-    held_ref[...] = keep_ref[:half] + got_ref[:half].astype(jnp.float32)
-    send_ref[...] = (keep_ref[half:] + got_ref[half:].astype(jnp.float32)).astype(jnp.bfloat16)
-
-
-def second_sum_kernel(keep_a, got_a, keep_b, got_b, send_ref, held_ref):
-    half = keep_a.shape[0] // 2
-    for i, (keep, got) in enumerate(((keep_a, got_a), (keep_b, got_b))):
-        rows = slice(i * half, (i + 1) * half)
-        held_ref[rows, :] = keep[:half] + got[:half].astype(jnp.float32)
-        send_ref[rows, :] = (keep[half:] + got[half:].astype(jnp.float32)).astype(jnp.bfloat16)
-
-
-def last_sum_kernel(keep_ref, got_ref, out_ref):
-    out_ref[...] = (keep_ref[...] + got_ref[...].astype(jnp.float32)).astype(jnp.bfloat16)
+            result = jnp.dot(hidden_ref[rows, :], ref[...], preferred_element_type=jnp.float32)
+            result = result * weight + total_ref[rows, columns]
+            for i, out in enumerate(outs[4 * part : 4 * part + 4]):
+                out[:, columns] = result[i * count : (i + 1) * count].astype(out.dtype)
+
+
+def sum_kernel(*refs):
+    total = refs[0][...].astype(jnp.float32)
+    for ref in refs[1:-1]:
+        total = total + ref[...].astype(jnp.float32)
+    refs[-1][...] = total.astype(jnp.bfloat16)
 
 
 def swap(block, distance):
@@ -259,42 +250,21 @@
     return lax.ppermute(block, "tensor", [(0, 1), (1, 0)])
 
 
-def halves(own, far):
-    half = own.shape[0] // 2
-    return [jnp.concatenate([own[i : i + half], far[i : i + half]]) for i in (0, half)]
-
-
-def spread(a1, b1, a2, b2):
-    a3, b3 = swap(a1, Y), swap(b1, X)
-    a4, b4 = swap(a2, Y), swap(b2, X)
-    return [a3, a4, b3, b4, a1, a2, b1, b2]
-
-
-def first_return(send_a, send_b, keep_a, keep_b):
-    quarter, width = keep_a.shape[0] // 2, keep_a.shape[1]
-    outs = (
-        jax.ShapeDtypeStruct((quarter, width), jnp.bfloat16),
-        jax.ShapeDtypeStruct((quarter, width), jnp.float32),
-    )
-    size = quarter * width
-    got_a, got_b = swap(send_a, Y), swap(send_b, X)
-    next_a, held_a = call(first_sum_kernel, outs, (keep_a, got_a), 8, size, 18 * size)
-    next_b, held_b = call(first_sum_kernel, outs, (keep_b, got_b), 8, size, 18 * size)
-    return next_a, next_b, held_a, held_b
-
-
-def last_returns(next_a, next_b, held_a, held_b):
-    outs = (
-        jax.ShapeDtypeStruct(held_a.shape, jnp.bfloat16),
-        jax.ShapeDtypeStruct(held_a.shape, jnp.float32),
-    )
-    size = held_a.size
-    got_a, got_b = swap(next_a, X), swap(next_b, Y)
-    next_z, held_z = call(
-        second_sum_kernel, outs, (held_a, got_a, held_b, got_b), 8, size, 18 * size
-    )
-    got_z = swap(next_z, Z_HIGH)
-    return call(last_sum_kernel, outs[0], (held_z, got_z), 8, size, 8 * size)
+def line(own):
+    return [swap(own, way) for way in Z_WAYS] + [own]
+
+
+def add(*terms):
+    out = jax.ShapeDtypeStruct(terms[0].shape, jnp.bfloat16)
+    size = terms[0].size
+    return call(sum_kernel, out, terms, 8, len(terms) * size, 4 * len(terms) * size)
+
+
+def send_back(parts):
+    leave, stay = parts[:4], parts[4:]
+    got = [swap(x, Y) for x in leave]
+    far = [swap(add(x, y), way) for x, y, way in zip(stay, got, Z_WAYS)]
+    return add(stay[3], got[3], *far)
 
 
 def local_pairs(
@@ -331,7 +301,6 @@
         + [pltpu.SemaphoreType.DMA((len(held),))],
         [hbm] * len(held),
     )
-    own, gate, up = lax.optimization_barrier((own, gate, up))
     both = call(
         pack_kernel,
         jax.ShapeDtypeStruct((gate.shape[0], 2 * ff), jnp.bfloat16),
@@ -342,15 +311,14 @@
         [pltpu.SemaphoreType.DMA((2,))],
         [hbm] * 2,
     )
+    both_by = swap(both, X)
     twins = (swap_core(both), swap_core(down))
-    far = [swap(x, Z_HIGH) for x in own]
-    both_by = swap(both, Z_LOW)
-    first_one = halves(own[0], far[0])
-    second_one = swap(first_one[0], X), swap(first_one[1], Y)
-    far[1], second_one = lax.optimization_barrier((far[1], second_one))
-    first_two = halves(own[1], far[1])
-    second_two = swap(first_two[0], X), swap(first_two[1], Y)
-    pieces = [spread(*first_one, *second_one), spread(*first_two, *second_two)]
+    line_one = line(own[0])
+    line_one[:2], twins, own_two = lax.optimization_barrier((line_one[:2], twins, own[1]))
+    line_two = line(own_two)
+    pieces_one = [swap(x, Y) for x in line_one] + line_one
+    pieces_one, line_two = lax.optimization_barrier((pieces_one, line_two))
+    pieces = [pieces_one, [swap(x, Y) for x in line_two] + line_two]
 
     rows = 8 * tok
     scratch = (pltpu.VMEM((rows, width + PACK), jnp.bfloat16),)
@@ -383,8 +351,8 @@
     def join(total, hid, weight):
         return call(
             join_kernel,
-            (jax.ShapeDtypeStruct((2 * tok, width), jnp.bfloat16),) * 2
-            + (jax.ShapeDtypeStruct((2 * tok, width), jnp.float32),) * 2,
+            (jax.ShapeDtypeStruct((tok, width), jnp.bfloat16),) * 4
+            + (jax.ShapeDtypeStruct((tok, width), jnp.float32),) * 4,
             (hid, weight, total, down_by, down_twin),
             14,
             2 * rows * width * ff,
@@ -392,10 +360,8 @@
         )
 
     total_one = own_total(pieces[0])
-    down_later, both_by, total_one, second_two = lax.optimization_barrier(
-        (down, both_by, total_one, second_two)
-    )
-    down_by = swap(down_later, Z_LOW)
+    down_later, both_by, total_one = lax.optimization_barrier((down, both_by, total_one))
+    down_by = swap(down_later, X)
     both_twin = swap_core(both_by)
     total_two = own_total(pieces[1])
     hidden_one, hidden_two = beside_hidden(pieces[0]), beside_hidden(pieces[1])
@@ -403,9 +369,7 @@
         (down_by, total_two, hidden_one, hidden_two)
     )
     down_twin = swap_core(down_by)
-    back_one = first_return(*join(total_one, *hidden_one))
-    back_two = first_return(*join(total_two, *hidden_two))
-    return last_returns(*back_one), last_returns(*back_two)
+    return send_back(join(total_one, *hidden_one)), send_back(join(total_two, *hidden_two))
 
 
 def solution(mesh):

time: 157 us -> 145 us (0.924)
  waiting for transfers between devices: 90.4 us -> 76.4 us
  starting transfers between devices: 40.7 us -> 49.2 us
  local copies, waits for them, and re-layouts: 8.92 us -> 2.3 us
    ppermute x26 -> x30, waiting for transfers between devices: 88.1 us -> 74.1 us  [swap(): lax.ppermute(block, 'expert', [(i, i ^ distance) for i in range(count)])]
    ppermute x26 -> x30, starting transfers between devices: 40.1 us -> 48.4 us  [swap(): lax.ppermute(block, 'expert', [(i, i ^ distance) for i in range(count)])]
    unnamed x24, local copies, waits for them, and re-layouts: 8.85 us -> 2.3 us
  transfers between devices with their start and end apart: 30 -> 34, of which waited for: 19 -> 18; matrix products, arithmetic and copies ran while one was open for 0% -> 0% of each run, Pallas kernels for 8% -> 10%
where the time goes in v9:
time: 145 us
  waiting for transfers between devices  76.4 us (53%)
  starting transfers between devices  49.2 us (34%)
  Pallas kernels  16 us (11%)
  local copies, waits for them, and re-layouts  2.3 us (2%)
    ppermute x30, waiting for transfers between devices, swap(): lax.ppermute(block, 'expert', [(i, i ^ distance) for i in range(count)])  74.1 us
    ppermute x30, starting transfers between devices, swap(): lax.ppermute(block, 'expert', [(i, i ^ distance) for i in range(count)])  48.4 us
    pallas_call x16, Pallas kernels, call(): pl.pallas_call(body, out_shape=outs, in_specs=specs or [smem if x.ndim ==...  16 us
  transfers between devices with their start and end apart: 34, of which 18 were waited for; matrix products, arithmetic and copies ran while one was open for 0% of the time, Pallas kernels for 10%

profile of v9, /device:TPU:0, one launch (start us, length us, event | category | flops | bytes accessed | tf_op | source)
XLA Modules:
  0.0 144.8 jit_solution(3632049625043371727)
XLA Ops:
  3.8 2.6 %collective-permute-start = (bf16[768,1024]{1,0:T(8,128)(2,1)S(1)}, bf16[768,1024]{1,0:T(8,128)(2,1)S(1)}, u32[]{:S(2)}, u32[]{:S(2)}) collective-permute-start(bf16[768,1024]{1,0:T(8,128)(2,1)S(1)} %shard_map.131.refs_8_), channel_id=1, source_target_pairs={{0,2},{2,0},{4,6},{6,4},{8,10},{10,8},{12,14},{14,12},{16,18},{18,... | collective-permute-start | bytes 4718600 | tf_op jit(solution)/shard_map/ppermute | solution.py:246
  8.0 1.6 %collective-permute-start.7 = (bf16[64,1664]{1,0:T(8,128)(2,1)S(1)}, bf16[64,1664]{1,0:T(8,128)(2,1)S(1)}, u32[]{:S(2)}, u32[]{:S(2)}) collective-permute-start(bf16[64,1664]{1,0:T(8,128)(2,1)S(1)} %get-tuple-element.62.refs_7_), channel_id=1, source_target_pairs={{0,8},{2,10},{4,12},{6,14},{8,0},{10,2},{12,4},{14,6},{16,24},{18,... | collective-permute-start | bytes 638984 | tf_op jit(solution)/shard_map/ppermute | solution.py:246
  9.6 2.6 %collective-permute-start.2 = (bf16[64,1664]{1,0:T(8,128)(2,1)S(1)}, bf16[64,1664]{1,0:T(8,128)(2,1)S(1)}, u32[]{:S(2)}, u32[]{:S(2)}) collective-permute-start(bf16[64,1664]{1,0:T(8,128)(2,1)S(1)} %get-tuple-element.62.refs_7_), channel_id=1, source_target_pairs={{0,16},{2,18},{4,20},{6,22},{8,24},{10,26},{12,28},{14,30},{16,0},... | collective-permute-start | bytes 638984 | tf_op jit(solution)/shard_map/ppermute | solution.py:246
  12.2 7.8 %collective-permute-done.7.refs_6_ = bf16[64,1664]{1,0:T(8,128)(2,1)S(1)} collective-permute-done((bf16[64,1664]{1,0:T(8,128)(2,1)S(1)}, bf16[64,1664]{1,0:T(8,128)(2,1)S(1)}, u32[]{:S(2)}, u32[]{:S(2)}) %collective-permute-start.7) | collective-permute-done | bytes 213024 | tf_op jit(solution)/shard_map/ppermute | solution.py:246
  20.0 2.5 %collective-permute-start.1 = (bf16[64,1664]{1,0:T(8,128)(2,1)S(1)}, bf16[64,1664]{1,0:T(8,128)(2,1)S(1)}, u32[]{:S(2)}, u32[]{:S(2)}) collective-permute-start(bf16[64,1664]{1,0:T(8,128)(2,1)S(1)} %get-tuple-element.62.refs_7_), channel_id=1, source_target_pairs={{0,24},{2,26},{4,28},{6,30},{8,16},{10,18},{12,20},{14,22},{16,8},... | collective-permute-start | bytes 638984 | tf_op jit(solution)/shard_map/ppermute | solution.py:246
  22.5 1.5 %collective-permute-start.9 = (bf16[64,1664]{1,0:T(8,128)(2,1)S(1)}, bf16[64,1664]{1,0:T(8,128)(2,1)S(1)}, u32[]{:S(2)}, u32[]{:S(2)}) collective-permute-start(bf16[64,1664]{1,0:T(8,128)(2,1)S(1)} %get-tuple-element.62.refs_7_), channel_id=1, source_target_pairs={{0,4},{2,6},{4,0},{6,2},{8,12},{10,14},{12,8},{14,10},{16,20},{18,... | collective-permute-start | bytes 638984 | tf_op jit(solution)/shard_map/ppermute | solution.py:246
  24.0 4.6 %collective-permute-done.1.refs_4_ = bf16[64,1664]{1,0:T(8,128)(2,1)S(1)} collective-permute-done((bf16[64,1664]{1,0:T(8,128)(2,1)S(1)}, bf16[64,1664]{1,0:T(8,128)(2,1)S(1)}, u32[]{:S(2)}, u32[]{:S(2)}) %collective-permute-start.1) | collective-permute-done | bytes 213024 | tf_op jit(solution)/shard_map/ppermute | solution.py:246
  28.6 1.5 %collective-permute-start.8 = (bf16[64,1664]{1,0:T(8,128)(2,1)S(1)}, bf16[64,1664]{1,0:T(8,128)(2,1)S(1)}, u32[]{:S(2)}, u32[]{:S(2)}) collective-permute-start(bf16[64,1664]{1,0:T(8,128)(2,1)S(1)} %collective-permute-done.7.refs_6_), channel_id=1, source_target_pairs={{0,4},{2,6},{4,0},{6,2},{8,12},{10,14},{12,8},{14,10},{16,20},{18,... | collective-permute-start | bytes 638984 | tf_op jit(solution)/shard_map/ppermute | solution.py:246
  30.6 1.5 %collective-permute-start.6 = (bf16[64,1664]{1,0:T(8,128)(2,1)S(1)}, bf16[64,1664]{1,0:T(8,128)(2,1)S(1)}, u32[]{:S(2)}, u32[]{:S(2)}) collective-permute-start(bf16[64,1664]{1,0:T(8,128)(2,1)S(1)} %collective-permute-done.2.refs_5_), channel_id=1, source_target_pairs={{0,4},{2,6},{4,0},{6,2},{8,12},{10,14},{12,8},{14,10},{16,20},{18,... | collective-permute-start | bytes 638984 | tf_op jit(solution)/shard_map/ppermute | solution.py:246
  32.1 3.4 %collective-permute-start.12 = (bf16[64,1664]{1,0:T(8,128)(2,1)S(1)}, bf16[64,1664]{1,0:T(8,128)(2,1)S(1)}, u32[]{:S(2)}, u32[]{:S(2)}) collective-permute-start(bf16[64,1664]{1,0:T(8,128)(2,1)S(1)} %get-tuple-element.69.refs_7_), channel_id=1, source_target_pairs={{0,8},{2,10},{4,12},{6,14},{8,0},{10,2},{12,4},{14,6},{16,24},{18,... | collective-permute-start | bytes 638984 | tf_op jit(solution)/shard_map/ppermute | solution.py:246
  36.8 4.5 %collective-permute-start.11 = (bf16[64,1664]{1,0:T(8,128)(2,1)S(1)}, bf16[64,1664]{1,0:T(8,128)(2,1)S(1)}, u32[]{:S(2)}, u32[]{:S(2)}) collective-permute-start(bf16[64,1664]{1,0:T(8,128)(2,1)S(1)} %get-tuple-element.69.refs_7_), channel_id=1, source_target_pairs={{0,16},{2,18},{4,20},{6,22},{8,24},{10,26},{12,28},{14,30},{16,0},... | collective-permute-start | bytes 638984 | tf_op jit(solution)/shard_map/ppermute | solution.py:246
  41.2 2.4 %collective-permute-start.10 = (bf16[64,1664]{1,0:T(8,128)(2,1)S(1)}, bf16[64,1664]{1,0:T(8,128)(2,1)S(1)}, u32[]{:S(2)}, u32[]{:S(2)}) collective-permute-start(bf16[64,1664]{1,0:T(8,128)(2,1)S(1)} %get-tuple-element.69.refs_7_), channel_id=1, source_target_pairs={{0,24},{2,26},{4,28},{6,30},{8,16},{10,18},{12,20},{14,22},{16,8},... | collective-permute-start | bytes 638984 | tf_op jit(solution)/shard_map/ppermute | solution.py:246
  43.7 11.8 %collective-permute-done.11.refs_5_ = bf16[64,1664]{1,0:T(8,128)(2,1)S(1)} collective-permute-done((bf16[64,1664]{1,0:T(8,128)(2,1)S(1)}, bf16[64,1664]{1,0:T(8,128)(2,1)S(1)}, u32[]{:S(2)}, u32[]{:S(2)}) %collective-permute-start.11) | collective-permute-done | bytes 213024 | tf_op jit(solution)/shard_map/ppermute | solution.py:246
  55.5 3.1 %shard_map.133.total_ref = f32[512,1536]{1,0:T(8,128)S(1)} custom-call(bf16[64,1664]{1,0:T(8,128)(2,1)S(1)} %collective-permute-done.5.refs_0_, bf16[64,1664]{1,0:T(8,128)(2,1)S(1)} %collective-permute-done.6.refs_1_, bf16[64,1664]{1,0:T(8,128)(2,1)S(1)} %collective-permute-done.8.refs_2_, bf16[64,1664]{1,0:T(8,128)(2,1)S(1)} %collective-permute-done.9.refs_3_, ...), custom_call_target="tpu_custom_call" | custom-call | flops 2415919104 | bytes 9437184 | tf_op jit(solution)/shard_map/pallas_call | solution.py:87
  62.2 4.6 %collective-permute-done.14.refs_0_ = bf16[64,1664]{1,0:T(8,128)(2,1)S(1)} collective-permute-done((bf16[64,1664]{1,0:T(8,128)(2,1)S(1)}, bf16[64,1664]{1,0:T(8,128)(2,1)S(1)}, u32[]{:S(2)}, u32[]{:S(2)}) %collective-permute-start.14) | collective-permute-done | bytes 213024 | tf_op jit(solution)/shard_map/ppermute | solution.py:246
  67.6 3.8 %collective-permute-done.15.refs_1_ = bf16[64,1664]{1,0:T(8,128)(2,1)S(1)} collective-permute-done((bf16[64,1664]{1,0:T(8,128)(2,1)S(1)}, bf16[64,1664]{1,0:T(8,128)(2,1)S(1)}, u32[]{:S(2)}, u32[]{:S(2)}) %collective-permute-start.15) | collective-permute-done | bytes 213024 | tf_op jit(solution)/shard_map/ppermute | solution.py:246
  71.4 4.6 %collective-permute-done.16.refs_2_ = bf16[64,1664]{1,0:T(8,128)(2,1)S(1)} collective-permute-done((bf16[64,1664]{1,0:T(8,128)(2,1)S(1)}, bf16[64,1664]{1,0:T(8,128)(2,1)S(1)}, u32[]{:S(2)}, u32[]{:S(2)}) %collective-permute-start.16) | collective-permute-done | bytes 213024 | tf_op jit(solution)/shard_map/ppermute | solution.py:246
  75.9 4.1 %collective-permute-done.17.refs_3_ = bf16[64,1664]{1,0:T(8,128)(2,1)S(1)} collective-permute-done((bf16[64,1664]{1,0:T(8,128)(2,1)S(1)}, bf16[64,1664]{1,0:T(8,128)(2,1)S(1)}, u32[]{:S(2)}, u32[]{:S(2)}) %collective-permute-start.17) | collective-permute-done | bytes 213024 | tf_op jit(solution)/shard_map/ppermute | solution.py:246
  80.1 3.1 %shard_map.134.total_ref = f32[512,1536]{1,0:T(8,128)S(1)} custom-call(bf16[64,1664]{1,0:T(8,128)(2,1)S(1)} %collective-permute-done.14.refs_0_, bf16[64,1664]{1,0:T(8,128)(2,1)S(1)} %collective-permute-done.15.refs_1_, bf16[64,1664]{1,0:T(8,128)(2,1)S(1)} %collective-permute-done.16.refs_2_, bf16[64,1664]{1,0:T(8,128)(2,1)S(1)} %collective-permute-done.17.refs_3_, ...), custom_call_target="tpu_custom_call" | custom-call | flops 2415919104 | bytes 9437184 | tf_op jit(solution)/shard_map/pallas_call | solution.py:87
  83.2 2.1 %shard_map.136 = (bf16[512,512]{1,0:T(8,128)(2,1)S(1)}, f32[512,128]{1,0:T(8,128)S(1)}) custom-call(bf16[64,1664]{1,0:T(8,128)(2,1)S(1)} %collective-permute-done.14.refs_0_, bf16[64,1664]{1,0:T(8,128)(2,1)S(1)} %collective-permute-done.15.refs_1_, bf16[64,1664]{1,0:T(8,128)(2,1)S(1)} %collective-permute-done.16.refs_2_, ...), custom_call_target="tpu_custom_call" | custom-call | flops 1610612736 | bytes 4718592 | tf_op jit(solution)/shard_map/pallas_call | solution.py:87
  85.3 2.1 %shard_map.135 = (bf16[512,512]{1,0:T(8,128)(2,1)S(1)}, f32[512,128]{1,0:T(8,128)S(1)}) custom-call(bf16[64,1664]{1,0:T(8,128)(2,1)S(1)} %collective-permute-done.5.refs_0_, bf16[64,1664]{1,0:T(8,128)(2,1)S(1)} %collective-permute-done.6.refs_1_, bf16[64,1664]{1,0:T(8,128)(2,1)S(1)} %collective-permute-done.8.refs_2_, ...), custom_call_target="tpu_custom_call" | custom-call | flops 1610612736 | bytes 4718592 | tf_op jit(solution)/shard_map/pallas_call | solution.py:87
  87.6 2.3 %collective-permute-done.19.down_b = bf16[512,768]{1,0:T(8,128)(2,1)S(1)} collective-permute-done((bf16[512,768]{1,0:T(8,128)(2,1)S(1)}, bf16[512,768]{1,0:T(8,128)(2,1)S(1)}, u32[]{:S(2)}, u32[]{:S(2)}) %collective-permute-start.19) | collective-permute-done | bytes 786464 | tf_op jit(solution)/shard_map/ppermute | solution.py:250
  96.8 1.8 %collective-permute-done.28.refs_1_ = bf16[64,1536]{1,0:T(8,128)(2,1)S(1)} collective-permute-done((bf16[64,1536]{1,0:T(8,128)(2,1)S(1)}, bf16[64,1536]{1,0:T(8,128)(2,1)S(1)}, u32[]{:S(2)}, u32[]{:S(2)}) %collective-permute-start.28) | collective-permute-done | bytes 196640 | tf_op jit(solution)/shard_map/ppermute | solution.py:246
  99.5 3.4 %collective-permute-done.30.refs_1_ = bf16[64,1536]{1,0:T(8,128)(2,1)S(1)} collective-permute-done((bf16[64,1536]{1,0:T(8,128)(2,1)S(1)}, bf16[64,1536]{1,0:T(8,128)(2,1)S(1)}, u32[]{:S(2)}, u32[]{:S(2)}) %collective-permute-start.30) | collective-permute-done | bytes 196640 | tf_op jit(solution)/shard_map/ppermute | solution.py:246
  103.7 3.4 %collective-permute-done.32.refs_1_ = bf16[64,1536]{1,0:T(8,128)(2,1)S(1)} collective-permute-done((bf16[64,1536]{1,0:T(8,128)(2,1)S(1)}, bf16[64,1536]{1,0:T(8,128)(2,1)S(1)}, u32[]{:S(2)}, u32[]{:S(2)}) %collective-permute-start.32) | collective-permute-done | bytes 196640 | tf_op jit(solution)/shard_map/ppermute | solution.py:246
  108.5 2.8 %collective-permute-done.21.refs_1_ = bf16[64,1536]{1,0:T(8,128)(2,1)S(1)} collective-permute-done((bf16[64,1536]{1,0:T(8,128)(2,1)S(1)}, bf16[64,1536]{1,0:T(8,128)(2,1)S(1)}, u32[]{:S(2)}, u32[]{:S(2)}) %collective-permute-start.21) | collective-permute-done | bytes 196640 | tf_op jit(solution)/shard_map/ppermute | solution.py:246
  111.3 3.3 %collective-permute-start.31 = (bf16[64,1536]{1,0:T(8,128)(2,1)S(1)}, bf16[64,1536]{1,0:T(8,128)(2,1)S(1)}, u32[]{:S(2)}, u32[]{:S(2)}) collective-permute-start(bf16[64,1536]{1,0:T(8,128)(2,1)S(1)} %shard_map.144), channel_id=1, source_target_pairs={{0,16},{2,18},{4,20},{6,22},{8,24},{10,26},{12,28},{14,30},{16,0},... | collective-permute-start | bytes 589832 | tf_op jit(solution)/shard_map/ppermute | solution.py:246
  116.4 3.4 %collective-permute-done.25.refs_1_ = bf16[64,1536]{1,0:T(8,128)(2,1)S(1)} collective-permute-done((bf16[64,1536]{1,0:T(8,128)(2,1)S(1)}, bf16[64,1536]{1,0:T(8,128)(2,1)S(1)}, u32[]{:S(2)}, u32[]{:S(2)}) %collective-permute-start.25) | collective-permute-done | bytes 196640 | tf_op jit(solution)/shard_map/ppermute | solution.py:246
  119.7 3.0 %collective-permute-start.33 = (bf16[64,1536]{1,0:T(8,128)(2,1)S(1)}, bf16[64,1536]{1,0:T(8,128)(2,1)S(1)}, u32[]{:S(2)}, u32[]{:S(2)}) collective-permute-start(bf16[64,1536]{1,0:T(8,128)(2,1)S(1)} %shard_map.145), channel_id=1, source_target_pairs={{0,8},{2,10},{4,12},{6,14},{8,0},{10,2},{12,4},{14,6},{16,24},{18,... | collective-permute-start | bytes 589832 | tf_op jit(solution)/shard_map/ppermute | solution.py:246
  125.3 3.0 %collective-permute-start.24 = (bf16[64,1536]{1,0:T(8,128)(2,1)S(1)}, bf16[64,1536]{1,0:T(8,128)(2,1)S(1)}, u32[]{:S(2)}, u32[]{:S(2)}) collective-permute-start(bf16[64,1536]{1,0:T(8,128)(2,1)S(1)} %shard_map.139), channel_id=1, source_target_pairs={{0,16},{2,18},{4,20},{6,22},{8,24},{10,26},{12,28},{14,30},{16,0},... | collective-permute-start | bytes 589832 | tf_op jit(solution)/shard_map/ppermute | solution.py:246
  128.4 7.0 %collective-permute-done.33.refs_4_ = bf16[64,1536]{1,0:T(8,128)(2,1)S(1)} collective-permute-done((bf16[64,1536]{1,0:T(8,128)(2,1)S(1)}, bf16[64,1536]{1,0:T(8,128)(2,1)S(1)}, u32[]{:S(2)}, u32[]{:S(2)}) %collective-permute-start.33) | collective-permute-done | bytes 196640 | tf_op jit(solution)/shard_map/ppermute | solution.py:246
  136.2 7.8 %collective-permute-done.24.refs_3_ = bf16[64,1536]{1,0:T(8,128)(2,1)S(1)} collective-permute-done((bf16[64,1536]{1,0:T(8,128)(2,1)S(1)}, bf16[64,1536]{1,0:T(8,128)(2,1)S(1)}, u32[]{:S(2)}, u32[]{:S(2)}) %collective-permute-start.24) | collective-permute-done | bytes 196640 | tf_op jit(solution)/shard_map/ppermute | solution.py:246
  (76 shorter events, 26.8 us)
Async XLA Ops:
  3.2 26.9 %collective-permute-start.3 = (bf16[768,1024]{1,0:T(8,128)(2,1)S(1)}, bf16[768,1024]{1,0:T(8,128)(2,1)S(1)}, u32[]{:S(2)}, u32[]{:S(2)}) collective-permute-start(bf16[768,1024]{1,0:T(8,128)(2,1)S(1)} %shard_map.131.refs_8_), channel_id=1, source_target_pairs={{0,1},{1,0},{2,3},{3,2},{4,5},{5,4},{6,7},{7,6},{8,9},{9,8},{10,11... | collective-permute-start | bytes 4718600 | tf_op jit(solution)/shard_map/ppermute | solution.py:250
  3.8 54.8 %collective-permute-start = (bf16[768,1024]{1,0:T(8,128)(2,1)S(1)}, bf16[768,1024]{1,0:T(8,128)(2,1)S(1)}, u32[]{:S(2)}, u32[]{:S(2)}) collective-permute-start(bf16[768,1024]{1,0:T(8,128)(2,1)S(1)} %shard_map.131.refs_8_), channel_id=1, source_target_pairs={{0,2},{2,0},{4,6},{6,4},{8,10},{10,8},{12,14},{14,12},{16,18},{18,... | collective-permute-start | bytes 4718600 | tf_op jit(solution)/shard_map/ppermute | solution.py:246
  6.3 23.8 %collective-permute-start.4 = (bf16[512,768]{1,0:T(8,128)(2,1)S(1)}, bf16[512,768]{1,0:T(8,128)(2,1)S(1)}, u32[]{:S(2)}, u32[]{:S(2)}) collective-permute-start(bf16[512,768]{1,0:T(8,128)(2,1)S(1)} %bitcast.7), channel_id=1, source_target_pairs={{0,1},{1,0},{2,3},{3,2},{4,5},{5,4},{6,7},{7,6},{8,9},{9,8},{10,11... | collective-permute-start | bytes 2359304 | tf_op jit(solution)/shard_map/ppermute | solution.py:250
  8.0 12.0 %collective-permute-start.7 = (bf16[64,1664]{1,0:T(8,128)(2,1)S(1)}, bf16[64,1664]{1,0:T(8,128)(2,1)S(1)}, u32[]{:S(2)}, u32[]{:S(2)}) collective-permute-start(bf16[64,1664]{1,0:T(8,128)(2,1)S(1)} %get-tuple-element.62.refs_7_), channel_id=1, source_target_pairs={{0,8},{2,10},{4,12},{6,14},{8,0},{10,2},{12,4},{14,6},{16,24},{18,... | collective-permute-start | bytes 638984 | tf_op jit(solution)/shard_map/ppermute | solution.py:246
  9.6 12.9 %collective-permute-start.2 = (bf16[64,1664]{1,0:T(8,128)(2,1)S(1)}, bf16[64,1664]{1,0:T(8,128)(2,1)S(1)}, u32[]{:S(2)}, u32[]{:S(2)}) collective-permute-start(bf16[64,1664]{1,0:T(8,128)(2,1)S(1)} %get-tuple-element.62.refs_7_), channel_id=1, source_target_pairs={{0,16},{2,18},{4,20},{6,22},{8,24},{10,26},{12,28},{14,30},{16,0},... | collective-permute-start | bytes 638984 | tf_op jit(solution)/shard_map/ppermute | solution.py:246
  20.0 8.6 %collective-permute-start.1 = (bf16[64,1664]{1,0:T(8,128)(2,1)S(1)}, bf16[64,1664]{1,0:T(8,128)(2,1)S(1)}, u32[]{:S(2)}, u32[]{:S(2)}) collective-permute-start(bf16[64,1664]{1,0:T(8,128)(2,1)S(1)} %get-tuple-element.62.refs_7_), channel_id=1, source_target_pairs={{0,24},{2,26},{4,28},{6,30},{8,16},{10,18},{12,20},{14,22},{16,8},... | collective-permute-start | bytes 638984 | tf_op jit(solution)/shard_map/ppermute | solution.py:246
  22.5 9.7 %collective-permute-start.9 = (bf16[64,1664]{1,0:T(8,128)(2,1)S(1)}, bf16[64,1664]{1,0:T(8,128)(2,1)S(1)}, u32[]{:S(2)}, u32[]{:S(2)}) collective-permute-start(bf16[64,1664]{1,0:T(8,128)(2,1)S(1)} %get-tuple-element.62.refs_7_), channel_id=1, source_target_pairs={{0,4},{2,6},{4,0},{6,2},{8,12},{10,14},{12,8},{14,10},{16,20},{18,... | collective-permute-start | bytes 638984 | tf_op jit(solution)/shard_map/ppermute | solution.py:246
  28.6 8.2 %collective-permute-start.8 = (bf16[64,1664]{1,0:T(8,128)(2,1)S(1)}, bf16[64,1664]{1,0:T(8,128)(2,1)S(1)}, u32[]{:S(2)}, u32[]{:S(2)}) collective-permute-start(bf16[64,1664]{1,0:T(8,128)(2,1)S(1)} %collective-permute-done.7.refs_6_), channel_id=1, source_target_pairs={{0,4},{2,6},{4,0},{6,2},{8,12},{10,14},{12,8},{14,10},{16,20},{18,... | collective-permute-start | bytes 638984 | tf_op jit(solution)/shard_map/ppermute | solution.py:246
  30.1 11.1 %collective-permute-start.5 = (bf16[64,1664]{1,0:T(8,128)(2,1)S(1)}, bf16[64,1664]{1,0:T(8,128)(2,1)S(1)}, u32[]{:S(2)}, u32[]{:S(2)}) collective-permute-start(bf16[64,1664]{1,0:T(8,128)(2,1)S(1)} %collective-permute-done.1.refs_4_), channel_id=1, source_target_pairs={{0,4},{2,6},{4,0},{6,2},{8,12},{10,14},{12,8},{14,10},{16,20},{18,... | collective-permute-start | bytes 638984 | tf_op jit(solution)/shard_map/ppermute | solution.py:246
  30.6 13.1 %collective-permute-start.6 = (bf16[64,1664]{1,0:T(8,128)(2,1)S(1)}, bf16[64,1664]{1,0:T(8,128)(2,1)S(1)}, u32[]{:S(2)}, u32[]{:S(2)}) collective-permute-start(bf16[64,1664]{1,0:T(8,128)(2,1)S(1)} %collective-permute-done.2.refs_5_), channel_id=1, source_target_pairs={{0,4},{2,6},{4,0},{6,2},{8,12},{10,14},{12,8},{14,10},{16,20},{18,... | collective-permute-start | bytes 638984 | tf_op jit(solution)/shard_map/ppermute | solution.py:246
  32.1 11.5 %collective-permute-start.12 = (bf16[64,1664]{1,0:T(8,128)(2,1)S(1)}, bf16[64,1664]{1,0:T(8,128)(2,1)S(1)}, u32[]{:S(2)}, u32[]{:S(2)}) collective-permute-start(bf16[64,1664]{1,0:T(8,128)(2,1)S(1)} %get-tuple-element.69.refs_7_), channel_id=1, source_target_pairs={{0,8},{2,10},{4,12},{6,14},{8,0},{10,2},{12,4},{14,6},{16,24},{18,... | collective-permute-start | bytes 638984 | tf_op jit(solution)/shard_map/ppermute | solution.py:246
  36.8 18.7 %collective-permute-start.11 = (bf16[64,1664]{1,0:T(8,128)(2,1)S(1)}, bf16[64,1664]{1,0:T(8,128)(2,1)S(1)}, u32[]{:S(2)}, u32[]{:S(2)}) collective-permute-start(bf16[64,1664]{1,0:T(8,128)(2,1)S(1)} %get-tuple-element.69.refs_7_), channel_id=1, source_target_pairs={{0,16},{2,18},{4,20},{6,22},{8,24},{10,26},{12,28},{14,30},{16,0},... | collective-permute-start | bytes 638984 | tf_op jit(solution)/shard_map/ppermute | solution.py:246
  41.2 14.2 %collective-permute-start.10 = (bf16[64,1664]{1,0:T(8,128)(2,1)S(1)}, bf16[64,1664]{1,0:T(8,128)(2,1)S(1)}, u32[]{:S(2)}, u32[]{:S(2)}) collective-permute-start(bf16[64,1664]{1,0:T(8,128)(2,1)S(1)} %get-tuple-element.69.refs_7_), channel_id=1, source_target_pairs={{0,24},{2,26},{4,28},{6,30},{8,16},{10,18},{12,20},{14,22},{16,8},... | collective-permute-start | bytes 638984 | tf_op jit(solution)/shard_map/ppermute | solution.py:246
  58.6 24.6 %collective-permute-start.18 = (bf16[768,1024]{1,0:T(8,128)(2,1)S(1)}, bf16[768,1024]{1,0:T(8,128)(2,1)S(1)}, u32[]{:S(2)}, u32[]{:S(2)}) collective-permute-start(bf16[768,1024]{1,0:T(8,128)(2,1)S(1)} %collective-permute-done.refs_8_), channel_id=1, source_target_pairs={{0,1},{1,0},{2,3},{3,2},{4,5},{5,4},{6,7},{7,6},{8,9},{9,8},{10,11... | collective-permute-start | bytes 4718600 | tf_op jit(solution)/shard_map/ppermute | solution.py:250
  58.7 8.1 %collective-permute-start.14 = (bf16[64,1664]{1,0:T(8,128)(2,1)S(1)}, bf16[64,1664]{1,0:T(8,128)(2,1)S(1)}, u32[]{:S(2)}, u32[]{:S(2)}) collective-permute-start(bf16[64,1664]{1,0:T(8,128)(2,1)S(1)} %collective-permute-done.10.refs_4_), channel_id=1, source_target_pairs={{0,4},{2,6},{4,0},{6,2},{8,12},{10,14},{12,8},{14,10},{16,20},{18,... | collective-permute-start | bytes 638984 | tf_op jit(solution)/shard_map/ppermute | solution.py:246
  59.5 28.0 %collective-permute-start.13 = (bf16[512,768]{1,0:T(8,128)(2,1)S(1)}, bf16[512,768]{1,0:T(8,128)(2,1)S(1)}, u32[]{:S(2)}, u32[]{:S(2)}) collective-permute-start(bf16[512,768]{1,0:T(8,128)(2,1)S(1)} %bitcast.9), channel_id=1, source_target_pairs={{0,2},{2,0},{4,6},{6,4},{8,10},{10,8},{12,14},{14,12},{16,18},{18,... | collective-permute-start | bytes 2359304 | tf_op jit(solution)/shard_map/ppermute | solution.py:246
  60.2 11.2 %collective-permute-start.15 = (bf16[64,1664]{1,0:T(8,128)(2,1)S(1)}, bf16[64,1664]{1,0:T(8,128)(2,1)S(1)}, u32[]{:S(2)}, u32[]{:S(2)}) collective-permute-start(bf16[64,1664]{1,0:T(8,128)(2,1)S(1)} %collective-permute-done.11.refs_5_), channel_id=1, source_target_pairs={{0,4},{2,6},{4,0},{6,2},{8,12},{10,14},{12,8},{14,10},{16,20},{18,... | collective-permute-start | bytes 638984 | tf_op jit(solution)/shard_map/ppermute | solution.py:246
  61.4 14.5 %collective-permute-start.16 = (bf16[64,1664]{1,0:T(8,128)(2,1)S(1)}, bf16[64,1664]{1,0:T(8,128)(2,1)S(1)}, u32[]{:S(2)}, u32[]{:S(2)}) collective-permute-start(bf16[64,1664]{1,0:T(8,128)(2,1)S(1)} %collective-permute-done.12.refs_6_), channel_id=1, source_target_pairs={{0,4},{2,6},{4,0},{6,2},{8,12},{10,14},{12,8},{14,10},{16,20},{18,... | collective-permute-start | bytes 638984 | tf_op jit(solution)/shard_map/ppermute | solution.py:246
  66.8 13.2 %collective-permute-start.17 = (bf16[64,1664]{1,0:T(8,128)(2,1)S(1)}, bf16[64,1664]{1,0:T(8,128)(2,1)S(1)}, u32[]{:S(2)}, u32[]{:S(2)}) collective-permute-start(bf16[64,1664]{1,0:T(8,128)(2,1)S(1)} %get-tuple-element.69.refs_7_), channel_id=1, source_target_pairs={{0,4},{2,6},{4,0},{6,2},{8,12},{10,14},{12,8},{14,10},{16,20},{18,... | collective-permute-start | bytes 638984 | tf_op jit(solution)/shard_map/ppermute | solution.py:246
  91.7 11.2 %collective-permute-start.30 = (bf16[64,1536]{1,0:T(8,128)(2,1)S(1)}, bf16[64,1536]{1,0:T(8,128)(2,1)S(1)}, u32[]{:S(2)}, u32[]{:S(2)}) collective-permute-start(bf16[64,1536]{1,0:T(8,128)(2,1)S(1)} %get-tuple-element.95), channel_id=1, source_target_pairs={{0,4},{2,6},{4,0},{6,2},{8,12},{10,14},{12,8},{14,10},{16,20},{18,... | collective-permute-start | bytes 589832 | tf_op jit(solution)/shard_map/ppermute | solution.py:246
  93.0 14.1 %collective-permute-start.32 = (bf16[64,1536]{1,0:T(8,128)(2,1)S(1)}, bf16[64,1536]{1,0:T(8,128)(2,1)S(1)}, u32[]{:S(2)}, u32[]{:S(2)}) collective-permute-start(bf16[64,1536]{1,0:T(8,128)(2,1)S(1)} %get-tuple-element.97), channel_id=1, source_target_pairs={{0,4},{2,6},{4,0},{6,2},{8,12},{10,14},{12,8},{14,10},{16,20},{18,... | collective-permute-start | bytes 589832 | tf_op jit(solution)/shard_map/ppermute | solution.py:246
  94.7 16.6 %collective-permute-start.21 = (bf16[64,1536]{1,0:T(8,128)(2,1)S(1)}, bf16[64,1536]{1,0:T(8,128)(2,1)S(1)}, u32[]{:S(2)}, u32[]{:S(2)}) collective-permute-start(bf16[64,1536]{1,0:T(8,128)(2,1)S(1)} %get-tuple-element.82), channel_id=1, source_target_pairs={{0,4},{2,6},{4,0},{6,2},{8,12},{10,14},{12,8},{14,10},{16,20},{18,... | collective-permute-start | bytes 589832 | tf_op jit(solution)/shard_map/ppermute | solution.py:246
  96.1 19.5 %collective-permute-start.23 = (bf16[64,1536]{1,0:T(8,128)(2,1)S(1)}, bf16[64,1536]{1,0:T(8,128)(2,1)S(1)}, u32[]{:S(2)}, u32[]{:S(2)}) collective-permute-start(bf16[64,1536]{1,0:T(8,128)(2,1)S(1)} %get-tuple-element.84), channel_id=1, source_target_pairs={{0,4},{2,6},{4,0},{6,2},{8,12},{10,14},{12,8},{14,10},{16,20},{18,... | collective-permute-start | bytes 589832 | tf_op jit(solution)/shard_map/ppermute | solution.py:246
  98.7 21.1 %collective-permute-start.25 = (bf16[64,1536]{1,0:T(8,128)(2,1)S(1)}, bf16[64,1536]{1,0:T(8,128)(2,1)S(1)}, u32[]{:S(2)}, u32[]{:S(2)}) collective-permute-start(bf16[64,1536]{1,0:T(8,128)(2,1)S(1)} %get-tuple-element.86), channel_id=1, source_target_pairs={{0,4},{2,6},{4,0},{6,2},{8,12},{10,14},{12,8},{14,10},{16,20},{18,... | collective-permute-start | bytes 589832 | tf_op jit(solution)/shard_map/ppermute | solution.py:246
  102.9 21.1 %collective-permute-start.27 = (bf16[64,1536]{1,0:T(8,128)(2,1)S(1)}, bf16[64,1536]{1,0:T(8,128)(2,1)S(1)}, u32[]{:S(2)}, u32[]{:S(2)}) collective-permute-start(bf16[64,1536]{1,0:T(8,128)(2,1)S(1)} %get-tuple-element.91), channel_id=1, source_target_pairs={{0,4},{2,6},{4,0},{6,2},{8,12},{10,14},{12,8},{14,10},{16,20},{18,... | collective-permute-start | bytes 589832 | tf_op jit(solution)/shard_map/ppermute | solution.py:246
  107.1 18.3 %collective-permute-start.29 = (bf16[64,1536]{1,0:T(8,128)(2,1)S(1)}, bf16[64,1536]{1,0:T(8,128)(2,1)S(1)}, u32[]{:S(2)}, u32[]{:S(2)}) collective-permute-start(bf16[64,1536]{1,0:T(8,128)(2,1)S(1)} %shard_map.143), channel_id=1, source_target_pairs={{0,24},{2,26},{4,28},{6,30},{8,16},{10,18},{12,20},{14,22},{16,8},... | collective-permute-start | bytes 589832 | tf_op jit(solution)/shard_map/ppermute | solution.py:246
  111.3 17.1 %collective-permute-start.31 = (bf16[64,1536]{1,0:T(8,128)(2,1)S(1)}, bf16[64,1536]{1,0:T(8,128)(2,1)S(1)}, u32[]{:S(2)}, u32[]{:S(2)}) collective-permute-start(bf16[64,1536]{1,0:T(8,128)(2,1)S(1)} %shard_map.144), channel_id=1, source_target_pairs={{0,16},{2,18},{4,20},{6,22},{8,24},{10,26},{12,28},{14,30},{16,0},... | collective-permute-start | bytes 589832 | tf_op jit(solution)/shard_map/ppermute | solution.py:246
  115.5 20.7 %collective-permute-start.20 = (bf16[64,1536]{1,0:T(8,128)(2,1)S(1)}, bf16[64,1536]{1,0:T(8,128)(2,1)S(1)}, u32[]{:S(2)}, u32[]{:S(2)}) collective-permute-start(bf16[64,1536]{1,0:T(8,128)(2,1)S(1)} %get-tuple-element.80), channel_id=1, source_target_pairs={{0,4},{2,6},{4,0},{6,2},{8,12},{10,14},{12,8},{14,10},{16,20},{18,... | collective-permute-start | bytes 589832 | tf_op jit(solution)/shard_map/ppermute | solution.py:246
  119.7 15.7 %collective-permute-start.33 = (bf16[64,1536]{1,0:T(8,128)(2,1)S(1)}, bf16[64,1536]{1,0:T(8,128)(2,1)S(1)}, u32[]{:S(2)}, u32[]{:S(2)}) collective-permute-start(bf16[64,1536]{1,0:T(8,128)(2,1)S(1)} %shard_map.145), channel_id=1, source_target_pairs={{0,8},{2,10},{4,12},{6,14},{8,0},{10,2},{12,4},{14,6},{16,24},{18,... | collective-permute-start | bytes 589832 | tf_op jit(solution)/shard_map/ppermute | solution.py:246
  123.9 12.3 %collective-permute-start.22 = (bf16[64,1536]{1,0:T(8,128)(2,1)S(1)}, bf16[64,1536]{1,0:T(8,128)(2,1)S(1)}, u32[]{:S(2)}, u32[]{:S(2)}) collective-permute-start(bf16[64,1536]{1,0:T(8,128)(2,1)S(1)} %shard_map.138), channel_id=1, source_target_pairs={{0,24},{2,26},{4,28},{6,30},{8,16},{10,18},{12,20},{14,22},{16,8},... | collective-permute-start | bytes 589832 | tf_op jit(solution)/shard_map/ppermute | solution.py:246
  125.3 18.7 %collective-permute-start.24 = (bf16[64,1536]{1,0:T(8,128)(2,1)S(1)}, bf16[64,1536]{1,0:T(8,128)(2,1)S(1)}, u32[]{:S(2)}, u32[]{:S(2)}) collective-permute-start(bf16[64,1536]{1,0:T(8,128)(2,1)S(1)} %shard_map.139), channel_id=1, source_target_pairs={{0,16},{2,18},{4,20},{6,22},{8,24},{10,26},{12,28},{14,30},{16,0},... | collective-permute-start | bytes 589832 | tf_op jit(solution)/shard_map/ppermute | solution.py:246
  128.4 15.6 %collective-permute-start.26 = (bf16[64,1536]{1,0:T(8,128)(2,1)S(1)}, bf16[64,1536]{1,0:T(8,128)(2,1)S(1)}, u32[]{:S(2)}, u32[]{:S(2)}) collective-permute-start(bf16[64,1536]{1,0:T(8,128)(2,1)S(1)} %shard_map.140), channel_id=1, source_target_pairs={{0,8},{2,10},{4,12},{6,14},{8,0},{10,2},{12,4},{14,6},{16,24},{18,... | collective-permute-start | bytes 589832 | tf_op jit(solution)/shard_map/ppermute | solution.py:246
  (14 other events, 48.2 us)

commit v10 on v5

--- a/solution.py
+++ b/solution.py
@@ -144,11 +144,13 @@
         out_ref[:, width:] = turned.astype(jnp.bfloat16)
 
 
-def pack_kernel(gate_ref, up_ref, both_ref, sems):
-    ff = gate_ref.shape[1]
+def pack_kernel(gate_ref, up_ref, down_ref, both_ref, first_ref, last_ref, sems):
+    ff, half = gate_ref.shape[1], first_ref.shape[0]
     copies = [
-        pltpu.make_async_copy(gate_ref, both_ref.at[:, :ff], sems.at[0]),
-        pltpu.make_async_copy(up_ref, both_ref.at[:, ff:], sems.at[1]),
+        pltpu.make_async_copy(down_ref.at[:half, :], first_ref, sems.at[0]),
+        pltpu.make_async_copy(down_ref.at[half:, :], last_ref, sems.at[1]),
+        pltpu.make_async_copy(gate_ref, both_ref.at[:, :ff], sems.at[2]),
+        pltpu.make_async_copy(up_ref, both_ref.at[:, ff:], sems.at[3]),
     ]
     for copy in copies:
         copy.start()
@@ -217,16 +219,21 @@
         weight_ref[pl.ds(begin, block), :] = jnp.broadcast_to(weight, (block, PACK))
 
 
-def join_kernel(hidden_ref, weight_ref, total_ref, down_a, down_b, send_a, send_b, keep_a, keep_b):
+def join_kernel(
+    hidden_ref, weight_ref, total_ref, first_a, last_a, first_b, last_b, send_a, send_b, keep_a, keep_b
+):
     place = lax.axis_index("tensor")
     count = send_a.shape[0]
+    inner, width = first_a.shape
     for pair, outs in ((0, (send_a, send_b)), (1, (keep_a, keep_b))):
         rows = slice(pair * 2 * count, (pair + 1) * 2 * count)
         weight = weight_ref[rows, :1]
-        for which, ref in enumerate((down_a, down_b)):
+        for which, (first, last) in enumerate(((first_a, last_a), (first_b, last_b))):
             half = place if which == 0 else 1 - place
-            columns = pl.ds(pl.multiple_of(half * ref.shape[1], ref.shape[1]), ref.shape[1])
-            part = jnp.dot(hidden_ref[rows, :], ref[...], preferred_element_type=jnp.float32)
+            columns = pl.ds(pl.multiple_of(half * width, width), width)
+            part = jnp.dot(
+                hidden_ref[rows, :inner], first[...], preferred_element_type=jnp.float32
+            ) + jnp.dot(hidden_ref[rows, inner:], last[...], preferred_element_type=jnp.float32)
             part = part * weight + total_ref[rows, columns]
             outs[0][:, columns] = part[:count].astype(outs[0].dtype)
             outs[1][:, columns] = part[count:].astype(outs[1].dtype)
@@ -331,19 +338,23 @@
         + [pltpu.SemaphoreType.DMA((len(held),))],
         [hbm] * len(held),
     )
-    both = call(
+    half_down = jax.ShapeDtypeStruct((ff // 2, down.shape[1]), jnp.bfloat16)
+    both, down_first, down_last = call(
         pack_kernel,
-        jax.ShapeDtypeStruct((gate.shape[0], 2 * ff), jnp.bfloat16),
-        (gate, up),
-        8,
+        (jax.ShapeDtypeStruct((gate.shape[0], 2 * ff), jnp.bfloat16), half_down, half_down),
+        (gate, up, down),
+        12,
         0,
-        8 * gate.size,
-        [pltpu.SemaphoreType.DMA((2,))],
-        [hbm] * 2,
-    )
+        12 * gate.size,
+        [pltpu.SemaphoreType.DMA((4,))],
+        [hbm] * 3,
+    )
+    by_first = swap(down_first, Z_LOW)
     twins = (swap_core(both), swap_core(down))
     far = [swap(x, Z_HIGH) for x in own]
-    far[0], twins, both_later = lax.optimization_barrier((far[0], twins, both))
+    far[0], twins, both_later, by_first = lax.optimization_barrier(
+        (far[0], twins, both, by_first)
+    )
     both_by = swap(both_later, Z_LOW)
     first_one = halves(own[0], far[0])
     second_one = swap(first_one[0], X), swap(first_one[1], Y)
@@ -385,24 +396,25 @@
             join_kernel,
             (jax.ShapeDtypeStruct((2 * tok, width), jnp.bfloat16),) * 2
             + (jax.ShapeDtypeStruct((2 * tok, width), jnp.float32),) * 2,
-            (hid, weight, total, down_by, down_twin),
+            (hid, weight, total, *down_by),
             14,
             2 * rows * width * ff,
             2 * width * ff + 8 * rows * width,
         )
 
     total_one = own_total(pieces[0])
-    down_later, both_by, total_one, pieces = lax.optimization_barrier(
-        (down, both_by, total_one, pieces)
-    )
-    down_by = swap(down_later, Z_LOW)
+    down_last, both_by, total_one, pieces = lax.optimization_barrier(
+        (down_last, both_by, total_one, pieces)
+    )
+    by_last = swap(down_last, Z_LOW)
+    twin_first = swap_core(by_first)
     both_twin = swap_core(both_by)
     total_two = own_total(pieces[1])
     hidden_one, hidden_two = beside_hidden(pieces[0]), beside_hidden(pieces[1])
-    down_by, total_two, hidden_one, hidden_two = lax.optimization_barrier(
-        (down_by, total_two, hidden_one, hidden_two)
-    )
-    down_twin = swap_core(down_by)
+    by_last, twin_first, total_two, hidden_one, hidden_two = lax.optimization_barrier(
+        (by_last, twin_first, total_two, hidden_one, hidden_two)
+    )
+    down_by = (by_first, by_last, twin_first, swap_core(by_last))
     back_one = first_return(*join(total_one, *hidden_one))
     back_two = first_return(*join(total_two, *hidden_two))
     return last_returns(*back_one), last_returns(*back_two)

time: 132 us -> 124 us (0.939)
  waiting for transfers between devices: 76 us -> 64.2 us
  starting transfers between devices: 35.9 us -> 38.7 us
    ppermute x26 -> x27, waiting for transfers between devices: 73.7 us -> 62.5 us  [swap(): lax.ppermute(block, 'expert', [(i, i ^ distance) for i in range(count)])]
    ppermute x26 -> x27, starting transfers between devices: 35 us -> 37.6 us  [swap(): lax.ppermute(block, 'expert', [(i, i ^ distance) for i in range(count)])]
    unnamed x24 -> x26, local copies, waits for them, and re-layouts: 2.57 us -> 3.45 us
  transfers between devices with their start and end apart: 30 -> 32, of which waited for: 18 -> 19; matrix products, arithmetic and copies ran while one was open for 0% -> 0% of each run, Pallas kernels for 11% -> 11%
where the time goes in v10:
time: 124 us
  waiting for transfers between devices  64.2 us (52%)
  starting transfers between devices  38.7 us (31%)
  Pallas kernels  16.4 us (13%)
  local copies, waits for them, and re-layouts  3.51 us (3%)
    ppermute x27, waiting for transfers between devices, swap(): lax.ppermute(block, 'expert', [(i, i ^ distance) for i in range(count)])  62.5 us
    ppermute x27, starting transfers between devices, swap(): lax.ppermute(block, 'expert', [(i, i ^ distance) for i in range(count)])  37.6 us
    pallas_call x16, Pallas kernels, call(): pl.pallas_call(body, out_shape=outs, in_specs=specs or [smem if x.ndim ==...  16.4 us
    unnamed x26, local copies, waits for them, and re-layouts  3.45 us
  transfers between devices with their start and end apart: 32, of which 19 were waited for; matrix products, arithmetic and copies ran while one was open for 0% of the time, Pallas kernels for 11%

profile of v10, /device:TPU:0, one launch (start us, length us, event | category | flops | bytes accessed | tf_op | source)
XLA Modules:
  0.0 123.9 jit_solution(17171976799062745406)
XLA Ops:
  5.4 3.0 %collective-permute-start.3 = (bf16[256,768]{1,0:T(8,128)(2,1)S(1)}, bf16[256,768]{1,0:T(8,128)(2,1)S(1)}, u32[]{:S(2)}, u32[]{:S(2)}) collective-permute-start(bf16[256,768]{1,0:T(8,128)(2,1)S(1)} %get-tuple-element.68), channel_id=1, source_target_pairs={{0,8},{2,10},{4,12},{6,14},{8,0},{10,2},{12,4},{14,6},{16,24},{18,... | collective-permute-start | bytes 1179656 | tf_op jit(solution)/shard_map/ppermute | solution.py:262
  9.8 2.7 %collective-permute-start = (bf16[64,1664]{1,0:T(8,128)(2,1)S(1)}, bf16[64,1664]{1,0:T(8,128)(2,1)S(1)}, u32[]{:S(2)}, u32[]{:S(2)}) collective-permute-start(bf16[64,1664]{1,0:T(8,128)(2,1)S(1)} %get-tuple-element.66), channel_id=1, source_target_pairs={{0,16},{2,18},{4,20},{6,22},{8,24},{10,26},{12,28},{14,30},{16,0},... | collective-permute-start | bytes 638984 | tf_op jit(solution)/shard_map/ppermute | solution.py:262
  12.9 9.6 %collective-permute-done = bf16[64,1664]{1,0:T(8,128)(2,1)S(1)} collective-permute-done((bf16[64,1664]{1,0:T(8,128)(2,1)S(1)}, bf16[64,1664]{1,0:T(8,128)(2,1)S(1)}, u32[]{:S(2)}, u32[]{:S(2)}) %collective-permute-start) | collective-permute-done | bytes 213024 | tf_op jit(solution)/shard_map/ppermute | solution.py:262
  22.5 2.0 %collective-permute-done.3.first_a = bf16[256,768]{1,0:T(8,128)(2,1)S(1)} collective-permute-done((bf16[256,768]{1,0:T(8,128)(2,1)S(1)}, bf16[256,768]{1,0:T(8,128)(2,1)S(1)}, u32[]{:S(2)}, u32[]{:S(2)}) %collective-permute-start.3) | collective-permute-done | bytes 393248 | tf_op jit(solution)/shard_map/ppermute | solution.py:262
  24.6 1.7 %collective-permute-start.7 = (bf16[64,1664]{1,0:T(8,128)(2,1)S(1)}, bf16[64,1664]{1,0:T(8,128)(2,1)S(1)}, u32[]{:S(2)}, u32[]{:S(2)}) collective-permute-start(bf16[64,1664]{1,0:T(8,128)(2,1)S(1)} %pad_maximum_fusion.refs_4_), channel_id=1, source_target_pairs={{0,2},{2,0},{4,6},{6,4},{8,10},{10,8},{12,14},{14,12},{16,18},{18,... | collective-permute-start | bytes 638984 | tf_op jit(solution)/shard_map/ppermute | solution.py:262
  26.3 1.6 %collective-permute-start.8 = (bf16[64,1664]{1,0:T(8,128)(2,1)S(1)}, bf16[64,1664]{1,0:T(8,128)(2,1)S(1)}, u32[]{:S(2)}, u32[]{:S(2)}) collective-permute-start(bf16[64,1664]{1,0:T(8,128)(2,1)S(1)} %pad_maximum_fusion.1.refs_6_), channel_id=1, source_target_pairs={{0,4},{2,6},{4,0},{6,2},{8,12},{10,14},{12,8},{14,10},{16,20},{18,... | collective-permute-start | bytes 638984 | tf_op jit(solution)/shard_map/ppermute | solution.py:262
  29.8 1.8 %collective-permute-done.6 = bf16[64,1664]{1,0:T(8,128)(2,1)S(1)} collective-permute-done((bf16[64,1664]{1,0:T(8,128)(2,1)S(1)}, bf16[64,1664]{1,0:T(8,128)(2,1)S(1)}, u32[]{:S(2)}, u32[]{:S(2)}) %collective-permute-start.6) | collective-permute-done | bytes 213024 | tf_op jit(solution)/shard_map/ppermute | solution.py:262
  31.6 1.5 %collective-permute-start.5 = (bf16[64,1664]{1,0:T(8,128)(2,1)S(1)}, bf16[64,1664]{1,0:T(8,128)(2,1)S(1)}, u32[]{:S(2)}, u32[]{:S(2)}) collective-permute-start(bf16[64,1664]{1,0:T(8,128)(2,1)S(1)} %pad_maximum_fusion.refs_4_), channel_id=1, source_target_pairs={{0,4},{2,6},{4,0},{6,2},{8,12},{10,14},{12,8},{14,10},{16,20},{18,... | collective-permute-start | bytes 638984 | tf_op jit(solution)/shard_map/ppermute | solution.py:262
  33.1 1.5 %collective-permute-start.11 = (bf16[64,1664]{1,0:T(8,128)(2,1)S(1)}, bf16[64,1664]{1,0:T(8,128)(2,1)S(1)}, u32[]{:S(2)}, u32[]{:S(2)}) collective-permute-start(bf16[64,1664]{1,0:T(8,128)(2,1)S(1)} %collective-permute-done.8.refs_7_), channel_id=1, source_target_pairs={{0,2},{2,0},{4,6},{6,4},{8,10},{10,8},{12,14},{14,12},{16,18},{18,... | collective-permute-start | bytes 638984 | tf_op jit(solution)/shard_map/ppermute | solution.py:262
  39.7 1.6 %collective-permute-start.16 = (bf16[64,1664]{1,0:T(8,128)(2,1)S(1)}, bf16[64,1664]{1,0:T(8,128)(2,1)S(1)}, u32[]{:S(2)}, u32[]{:S(2)}) collective-permute-start(bf16[64,1664]{1,0:T(8,128)(2,1)S(1)} %pad_maximum_fusion.3.refs_6_), channel_id=1, source_target_pairs={{0,4},{2,6},{4,0},{6,2},{8,12},{10,14},{12,8},{14,10},{16,20},{18,... | collective-permute-start | bytes 638984 | tf_op jit(solution)/shard_map/ppermute | solution.py:262
  42.0 1.6 %collective-permute-start.12 = (bf16[64,1664]{1,0:T(8,128)(2,1)S(1)}, bf16[64,1664]{1,0:T(8,128)(2,1)S(1)}, u32[]{:S(2)}, u32[]{:S(2)}) collective-permute-start(bf16[64,1664]{1,0:T(8,128)(2,1)S(1)} %pad_maximum_fusion.2.refs_4_), channel_id=1, source_target_pairs={{0,4},{2,6},{4,0},{6,2},{8,12},{10,14},{12,8},{14,10},{16,20},{18,... | collective-permute-start | bytes 638984 | tf_op jit(solution)/shard_map/ppermute | solution.py:262
  44.3 1.5 %collective-permute-start.15 = (bf16[64,1664]{1,0:T(8,128)(2,1)S(1)}, bf16[64,1664]{1,0:T(8,128)(2,1)S(1)}, u32[]{:S(2)}, u32[]{:S(2)}) collective-permute-start(bf16[64,1664]{1,0:T(8,128)(2,1)S(1)} %pad_maximum_fusion.3.refs_6_), channel_id=1, source_target_pairs={{0,2},{2,0},{4,6},{6,4},{8,10},{10,8},{12,14},{14,12},{16,18},{18,... | collective-permute-start | bytes 638984 | tf_op jit(solution)/shard_map/ppermute | solution.py:262
  46.6 1.6 %collective-permute-start.14 = (bf16[64,1664]{1,0:T(8,128)(2,1)S(1)}, bf16[64,1664]{1,0:T(8,128)(2,1)S(1)}, u32[]{:S(2)}, u32[]{:S(2)}) collective-permute-start(bf16[64,1664]{1,0:T(8,128)(2,1)S(1)} %collective-permute-done.13.refs_5_), channel_id=1, source_target_pairs={{0,4},{2,6},{4,0},{6,2},{8,12},{10,14},{12,8},{14,10},{16,20},{18,... | collective-permute-start | bytes 638984 | tf_op jit(solution)/shard_map/ppermute | solution.py:262
  48.9 1.5 %collective-permute-start.17 = (bf16[64,1664]{1,0:T(8,128)(2,1)S(1)}, bf16[64,1664]{1,0:T(8,128)(2,1)S(1)}, u32[]{:S(2)}, u32[]{:S(2)}) collective-permute-start(bf16[64,1664]{1,0:T(8,128)(2,1)S(1)} %collective-permute-done.16.refs_7_), channel_id=1, source_target_pairs={{0,2},{2,0},{4,6},{6,4},{8,10},{10,8},{12,14},{14,12},{16,18},{18,... | collective-permute-start | bytes 638984 | tf_op jit(solution)/shard_map/ppermute | solution.py:262
  50.4 3.1 %shard_map.133.total_ref = f32[512,1536]{1,0:T(8,128)S(1)} custom-call(bf16[64,1664]{1,0:T(8,128)(2,1)S(1)} %collective-permute-done.5.refs_0_, bf16[64,1664]{1,0:T(8,128)(2,1)S(1)} %collective-permute-done.9.refs_1_, bf16[64,1664]{1,0:T(8,128)(2,1)S(1)} %collective-permute-done.10.refs_2_, bf16[64,1664]{1,0:T(8,128)(2,1)S(1)} %collective-permute-done.11.refs_3_, ...), custom_call_target="tpu_custom_call" | custom-call | flops 2415919104 | bytes 9437184 | tf_op jit(solution)/shard_map/pallas_call | solution.py:86
  53.6 2.3 %collective-permute-done.14.refs_1_ = bf16[64,1664]{1,0:T(8,128)(2,1)S(1)} collective-permute-done((bf16[64,1664]{1,0:T(8,128)(2,1)S(1)}, bf16[64,1664]{1,0:T(8,128)(2,1)S(1)}, u32[]{:S(2)}, u32[]{:S(2)}) %collective-permute-start.14) | collective-permute-done | bytes 213024 | tf_op jit(solution)/shard_map/ppermute | solution.py:262
  55.9 9.3 %collective-permute-done.4.refs_8_ = bf16[768,1024]{1,0:T(8,128)(2,1)S(1)} collective-permute-done((bf16[768,1024]{1,0:T(8,128)(2,1)S(1)}, bf16[768,1024]{1,0:T(8,128)(2,1)S(1)}, u32[]{:S(2)}, u32[]{:S(2)}) %collective-permute-start.4) | collective-permute-done | bytes 1572896 | tf_op jit(solution)/shard_map/ppermute | solution.py:262
  65.7 3.1 %shard_map.134.total_ref = f32[512,1536]{1,0:T(8,128)S(1)} custom-call(bf16[64,1664]{1,0:T(8,128)(2,1)S(1)} %collective-permute-done.12.refs_0_, bf16[64,1664]{1,0:T(8,128)(2,1)S(1)} %collective-permute-done.14.refs_1_, bf16[64,1664]{1,0:T(8,128)(2,1)S(1)} %collective-permute-done.15.refs_2_, bf16[64,1664]{1,0:T(8,128)(2,1)S(1)} %collective-permute-done.17.refs_3_, ...), custom_call_target="tpu_custom_call" | custom-call | flops 2415919104 | bytes 9437184 | tf_op jit(solution)/shard_map/pallas_call | solution.py:86
  68.9 2.1 %shard_map.136 = (bf16[512,512]{1,0:T(8,128)(2,1)S(1)}, f32[512,128]{1,0:T(8,128)S(1)}) custom-call(bf16[64,1664]{1,0:T(8,128)(2,1)S(1)} %collective-permute-done.12.refs_0_, bf16[64,1664]{1,0:T(8,128)(2,1)S(1)} %collective-permute-done.14.refs_1_, bf16[64,1664]{1,0:T(8,128)(2,1)S(1)} %collective-permute-done.15.refs_2_, ...), custom_call_target="tpu_custom_call" | custom-call | flops 1610612736 | bytes 4718592 | tf_op jit(solution)/shard_map/pallas_call | solution.py:86
  71.0 2.1 %shard_map.135 = (bf16[512,512]{1,0:T(8,128)(2,1)S(1)}, f32[512,128]{1,0:T(8,128)S(1)}) custom-call(bf16[64,1664]{1,0:T(8,128)(2,1)S(1)} %collective-permute-done.5.refs_0_, bf16[64,1664]{1,0:T(8,128)(2,1)S(1)} %collective-permute-done.9.refs_1_, bf16[64,1664]{1,0:T(8,128)(2,1)S(1)} %collective-permute-done.10.refs_2_, ...), custom_call_target="tpu_custom_call" | custom-call | flops 1610612736 | bytes 4718592 | tf_op jit(solution)/shard_map/pallas_call | solution.py:86
  73.2 3.6 %collective-permute-done.18.last_a = bf16[256,768]{1,0:T(8,128)(2,1)S(1)} collective-permute-done((bf16[256,768]{1,0:T(8,128)(2,1)S(1)}, bf16[256,768]{1,0:T(8,128)(2,1)S(1)}, u32[]{:S(2)}, u32[]{:S(2)}) %collective-permute-start.18) | collective-permute-done | bytes 393248 | tf_op jit(solution)/shard_map/ppermute | solution.py:262
  76.8 1.7 %collective-permute-done.21.last_b = bf16[256,768]{1,0:T(8,128)(2,1)S(1)} collective-permute-done((bf16[256,768]{1,0:T(8,128)(2,1)S(1)}, bf16[256,768]{1,0:T(8,128)(2,1)S(1)}, u32[]{:S(2)}, u32[]{:S(2)}) %collective-permute-start.21) | collective-permute-done | bytes 393248 | tf_op jit(solution)/shard_map/ppermute | solution.py:266
  83.2 1.5 %collective-permute-start.22 = (bf16[128,1536]{1,0:T(8,128)(2,1)S(1)}, bf16[128,1536]{1,0:T(8,128)(2,1)S(1)}, u32[]{:S(2)}, u32[]{:S(2)}) collective-permute-start(bf16[128,1536]{1,0:T(8,128)(2,1)S(1)} %get-tuple-element.106), channel_id=1, source_target_pairs={{0,4},{2,6},{4,0},{6,2},{8,12},{10,14},{12,8},{14,10},{16,20},{18,... | collective-permute-start | bytes 1179656 | tf_op jit(solution)/shard_map/ppermute | solution.py:262
  84.7 6.8 %collective-permute-done.29.got_ref = bf16[128,1536]{1,0:T(8,128)(2,1)S(1)} collective-permute-done((bf16[128,1536]{1,0:T(8,128)(2,1)S(1)}, bf16[128,1536]{1,0:T(8,128)(2,1)S(1)}, u32[]{:S(2)}, u32[]{:S(2)}) %collective-permute-start.29) | collective-permute-done | bytes 393248 | tf_op jit(solution)/shard_map/ppermute | solution.py:262
  92.2 1.5 %collective-permute-start.28 = (bf16[64,1536]{1,0:T(8,128)(2,1)S(1)}, bf16[64,1536]{1,0:T(8,128)(2,1)S(1)}, u32[]{:S(2)}, u32[]{:S(2)}) collective-permute-start(bf16[64,1536]{1,0:T(8,128)(2,1)S(1)} %get-tuple-element.121), channel_id=1, source_target_pairs={{0,2},{2,0},{4,6},{6,4},{8,10},{10,8},{12,14},{14,12},{16,18},{18,... | collective-permute-start | bytes 589832 | tf_op jit(solution)/shard_map/ppermute | solution.py:262
  93.7 6.2 %collective-permute-done.24.got_ref = bf16[128,1536]{1,0:T(8,128)(2,1)S(1)} collective-permute-done((bf16[128,1536]{1,0:T(8,128)(2,1)S(1)}, bf16[128,1536]{1,0:T(8,128)(2,1)S(1)}, u32[]{:S(2)}, u32[]{:S(2)}) %collective-permute-start.24) | collective-permute-done | bytes 393248 | tf_op jit(solution)/shard_map/ppermute | solution.py:262
  100.7 1.5 %collective-permute-start.23 = (bf16[64,1536]{1,0:T(8,128)(2,1)S(1)}, bf16[64,1536]{1,0:T(8,128)(2,1)S(1)}, u32[]{:S(2)}, u32[]{:S(2)}) collective-permute-start(bf16[64,1536]{1,0:T(8,128)(2,1)S(1)} %get-tuple-element.108), channel_id=1, source_target_pairs={{0,2},{2,0},{4,6},{6,4},{8,10},{10,8},{12,14},{14,12},{16,18},{18,... | collective-permute-start | bytes 589832 | tf_op jit(solution)/shard_map/ppermute | solution.py:262
  102.2 2.6 %collective-permute-done.30.got_b = bf16[64,1536]{1,0:T(8,128)(2,1)S(1)} collective-permute-done((bf16[64,1536]{1,0:T(8,128)(2,1)S(1)}, bf16[64,1536]{1,0:T(8,128)(2,1)S(1)}, u32[]{:S(2)}, u32[]{:S(2)}) %collective-permute-start.30) | collective-permute-done | bytes 196640 | tf_op jit(solution)/shard_map/ppermute | solution.py:262
  104.8 2.3 %collective-permute-start.31 = (bf16[64,1536]{1,0:T(8,128)(2,1)S(1)}, bf16[64,1536]{1,0:T(8,128)(2,1)S(1)}, u32[]{:S(2)}, u32[]{:S(2)}) collective-permute-start(bf16[64,1536]{1,0:T(8,128)(2,1)S(1)} %get-tuple-element.127), channel_id=1, source_target_pairs={{0,16},{2,18},{4,20},{6,22},{8,24},{10,26},{12,28},{14,30},{16,0},... | collective-permute-start | bytes 589832 | tf_op jit(solution)/shard_map/ppermute | solution.py:262
  107.9 2.3 %collective-permute-start.26 = (bf16[64,1536]{1,0:T(8,128)(2,1)S(1)}, bf16[64,1536]{1,0:T(8,128)(2,1)S(1)}, u32[]{:S(2)}, u32[]{:S(2)}) collective-permute-start(bf16[64,1536]{1,0:T(8,128)(2,1)S(1)} %get-tuple-element.114), channel_id=1, source_target_pairs={{0,16},{2,18},{4,20},{6,22},{8,24},{10,26},{12,28},{14,30},{16,0},... | collective-permute-start | bytes 589832 | tf_op jit(solution)/shard_map/ppermute | solution.py:262
  110.2 9.7 %collective-permute-done.31.got_ref = bf16[64,1536]{1,0:T(8,128)(2,1)S(1)} collective-permute-done((bf16[64,1536]{1,0:T(8,128)(2,1)S(1)}, bf16[64,1536]{1,0:T(8,128)(2,1)S(1)}, u32[]{:S(2)}, u32[]{:S(2)}) %collective-permute-start.31) | collective-permute-done | bytes 196640 | tf_op jit(solution)/shard_map/ppermute | solution.py:262
  120.6 2.5 %collective-permute-done.26.got_ref = bf16[64,1536]{1,0:T(8,128)(2,1)S(1)} collective-permute-done((bf16[64,1536]{1,0:T(8,128)(2,1)S(1)}, bf16[64,1536]{1,0:T(8,128)(2,1)S(1)}, u32[]{:S(2)}, u32[]{:S(2)}) %collective-permute-start.26) | collective-permute-done | bytes 196640 | tf_op jit(solution)/shard_map/ppermute | solution.py:262
  (81 shorter events, 25.2 us)
Async XLA Ops:
  4.8 19.7 %collective-permute-start.1 = (bf16[768,1024]{1,0:T(8,128)(2,1)S(1)}, bf16[768,1024]{1,0:T(8,128)(2,1)S(1)}, u32[]{:S(2)}, u32[]{:S(2)}) collective-permute-start(bf16[768,1024]{1,0:T(8,128)(2,1)S(1)} %get-tuple-element.69.refs_8_), channel_id=1, source_target_pairs={{0,1},{1,0},{2,3},{3,2},{4,5},{5,4},{6,7},{7,6},{8,9},{9,8},{10,11... | collective-permute-start | bytes 4718600 | tf_op jit(solution)/shard_map/ppermute | solution.py:266
  5.3 19.2 %collective-permute-start.2 = (bf16[512,768]{1,0:T(8,128)(2,1)S(1)}, bf16[512,768]{1,0:T(8,128)(2,1)S(1)}, u32[]{:S(2)}, u32[]{:S(2)}) collective-permute-start(bf16[512,768]{1,0:T(8,128)(2,1)S(1)} %bitcast.8), channel_id=1, source_target_pairs={{0,1},{1,0},{2,3},{3,2},{4,5},{5,4},{6,7},{7,6},{8,9},{9,8},{10,11... | collective-permute-start | bytes 2359304 | tf_op jit(solution)/shard_map/ppermute | solution.py:266
  5.4 19.1 %collective-permute-start.3 = (bf16[256,768]{1,0:T(8,128)(2,1)S(1)}, bf16[256,768]{1,0:T(8,128)(2,1)S(1)}, u32[]{:S(2)}, u32[]{:S(2)}) collective-permute-start(bf16[256,768]{1,0:T(8,128)(2,1)S(1)} %get-tuple-element.68), channel_id=1, source_target_pairs={{0,8},{2,10},{4,12},{6,14},{8,0},{10,2},{12,4},{14,6},{16,24},{18,... | collective-permute-start | bytes 1179656 | tf_op jit(solution)/shard_map/ppermute | solution.py:262
  9.8 12.6 %collective-permute-start = (bf16[64,1664]{1,0:T(8,128)(2,1)S(1)}, bf16[64,1664]{1,0:T(8,128)(2,1)S(1)}, u32[]{:S(2)}, u32[]{:S(2)}) collective-permute-start(bf16[64,1664]{1,0:T(8,128)(2,1)S(1)} %get-tuple-element.66), channel_id=1, source_target_pairs={{0,16},{2,18},{4,20},{6,22},{8,24},{10,26},{12,28},{14,30},{16,0},... | collective-permute-start | bytes 638984 | tf_op jit(solution)/shard_map/ppermute | solution.py:262
  12.5 19.1 %collective-permute-start.6 = (bf16[64,1664]{1,0:T(8,128)(2,1)S(1)}, bf16[64,1664]{1,0:T(8,128)(2,1)S(1)}, u32[]{:S(2)}, u32[]{:S(2)}) collective-permute-start(bf16[64,1664]{1,0:T(8,128)(2,1)S(1)} %get-tuple-element.71), channel_id=1, source_target_pairs={{0,16},{2,18},{4,20},{6,22},{8,24},{10,26},{12,28},{14,30},{16,0},... | collective-permute-start | bytes 638984 | tf_op jit(solution)/shard_map/ppermute | solution.py:262
  24.6 8.6 %collective-permute-start.7 = (bf16[64,1664]{1,0:T(8,128)(2,1)S(1)}, bf16[64,1664]{1,0:T(8,128)(2,1)S(1)}, u32[]{:S(2)}, u32[]{:S(2)}) collective-permute-start(bf16[64,1664]{1,0:T(8,128)(2,1)S(1)} %pad_maximum_fusion.refs_4_), channel_id=1, source_target_pairs={{0,2},{2,0},{4,6},{6,4},{8,10},{10,8},{12,14},{14,12},{16,18},{18,... | collective-permute-start | bytes 638984 | tf_op jit(solution)/shard_map/ppermute | solution.py:262
  26.3 6.8 %collective-permute-start.8 = (bf16[64,1664]{1,0:T(8,128)(2,1)S(1)}, bf16[64,1664]{1,0:T(8,128)(2,1)S(1)}, u32[]{:S(2)}, u32[]{:S(2)}) collective-permute-start(bf16[64,1664]{1,0:T(8,128)(2,1)S(1)} %pad_maximum_fusion.1.refs_6_), channel_id=1, source_target_pairs={{0,4},{2,6},{4,0},{6,2},{8,12},{10,14},{12,8},{14,10},{16,20},{18,... | collective-permute-start | bytes 638984 | tf_op jit(solution)/shard_map/ppermute | solution.py:262
  27.9 37.3 %collective-permute-start.4 = (bf16[768,1024]{1,0:T(8,128)(2,1)S(1)}, bf16[768,1024]{1,0:T(8,128)(2,1)S(1)}, u32[]{:S(2)}, u32[]{:S(2)}) collective-permute-start(bf16[768,1024]{1,0:T(8,128)(2,1)S(1)} %get-tuple-element.69.refs_8_), channel_id=1, source_target_pairs={{0,8},{2,10},{4,12},{6,14},{8,0},{10,2},{12,4},{14,6},{16,24},{18,... | collective-permute-start | bytes 4718600 | tf_op jit(solution)/shard_map/ppermute | solution.py:262
  29.3 8.2 %collective-permute-start.10 = (bf16[64,1664]{1,0:T(8,128)(2,1)S(1)}, bf16[64,1664]{1,0:T(8,128)(2,1)S(1)}, u32[]{:S(2)}, u32[]{:S(2)}) collective-permute-start(bf16[64,1664]{1,0:T(8,128)(2,1)S(1)} %pad_maximum_fusion.1.refs_6_), channel_id=1, source_target_pairs={{0,2},{2,0},{4,6},{6,4},{8,10},{10,8},{12,14},{14,12},{16,18},{18,... | collective-permute-start | bytes 638984 | tf_op jit(solution)/shard_map/ppermute | solution.py:262
  31.6 8.1 %collective-permute-start.5 = (bf16[64,1664]{1,0:T(8,128)(2,1)S(1)}, bf16[64,1664]{1,0:T(8,128)(2,1)S(1)}, u32[]{:S(2)}, u32[]{:S(2)}) collective-permute-start(bf16[64,1664]{1,0:T(8,128)(2,1)S(1)} %pad_maximum_fusion.refs_4_), channel_id=1, source_target_pairs={{0,4},{2,6},{4,0},{6,2},{8,12},{10,14},{12,8},{14,10},{16,20},{18,... | collective-permute-start | bytes 638984 | tf_op jit(solution)/shard_map/ppermute | solution.py:262
  33.1 8.9 %collective-permute-start.11 = (bf16[64,1664]{1,0:T(8,128)(2,1)S(1)}, bf16[64,1664]{1,0:T(8,128)(2,1)S(1)}, u32[]{:S(2)}, u32[]{:S(2)}) collective-permute-start(bf16[64,1664]{1,0:T(8,128)(2,1)S(1)} %collective-permute-done.8.refs_7_), channel_id=1, source_target_pairs={{0,2},{2,0},{4,6},{6,4},{8,10},{10,8},{12,14},{14,12},{16,18},{18,... | collective-permute-start | bytes 638984 | tf_op jit(solution)/shard_map/ppermute | solution.py:262
  34.6 9.7 %collective-permute-start.9 = (bf16[64,1664]{1,0:T(8,128)(2,1)S(1)}, bf16[64,1664]{1,0:T(8,128)(2,1)S(1)}, u32[]{:S(2)}, u32[]{:S(2)}) collective-permute-start(bf16[64,1664]{1,0:T(8,128)(2,1)S(1)} %collective-permute-done.7.refs_5_), channel_id=1, source_target_pairs={{0,4},{2,6},{4,0},{6,2},{8,12},{10,14},{12,8},{14,10},{16,20},{18,... | collective-permute-start | bytes 638984 | tf_op jit(solution)/shard_map/ppermute | solution.py:262
  37.5 9.1 %collective-permute-start.13 = (bf16[64,1664]{1,0:T(8,128)(2,1)S(1)}, bf16[64,1664]{1,0:T(8,128)(2,1)S(1)}, u32[]{:S(2)}, u32[]{:S(2)}) collective-permute-start(bf16[64,1664]{1,0:T(8,128)(2,1)S(1)} %pad_maximum_fusion.2.refs_4_), channel_id=1, source_target_pairs={{0,2},{2,0},{4,6},{6,4},{8,10},{10,8},{12,14},{14,12},{16,18},{18,... | collective-permute-start | bytes 638984 | tf_op jit(solution)/shard_map/ppermute | solution.py:262
  39.7 9.1 %collective-permute-start.16 = (bf16[64,1664]{1,0:T(8,128)(2,1)S(1)}, bf16[64,1664]{1,0:T(8,128)(2,1)S(1)}, u32[]{:S(2)}, u32[]{:S(2)}) collective-permute-start(bf16[64,1664]{1,0:T(8,128)(2,1)S(1)} %pad_maximum_fusion.3.refs_6_), channel_id=1, source_target_pairs={{0,4},{2,6},{4,0},{6,2},{8,12},{10,14},{12,8},{14,10},{16,20},{18,... | collective-permute-start | bytes 638984 | tf_op jit(solution)/shard_map/ppermute | solution.py:262
  42.0 11.5 %collective-permute-start.12 = (bf16[64,1664]{1,0:T(8,128)(2,1)S(1)}, bf16[64,1664]{1,0:T(8,128)(2,1)S(1)}, u32[]{:S(2)}, u32[]{:S(2)}) collective-permute-start(bf16[64,1664]{1,0:T(8,128)(2,1)S(1)} %pad_maximum_fusion.2.refs_4_), channel_id=1, source_target_pairs={{0,4},{2,6},{4,0},{6,2},{8,12},{10,14},{12,8},{14,10},{16,20},{18,... | collective-permute-start | bytes 638984 | tf_op jit(solution)/shard_map/ppermute | solution.py:262
  44.3 9.3 %collective-permute-start.15 = (bf16[64,1664]{1,0:T(8,128)(2,1)S(1)}, bf16[64,1664]{1,0:T(8,128)(2,1)S(1)}, u32[]{:S(2)}, u32[]{:S(2)}) collective-permute-start(bf16[64,1664]{1,0:T(8,128)(2,1)S(1)} %pad_maximum_fusion.3.refs_6_), channel_id=1, source_target_pairs={{0,2},{2,0},{4,6},{6,4},{8,10},{10,8},{12,14},{14,12},{16,18},{18,... | collective-permute-start | bytes 638984 | tf_op jit(solution)/shard_map/ppermute | solution.py:262
  46.6 9.3 %collective-permute-start.14 = (bf16[64,1664]{1,0:T(8,128)(2,1)S(1)}, bf16[64,1664]{1,0:T(8,128)(2,1)S(1)}, u32[]{:S(2)}, u32[]{:S(2)}) collective-permute-start(bf16[64,1664]{1,0:T(8,128)(2,1)S(1)} %collective-permute-done.13.refs_5_), channel_id=1, source_target_pairs={{0,4},{2,6},{4,0},{6,2},{8,12},{10,14},{12,8},{14,10},{16,20},{18,... | collective-permute-start | bytes 638984 | tf_op jit(solution)/shard_map/ppermute | solution.py:262
  48.9 7.0 %collective-permute-start.17 = (bf16[64,1664]{1,0:T(8,128)(2,1)S(1)}, bf16[64,1664]{1,0:T(8,128)(2,1)S(1)}, u32[]{:S(2)}, u32[]{:S(2)}) collective-permute-start(bf16[64,1664]{1,0:T(8,128)(2,1)S(1)} %collective-permute-done.16.refs_7_), channel_id=1, source_target_pairs={{0,2},{2,0},{4,6},{6,4},{8,10},{10,8},{12,14},{14,12},{16,18},{18,... | collective-permute-start | bytes 638984 | tf_op jit(solution)/shard_map/ppermute | solution.py:262
  65.2 3.7 %collective-permute-start.20 = (bf16[768,1024]{1,0:T(8,128)(2,1)S(1)}, bf16[768,1024]{1,0:T(8,128)(2,1)S(1)}, u32[]{:S(2)}, u32[]{:S(2)}) collective-permute-start(bf16[768,1024]{1,0:T(8,128)(2,1)S(1)} %collective-permute-done.4.refs_8_), channel_id=1, source_target_pairs={{0,1},{1,0},{2,3},{3,2},{4,5},{5,4},{6,7},{7,6},{8,9},{9,8},{10,11... | collective-permute-start | bytes 4718600 | tf_op jit(solution)/shard_map/ppermute | solution.py:266
  65.2 7.9 %collective-permute-start.19 = (bf16[256,768]{1,0:T(8,128)(2,1)S(1)}, bf16[256,768]{1,0:T(8,128)(2,1)S(1)}, u32[]{:S(2)}, u32[]{:S(2)}) collective-permute-start(bf16[256,768]{1,0:T(8,128)(2,1)S(1)} %collective-permute-done.3.first_a), channel_id=1, source_target_pairs={{0,1},{1,0},{2,3},{3,2},{4,5},{5,4},{6,7},{7,6},{8,9},{9,8},{10,11... | collective-permute-start | bytes 1179656 | tf_op jit(solution)/shard_map/ppermute | solution.py:266
  65.7 11.0 %collective-permute-start.18 = (bf16[256,768]{1,0:T(8,128)(2,1)S(1)}, bf16[256,768]{1,0:T(8,128)(2,1)S(1)}, u32[]{:S(2)}, u32[]{:S(2)}) collective-permute-start(bf16[256,768]{1,0:T(8,128)(2,1)S(1)} %get-tuple-element.77), channel_id=1, source_target_pairs={{0,8},{2,10},{4,12},{6,14},{8,0},{10,2},{12,4},{14,6},{16,24},{18,... | collective-permute-start | bytes 1179656 | tf_op jit(solution)/shard_map/ppermute | solution.py:262
  76.8 1.7 %collective-permute-start.21 = (bf16[256,768]{1,0:T(8,128)(2,1)S(1)}, bf16[256,768]{1,0:T(8,128)(2,1)S(1)}, u32[]{:S(2)}, u32[]{:S(2)}) collective-permute-start(bf16[256,768]{1,0:T(8,128)(2,1)S(1)} %collective-permute-done.18.last_a), channel_id=1, source_target_pairs={{0,1},{1,0},{2,3},{3,2},{4,5},{5,4},{6,7},{7,6},{8,9},{9,8},{10,11... | collective-permute-start | bytes 1179656 | tf_op jit(solution)/shard_map/ppermute | solution.py:266
  79.5 12.0 %collective-permute-start.29 = (bf16[128,1536]{1,0:T(8,128)(2,1)S(1)}, bf16[128,1536]{1,0:T(8,128)(2,1)S(1)}, u32[]{:S(2)}, u32[]{:S(2)}) collective-permute-start(bf16[128,1536]{1,0:T(8,128)(2,1)S(1)} %get-tuple-element.123), channel_id=1, source_target_pairs={{0,2},{2,0},{4,6},{6,4},{8,10},{10,8},{12,14},{14,12},{16,18},{18,... | collective-permute-start | bytes 1179656 | tf_op jit(solution)/shard_map/ppermute | solution.py:262
  80.1 12.1 %collective-permute-start.27 = (bf16[128,1536]{1,0:T(8,128)(2,1)S(1)}, bf16[128,1536]{1,0:T(8,128)(2,1)S(1)}, u32[]{:S(2)}, u32[]{:S(2)}) collective-permute-start(bf16[128,1536]{1,0:T(8,128)(2,1)S(1)} %get-tuple-element.119), channel_id=1, source_target_pairs={{0,4},{2,6},{4,0},{6,2},{8,12},{10,14},{12,8},{14,10},{16,20},{18,... | collective-permute-start | bytes 1179656 | tf_op jit(solution)/shard_map/ppermute | solution.py:262
  81.8 18.2 %collective-permute-start.24 = (bf16[128,1536]{1,0:T(8,128)(2,1)S(1)}, bf16[128,1536]{1,0:T(8,128)(2,1)S(1)}, u32[]{:S(2)}, u32[]{:S(2)}) collective-permute-start(bf16[128,1536]{1,0:T(8,128)(2,1)S(1)} %get-tuple-element.110), channel_id=1, source_target_pairs={{0,2},{2,0},{4,6},{6,4},{8,10},{10,8},{12,14},{14,12},{16,18},{18,... | collective-permute-start | bytes 1179656 | tf_op jit(solution)/shard_map/ppermute | solution.py:262
  83.2 17.4 %collective-permute-start.22 = (bf16[128,1536]{1,0:T(8,128)(2,1)S(1)}, bf16[128,1536]{1,0:T(8,128)(2,1)S(1)}, u32[]{:S(2)}, u32[]{:S(2)}) collective-permute-start(bf16[128,1536]{1,0:T(8,128)(2,1)S(1)} %get-tuple-element.106), channel_id=1, source_target_pairs={{0,4},{2,6},{4,0},{6,2},{8,12},{10,14},{12,8},{14,10},{16,20},{18,... | collective-permute-start | bytes 1179656 | tf_op jit(solution)/shard_map/ppermute | solution.py:262
  91.6 13.1 %collective-permute-start.30 = (bf16[64,1536]{1,0:T(8,128)(2,1)S(1)}, bf16[64,1536]{1,0:T(8,128)(2,1)S(1)}, u32[]{:S(2)}, u32[]{:S(2)}) collective-permute-start(bf16[64,1536]{1,0:T(8,128)(2,1)S(1)} %get-tuple-element.125), channel_id=1, source_target_pairs={{0,4},{2,6},{4,0},{6,2},{8,12},{10,14},{12,8},{14,10},{16,20},{18,... | collective-permute-start | bytes 589832 | tf_op jit(solution)/shard_map/ppermute | solution.py:262
  92.2 12.5 %collective-permute-start.28 = (bf16[64,1536]{1,0:T(8,128)(2,1)S(1)}, bf16[64,1536]{1,0:T(8,128)(2,1)S(1)}, u32[]{:S(2)}, u32[]{:S(2)}) collective-permute-start(bf16[64,1536]{1,0:T(8,128)(2,1)S(1)} %get-tuple-element.121), channel_id=1, source_target_pairs={{0,2},{2,0},{4,6},{6,4},{8,10},{10,8},{12,14},{14,12},{16,18},{18,... | collective-permute-start | bytes 589832 | tf_op jit(solution)/shard_map/ppermute | solution.py:262
  100.0 7.8 %collective-permute-start.25 = (bf16[64,1536]{1,0:T(8,128)(2,1)S(1)}, bf16[64,1536]{1,0:T(8,128)(2,1)S(1)}, u32[]{:S(2)}, u32[]{:S(2)}) collective-permute-start(bf16[64,1536]{1,0:T(8,128)(2,1)S(1)} %get-tuple-element.112), channel_id=1, source_target_pairs={{0,4},{2,6},{4,0},{6,2},{8,12},{10,14},{12,8},{14,10},{16,20},{18,... | collective-permute-start | bytes 589832 | tf_op jit(solution)/shard_map/ppermute | solution.py:262
  100.7 7.2 %collective-permute-start.23 = (bf16[64,1536]{1,0:T(8,128)(2,1)S(1)}, bf16[64,1536]{1,0:T(8,128)(2,1)S(1)}, u32[]{:S(2)}, u32[]{:S(2)}) collective-permute-start(bf16[64,1536]{1,0:T(8,128)(2,1)S(1)} %get-tuple-element.108), channel_id=1, source_target_pairs={{0,2},{2,0},{4,6},{6,4},{8,10},{10,8},{12,14},{14,12},{16,18},{18,... | collective-permute-start | bytes 589832 | tf_op jit(solution)/shard_map/ppermute | solution.py:262
  104.8 15.1 %collective-permute-start.31 = (bf16[64,1536]{1,0:T(8,128)(2,1)S(1)}, bf16[64,1536]{1,0:T(8,128)(2,1)S(1)}, u32[]{:S(2)}, u32[]{:S(2)}) collective-permute-start(bf16[64,1536]{1,0:T(8,128)(2,1)S(1)} %get-tuple-element.127), channel_id=1, source_target_pairs={{0,16},{2,18},{4,20},{6,22},{8,24},{10,26},{12,28},{14,30},{16,0},... | collective-permute-start | bytes 589832 | tf_op jit(solution)/shard_map/ppermute | solution.py:262
  107.9 15.3 %collective-permute-start.26 = (bf16[64,1536]{1,0:T(8,128)(2,1)S(1)}, bf16[64,1536]{1,0:T(8,128)(2,1)S(1)}, u32[]{:S(2)}, u32[]{:S(2)}) collective-permute-start(bf16[64,1536]{1,0:T(8,128)(2,1)S(1)} %get-tuple-element.114), channel_id=1, source_target_pairs={{0,16},{2,18},{4,20},{6,22},{8,24},{10,26},{12,28},{14,30},{16,0},... | collective-permute-start | bytes 589832 | tf_op jit(solution)/shard_map/ppermute | solution.py:262
  (13 other events, 90.5 us)

commit v11 on v10

--- a/solution.py
+++ b/solution.py
@@ -343,7 +343,7 @@
         pack_kernel,
         (jax.ShapeDtypeStruct((gate.shape[0], 2 * ff), jnp.bfloat16), half_down, half_down),
         (gate, up, down),
-        12,
+        59,
         0,
         12 * gate.size,
         [pltpu.SemaphoreType.DMA((4,))],
@@ -352,13 +352,11 @@
     by_first = swap(down_first, Z_LOW)
     twins = (swap_core(both), swap_core(down))
     far = [swap(x, Z_HIGH) for x in own]
-    far[0], twins, both_later, by_first = lax.optimization_barrier(
-        (far[0], twins, both, by_first)
-    )
+    far[0], twins, both_later = lax.optimization_barrier((far[0], twins, both))
     both_by = swap(both_later, Z_LOW)
     first_one = halves(own[0], far[0])
     second_one = swap(first_one[0], X), swap(first_one[1], Y)
-    far[1], second_one = lax.optimization_barrier((far[1], second_one))
+    far[1], second_one, by_first = lax.optimization_barrier((far[1], second_one, by_first))
     first_two = halves(own[1], far[1])
     second_two = swap(first_two[0], X), swap(first_two[1], Y)
     pieces = [spread(*first_one, *second_one), spread(*first_two, *second_two)]
@@ -372,7 +370,7 @@
             jax.ShapeDtypeStruct((rows, width), jnp.float32),
             (*p, both, twins[0], down, twins[1]),
             20,
-            6 * rows * width * ff,
+            0,
             6 * width * ff + 6 * rows * width,
             scratch,
         )
@@ -403,10 +401,9 @@
         )
 
     total_one = own_total(pieces[0])
-    down_last, both_by, total_one, pieces = lax.optimization_barrier(
-        (down_last, both_by, total_one, pieces)
-    )
+    down_last, far[1] = lax.optimization_barrier((down_last, far[1]))
     by_last = swap(down_last, Z_LOW)
+    both_by, total_one, pieces = lax.optimization_barrier((both_by, total_one, pieces))
     twin_first = swap_core(by_first)
     both_twin = swap_core(both_by)
     total_two = own_total(pieces[1])

time: 124 us -> 122 us (0.984)
  local copies, waits for them, and re-layouts: 3.51 us -> 0.11 us
  Pallas kernels: 16.4 us -> 18.9 us
    unnamed x26 -> x24, local copies, waits for them, and re-layouts: 3.45 us -> 0.05 us
    pallas_call x16, Pallas kernels: 16.4 us -> 18.9 us  [call(): pl.pallas_call(body, out_shape=outs, in_specs=specs or [smem if x.ndim ==...]
  transfers between devices with their start and end apart: 32 -> 32, of which waited for: 19 -> 16; matrix products, arithmetic and copies ran while one was open for 0% -> 0% of each run, Pallas kernels for 11% -> 11%
where the time goes in v11:
time: 122 us
  waiting for transfers between devices  63.2 us (52%)
  starting transfers between devices  39.1 us (32%)
  Pallas kernels  18.9 us (15%)
    ppermute x27, waiting for transfers between devices, swap(): lax.ppermute(block, 'expert', [(i, i ^ distance) for i in range(count)])  61.4 us
    ppermute x27, starting transfers between devices, swap(): lax.ppermute(block, 'expert', [(i, i ^ distance) for i in range(count)])  38.3 us
    pallas_call x16, Pallas kernels, call(): pl.pallas_call(body, out_shape=outs, in_specs=specs or [smem if x.ndim ==...  18.9 us
  transfers between devices with their start and end apart: 32, of which 16 were waited for; matrix products, arithmetic and copies ran while one was open for 0% of the time, Pallas kernels for 11%

profile of v11, /device:TPU:0, one launch (start us, length us, event | category | flops | bytes accessed | tf_op | source)
XLA Modules:
  0.0 122.4 jit_solution(2267495865227652040)
XLA Ops:
  0.7 3.2 %shard_map.131 = (bf16[768,1024]{1,0:T(8,128)(2,1)}, bf16[256,768]{1,0:T(8,128)(2,1)}, bf16[256,768]{1,0:T(8,128)(2,1)}) custom-call(bf16[768,512]{1,0:T(8,128)(2,1)} %bitcast.15, bf16[768,512]{1,0:T(8,128)(2,1)} %bitcast.16, bf16[512,768]{1,0:T(8,128)(2,1)} %bitcast.7), custom_call_target="tpu_custom_call" | custom-call | bytes 4718592 | tf_op jit(solution)/shard_map/pallas_call | solution.py:86
  6.0 4.1 %collective-permute-start.1 = (bf16[64,1664]{1,0:T(8,128)(2,1)S(1)}, bf16[64,1664]{1,0:T(8,128)(2,1)S(1)}, u32[]{:S(2)}, u32[]{:S(2)}) collective-permute-start(bf16[64,1664]{1,0:T(8,128)(2,1)S(1)} %get-tuple-element.67), channel_id=1, source_target_pairs={{0,16},{2,18},{4,20},{6,22},{8,24},{10,26},{12,28},{14,30},{16,0},... | collective-permute-start | bytes 638984 | tf_op jit(solution)/shard_map/ppermute | solution.py:262
  10.0 1.6 %collective-permute-start.6 = (bf16[256,768]{1,0:T(8,128)(2,1)}, bf16[256,768]{1,0:T(8,128)(2,1)S(1)}, u32[]{:S(2)}, u32[]{:S(2)}) collective-permute-start(bf16[256,768]{1,0:T(8,128)(2,1)} %get-tuple-element.70), channel_id=1, source_target_pairs={{0,8},{2,10},{4,12},{6,14},{8,0},{10,2},{12,4},{14,6},{16,24},{18,... | collective-permute-start | bytes 1179656 | tf_op jit(solution)/shard_map/ppermute | solution.py:262
  12.0 8.8 %collective-permute-done.1 = bf16[64,1664]{1,0:T(8,128)(2,1)S(1)} collective-permute-done((bf16[64,1664]{1,0:T(8,128)(2,1)S(1)}, bf16[64,1664]{1,0:T(8,128)(2,1)S(1)}, u32[]{:S(2)}, u32[]{:S(2)}) %collective-permute-start.1) | collective-permute-done | bytes 213024 | tf_op jit(solution)/shard_map/ppermute | solution.py:262
  20.8 2.0 %collective-permute-start.5 = (bf16[64,1664]{1,0:T(8,128)(2,1)S(1)}, bf16[64,1664]{1,0:T(8,128)(2,1)S(1)}, u32[]{:S(2)}, u32[]{:S(2)}) collective-permute-start(bf16[64,1664]{1,0:T(8,128)(2,1)S(1)} %pad_maximum_fusion.1.refs_6_), channel_id=1, source_target_pairs={{0,4},{2,6},{4,0},{6,2},{8,12},{10,14},{12,8},{14,10},{16,20},{18,... | collective-permute-start | bytes 638984 | tf_op jit(solution)/shard_map/ppermute | solution.py:262
  22.8 1.6 %collective-permute-start.4 = (bf16[64,1664]{1,0:T(8,128)(2,1)S(1)}, bf16[64,1664]{1,0:T(8,128)(2,1)S(1)}, u32[]{:S(2)}, u32[]{:S(2)}) collective-permute-start(bf16[64,1664]{1,0:T(8,128)(2,1)S(1)} %pad_maximum_fusion.refs_4_), channel_id=1, source_target_pairs={{0,2},{2,0},{4,6},{6,4},{8,10},{10,8},{12,14},{14,12},{16,18},{18,... | collective-permute-start | bytes 638984 | tf_op jit(solution)/shard_map/ppermute | solution.py:262
  24.4 4.4 %collective-permute-done = bf16[64,1664]{1,0:T(8,128)(2,1)S(1)} collective-permute-done((bf16[64,1664]{1,0:T(8,128)(2,1)S(1)}, bf16[64,1664]{1,0:T(8,128)(2,1)S(1)}, u32[]{:S(2)}, u32[]{:S(2)}) %collective-permute-start) | collective-permute-done | bytes 213024 | tf_op jit(solution)/shard_map/ppermute | solution.py:262
  30.3 1.6 %collective-permute-start.10 = (bf16[64,1664]{1,0:T(8,128)(2,1)S(1)}, bf16[64,1664]{1,0:T(8,128)(2,1)S(1)}, u32[]{:S(2)}, u32[]{:S(2)}) collective-permute-start(bf16[64,1664]{1,0:T(8,128)(2,1)S(1)} %pad_maximum_fusion.refs_4_), channel_id=1, source_target_pairs={{0,4},{2,6},{4,0},{6,2},{8,12},{10,14},{12,8},{14,10},{16,20},{18,... | collective-permute-start | bytes 638984 | tf_op jit(solution)/shard_map/ppermute | solution.py:262
  32.3 1.5 %collective-permute-start.13 = (bf16[64,1664]{1,0:T(8,128)(2,1)S(1)}, bf16[64,1664]{1,0:T(8,128)(2,1)S(1)}, u32[]{:S(2)}, u32[]{:S(2)}) collective-permute-start(bf16[64,1664]{1,0:T(8,128)(2,1)S(1)} %collective-permute-done.5.refs_7_), channel_id=1, source_target_pairs={{0,2},{2,0},{4,6},{6,4},{8,10},{10,8},{12,14},{14,12},{16,18},{18,... | collective-permute-start | bytes 638984 | tf_op jit(solution)/shard_map/ppermute | solution.py:262
  33.9 2.9 %collective-permute-done.12.refs_2_ = bf16[64,1664]{1,0:T(8,128)(2,1)S(1)} collective-permute-done((bf16[64,1664]{1,0:T(8,128)(2,1)S(1)}, bf16[64,1664]{1,0:T(8,128)(2,1)S(1)}, u32[]{:S(2)}, u32[]{:S(2)}) %collective-permute-start.12) | collective-permute-done | bytes 213024 | tf_op jit(solution)/shard_map/ppermute | solution.py:262
  36.8 1.6 %collective-permute-start.15 = (bf16[64,1664]{1,0:T(8,128)(2,1)S(1)}, bf16[64,1664]{1,0:T(8,128)(2,1)S(1)}, u32[]{:S(2)}, u32[]{:S(2)}) collective-permute-start(bf16[64,1664]{1,0:T(8,128)(2,1)S(1)} %pad_maximum_fusion.2.refs_4_), channel_id=1, source_target_pairs={{0,2},{2,0},{4,6},{6,4},{8,10},{10,8},{12,14},{14,12},{16,18},{18,... | collective-permute-start | bytes 638984 | tf_op jit(solution)/shard_map/ppermute | solution.py:262
  38.4 1.6 %collective-permute-start.18 = (bf16[64,1664]{1,0:T(8,128)(2,1)S(1)}, bf16[64,1664]{1,0:T(8,128)(2,1)S(1)}, u32[]{:S(2)}, u32[]{:S(2)}) collective-permute-start(bf16[64,1664]{1,0:T(8,128)(2,1)S(1)} %pad_maximum_fusion.3.refs_6_), channel_id=1, source_target_pairs={{0,4},{2,6},{4,0},{6,2},{8,12},{10,14},{12,8},{14,10},{16,20},{18,... | collective-permute-start | bytes 638984 | tf_op jit(solution)/shard_map/ppermute | solution.py:262
  40.0 3.0 %collective-permute-done.11.refs_1_ = bf16[64,1664]{1,0:T(8,128)(2,1)S(1)} collective-permute-done((bf16[64,1664]{1,0:T(8,128)(2,1)S(1)}, bf16[64,1664]{1,0:T(8,128)(2,1)S(1)}, u32[]{:S(2)}, u32[]{:S(2)}) %collective-permute-start.11) | collective-permute-done | bytes 213024 | tf_op jit(solution)/shard_map/ppermute | solution.py:262
  43.0 1.6 %collective-permute-start.14 = (bf16[64,1664]{1,0:T(8,128)(2,1)S(1)}, bf16[64,1664]{1,0:T(8,128)(2,1)S(1)}, u32[]{:S(2)}, u32[]{:S(2)}) collective-permute-start(bf16[64,1664]{1,0:T(8,128)(2,1)S(1)} %pad_maximum_fusion.2.refs_4_), channel_id=1, source_target_pairs={{0,4},{2,6},{4,0},{6,2},{8,12},{10,14},{12,8},{14,10},{16,20},{18,... | collective-permute-start | bytes 638984 | tf_op jit(solution)/shard_map/ppermute | solution.py:262
  49.1 3.1 %shard_map.133.total_ref = f32[512,1536]{1,0:T(8,128)S(1)} custom-call(bf16[64,1664]{1,0:T(8,128)(2,1)S(1)} %collective-permute-done.10.refs_0_, bf16[64,1664]{1,0:T(8,128)(2,1)S(1)} %collective-permute-done.11.refs_1_, bf16[64,1664]{1,0:T(8,128)(2,1)S(1)} %collective-permute-done.12.refs_2_, bf16[64,1664]{1,0:T(8,128)(2,1)S(1)} %collective-permute-done.13.refs_3_, ...), custom_call_target="tpu_custom_call" | custom-call | bytes 9437184 | tf_op jit(solution)/shard_map/pallas_call | solution.py:86
  53.8 9.0 %collective-permute-done.9.refs_8_ = bf16[768,1024]{1,0:T(8,128)(2,1)S(1)} collective-permute-done((bf16[768,1024]{1,0:T(8,128)(2,1)S(1)}, bf16[768,1024]{1,0:T(8,128)(2,1)S(1)}, u32[]{:S(2)}, u32[]{:S(2)}) %collective-permute-start.9) | collective-permute-done | bytes 1572896 | tf_op jit(solution)/shard_map/ppermute | solution.py:262
  64.3 3.1 %shard_map.134.total_ref = f32[512,1536]{1,0:T(8,128)S(1)} custom-call(bf16[64,1664]{1,0:T(8,128)(2,1)S(1)} %collective-permute-done.14.refs_0_, bf16[64,1664]{1,0:T(8,128)(2,1)S(1)} %collective-permute-done.16.refs_1_, bf16[64,1664]{1,0:T(8,128)(2,1)S(1)} %collective-permute-done.17.refs_2_, bf16[64,1664]{1,0:T(8,128)(2,1)S(1)} %collective-permute-done.19.refs_3_, ...), custom_call_target="tpu_custom_call" | custom-call | bytes 9437184 | tf_op jit(solution)/shard_map/pallas_call | solution.py:86
  67.5 2.1 %shard_map.136 = (bf16[512,512]{1,0:T(8,128)(2,1)S(1)}, f32[512,128]{1,0:T(8,128)S(1)}) custom-call(bf16[64,1664]{1,0:T(8,128)(2,1)S(1)} %collective-permute-done.14.refs_0_, bf16[64,1664]{1,0:T(8,128)(2,1)S(1)} %collective-permute-done.16.refs_1_, bf16[64,1664]{1,0:T(8,128)(2,1)S(1)} %collective-permute-done.17.refs_2_, ...), custom_call_target="tpu_custom_call" | custom-call | flops 1610612736 | bytes 4718592 | tf_op jit(solution)/shard_map/pallas_call | solution.py:86
  69.6 2.2 %shard_map.135 = (bf16[512,512]{1,0:T(8,128)(2,1)S(1)}, f32[512,128]{1,0:T(8,128)S(1)}) custom-call(bf16[64,1664]{1,0:T(8,128)(2,1)S(1)} %collective-permute-done.10.refs_0_, bf16[64,1664]{1,0:T(8,128)(2,1)S(1)} %collective-permute-done.11.refs_1_, bf16[64,1664]{1,0:T(8,128)(2,1)S(1)} %collective-permute-done.12.refs_2_, ...), custom_call_target="tpu_custom_call" | custom-call | flops 1610612736 | bytes 4718592 | tf_op jit(solution)/shard_map/pallas_call | solution.py:86
  71.8 2.5 %collective-permute-done.7.last_a = bf16[256,768]{1,0:T(8,128)(2,1)S(1)} collective-permute-done((bf16[256,768]{1,0:T(8,128)(2,1)S(1)}, bf16[256,768]{1,0:T(8,128)(2,1)S(1)}, u32[]{:S(2)}, u32[]{:S(2)}) %collective-permute-start.7) | collective-permute-done | bytes 393248 | tf_op jit(solution)/shard_map/ppermute | solution.py:262
  74.3 1.7 %collective-permute-done.21.last_b = bf16[256,768]{1,0:T(8,128)(2,1)S(1)} collective-permute-done((bf16[256,768]{1,0:T(8,128)(2,1)S(1)}, bf16[256,768]{1,0:T(8,128)(2,1)S(1)}, u32[]{:S(2)}, u32[]{:S(2)}) %collective-permute-start.21) | collective-permute-done | bytes 393248 | tf_op jit(solution)/shard_map/ppermute | solution.py:266
  77.0 1.6 %collective-permute-start.29 = (bf16[128,1536]{1,0:T(8,128)(2,1)S(1)}, bf16[128,1536]{1,0:T(8,128)(2,1)S(1)}, u32[]{:S(2)}, u32[]{:S(2)}) collective-permute-start(bf16[128,1536]{1,0:T(8,128)(2,1)S(1)} %get-tuple-element.123), channel_id=1, source_target_pairs={{0,2},{2,0},{4,6},{6,4},{8,10},{10,8},{12,14},{14,12},{16,18},{18,... | collective-permute-start | bytes 1179656 | tf_op jit(solution)/shard_map/ppermute | solution.py:262
  82.2 6.8 %collective-permute-done.29.got_ref = bf16[128,1536]{1,0:T(8,128)(2,1)S(1)} collective-permute-done((bf16[128,1536]{1,0:T(8,128)(2,1)S(1)}, bf16[128,1536]{1,0:T(8,128)(2,1)S(1)}, u32[]{:S(2)}, u32[]{:S(2)}) %collective-permute-start.29) | collective-permute-done | bytes 393248 | tf_op jit(solution)/shard_map/ppermute | solution.py:262
  89.1 1.6 %collective-permute-start.30 = (bf16[64,1536]{1,0:T(8,128)(2,1)S(1)}, bf16[64,1536]{1,0:T(8,128)(2,1)S(1)}, u32[]{:S(2)}, u32[]{:S(2)}) collective-permute-start(bf16[64,1536]{1,0:T(8,128)(2,1)S(1)} %get-tuple-element.125), channel_id=1, source_target_pairs={{0,4},{2,6},{4,0},{6,2},{8,12},{10,14},{12,8},{14,10},{16,20},{18,... | collective-permute-start | bytes 589832 | tf_op jit(solution)/shard_map/ppermute | solution.py:262
  90.8 1.6 %collective-permute-start.28 = (bf16[64,1536]{1,0:T(8,128)(2,1)S(1)}, bf16[64,1536]{1,0:T(8,128)(2,1)S(1)}, u32[]{:S(2)}, u32[]{:S(2)}) collective-permute-start(bf16[64,1536]{1,0:T(8,128)(2,1)S(1)} %get-tuple-element.121), channel_id=1, source_target_pairs={{0,2},{2,0},{4,6},{6,4},{8,10},{10,8},{12,14},{14,12},{16,18},{18,... | collective-permute-start | bytes 589832 | tf_op jit(solution)/shard_map/ppermute | solution.py:262
  92.4 5.1 %collective-permute-done.24.got_ref = bf16[128,1536]{1,0:T(8,128)(2,1)S(1)} collective-permute-done((bf16[128,1536]{1,0:T(8,128)(2,1)S(1)}, bf16[128,1536]{1,0:T(8,128)(2,1)S(1)}, u32[]{:S(2)}, u32[]{:S(2)}) %collective-permute-start.24) | collective-permute-done | bytes 393248 | tf_op jit(solution)/shard_map/ppermute | solution.py:262
  97.6 1.6 %collective-permute-start.25 = (bf16[64,1536]{1,0:T(8,128)(2,1)S(1)}, bf16[64,1536]{1,0:T(8,128)(2,1)S(1)}, u32[]{:S(2)}, u32[]{:S(2)}) collective-permute-start(bf16[64,1536]{1,0:T(8,128)(2,1)S(1)} %get-tuple-element.112), channel_id=1, source_target_pairs={{0,4},{2,6},{4,0},{6,2},{8,12},{10,14},{12,8},{14,10},{16,20},{18,... | collective-permute-start | bytes 589832 | tf_op jit(solution)/shard_map/ppermute | solution.py:262
  99.3 1.6 %collective-permute-start.23 = (bf16[64,1536]{1,0:T(8,128)(2,1)S(1)}, bf16[64,1536]{1,0:T(8,128)(2,1)S(1)}, u32[]{:S(2)}, u32[]{:S(2)}) collective-permute-start(bf16[64,1536]{1,0:T(8,128)(2,1)S(1)} %get-tuple-element.108), channel_id=1, source_target_pairs={{0,2},{2,0},{4,6},{6,4},{8,10},{10,8},{12,14},{14,12},{16,18},{18,... | collective-permute-start | bytes 589832 | tf_op jit(solution)/shard_map/ppermute | solution.py:262
  100.8 2.5 %collective-permute-done.30.got_b = bf16[64,1536]{1,0:T(8,128)(2,1)S(1)} collective-permute-done((bf16[64,1536]{1,0:T(8,128)(2,1)S(1)}, bf16[64,1536]{1,0:T(8,128)(2,1)S(1)}, u32[]{:S(2)}, u32[]{:S(2)}) %collective-permute-start.30) | collective-permute-done | bytes 196640 | tf_op jit(solution)/shard_map/ppermute | solution.py:262
  104.7 1.7 %collective-permute-done.25.got_b = bf16[64,1536]{1,0:T(8,128)(2,1)S(1)} collective-permute-done((bf16[64,1536]{1,0:T(8,128)(2,1)S(1)}, bf16[64,1536]{1,0:T(8,128)(2,1)S(1)}, u32[]{:S(2)}, u32[]{:S(2)}) %collective-permute-start.25) | collective-permute-done | bytes 196640 | tf_op jit(solution)/shard_map/ppermute | solution.py:262
  107.8 10.7 %collective-permute-done.31.got_ref = bf16[64,1536]{1,0:T(8,128)(2,1)S(1)} collective-permute-done((bf16[64,1536]{1,0:T(8,128)(2,1)S(1)}, bf16[64,1536]{1,0:T(8,128)(2,1)S(1)}, u32[]{:S(2)}, u32[]{:S(2)}) %collective-permute-start.31) | collective-permute-done | bytes 196640 | tf_op jit(solution)/shard_map/ppermute | solution.py:262
  119.2 2.5 %collective-permute-done.26.got_ref = bf16[64,1536]{1,0:T(8,128)(2,1)S(1)} collective-permute-done((bf16[64,1536]{1,0:T(8,128)(2,1)S(1)}, bf16[64,1536]{1,0:T(8,128)(2,1)S(1)}, u32[]{:S(2)}, u32[]{:S(2)}) %collective-permute-start.26) | collective-permute-done | bytes 196640 | tf_op jit(solution)/shard_map/ppermute | solution.py:262
  (79 shorter events, 21.3 us)
Async XLA Ops:
  3.9 16.9 %collective-permute-start.2 = (bf16[768,1024]{1,0:T(8,128)(2,1)}, bf16[768,1024]{1,0:T(8,128)(2,1)S(1)}, u32[]{:S(2)}, u32[]{:S(2)}) collective-permute-start(bf16[768,1024]{1,0:T(8,128)(2,1)} %get-tuple-element.74.refs_8_), channel_id=1, source_target_pairs={{0,1},{1,0},{2,3},{3,2},{4,5},{5,4},{6,7},{7,6},{8,9},{9,8},{10,11... | collective-permute-start | bytes 4718600 | tf_op jit(solution)/shard_map/ppermute | solution.py:266
  4.4 16.3 %collective-permute-start.3 = (bf16[512,768]{1,0:T(8,128)(2,1)S(1)}, bf16[512,768]{1,0:T(8,128)(2,1)S(1)}, u32[]{:S(2)}, u32[]{:S(2)}) collective-permute-start(bf16[512,768]{1,0:T(8,128)(2,1)S(1)} %bitcast.8), channel_id=1, source_target_pairs={{0,1},{1,0},{2,3},{3,2},{4,5},{5,4},{6,7},{7,6},{8,9},{9,8},{10,11... | collective-permute-start | bytes 2359304 | tf_op jit(solution)/shard_map/ppermute | solution.py:266
  6.0 14.8 %collective-permute-start.1 = (bf16[64,1664]{1,0:T(8,128)(2,1)S(1)}, bf16[64,1664]{1,0:T(8,128)(2,1)S(1)}, u32[]{:S(2)}, u32[]{:S(2)}) collective-permute-start(bf16[64,1664]{1,0:T(8,128)(2,1)S(1)} %get-tuple-element.67), channel_id=1, source_target_pairs={{0,16},{2,18},{4,20},{6,22},{8,24},{10,26},{12,28},{14,30},{16,0},... | collective-permute-start | bytes 638984 | tf_op jit(solution)/shard_map/ppermute | solution.py:262
  10.0 20.2 %collective-permute-start.6 = (bf16[256,768]{1,0:T(8,128)(2,1)}, bf16[256,768]{1,0:T(8,128)(2,1)S(1)}, u32[]{:S(2)}, u32[]{:S(2)}) collective-permute-start(bf16[256,768]{1,0:T(8,128)(2,1)} %get-tuple-element.70), channel_id=1, source_target_pairs={{0,8},{2,10},{4,12},{6,14},{8,0},{10,2},{12,4},{14,6},{16,24},{18,... | collective-permute-start | bytes 1179656 | tf_op jit(solution)/shard_map/ppermute | solution.py:262
  11.6 17.1 %collective-permute-start = (bf16[64,1664]{1,0:T(8,128)(2,1)S(1)}, bf16[64,1664]{1,0:T(8,128)(2,1)S(1)}, u32[]{:S(2)}, u32[]{:S(2)}) collective-permute-start(bf16[64,1664]{1,0:T(8,128)(2,1)S(1)} %get-tuple-element.66), channel_id=1, source_target_pairs={{0,16},{2,18},{4,20},{6,22},{8,24},{10,26},{12,28},{14,30},{16,0},... | collective-permute-start | bytes 638984 | tf_op jit(solution)/shard_map/ppermute | solution.py:262
  20.8 11.0 %collective-permute-start.5 = (bf16[64,1664]{1,0:T(8,128)(2,1)S(1)}, bf16[64,1664]{1,0:T(8,128)(2,1)S(1)}, u32[]{:S(2)}, u32[]{:S(2)}) collective-permute-start(bf16[64,1664]{1,0:T(8,128)(2,1)S(1)} %pad_maximum_fusion.1.refs_6_), channel_id=1, source_target_pairs={{0,4},{2,6},{4,0},{6,2},{8,12},{10,14},{12,8},{14,10},{16,20},{18,... | collective-permute-start | bytes 638984 | tf_op jit(solution)/shard_map/ppermute | solution.py:262
  22.8 40.0 %collective-permute-start.9 = (bf16[768,1024]{1,0:T(8,128)(2,1)S(1)}, bf16[768,1024]{1,0:T(8,128)(2,1)S(1)}, u32[]{:S(2)}, u32[]{:S(2)}) collective-permute-start(bf16[768,1024]{1,0:T(8,128)(2,1)S(1)} %copy-done.1), channel_id=1, source_target_pairs={{0,8},{2,10},{4,12},{6,14},{8,0},{10,2},{12,4},{14,6},{16,24},{18,... | collective-permute-start | bytes 4718600 | tf_op jit(solution)/shard_map/ppermute | solution.py:262
  22.8 9.0 %collective-permute-start.4 = (bf16[64,1664]{1,0:T(8,128)(2,1)S(1)}, bf16[64,1664]{1,0:T(8,128)(2,1)S(1)}, u32[]{:S(2)}, u32[]{:S(2)}) collective-permute-start(bf16[64,1664]{1,0:T(8,128)(2,1)S(1)} %pad_maximum_fusion.refs_4_), channel_id=1, source_target_pairs={{0,2},{2,0},{4,6},{6,4},{8,10},{10,8},{12,14},{14,12},{16,18},{18,... | collective-permute-start | bytes 638984 | tf_op jit(solution)/shard_map/ppermute | solution.py:262
  28.8 8.0 %collective-permute-start.12 = (bf16[64,1664]{1,0:T(8,128)(2,1)S(1)}, bf16[64,1664]{1,0:T(8,128)(2,1)S(1)}, u32[]{:S(2)}, u32[]{:S(2)}) collective-permute-start(bf16[64,1664]{1,0:T(8,128)(2,1)S(1)} %pad_maximum_fusion.1.refs_6_), channel_id=1, source_target_pairs={{0,2},{2,0},{4,6},{6,4},{8,10},{10,8},{12,14},{14,12},{16,18},{18,... | collective-permute-start | bytes 638984 | tf_op jit(solution)/shard_map/ppermute | solution.py:262
  30.3 8.2 %collective-permute-start.10 = (bf16[64,1664]{1,0:T(8,128)(2,1)S(1)}, bf16[64,1664]{1,0:T(8,128)(2,1)S(1)}, u32[]{:S(2)}, u32[]{:S(2)}) collective-permute-start(bf16[64,1664]{1,0:T(8,128)(2,1)S(1)} %pad_maximum_fusion.refs_4_), channel_id=1, source_target_pairs={{0,4},{2,6},{4,0},{6,2},{8,12},{10,14},{12,8},{14,10},{16,20},{18,... | collective-permute-start | bytes 638984 | tf_op jit(solution)/shard_map/ppermute | solution.py:262
  31.8 11.2 %collective-permute-start.11 = (bf16[64,1664]{1,0:T(8,128)(2,1)S(1)}, bf16[64,1664]{1,0:T(8,128)(2,1)S(1)}, u32[]{:S(2)}, u32[]{:S(2)}) collective-permute-start(bf16[64,1664]{1,0:T(8,128)(2,1)S(1)} %collective-permute-done.4.refs_5_), channel_id=1, source_target_pairs={{0,4},{2,6},{4,0},{6,2},{8,12},{10,14},{12,8},{14,10},{16,20},{18,... | collective-permute-start | bytes 638984 | tf_op jit(solution)/shard_map/ppermute | solution.py:262
  32.3 12.3 %collective-permute-start.13 = (bf16[64,1664]{1,0:T(8,128)(2,1)S(1)}, bf16[64,1664]{1,0:T(8,128)(2,1)S(1)}, u32[]{:S(2)}, u32[]{:S(2)}) collective-permute-start(bf16[64,1664]{1,0:T(8,128)(2,1)S(1)} %collective-permute-done.5.refs_7_), channel_id=1, source_target_pairs={{0,2},{2,0},{4,6},{6,4},{8,10},{10,8},{12,14},{14,12},{16,18},{18,... | collective-permute-start | bytes 638984 | tf_op jit(solution)/shard_map/ppermute | solution.py:262
  36.8 9.3 %collective-permute-start.15 = (bf16[64,1664]{1,0:T(8,128)(2,1)S(1)}, bf16[64,1664]{1,0:T(8,128)(2,1)S(1)}, u32[]{:S(2)}, u32[]{:S(2)}) collective-permute-start(bf16[64,1664]{1,0:T(8,128)(2,1)S(1)} %pad_maximum_fusion.2.refs_4_), channel_id=1, source_target_pairs={{0,2},{2,0},{4,6},{6,4},{8,10},{10,8},{12,14},{14,12},{16,18},{18,... | collective-permute-start | bytes 638984 | tf_op jit(solution)/shard_map/ppermute | solution.py:262
  38.4 9.1 %collective-permute-start.18 = (bf16[64,1664]{1,0:T(8,128)(2,1)S(1)}, bf16[64,1664]{1,0:T(8,128)(2,1)S(1)}, u32[]{:S(2)}, u32[]{:S(2)}) collective-permute-start(bf16[64,1664]{1,0:T(8,128)(2,1)S(1)} %pad_maximum_fusion.3.refs_6_), channel_id=1, source_target_pairs={{0,4},{2,6},{4,0},{6,2},{8,12},{10,14},{12,8},{14,10},{16,20},{18,... | collective-permute-start | bytes 638984 | tf_op jit(solution)/shard_map/ppermute | solution.py:262
  43.0 9.2 %collective-permute-start.14 = (bf16[64,1664]{1,0:T(8,128)(2,1)S(1)}, bf16[64,1664]{1,0:T(8,128)(2,1)S(1)}, u32[]{:S(2)}, u32[]{:S(2)}) collective-permute-start(bf16[64,1664]{1,0:T(8,128)(2,1)S(1)} %pad_maximum_fusion.2.refs_4_), channel_id=1, source_target_pairs={{0,4},{2,6},{4,0},{6,2},{8,12},{10,14},{12,8},{14,10},{16,20},{18,... | collective-permute-start | bytes 638984 | tf_op jit(solution)/shard_map/ppermute | solution.py:262
  44.6 7.7 %collective-permute-start.17 = (bf16[64,1664]{1,0:T(8,128)(2,1)S(1)}, bf16[64,1664]{1,0:T(8,128)(2,1)S(1)}, u32[]{:S(2)}, u32[]{:S(2)}) collective-permute-start(bf16[64,1664]{1,0:T(8,128)(2,1)S(1)} %pad_maximum_fusion.3.refs_6_), channel_id=1, source_target_pairs={{0,2},{2,0},{4,6},{6,4},{8,10},{10,8},{12,14},{14,12},{16,18},{18,... | collective-permute-start | bytes 638984 | tf_op jit(solution)/shard_map/ppermute | solution.py:262
  46.1 7.7 %collective-permute-start.16 = (bf16[64,1664]{1,0:T(8,128)(2,1)S(1)}, bf16[64,1664]{1,0:T(8,128)(2,1)S(1)}, u32[]{:S(2)}, u32[]{:S(2)}) collective-permute-start(bf16[64,1664]{1,0:T(8,128)(2,1)S(1)} %collective-permute-done.15.refs_5_), channel_id=1, source_target_pairs={{0,4},{2,6},{4,0},{6,2},{8,12},{10,14},{12,8},{14,10},{16,20},{18,... | collective-permute-start | bytes 638984 | tf_op jit(solution)/shard_map/ppermute | solution.py:262
  47.6 6.2 %collective-permute-start.19 = (bf16[64,1664]{1,0:T(8,128)(2,1)S(1)}, bf16[64,1664]{1,0:T(8,128)(2,1)S(1)}, u32[]{:S(2)}, u32[]{:S(2)}) collective-permute-start(bf16[64,1664]{1,0:T(8,128)(2,1)S(1)} %collective-permute-done.18.refs_7_), channel_id=1, source_target_pairs={{0,2},{2,0},{4,6},{6,4},{8,10},{10,8},{12,14},{14,12},{16,18},{18,... | collective-permute-start | bytes 638984 | tf_op jit(solution)/shard_map/ppermute | solution.py:262
  62.8 4.7 %collective-permute-start.20 = (bf16[768,1024]{1,0:T(8,128)(2,1)S(1)}, bf16[768,1024]{1,0:T(8,128)(2,1)S(1)}, u32[]{:S(2)}, u32[]{:S(2)}) collective-permute-start(bf16[768,1024]{1,0:T(8,128)(2,1)S(1)} %collective-permute-done.9.refs_8_), channel_id=1, source_target_pairs={{0,1},{1,0},{2,3},{3,2},{4,5},{5,4},{6,7},{7,6},{8,9},{9,8},{10,11... | collective-permute-start | bytes 4718600 | tf_op jit(solution)/shard_map/ppermute | solution.py:266
  62.8 11.5 %collective-permute-start.7 = (bf16[256,768]{1,0:T(8,128)(2,1)S(1)}, bf16[256,768]{1,0:T(8,128)(2,1)S(1)}, u32[]{:S(2)}, u32[]{:S(2)}) collective-permute-start(bf16[256,768]{1,0:T(8,128)(2,1)S(1)} %copy-done.11), channel_id=1, source_target_pairs={{0,8},{2,10},{4,12},{6,14},{8,0},{10,2},{12,4},{14,6},{16,24},{18,... | collective-permute-start | bytes 1179656 | tf_op jit(solution)/shard_map/ppermute | solution.py:262
  64.1 10.2 %collective-permute-start.8 = (bf16[256,768]{1,0:T(8,128)(2,1)S(1)}, bf16[256,768]{1,0:T(8,128)(2,1)S(1)}, u32[]{:S(2)}, u32[]{:S(2)}) collective-permute-start(bf16[256,768]{1,0:T(8,128)(2,1)S(1)} %collective-permute-done.6.first_a), channel_id=1, source_target_pairs={{0,1},{1,0},{2,3},{3,2},{4,5},{5,4},{6,7},{7,6},{8,9},{9,8},{10,11... | collective-permute-start | bytes 1179656 | tf_op jit(solution)/shard_map/ppermute | solution.py:266
  74.3 1.7 %collective-permute-start.21 = (bf16[256,768]{1,0:T(8,128)(2,1)S(1)}, bf16[256,768]{1,0:T(8,128)(2,1)S(1)}, u32[]{:S(2)}, u32[]{:S(2)}) collective-permute-start(bf16[256,768]{1,0:T(8,128)(2,1)S(1)} %collective-permute-done.7.last_a), channel_id=1, source_target_pairs={{0,1},{1,0},{2,3},{3,2},{4,5},{5,4},{6,7},{7,6},{8,9},{9,8},{10,11... | collective-permute-start | bytes 1179656 | tf_op jit(solution)/shard_map/ppermute | solution.py:266
  77.0 12.0 %collective-permute-start.29 = (bf16[128,1536]{1,0:T(8,128)(2,1)S(1)}, bf16[128,1536]{1,0:T(8,128)(2,1)S(1)}, u32[]{:S(2)}, u32[]{:S(2)}) collective-permute-start(bf16[128,1536]{1,0:T(8,128)(2,1)S(1)} %get-tuple-element.123), channel_id=1, source_target_pairs={{0,2},{2,0},{4,6},{6,4},{8,10},{10,8},{12,14},{14,12},{16,18},{18,... | collective-permute-start | bytes 1179656 | tf_op jit(solution)/shard_map/ppermute | solution.py:262
  78.6 12.1 %collective-permute-start.27 = (bf16[128,1536]{1,0:T(8,128)(2,1)S(1)}, bf16[128,1536]{1,0:T(8,128)(2,1)S(1)}, u32[]{:S(2)}, u32[]{:S(2)}) collective-permute-start(bf16[128,1536]{1,0:T(8,128)(2,1)S(1)} %get-tuple-element.119), channel_id=1, source_target_pairs={{0,4},{2,6},{4,0},{6,2},{8,12},{10,14},{12,8},{14,10},{16,20},{18,... | collective-permute-start | bytes 1179656 | tf_op jit(solution)/shard_map/ppermute | solution.py:262
  81.2 16.3 %collective-permute-start.24 = (bf16[128,1536]{1,0:T(8,128)(2,1)S(1)}, bf16[128,1536]{1,0:T(8,128)(2,1)S(1)}, u32[]{:S(2)}, u32[]{:S(2)}) collective-permute-start(bf16[128,1536]{1,0:T(8,128)(2,1)S(1)} %get-tuple-element.110), channel_id=1, source_target_pairs={{0,2},{2,0},{4,6},{6,4},{8,10},{10,8},{12,14},{14,12},{16,18},{18,... | collective-permute-start | bytes 1179656 | tf_op jit(solution)/shard_map/ppermute | solution.py:262
  81.8 17.4 %collective-permute-start.22 = (bf16[128,1536]{1,0:T(8,128)(2,1)S(1)}, bf16[128,1536]{1,0:T(8,128)(2,1)S(1)}, u32[]{:S(2)}, u32[]{:S(2)}) collective-permute-start(bf16[128,1536]{1,0:T(8,128)(2,1)S(1)} %get-tuple-element.106), channel_id=1, source_target_pairs={{0,4},{2,6},{4,0},{6,2},{8,12},{10,14},{12,8},{14,10},{16,20},{18,... | collective-permute-start | bytes 1179656 | tf_op jit(solution)/shard_map/ppermute | solution.py:262
  89.1 14.1 %collective-permute-start.30 = (bf16[64,1536]{1,0:T(8,128)(2,1)S(1)}, bf16[64,1536]{1,0:T(8,128)(2,1)S(1)}, u32[]{:S(2)}, u32[]{:S(2)}) collective-permute-start(bf16[64,1536]{1,0:T(8,128)(2,1)S(1)} %get-tuple-element.125), channel_id=1, source_target_pairs={{0,4},{2,6},{4,0},{6,2},{8,12},{10,14},{12,8},{14,10},{16,20},{18,... | collective-permute-start | bytes 589832 | tf_op jit(solution)/shard_map/ppermute | solution.py:262
  90.8 12.4 %collective-permute-start.28 = (bf16[64,1536]{1,0:T(8,128)(2,1)S(1)}, bf16[64,1536]{1,0:T(8,128)(2,1)S(1)}, u32[]{:S(2)}, u32[]{:S(2)}) collective-permute-start(bf16[64,1536]{1,0:T(8,128)(2,1)S(1)} %get-tuple-element.121), channel_id=1, source_target_pairs={{0,2},{2,0},{4,6},{6,4},{8,10},{10,8},{12,14},{14,12},{16,18},{18,... | collective-permute-start | bytes 589832 | tf_op jit(solution)/shard_map/ppermute | solution.py:262
  97.6 8.8 %collective-permute-start.25 = (bf16[64,1536]{1,0:T(8,128)(2,1)S(1)}, bf16[64,1536]{1,0:T(8,128)(2,1)S(1)}, u32[]{:S(2)}, u32[]{:S(2)}) collective-permute-start(bf16[64,1536]{1,0:T(8,128)(2,1)S(1)} %get-tuple-element.112), channel_id=1, source_target_pairs={{0,4},{2,6},{4,0},{6,2},{8,12},{10,14},{12,8},{14,10},{16,20},{18,... | collective-permute-start | bytes 589832 | tf_op jit(solution)/shard_map/ppermute | solution.py:262
  99.3 7.1 %collective-permute-start.23 = (bf16[64,1536]{1,0:T(8,128)(2,1)S(1)}, bf16[64,1536]{1,0:T(8,128)(2,1)S(1)}, u32[]{:S(2)}, u32[]{:S(2)}) collective-permute-start(bf16[64,1536]{1,0:T(8,128)(2,1)S(1)} %get-tuple-element.108), channel_id=1, source_target_pairs={{0,2},{2,0},{4,6},{6,4},{8,10},{10,8},{12,14},{14,12},{16,18},{18,... | collective-permute-start | bytes 589832 | tf_op jit(solution)/shard_map/ppermute | solution.py:262
  103.3 15.1 %collective-permute-start.31 = (bf16[64,1536]{1,0:T(8,128)(2,1)S(1)}, bf16[64,1536]{1,0:T(8,128)(2,1)S(1)}, u32[]{:S(2)}, u32[]{:S(2)}) collective-permute-start(bf16[64,1536]{1,0:T(8,128)(2,1)S(1)} %get-tuple-element.127), channel_id=1, source_target_pairs={{0,16},{2,18},{4,20},{6,22},{8,24},{10,26},{12,28},{14,30},{16,0},... | collective-permute-start | bytes 589832 | tf_op jit(solution)/shard_map/ppermute | solution.py:262
  106.4 15.2 %collective-permute-start.26 = (bf16[64,1536]{1,0:T(8,128)(2,1)S(1)}, bf16[64,1536]{1,0:T(8,128)(2,1)S(1)}, u32[]{:S(2)}, u32[]{:S(2)}) collective-permute-start(bf16[64,1536]{1,0:T(8,128)(2,1)S(1)} %get-tuple-element.114), channel_id=1, source_target_pairs={{0,16},{2,18},{4,20},{6,22},{8,24},{10,26},{12,28},{14,30},{16,0},... | collective-permute-start | bytes 589832 | tf_op jit(solution)/shard_map/ppermute | solution.py:262
  (12 other events, 86.2 us)

commit v12 on v11

--- a/solution.py
+++ b/solution.py
@@ -219,24 +219,35 @@
         weight_ref[pl.ds(begin, block), :] = jnp.broadcast_to(weight, (block, PACK))
 
 
-def join_kernel(
-    hidden_ref, weight_ref, total_ref, first_a, last_a, first_b, last_b, send_a, send_b, keep_a, keep_b
-):
+def join_kernel(hidden_ref, weight_ref, total_ref, first_a, last_a, first_b, last_b, *outs):
     place = lax.axis_index("tensor")
-    count = send_a.shape[0]
     inner, width = first_a.shape
-    for pair, outs in ((0, (send_a, send_b)), (1, (keep_a, keep_b))):
-        rows = slice(pair * 2 * count, (pair + 1) * 2 * count)
+    per, count = len(outs) // 2, outs[0].shape[0]
+    for part in range(2):
+        rows = slice(part * per * count, (part + 1) * per * count)
         weight = weight_ref[rows, :1]
         for which, (first, last) in enumerate(((first_a, last_a), (first_b, last_b))):
             half = place if which == 0 else 1 - place
             columns = pl.ds(pl.multiple_of(half * width, width), width)
-            part = jnp.dot(
+            result = jnp.dot(
                 hidden_ref[rows, :inner], first[...], preferred_element_type=jnp.float32
             ) + jnp.dot(hidden_ref[rows, inner:], last[...], preferred_element_type=jnp.float32)
-            part = part * weight + total_ref[rows, columns]
-            outs[0][:, columns] = part[:count].astype(outs[0].dtype)
-            outs[1][:, columns] = part[count:].astype(outs[1].dtype)
+            result = result * weight + total_ref[rows, columns]
+            for i, out in enumerate(outs[per * part : per * (part + 1)]):
+                out[:, columns] = result[i * count : (i + 1) * count].astype(out.dtype)
+
+
+def part_sum_kernel(keep_ref, got_ref, send_ref):
+    send_ref[...] = (keep_ref[...] + got_ref[...].astype(jnp.float32)).astype(jnp.bfloat16)
+
+
+def three_sum_kernel(keep_a, got_a, far_a, keep_b, got_b, far_b, send_ref, held_ref):
+    half = keep_a.shape[0] // 2
+    for i, (keep, got, far) in enumerate(((keep_a, got_a, far_a), (keep_b, got_b, far_b))):
+        rows = slice(i * half, (i + 1) * half)
+        total = keep[...] + got[...].astype(jnp.float32) + far[...].astype(jnp.float32)
+        held_ref[rows, :] = total[:half]
+        send_ref[rows, :] = total[half:].astype(jnp.bfloat16)
 
 
 def first_sum_kernel(keep_ref, got_ref, send_ref, held_ref):
@@ -274,34 +285,38 @@
 def spread(a1, b1, a2, b2):
     a3, b3 = swap(a1, Y), swap(b1, X)
     a4, b4 = swap(a2, Y), swap(b2, X)
-    return [a3, a4, b3, b4, a1, a2, b1, b2]
-
-
-def first_return(send_a, send_b, keep_a, keep_b):
-    quarter, width = keep_a.shape[0] // 2, keep_a.shape[1]
-    outs = (
-        jax.ShapeDtypeStruct((quarter, width), jnp.bfloat16),
-        jax.ShapeDtypeStruct((quarter, width), jnp.float32),
-    )
-    size = quarter * width
+    return a1, b1, a2, b2, a3, b3, a4, b4
+
+
+def send_back(one, two):
+    send_a, send_b, keep_a, keep_b = one
+    a4, b4, a3, b3, a2, b2, a1, b1 = two
+    half = jax.ShapeDtypeStruct(a1.shape, jnp.bfloat16)
+    held = jax.ShapeDtypeStruct(a1.shape, jnp.float32)
+    size = a1.size
     got_a, got_b = swap(send_a, Y), swap(send_b, X)
-    next_a, held_a = call(first_sum_kernel, outs, (keep_a, got_a), 8, size, 18 * size)
-    next_b, held_b = call(first_sum_kernel, outs, (keep_b, got_b), 8, size, 18 * size)
-    return next_a, next_b, held_a, held_b
-
-
-def last_returns(next_a, next_b, held_a, held_b):
-    outs = (
-        jax.ShapeDtypeStruct(held_a.shape, jnp.bfloat16),
-        jax.ShapeDtypeStruct(held_a.shape, jnp.float32),
-    )
-    size = held_a.size
-    got_a, got_b = swap(next_a, X), swap(next_b, Y)
+    got_a4, got_b4 = swap(a4, Y), swap(b4, X)
+    next_a, held_a = call(first_sum_kernel, (half, held), (keep_a, got_a), 8, size, 18 * size)
+    next_b, held_b = call(first_sum_kernel, (half, held), (keep_b, got_b), 8, size, 18 * size)
+    next_a, next_b, a2, b2, a3, b3 = lax.optimization_barrier((next_a, next_b, a2, b2, a3, b3))
+    far_a, far_b = swap(next_a, X), swap(next_b, Y)
     next_z, held_z = call(
-        second_sum_kernel, outs, (held_a, got_a, held_b, got_b), 8, size, 18 * size
-    )
+        second_sum_kernel, (half, held), (held_a, far_a, held_b, far_b), 8, size, 18 * size
+    )
+    next_a2 = call(part_sum_kernel, half, (a2, got_a4), 4, size, 8 * size)
+    next_b2 = call(part_sum_kernel, half, (b2, got_b4), 4, size, 8 * size)
+    got_a3, got_b3 = swap(a3, Y), swap(b3, X)
+    far_a2, far_b2 = swap(next_a2, X), swap(next_b2, Y)
     got_z = swap(next_z, Z_HIGH)
-    return call(last_sum_kernel, outs[0], (held_z, got_z), 8, size, 8 * size)
+    got_z, far_a2, far_b2 = lax.optimization_barrier((got_z, far_a2, far_b2))
+    next_z2, held_z2 = call(
+        three_sum_kernel, (half, held), (a1, got_a3, far_a2, b1, got_b3, far_b2), 8, size, 22 * size
+    )
+    got_z2 = swap(next_z2, Z_HIGH)
+    return (
+        call(last_sum_kernel, half, (held_z, got_z), 4, size, 8 * size),
+        call(last_sum_kernel, half, (held_z2, got_z2), 4, size, 8 * size),
+    )
 
 
 def local_pairs(
@@ -359,7 +374,10 @@
     far[1], second_one, by_first = lax.optimization_barrier((far[1], second_one, by_first))
     first_two = halves(own[1], far[1])
     second_two = swap(first_two[0], X), swap(first_two[1], Y)
-    pieces = [spread(*first_one, *second_one), spread(*first_two, *second_two)]
+    a1, b1, a2, b2, a3, b3, a4, b4 = spread(*first_one, *second_one)
+    pieces_one = [a3, a4, b3, b4, a1, a2, b1, b2]
+    a1, b1, a2, b2, a3, b3, a4, b4 = spread(*first_two, *second_two)
+    pieces = [pieces_one, [a4, b4, a3, b3, a2, b2, a1, b1]]
 
     rows = 8 * tok
     scratch = (pltpu.VMEM((rows, width + PACK), jnp.bfloat16),)
@@ -389,11 +407,12 @@
             scratch,
         )
 
-    def join(total, hid, weight):
+    def join(total, hid, weight, per):
+        count = rows // 2 // per
         return call(
             join_kernel,
-            (jax.ShapeDtypeStruct((2 * tok, width), jnp.bfloat16),) * 2
-            + (jax.ShapeDtypeStruct((2 * tok, width), jnp.float32),) * 2,
+            (jax.ShapeDtypeStruct((count, width), jnp.bfloat16),) * per
+            + (jax.ShapeDtypeStruct((count, width), jnp.float32),) * per,
             (hid, weight, total, *down_by),
             14,
             2 * rows * width * ff,
@@ -412,9 +431,7 @@
         (by_last, twin_first, total_two, hidden_one, hidden_two)
     )
     down_by = (by_first, by_last, twin_first, swap_core(by_last))
-    back_one = first_return(*join(total_one, *hidden_one))
-    back_two = first_return(*join(total_two, *hidden_two))
-    return last_returns(*back_one), last_returns(*back_two)
+    return send_back(join(total_one, *hidden_one, 2), join(total_two, *hidden_two, 4))
 
 
 def solution(mesh):

time: 122 us -> 120 us (0.984)
  waiting for transfers between devices: 63.2 us -> 59.9 us
    ppermute x27 -> x29, waiting for transfers between devices: 61.4 us -> 58.1 us  [swap(): lax.ppermute(block, 'expert', [(i, i ^ distance) for i in range(count)])]
    ppermute x27 -> x29, starting transfers between devices: 38.3 us -> 39.3 us  [swap(): lax.ppermute(block, 'expert', [(i, i ^ distance) for i in range(count)])]
  transfers between devices with their start and end apart: 32 -> 34, of which waited for: 16 -> 17; matrix products, arithmetic and copies ran while one was open for 0% -> 0% of each run, Pallas kernels for 11% -> 12%
where the time goes in v12:
time: 120 us
  waiting for transfers between devices  59.9 us (50%)
  starting transfers between devices  40.1 us (33%)
  Pallas kernels  18.9 us (16%)
    ppermute x29, waiting for transfers between devices, swap(): lax.ppermute(block, 'expert', [(i, i ^ distance) for i in range(count)])  58.1 us
    ppermute x29, starting transfers between devices, swap(): lax.ppermute(block, 'expert', [(i, i ^ distance) for i in range(count)])  39.3 us
    pallas_call x16, Pallas kernels, call(): pl.pallas_call(body, out_shape=outs, in_specs=specs or [smem if x.ndim ==...  18.9 us
  transfers between devices with their start and end apart: 34, of which 17 were waited for; matrix products, arithmetic and copies ran while one was open for 0% of the time, Pallas kernels for 12%

profile of v12, /device:TPU:0, one launch (start us, length us, event | category | flops | bytes accessed | tf_op | source)
XLA Modules:
  0.0 120.1 jit_solution(774779519200200766)
XLA Ops:
  0.7 3.2 %shard_map.131 = (bf16[768,1024]{1,0:T(8,128)(2,1)}, bf16[256,768]{1,0:T(8,128)(2,1)}, bf16[256,768]{1,0:T(8,128)(2,1)}) custom-call(bf16[768,512]{1,0:T(8,128)(2,1)} %bitcast.15, bf16[768,512]{1,0:T(8,128)(2,1)} %bitcast.16, bf16[512,768]{1,0:T(8,128)(2,1)} %bitcast.7), custom_call_target="tpu_custom_call" | custom-call | bytes 4718592 | tf_op jit(solution)/shard_map/pallas_call | solution.py:86
  6.0 4.1 %collective-permute-start.1 = (bf16[64,1664]{1,0:T(8,128)(2,1)S(1)}, bf16[64,1664]{1,0:T(8,128)(2,1)S(1)}, u32[]{:S(2)}, u32[]{:S(2)}) collective-permute-start(bf16[64,1664]{1,0:T(8,128)(2,1)S(1)} %get-tuple-element.76), channel_id=1, source_target_pairs={{0,16},{2,18},{4,20},{6,22},{8,24},{10,26},{12,28},{14,30},{16,0},... | collective-permute-start | bytes 638984 | tf_op jit(solution)/shard_map/ppermute | solution.py:273
  10.0 1.6 %collective-permute-start.6 = (bf16[256,768]{1,0:T(8,128)(2,1)}, bf16[256,768]{1,0:T(8,128)(2,1)S(1)}, u32[]{:S(2)}, u32[]{:S(2)}) collective-permute-start(bf16[256,768]{1,0:T(8,128)(2,1)} %get-tuple-element.79), channel_id=1, source_target_pairs={{0,8},{2,10},{4,12},{6,14},{8,0},{10,2},{12,4},{14,6},{16,24},{18,... | collective-permute-start | bytes 1179656 | tf_op jit(solution)/shard_map/ppermute | solution.py:273
  12.0 8.8 %collective-permute-done.1 = bf16[64,1664]{1,0:T(8,128)(2,1)S(1)} collective-permute-done((bf16[64,1664]{1,0:T(8,128)(2,1)S(1)}, bf16[64,1664]{1,0:T(8,128)(2,1)S(1)}, u32[]{:S(2)}, u32[]{:S(2)}) %collective-permute-start.1) | collective-permute-done | bytes 213024 | tf_op jit(solution)/shard_map/ppermute | solution.py:273
  20.8 2.0 %collective-permute-start.5 = (bf16[64,1664]{1,0:T(8,128)(2,1)S(1)}, bf16[64,1664]{1,0:T(8,128)(2,1)S(1)}, u32[]{:S(2)}, u32[]{:S(2)}) collective-permute-start(bf16[64,1664]{1,0:T(8,128)(2,1)S(1)} %pad_maximum_fusion.1.refs_6_), channel_id=1, source_target_pairs={{0,4},{2,6},{4,0},{6,2},{8,12},{10,14},{12,8},{14,10},{16,20},{18,... | collective-permute-start | bytes 638984 | tf_op jit(solution)/shard_map/ppermute | solution.py:273
  22.8 1.6 %collective-permute-start.4 = (bf16[64,1664]{1,0:T(8,128)(2,1)S(1)}, bf16[64,1664]{1,0:T(8,128)(2,1)S(1)}, u32[]{:S(2)}, u32[]{:S(2)}) collective-permute-start(bf16[64,1664]{1,0:T(8,128)(2,1)S(1)} %pad_maximum_fusion.refs_4_), channel_id=1, source_target_pairs={{0,2},{2,0},{4,6},{6,4},{8,10},{10,8},{12,14},{14,12},{16,18},{18,... | collective-permute-start | bytes 638984 | tf_op jit(solution)/shard_map/ppermute | solution.py:273
  24.4 4.4 %collective-permute-done = bf16[64,1664]{1,0:T(8,128)(2,1)S(1)} collective-permute-done((bf16[64,1664]{1,0:T(8,128)(2,1)S(1)}, bf16[64,1664]{1,0:T(8,128)(2,1)S(1)}, u32[]{:S(2)}, u32[]{:S(2)}) %collective-permute-start) | collective-permute-done | bytes 213024 | tf_op jit(solution)/shard_map/ppermute | solution.py:273
  30.3 1.6 %collective-permute-start.10 = (bf16[64,1664]{1,0:T(8,128)(2,1)S(1)}, bf16[64,1664]{1,0:T(8,128)(2,1)S(1)}, u32[]{:S(2)}, u32[]{:S(2)}) collective-permute-start(bf16[64,1664]{1,0:T(8,128)(2,1)S(1)} %pad_maximum_fusion.refs_4_), channel_id=1, source_target_pairs={{0,4},{2,6},{4,0},{6,2},{8,12},{10,14},{12,8},{14,10},{16,20},{18,... | collective-permute-start | bytes 638984 | tf_op jit(solution)/shard_map/ppermute | solution.py:273
  32.3 1.5 %collective-permute-start.13 = (bf16[64,1664]{1,0:T(8,128)(2,1)S(1)}, bf16[64,1664]{1,0:T(8,128)(2,1)S(1)}, u32[]{:S(2)}, u32[]{:S(2)}) collective-permute-start(bf16[64,1664]{1,0:T(8,128)(2,1)S(1)} %collective-permute-done.5.refs_7_), channel_id=1, source_target_pairs={{0,2},{2,0},{4,6},{6,4},{8,10},{10,8},{12,14},{14,12},{16,18},{18,... | collective-permute-start | bytes 638984 | tf_op jit(solution)/shard_map/ppermute | solution.py:273
  33.9 2.9 %collective-permute-done.12.refs_2_ = bf16[64,1664]{1,0:T(8,128)(2,1)S(1)} collective-permute-done((bf16[64,1664]{1,0:T(8,128)(2,1)S(1)}, bf16[64,1664]{1,0:T(8,128)(2,1)S(1)}, u32[]{:S(2)}, u32[]{:S(2)}) %collective-permute-start.12) | collective-permute-done | bytes 213024 | tf_op jit(solution)/shard_map/ppermute | solution.py:273
  36.8 1.6 %collective-permute-start.14 = (bf16[64,1664]{1,0:T(8,128)(2,1)S(1)}, bf16[64,1664]{1,0:T(8,128)(2,1)S(1)}, u32[]{:S(2)}, u32[]{:S(2)}) collective-permute-start(bf16[64,1664]{1,0:T(8,128)(2,1)S(1)} %pad_maximum_fusion.2.refs_6_), channel_id=1, source_target_pairs={{0,2},{2,0},{4,6},{6,4},{8,10},{10,8},{12,14},{14,12},{16,18},{18,... | collective-permute-start | bytes 638984 | tf_op jit(solution)/shard_map/ppermute | solution.py:273
  38.4 1.6 %collective-permute-start.16 = (bf16[64,1664]{1,0:T(8,128)(2,1)S(1)}, bf16[64,1664]{1,0:T(8,128)(2,1)S(1)}, u32[]{:S(2)}, u32[]{:S(2)}) collective-permute-start(bf16[64,1664]{1,0:T(8,128)(2,1)S(1)} %pad_maximum_fusion.3.refs_7_), channel_id=1, source_target_pairs={{0,4},{2,6},{4,0},{6,2},{8,12},{10,14},{12,8},{14,10},{16,20},{18,... | collective-permute-start | bytes 638984 | tf_op jit(solution)/shard_map/ppermute | solution.py:273
  40.0 3.0 %collective-permute-done.11.refs_1_ = bf16[64,1664]{1,0:T(8,128)(2,1)S(1)} collective-permute-done((bf16[64,1664]{1,0:T(8,128)(2,1)S(1)}, bf16[64,1664]{1,0:T(8,128)(2,1)S(1)}, u32[]{:S(2)}, u32[]{:S(2)}) %collective-permute-start.11) | collective-permute-done | bytes 213024 | tf_op jit(solution)/shard_map/ppermute | solution.py:273
  43.0 1.6 %collective-permute-start.18 = (bf16[64,1664]{1,0:T(8,128)(2,1)S(1)}, bf16[64,1664]{1,0:T(8,128)(2,1)S(1)}, u32[]{:S(2)}, u32[]{:S(2)}) collective-permute-start(bf16[64,1664]{1,0:T(8,128)(2,1)S(1)} %pad_maximum_fusion.2.refs_6_), channel_id=1, source_target_pairs={{0,4},{2,6},{4,0},{6,2},{8,12},{10,14},{12,8},{14,10},{16,20},{18,... | collective-permute-start | bytes 638984 | tf_op jit(solution)/shard_map/ppermute | solution.py:273
  47.6 1.5 %collective-permute-start.17 = (bf16[64,1664]{1,0:T(8,128)(2,1)S(1)}, bf16[64,1664]{1,0:T(8,128)(2,1)S(1)}, u32[]{:S(2)}, u32[]{:S(2)}) collective-permute-start(bf16[64,1664]{1,0:T(8,128)(2,1)S(1)} %collective-permute-done.16.refs_5_), channel_id=1, source_target_pairs={{0,2},{2,0},{4,6},{6,4},{8,10},{10,8},{12,14},{14,12},{16,18},{18,... | collective-permute-start | bytes 638984 | tf_op jit(solution)/shard_map/ppermute | solution.py:273
  49.1 3.1 %shard_map.133.total_ref = f32[512,1536]{1,0:T(8,128)S(1)} custom-call(bf16[64,1664]{1,0:T(8,128)(2,1)S(1)} %collective-permute-done.10.refs_0_, bf16[64,1664]{1,0:T(8,128)(2,1)S(1)} %collective-permute-done.11.refs_1_, bf16[64,1664]{1,0:T(8,128)(2,1)S(1)} %collective-permute-done.12.refs_2_, bf16[64,1664]{1,0:T(8,128)(2,1)S(1)} %collective-permute-done.13.refs_3_, ...), custom_call_target="tpu_custom_call" | custom-call | bytes 9437184 | tf_op jit(solution)/shard_map/pallas_call | solution.py:86
  53.8 9.0 %collective-permute-done.9.refs_8_ = bf16[768,1024]{1,0:T(8,128)(2,1)S(1)} collective-permute-done((bf16[768,1024]{1,0:T(8,128)(2,1)S(1)}, bf16[768,1024]{1,0:T(8,128)(2,1)S(1)}, u32[]{:S(2)}, u32[]{:S(2)}) %collective-permute-start.9) | collective-permute-done | bytes 1572896 | tf_op jit(solution)/shard_map/ppermute | solution.py:273
  64.3 3.1 %shard_map.134.total_ref = f32[512,1536]{1,0:T(8,128)S(1)} custom-call(bf16[64,1664]{1,0:T(8,128)(2,1)S(1)} %collective-permute-done.15.refs_0_, bf16[64,1664]{1,0:T(8,128)(2,1)S(1)} %collective-permute-done.17.refs_1_, bf16[64,1664]{1,0:T(8,128)(2,1)S(1)} %collective-permute-done.18.refs_2_, bf16[64,1664]{1,0:T(8,128)(2,1)S(1)} %collective-permute-done.19.refs_3_, ...), custom_call_target="tpu_custom_call" | custom-call | bytes 9437184 | tf_op jit(solution)/shard_map/pallas_call | solution.py:86
  67.5 2.1 %shard_map.136 = (bf16[512,512]{1,0:T(8,128)(2,1)S(1)}, f32[512,128]{1,0:T(8,128)S(1)}) custom-call(bf16[64,1664]{1,0:T(8,128)(2,1)S(1)} %collective-permute-done.15.refs_0_, bf16[64,1664]{1,0:T(8,128)(2,1)S(1)} %collective-permute-done.17.refs_1_, bf16[64,1664]{1,0:T(8,128)(2,1)S(1)} %collective-permute-done.18.refs_2_, ...), custom_call_target="tpu_custom_call" | custom-call | flops 1610612736 | bytes 4718592 | tf_op jit(solution)/shard_map/pallas_call | solution.py:86
  69.6 2.2 %shard_map.135 = (bf16[512,512]{1,0:T(8,128)(2,1)S(1)}, f32[512,128]{1,0:T(8,128)S(1)}) custom-call(bf16[64,1664]{1,0:T(8,128)(2,1)S(1)} %collective-permute-done.10.refs_0_, bf16[64,1664]{1,0:T(8,128)(2,1)S(1)} %collective-permute-done.11.refs_1_, bf16[64,1664]{1,0:T(8,128)(2,1)S(1)} %collective-permute-done.12.refs_2_, ...), custom_call_target="tpu_custom_call" | custom-call | flops 1610612736 | bytes 4718592 | tf_op jit(solution)/shard_map/pallas_call | solution.py:86
  71.8 2.5 %collective-permute-done.7.last_a = bf16[256,768]{1,0:T(8,128)(2,1)S(1)} collective-permute-done((bf16[256,768]{1,0:T(8,128)(2,1)S(1)}, bf16[256,768]{1,0:T(8,128)(2,1)S(1)}, u32[]{:S(2)}, u32[]{:S(2)}) %collective-permute-start.7) | collective-permute-done | bytes 393248 | tf_op jit(solution)/shard_map/ppermute | solution.py:273
  74.3 1.7 %collective-permute-done.21.last_b = bf16[256,768]{1,0:T(8,128)(2,1)S(1)} collective-permute-done((bf16[256,768]{1,0:T(8,128)(2,1)S(1)}, bf16[256,768]{1,0:T(8,128)(2,1)S(1)}, u32[]{:S(2)}, u32[]{:S(2)}) %collective-permute-start.21) | collective-permute-done | bytes 393248 | tf_op jit(solution)/shard_map/ppermute | solution.py:277
  77.0 1.6 %collective-permute-start.23 = (bf16[128,1536]{1,0:T(8,128)(2,1)S(1)}, bf16[128,1536]{1,0:T(8,128)(2,1)S(1)}, u32[]{:S(2)}, u32[]{:S(2)}) collective-permute-start(bf16[128,1536]{1,0:T(8,128)(2,1)S(1)} %get-tuple-element.119), channel_id=1, source_target_pairs={{0,2},{2,0},{4,6},{6,4},{8,10},{10,8},{12,14},{14,12},{16,18},{18,... | collective-permute-start | bytes 1179656 | tf_op jit(solution)/shard_map/ppermute | solution.py:273
  78.6 1.5 %collective-permute-start.22 = (bf16[128,1536]{1,0:T(8,128)(2,1)S(1)}, bf16[128,1536]{1,0:T(8,128)(2,1)S(1)}, u32[]{:S(2)}, u32[]{:S(2)}) collective-permute-start(bf16[128,1536]{1,0:T(8,128)(2,1)S(1)} %get-tuple-element.115), channel_id=1, source_target_pairs={{0,4},{2,6},{4,0},{6,2},{8,12},{10,14},{12,8},{14,10},{16,20},{18,... | collective-permute-start | bytes 1179656 | tf_op jit(solution)/shard_map/ppermute | solution.py:273
  82.2 6.8 %collective-permute-done.23.got_ref = bf16[128,1536]{1,0:T(8,128)(2,1)S(1)} collective-permute-done((bf16[128,1536]{1,0:T(8,128)(2,1)S(1)}, bf16[128,1536]{1,0:T(8,128)(2,1)S(1)}, u32[]{:S(2)}, u32[]{:S(2)}) %collective-permute-start.23) | collective-permute-done | bytes 393248 | tf_op jit(solution)/shard_map/ppermute | solution.py:273
  91.3 1.6 %collective-permute-start.25 = (bf16[64,1536]{1,0:T(8,128)(2,1)S(1)}, bf16[64,1536]{1,0:T(8,128)(2,1)S(1)}, u32[]{:S(2)}, u32[]{:S(2)}) collective-permute-start(bf16[64,1536]{1,0:T(8,128)(2,1)S(1)} %get-tuple-element.130), channel_id=1, source_target_pairs={{0,4},{2,6},{4,0},{6,2},{8,12},{10,14},{12,8},{14,10},{16,20},{18,... | collective-permute-start | bytes 589832 | tf_op jit(solution)/shard_map/ppermute | solution.py:273
  93.3 1.6 %collective-permute-start.30 = (bf16[64,1536]{1,0:T(8,128)(2,1)S(1)}, bf16[64,1536]{1,0:T(8,128)(2,1)S(1)}, u32[]{:S(2)}, u32[]{:S(2)}) collective-permute-start(bf16[64,1536]{1,0:T(8,128)(2,1)S(1)} %shard_map.143), channel_id=1, source_target_pairs={{0,4},{2,6},{4,0},{6,2},{8,12},{10,14},{12,8},{14,10},{16,20},{18,... | collective-permute-start | bytes 589832 | tf_op jit(solution)/shard_map/ppermute | solution.py:273
  95.0 1.6 %collective-permute-start.28 = (bf16[64,1536]{1,0:T(8,128)(2,1)S(1)}, bf16[64,1536]{1,0:T(8,128)(2,1)S(1)}, u32[]{:S(2)}, u32[]{:S(2)}) collective-permute-start(bf16[64,1536]{1,0:T(8,128)(2,1)S(1)} %shard_map.142), channel_id=1, source_target_pairs={{0,2},{2,0},{4,6},{6,4},{8,10},{10,8},{12,14},{14,12},{16,18},{18,... | collective-permute-start | bytes 589832 | tf_op jit(solution)/shard_map/ppermute | solution.py:273
  97.4 1.6 %collective-permute-done.25.got_b = bf16[64,1536]{1,0:T(8,128)(2,1)S(1)} collective-permute-done((bf16[64,1536]{1,0:T(8,128)(2,1)S(1)}, bf16[64,1536]{1,0:T(8,128)(2,1)S(1)}, u32[]{:S(2)}, u32[]{:S(2)}) %collective-permute-start.25) | collective-permute-done | bytes 196640 | tf_op jit(solution)/shard_map/ppermute | solution.py:273
  100.6 1.5 %collective-permute-start.31 = (bf16[64,1536]{1,0:T(8,128)(2,1)S(1)}, bf16[64,1536]{1,0:T(8,128)(2,1)S(1)}, u32[]{:S(2)}, u32[]{:S(2)}) collective-permute-start(bf16[64,1536]{1,0:T(8,128)(2,1)S(1)} %get-tuple-element.139), channel_id=1, source_target_pairs={{0,4},{2,6},{4,0},{6,2},{8,12},{10,14},{12,8},{14,10},{16,20},{18,... | collective-permute-start | bytes 589832 | tf_op jit(solution)/shard_map/ppermute | solution.py:273
  103.6 5.4 %collective-permute-done.26.got_ref = bf16[64,1536]{1,0:T(8,128)(2,1)S(1)} collective-permute-done((bf16[64,1536]{1,0:T(8,128)(2,1)S(1)}, bf16[64,1536]{1,0:T(8,128)(2,1)S(1)}, u32[]{:S(2)}, u32[]{:S(2)}) %collective-permute-start.26) | collective-permute-done | bytes 196640 | tf_op jit(solution)/shard_map/ppermute | solution.py:273
  110.3 9.1 %collective-permute-done.33.got_ref = bf16[64,1536]{1,0:T(8,128)(2,1)S(1)} collective-permute-done((bf16[64,1536]{1,0:T(8,128)(2,1)S(1)}, bf16[64,1536]{1,0:T(8,128)(2,1)S(1)}, u32[]{:S(2)}, u32[]{:S(2)}) %collective-permute-start.33) | collective-permute-done | bytes 196640 | tf_op jit(solution)/shard_map/ppermute | solution.py:273
  (83 shorter events, 22.3 us)
Async XLA Ops:
  3.9 16.9 %collective-permute-start.2 = (bf16[768,1024]{1,0:T(8,128)(2,1)}, bf16[768,1024]{1,0:T(8,128)(2,1)S(1)}, u32[]{:S(2)}, u32[]{:S(2)}) collective-permute-start(bf16[768,1024]{1,0:T(8,128)(2,1)} %get-tuple-element.83.refs_8_), channel_id=1, source_target_pairs={{0,1},{1,0},{2,3},{3,2},{4,5},{5,4},{6,7},{7,6},{8,9},{9,8},{10,11... | collective-permute-start | bytes 4718600 | tf_op jit(solution)/shard_map/ppermute | solution.py:277
  4.4 16.3 %collective-permute-start.3 = (bf16[512,768]{1,0:T(8,128)(2,1)S(1)}, bf16[512,768]{1,0:T(8,128)(2,1)S(1)}, u32[]{:S(2)}, u32[]{:S(2)}) collective-permute-start(bf16[512,768]{1,0:T(8,128)(2,1)S(1)} %bitcast.8), channel_id=1, source_target_pairs={{0,1},{1,0},{2,3},{3,2},{4,5},{5,4},{6,7},{7,6},{8,9},{9,8},{10,11... | collective-permute-start | bytes 2359304 | tf_op jit(solution)/shard_map/ppermute | solution.py:277
  6.0 14.8 %collective-permute-start.1 = (bf16[64,1664]{1,0:T(8,128)(2,1)S(1)}, bf16[64,1664]{1,0:T(8,128)(2,1)S(1)}, u32[]{:S(2)}, u32[]{:S(2)}) collective-permute-start(bf16[64,1664]{1,0:T(8,128)(2,1)S(1)} %get-tuple-element.76), channel_id=1, source_target_pairs={{0,16},{2,18},{4,20},{6,22},{8,24},{10,26},{12,28},{14,30},{16,0},... | collective-permute-start | bytes 638984 | tf_op jit(solution)/shard_map/ppermute | solution.py:273
  10.0 20.2 %collective-permute-start.6 = (bf16[256,768]{1,0:T(8,128)(2,1)}, bf16[256,768]{1,0:T(8,128)(2,1)S(1)}, u32[]{:S(2)}, u32[]{:S(2)}) collective-permute-start(bf16[256,768]{1,0:T(8,128)(2,1)} %get-tuple-element.79), channel_id=1, source_target_pairs={{0,8},{2,10},{4,12},{6,14},{8,0},{10,2},{12,4},{14,6},{16,24},{18,... | collective-permute-start | bytes 1179656 | tf_op jit(solution)/shard_map/ppermute | solution.py:273
  11.6 17.1 %collective-permute-start = (bf16[64,1664]{1,0:T(8,128)(2,1)S(1)}, bf16[64,1664]{1,0:T(8,128)(2,1)S(1)}, u32[]{:S(2)}, u32[]{:S(2)}) collective-permute-start(bf16[64,1664]{1,0:T(8,128)(2,1)S(1)} %get-tuple-element.75), channel_id=1, source_target_pairs={{0,16},{2,18},{4,20},{6,22},{8,24},{10,26},{12,28},{14,30},{16,0},... | collective-permute-start | bytes 638984 | tf_op jit(solution)/shard_map/ppermute | solution.py:273
  20.8 11.0 %collective-permute-start.5 = (bf16[64,1664]{1,0:T(8,128)(2,1)S(1)}, bf16[64,1664]{1,0:T(8,128)(2,1)S(1)}, u32[]{:S(2)}, u32[]{:S(2)}) collective-permute-start(bf16[64,1664]{1,0:T(8,128)(2,1)S(1)} %pad_maximum_fusion.1.refs_6_), channel_id=1, source_target_pairs={{0,4},{2,6},{4,0},{6,2},{8,12},{10,14},{12,8},{14,10},{16,20},{18,... | collective-permute-start | bytes 638984 | tf_op jit(solution)/shard_map/ppermute | solution.py:273
  22.8 40.0 %collective-permute-start.9 = (bf16[768,1024]{1,0:T(8,128)(2,1)S(1)}, bf16[768,1024]{1,0:T(8,128)(2,1)S(1)}, u32[]{:S(2)}, u32[]{:S(2)}) collective-permute-start(bf16[768,1024]{1,0:T(8,128)(2,1)S(1)} %copy-done.1), channel_id=1, source_target_pairs={{0,8},{2,10},{4,12},{6,14},{8,0},{10,2},{12,4},{14,6},{16,24},{18,... | collective-permute-start | bytes 4718600 | tf_op jit(solution)/shard_map/ppermute | solution.py:273
  22.8 9.0 %collective-permute-start.4 = (bf16[64,1664]{1,0:T(8,128)(2,1)S(1)}, bf16[64,1664]{1,0:T(8,128)(2,1)S(1)}, u32[]{:S(2)}, u32[]{:S(2)}) collective-permute-start(bf16[64,1664]{1,0:T(8,128)(2,1)S(1)} %pad_maximum_fusion.refs_4_), channel_id=1, source_target_pairs={{0,2},{2,0},{4,6},{6,4},{8,10},{10,8},{12,14},{14,12},{16,18},{18,... | collective-permute-start | bytes 638984 | tf_op jit(solution)/shard_map/ppermute | solution.py:273
  28.8 8.0 %collective-permute-start.12 = (bf16[64,1664]{1,0:T(8,128)(2,1)S(1)}, bf16[64,1664]{1,0:T(8,128)(2,1)S(1)}, u32[]{:S(2)}, u32[]{:S(2)}) collective-permute-start(bf16[64,1664]{1,0:T(8,128)(2,1)S(1)} %pad_maximum_fusion.1.refs_6_), channel_id=1, source_target_pairs={{0,2},{2,0},{4,6},{6,4},{8,10},{10,8},{12,14},{14,12},{16,18},{18,... | collective-permute-start | bytes 638984 | tf_op jit(solution)/shard_map/ppermute | solution.py:273
  30.3 8.2 %collective-permute-start.10 = (bf16[64,1664]{1,0:T(8,128)(2,1)S(1)}, bf16[64,1664]{1,0:T(8,128)(2,1)S(1)}, u32[]{:S(2)}, u32[]{:S(2)}) collective-permute-start(bf16[64,1664]{1,0:T(8,128)(2,1)S(1)} %pad_maximum_fusion.refs_4_), channel_id=1, source_target_pairs={{0,4},{2,6},{4,0},{6,2},{8,12},{10,14},{12,8},{14,10},{16,20},{18,... | collective-permute-start | bytes 638984 | tf_op jit(solution)/shard_map/ppermute | solution.py:273
  31.8 11.2 %collective-permute-start.11 = (bf16[64,1664]{1,0:T(8,128)(2,1)S(1)}, bf16[64,1664]{1,0:T(8,128)(2,1)S(1)}, u32[]{:S(2)}, u32[]{:S(2)}) collective-permute-start(bf16[64,1664]{1,0:T(8,128)(2,1)S(1)} %collective-permute-done.4.refs_5_), channel_id=1, source_target_pairs={{0,4},{2,6},{4,0},{6,2},{8,12},{10,14},{12,8},{14,10},{16,20},{18,... | collective-permute-start | bytes 638984 | tf_op jit(solution)/shard_map/ppermute | solution.py:273
  32.3 12.3 %collective-permute-start.13 = (bf16[64,1664]{1,0:T(8,128)(2,1)S(1)}, bf16[64,1664]{1,0:T(8,128)(2,1)S(1)}, u32[]{:S(2)}, u32[]{:S(2)}) collective-permute-start(bf16[64,1664]{1,0:T(8,128)(2,1)S(1)} %collective-permute-done.5.refs_7_), channel_id=1, source_target_pairs={{0,2},{2,0},{4,6},{6,4},{8,10},{10,8},{12,14},{14,12},{16,18},{18,... | collective-permute-start | bytes 638984 | tf_op jit(solution)/shard_map/ppermute | solution.py:273
  36.8 9.3 %collective-permute-start.14 = (bf16[64,1664]{1,0:T(8,128)(2,1)S(1)}, bf16[64,1664]{1,0:T(8,128)(2,1)S(1)}, u32[]{:S(2)}, u32[]{:S(2)}) collective-permute-start(bf16[64,1664]{1,0:T(8,128)(2,1)S(1)} %pad_maximum_fusion.2.refs_6_), channel_id=1, source_target_pairs={{0,2},{2,0},{4,6},{6,4},{8,10},{10,8},{12,14},{14,12},{16,18},{18,... | collective-permute-start | bytes 638984 | tf_op jit(solution)/shard_map/ppermute | solution.py:273
  38.4 9.1 %collective-permute-start.16 = (bf16[64,1664]{1,0:T(8,128)(2,1)S(1)}, bf16[64,1664]{1,0:T(8,128)(2,1)S(1)}, u32[]{:S(2)}, u32[]{:S(2)}) collective-permute-start(bf16[64,1664]{1,0:T(8,128)(2,1)S(1)} %pad_maximum_fusion.3.refs_7_), channel_id=1, source_target_pairs={{0,4},{2,6},{4,0},{6,2},{8,12},{10,14},{12,8},{14,10},{16,20},{18,... | collective-permute-start | bytes 638984 | tf_op jit(solution)/shard_map/ppermute | solution.py:273
  43.0 9.2 %collective-permute-start.18 = (bf16[64,1664]{1,0:T(8,128)(2,1)S(1)}, bf16[64,1664]{1,0:T(8,128)(2,1)S(1)}, u32[]{:S(2)}, u32[]{:S(2)}) collective-permute-start(bf16[64,1664]{1,0:T(8,128)(2,1)S(1)} %pad_maximum_fusion.2.refs_6_), channel_id=1, source_target_pairs={{0,4},{2,6},{4,0},{6,2},{8,12},{10,14},{12,8},{14,10},{16,20},{18,... | collective-permute-start | bytes 638984 | tf_op jit(solution)/shard_map/ppermute | solution.py:273
  44.6 7.7 %collective-permute-start.19 = (bf16[64,1664]{1,0:T(8,128)(2,1)S(1)}, bf16[64,1664]{1,0:T(8,128)(2,1)S(1)}, u32[]{:S(2)}, u32[]{:S(2)}) collective-permute-start(bf16[64,1664]{1,0:T(8,128)(2,1)S(1)} %pad_maximum_fusion.3.refs_7_), channel_id=1, source_target_pairs={{0,2},{2,0},{4,6},{6,4},{8,10},{10,8},{12,14},{14,12},{16,18},{18,... | collective-permute-start | bytes 638984 | tf_op jit(solution)/shard_map/ppermute | solution.py:273
  46.1 7.7 %collective-permute-start.15 = (bf16[64,1664]{1,0:T(8,128)(2,1)S(1)}, bf16[64,1664]{1,0:T(8,128)(2,1)S(1)}, u32[]{:S(2)}, u32[]{:S(2)}) collective-permute-start(bf16[64,1664]{1,0:T(8,128)(2,1)S(1)} %collective-permute-done.14.refs_4_), channel_id=1, source_target_pairs={{0,4},{2,6},{4,0},{6,2},{8,12},{10,14},{12,8},{14,10},{16,20},{18,... | collective-permute-start | bytes 638984 | tf_op jit(solution)/shard_map/ppermute | solution.py:273
  47.6 6.2 %collective-permute-start.17 = (bf16[64,1664]{1,0:T(8,128)(2,1)S(1)}, bf16[64,1664]{1,0:T(8,128)(2,1)S(1)}, u32[]{:S(2)}, u32[]{:S(2)}) collective-permute-start(bf16[64,1664]{1,0:T(8,128)(2,1)S(1)} %collective-permute-done.16.refs_5_), channel_id=1, source_target_pairs={{0,2},{2,0},{4,6},{6,4},{8,10},{10,8},{12,14},{14,12},{16,18},{18,... | collective-permute-start | bytes 638984 | tf_op jit(solution)/shard_map/ppermute | solution.py:273
  62.8 11.5 %collective-permute-start.7 = (bf16[256,768]{1,0:T(8,128)(2,1)S(1)}, bf16[256,768]{1,0:T(8,128)(2,1)S(1)}, u32[]{:S(2)}, u32[]{:S(2)}) collective-permute-start(bf16[256,768]{1,0:T(8,128)(2,1)S(1)} %copy-done.11), channel_id=1, source_target_pairs={{0,8},{2,10},{4,12},{6,14},{8,0},{10,2},{12,4},{14,6},{16,24},{18,... | collective-permute-start | bytes 1179656 | tf_op jit(solution)/shard_map/ppermute | solution.py:273
  64.1 10.2 %collective-permute-start.8 = (bf16[256,768]{1,0:T(8,128)(2,1)S(1)}, bf16[256,768]{1,0:T(8,128)(2,1)S(1)}, u32[]{:S(2)}, u32[]{:S(2)}) collective-permute-start(bf16[256,768]{1,0:T(8,128)(2,1)S(1)} %collective-permute-done.6.first_a), channel_id=1, source_target_pairs={{0,1},{1,0},{2,3},{3,2},{4,5},{5,4},{6,7},{7,6},{8,9},{9,8},{10,11... | collective-permute-start | bytes 1179656 | tf_op jit(solution)/shard_map/ppermute | solution.py:277
  77.0 12.0 %collective-permute-start.23 = (bf16[128,1536]{1,0:T(8,128)(2,1)S(1)}, bf16[128,1536]{1,0:T(8,128)(2,1)S(1)}, u32[]{:S(2)}, u32[]{:S(2)}) collective-permute-start(bf16[128,1536]{1,0:T(8,128)(2,1)S(1)} %get-tuple-element.119), channel_id=1, source_target_pairs={{0,2},{2,0},{4,6},{6,4},{8,10},{10,8},{12,14},{14,12},{16,18},{18,... | collective-permute-start | bytes 1179656 | tf_op jit(solution)/shard_map/ppermute | solution.py:273
  78.6 12.0 %collective-permute-start.22 = (bf16[128,1536]{1,0:T(8,128)(2,1)S(1)}, bf16[128,1536]{1,0:T(8,128)(2,1)S(1)}, u32[]{:S(2)}, u32[]{:S(2)}) collective-permute-start(bf16[128,1536]{1,0:T(8,128)(2,1)S(1)} %get-tuple-element.115), channel_id=1, source_target_pairs={{0,4},{2,6},{4,0},{6,2},{8,12},{10,14},{12,8},{14,10},{16,20},{18,... | collective-permute-start | bytes 1179656 | tf_op jit(solution)/shard_map/ppermute | solution.py:273
  81.2 12.1 %collective-permute-start.29 = (bf16[64,1536]{1,0:T(8,128)(2,1)S(1)}, bf16[64,1536]{1,0:T(8,128)(2,1)S(1)}, u32[]{:S(2)}, u32[]{:S(2)}) collective-permute-start(bf16[64,1536]{1,0:T(8,128)(2,1)S(1)} %get-tuple-element.136), channel_id=1, source_target_pairs={{0,2},{2,0},{4,6},{6,4},{8,10},{10,8},{12,14},{14,12},{16,18},{18,... | collective-permute-start | bytes 589832 | tf_op jit(solution)/shard_map/ppermute | solution.py:273
  81.8 13.2 %collective-permute-start.27 = (bf16[64,1536]{1,0:T(8,128)(2,1)S(1)}, bf16[64,1536]{1,0:T(8,128)(2,1)S(1)}, u32[]{:S(2)}, u32[]{:S(2)}) collective-permute-start(bf16[64,1536]{1,0:T(8,128)(2,1)S(1)} %get-tuple-element.134), channel_id=1, source_target_pairs={{0,4},{2,6},{4,0},{6,2},{8,12},{10,14},{12,8},{14,10},{16,20},{18,... | collective-permute-start | bytes 589832 | tf_op jit(solution)/shard_map/ppermute | solution.py:273
  90.7 6.7 %collective-permute-start.24 = (bf16[64,1536]{1,0:T(8,128)(2,1)S(1)}, bf16[64,1536]{1,0:T(8,128)(2,1)S(1)}, u32[]{:S(2)}, u32[]{:S(2)}) collective-permute-start(bf16[64,1536]{1,0:T(8,128)(2,1)S(1)} %get-tuple-element.128), channel_id=1, source_target_pairs={{0,2},{2,0},{4,6},{6,4},{8,10},{10,8},{12,14},{14,12},{16,18},{18,... | collective-permute-start | bytes 589832 | tf_op jit(solution)/shard_map/ppermute | solution.py:273
  91.3 7.8 %collective-permute-start.25 = (bf16[64,1536]{1,0:T(8,128)(2,1)S(1)}, bf16[64,1536]{1,0:T(8,128)(2,1)S(1)}, u32[]{:S(2)}, u32[]{:S(2)}) collective-permute-start(bf16[64,1536]{1,0:T(8,128)(2,1)S(1)} %get-tuple-element.130), channel_id=1, source_target_pairs={{0,4},{2,6},{4,0},{6,2},{8,12},{10,14},{12,8},{14,10},{16,20},{18,... | collective-permute-start | bytes 589832 | tf_op jit(solution)/shard_map/ppermute | solution.py:273
  93.3 10.2 %collective-permute-start.30 = (bf16[64,1536]{1,0:T(8,128)(2,1)S(1)}, bf16[64,1536]{1,0:T(8,128)(2,1)S(1)}, u32[]{:S(2)}, u32[]{:S(2)}) collective-permute-start(bf16[64,1536]{1,0:T(8,128)(2,1)S(1)} %shard_map.143), channel_id=1, source_target_pairs={{0,4},{2,6},{4,0},{6,2},{8,12},{10,14},{12,8},{14,10},{16,20},{18,... | collective-permute-start | bytes 589832 | tf_op jit(solution)/shard_map/ppermute | solution.py:273
  95.0 8.6 %collective-permute-start.28 = (bf16[64,1536]{1,0:T(8,128)(2,1)S(1)}, bf16[64,1536]{1,0:T(8,128)(2,1)S(1)}, u32[]{:S(2)}, u32[]{:S(2)}) collective-permute-start(bf16[64,1536]{1,0:T(8,128)(2,1)S(1)} %shard_map.142), channel_id=1, source_target_pairs={{0,2},{2,0},{4,6},{6,4},{8,10},{10,8},{12,14},{14,12},{16,18},{18,... | collective-permute-start | bytes 589832 | tf_op jit(solution)/shard_map/ppermute | solution.py:273
  99.1 9.9 %collective-permute-start.26 = (bf16[64,1536]{1,0:T(8,128)(2,1)S(1)}, bf16[64,1536]{1,0:T(8,128)(2,1)S(1)}, u32[]{:S(2)}, u32[]{:S(2)}) collective-permute-start(bf16[64,1536]{1,0:T(8,128)(2,1)S(1)} %get-tuple-element.132), channel_id=1, source_target_pairs={{0,16},{2,18},{4,20},{6,22},{8,24},{10,26},{12,28},{14,30},{16,0},... | collective-permute-start | bytes 589832 | tf_op jit(solution)/shard_map/ppermute | solution.py:273
  100.6 8.4 %collective-permute-start.31 = (bf16[64,1536]{1,0:T(8,128)(2,1)S(1)}, bf16[64,1536]{1,0:T(8,128)(2,1)S(1)}, u32[]{:S(2)}, u32[]{:S(2)}) collective-permute-start(bf16[64,1536]{1,0:T(8,128)(2,1)S(1)} %get-tuple-element.139), channel_id=1, source_target_pairs={{0,4},{2,6},{4,0},{6,2},{8,12},{10,14},{12,8},{14,10},{16,20},{18,... | collective-permute-start | bytes 589832 | tf_op jit(solution)/shard_map/ppermute | solution.py:273
  102.1 6.9 %collective-permute-start.32 = (bf16[64,1536]{1,0:T(8,128)(2,1)S(1)}, bf16[64,1536]{1,0:T(8,128)(2,1)S(1)}, u32[]{:S(2)}, u32[]{:S(2)}) collective-permute-start(bf16[64,1536]{1,0:T(8,128)(2,1)S(1)} %get-tuple-element.142), channel_id=1, source_target_pairs={{0,2},{2,0},{4,6},{6,4},{8,10},{10,8},{12,14},{14,12},{16,18},{18,... | collective-permute-start | bytes 589832 | tf_op jit(solution)/shard_map/ppermute | solution.py:273
  109.1 10.3 %collective-permute-start.33 = (bf16[64,1536]{1,0:T(8,128)(2,1)S(1)}, bf16[64,1536]{1,0:T(8,128)(2,1)S(1)}, u32[]{:S(2)}, u32[]{:S(2)}) collective-permute-start(bf16[64,1536]{1,0:T(8,128)(2,1)S(1)} %get-tuple-element.145), channel_id=1, source_target_pairs={{0,16},{2,18},{4,20},{6,22},{8,24},{10,26},{12,28},{14,30},{16,0},... | collective-permute-start | bytes 589832 | tf_op jit(solution)/shard_map/ppermute | solution.py:273
  (14 other events, 92.6 us)

commit v13 on v12

--- a/solution.py
+++ b/solution.py
@@ -144,13 +144,23 @@
         out_ref[:, width:] = turned.astype(jnp.bfloat16)
 
 
-def pack_kernel(gate_ref, up_ref, down_ref, both_ref, first_ref, last_ref, sems):
-    ff, half = gate_ref.shape[1], first_ref.shape[0]
+def halve_kernel(whole_ref, first_ref, last_ref, sems):
+    half = first_ref.shape[0]
     copies = [
-        pltpu.make_async_copy(down_ref.at[:half, :], first_ref, sems.at[0]),
-        pltpu.make_async_copy(down_ref.at[half:, :], last_ref, sems.at[1]),
-        pltpu.make_async_copy(gate_ref, both_ref.at[:, :ff], sems.at[2]),
-        pltpu.make_async_copy(up_ref, both_ref.at[:, ff:], sems.at[3]),
+        pltpu.make_async_copy(whole_ref.at[:half, :], first_ref, sems.at[0]),
+        pltpu.make_async_copy(whole_ref.at[half:, :], last_ref, sems.at[1]),
+    ]
+    for copy in copies:
+        copy.start()
+    for copy in copies:
+        copy.wait()
+
+
+def pack_kernel(gate_ref, up_ref, both_ref, sems):
+    ff = gate_ref.shape[1]
+    copies = [
+        pltpu.make_async_copy(gate_ref, both_ref.at[:, :ff], sems.at[0]),
+        pltpu.make_async_copy(up_ref, both_ref.at[:, ff:], sems.at[1]),
     ]
     for copy in copies:
         copy.start()
@@ -346,7 +356,7 @@
         prepare_kernel,
         (jax.ShapeDtypeStruct((tok, width + PACK), jnp.bfloat16),) * 2,
         held,
-        8,
+        59,
         10 * tok * width,
         8 * tok * width,
         [(pltpu.SMEM if x.ndim == 1 and x.dtype == jnp.int32 else pltpu.VMEM)(x.shape, x.dtype) for x in held]
@@ -354,29 +364,41 @@
         [hbm] * len(held),
     )
     half_down = jax.ShapeDtypeStruct((ff // 2, down.shape[1]), jnp.bfloat16)
-    both, down_first, down_last = call(
-        pack_kernel,
-        (jax.ShapeDtypeStruct((gate.shape[0], 2 * ff), jnp.bfloat16), half_down, half_down),
-        (gate, up, down),
+    down_first, down_last = call(
+        halve_kernel,
+        (half_down, half_down),
+        (down,),
         59,
         0,
-        12 * gate.size,
-        [pltpu.SemaphoreType.DMA((4,))],
-        [hbm] * 3,
+        4 * down.size,
+        [pltpu.SemaphoreType.DMA((2,))],
+        [hbm],
+    )
+    own, gate, up = lax.optimization_barrier((own, gate, up))
+    both = call(
+        pack_kernel,
+        jax.ShapeDtypeStruct((gate.shape[0], 2 * ff), jnp.bfloat16),
+        (gate, up),
+        16,
+        0,
+        8 * gate.size,
+        [pltpu.SemaphoreType.DMA((2,))],
+        [hbm] * 2,
     )
     by_first = swap(down_first, Z_LOW)
     twins = (swap_core(both), swap_core(down))
     far = [swap(x, Z_HIGH) for x in own]
-    far[0], twins, both_later = lax.optimization_barrier((far[0], twins, both))
+    far[0], by_first, both_later = lax.optimization_barrier((far[0], by_first, both))
     both_by = swap(both_later, Z_LOW)
     first_one = halves(own[0], far[0])
     second_one = swap(first_one[0], X), swap(first_one[1], Y)
-    far[1], second_one, by_first = lax.optimization_barrier((far[1], second_one, by_first))
+    far[1], second_one, twins = lax.optimization_barrier((far[1], second_one, twins))
     first_two = halves(own[1], far[1])
     second_two = swap(first_two[0], X), swap(first_two[1], Y)
     a1, b1, a2, b2, a3, b3, a4, b4 = spread(*first_one, *second_one)
     pieces_one = [a3, a4, b3, b4, a1, a2, b1, b2]
     a1, b1, a2, b2, a3, b3, a4, b4 = spread(*first_two, *second_two)
+    pieces_one, a3, b3 = lax.optimization_barrier((pieces_one, a3, b3))
     pieces = [pieces_one, [a4, b4, a3, b3, a2, b2, a1, b1]]
 
     rows = 8 * tok
@@ -419,13 +441,12 @@
             2 * width * ff + 8 * rows * width,
         )
 
-    total_one = own_total(pieces[0])
+    total_one, total_two = own_total(pieces[0]), own_total(pieces[1])
     down_last, far[1] = lax.optimization_barrier((down_last, far[1]))
     by_last = swap(down_last, Z_LOW)
-    both_by, total_one, pieces = lax.optimization_barrier((both_by, total_one, pieces))
+    both_by, total_one, total_two = lax.optimization_barrier((both_by, total_one, total_two))
     twin_first = swap_core(by_first)
     both_twin = swap_core(both_by)
-    total_two = own_total(pieces[1])
     hidden_one, hidden_two = beside_hidden(pieces[0]), beside_hidden(pieces[1])
     by_last, twin_first, total_two, hidden_one, hidden_two = lax.optimization_barrier(
         (by_last, twin_first, total_two, hidden_one, hidden_two)

time: 120 us -> 124 us (1.033)
  waiting for transfers between devices: 59.9 us -> 67.4 us
  starting transfers between devices: 40.1 us -> 35 us
  local copies, waits for them, and re-layouts: 0.11 us -> 1.57 us
    ppermute x29, waiting for transfers between devices: 58.1 us -> 63.3 us  [swap(): lax.ppermute(block, 'expert', [(i, i ^ distance) for i in range(count)])]
    ppermute x29, starting transfers between devices: 39.3 us -> 34.2 us  [swap(): lax.ppermute(block, 'expert', [(i, i ^ distance) for i in range(count)])]
    ppermute x5, waiting for transfers between devices: 1.73 us -> 4.07 us  [swap_core(): return lax.ppermute(block, 'tensor', [(0, 1), (1, 0)])]
    unnamed x24 -> x12, local copies, waits for them, and re-layouts: 0.05 us -> 1.51 us
    pallas_call x16 -> x17, Pallas kernels: 18.9 us -> 18.8 us  [call(): pl.pallas_call(body, out_shape=outs, in_specs=specs or [smem if x.ndim ==...]
  transfers between devices with their start and end apart: 34 -> 34, of which waited for: 17 -> 22; matrix products, arithmetic and copies ran while one was open for 0% -> 0% of each run, Pallas kernels for 12% -> 12%
where the time goes in v13:
time: 124 us
  waiting for transfers between devices  67.4 us (54%)
  starting transfers between devices  35 us (28%)
  Pallas kernels  18.8 us (15%)
  local copies, waits for them, and re-layouts  1.57 us (1%)
    ppermute x29, waiting for transfers between devices, swap(): lax.ppermute(block, 'expert', [(i, i ^ distance) for i in range(count)])  63.3 us
    ppermute x29, starting transfers between devices, swap(): lax.ppermute(block, 'expert', [(i, i ^ distance) for i in range(count)])  34.2 us
    pallas_call x17, Pallas kernels, call(): pl.pallas_call(body, out_shape=outs, in_specs=specs or [smem if x.ndim ==...  18.8 us
    ppermute x5, waiting for transfers between devices, swap_core(): return lax.ppermute(block, 'tensor', [(0, 1), (1, 0)])  4.07 us
  transfers between devices with their start and end apart: 34, of which 22 were waited for; matrix products, arithmetic and copies ran while one was open for 0% of the time, Pallas kernels for 12%

profile of v13, /device:TPU:0, one launch (start us, length us, event | category | flops | bytes accessed | tf_op | source)
XLA Modules:
  0.0 123.7 jit_solution(3884451315231668860)
XLA Ops:
  0.6 2.2 %shard_map.132 = (bf16[64,1664]{1,0:T(8,128)(2,1)}, bf16[64,1664]{1,0:T(8,128)(2,1)}) custom-call(bf16[1536]{0:T(1024)(128)(2,1)} %refs_0_.1, bf16[64,1536]{1,0:T(8,128)(2,1)} %refs_1_.1, bf16[64,1536]{1,0:T(8,128)(2,1)} %refs_2_.1, s32[8,64]{1,0:T(8,128)} %bitcast.13, s32[8,64]{1,0:T(8,128)} %bitcast.14, f32[8,64]{1,0:T(8,128)} %bitcast.15, ...), custom_call_target="tpu_custom_call" | custom-call | flops 983040 | bytes 786432 | tf_op jit(solution)/shard_map/pallas_call | solution.py:86
  2.8 4.1 %collective-permute-start.1 = (bf16[64,1664]{1,0:T(8,128)(2,1)}, bf16[64,1664]{1,0:T(8,128)(2,1)S(1)}, u32[]{:S(2)}, u32[]{:S(2)}) collective-permute-start(bf16[64,1664]{1,0:T(8,128)(2,1)} %get-tuple-element.76), channel_id=1, source_target_pairs={{0,16},{2,18},{4,20},{6,22},{8,24},{10,26},{12,28},{14,30},{16,0},... | collective-permute-start | bytes 638984 | tf_op jit(solution)/shard_map/ppermute | solution.py:283
  6.9 2.0 %shard_map.131 = (bf16[256,768]{1,0:T(8,128)(2,1)}, bf16[256,768]{1,0:T(8,128)(2,1)}) custom-call(bf16[512,768]{1,0:T(8,128)(2,1)} %bitcast.8), custom_call_target="tpu_custom_call" | custom-call | bytes 1572864 | tf_op jit(solution)/shard_map/pallas_call | solution.py:86
  9.0 1.6 %collective-permute-start.2 = (bf16[256,768]{1,0:T(8,128)(2,1)}, bf16[256,768]{1,0:T(8,128)(2,1)S(1)}, u32[]{:S(2)}, u32[]{:S(2)}) collective-permute-start(bf16[256,768]{1,0:T(8,128)(2,1)} %get-tuple-element.77), channel_id=1, source_target_pairs={{0,8},{2,10},{4,12},{6,14},{8,0},{10,2},{12,4},{14,6},{16,24},{18,... | collective-permute-start | bytes 1179656 | tf_op jit(solution)/shard_map/ppermute | solution.py:283
  13.1 4.5 %collective-permute-done.1 = bf16[64,1664]{1,0:T(8,128)(2,1)S(1)} collective-permute-done((bf16[64,1664]{1,0:T(8,128)(2,1)}, bf16[64,1664]{1,0:T(8,128)(2,1)S(1)}, u32[]{:S(2)}, u32[]{:S(2)}) %collective-permute-start.1) | collective-permute-done | bytes 213024 | tf_op jit(solution)/shard_map/ppermute | solution.py:283
  17.6 11.1 %collective-permute-done.2.first_a = bf16[256,768]{1,0:T(8,128)(2,1)S(1)} collective-permute-done((bf16[256,768]{1,0:T(8,128)(2,1)}, bf16[256,768]{1,0:T(8,128)(2,1)S(1)}, u32[]{:S(2)}, u32[]{:S(2)}) %collective-permute-start.2) | collective-permute-done | bytes 393248 | tf_op jit(solution)/shard_map/ppermute | solution.py:283
  28.8 1.6 %collective-permute-start.4 = (bf16[64,1664]{1,0:T(8,128)(2,1)S(1)}, bf16[64,1664]{1,0:T(8,128)(2,1)S(1)}, u32[]{:S(2)}, u32[]{:S(2)}) collective-permute-start(bf16[64,1664]{1,0:T(8,128)(2,1)S(1)} %pad_maximum_fusion.1.refs_6_), channel_id=1, source_target_pairs={{0,4},{2,6},{4,0},{6,2},{8,12},{10,14},{12,8},{14,10},{16,20},{18,... | collective-permute-start | bytes 638984 | tf_op jit(solution)/shard_map/ppermute | solution.py:283
  30.5 1.6 %collective-permute-start.3 = (bf16[64,1664]{1,0:T(8,128)(2,1)S(1)}, bf16[64,1664]{1,0:T(8,128)(2,1)S(1)}, u32[]{:S(2)}, u32[]{:S(2)}) collective-permute-start(bf16[64,1664]{1,0:T(8,128)(2,1)S(1)} %pad_maximum_fusion.refs_4_), channel_id=1, source_target_pairs={{0,2},{2,0},{4,6},{6,4},{8,10},{10,8},{12,14},{14,12},{16,18},{18,... | collective-permute-start | bytes 638984 | tf_op jit(solution)/shard_map/ppermute | solution.py:283
  32.0 3.8 %collective-permute-done.4.refs_7_ = bf16[64,1664]{1,0:T(8,128)(2,1)S(1)} collective-permute-done((bf16[64,1664]{1,0:T(8,128)(2,1)S(1)}, bf16[64,1664]{1,0:T(8,128)(2,1)S(1)}, u32[]{:S(2)}, u32[]{:S(2)}) %collective-permute-start.4) | collective-permute-done | bytes 213024 | tf_op jit(solution)/shard_map/ppermute | solution.py:283
  35.8 1.5 %collective-permute-start.12 = (bf16[64,1664]{1,0:T(8,128)(2,1)S(1)}, bf16[64,1664]{1,0:T(8,128)(2,1)S(1)}, u32[]{:S(2)}, u32[]{:S(2)}) collective-permute-start(bf16[64,1664]{1,0:T(8,128)(2,1)S(1)} %pad_maximum_fusion.1.refs_6_), channel_id=1, source_target_pairs={{0,2},{2,0},{4,6},{6,4},{8,10},{10,8},{12,14},{14,12},{16,18},{18,... | collective-permute-start | bytes 638984 | tf_op jit(solution)/shard_map/ppermute | solution.py:283
  37.4 1.5 %collective-permute-start.10 = (bf16[64,1664]{1,0:T(8,128)(2,1)S(1)}, bf16[64,1664]{1,0:T(8,128)(2,1)S(1)}, u32[]{:S(2)}, u32[]{:S(2)}) collective-permute-start(bf16[64,1664]{1,0:T(8,128)(2,1)S(1)} %pad_maximum_fusion.refs_4_), channel_id=1, source_target_pairs={{0,4},{2,6},{4,0},{6,2},{8,12},{10,14},{12,8},{14,10},{16,20},{18,... | collective-permute-start | bytes 638984 | tf_op jit(solution)/shard_map/ppermute | solution.py:283
  40.9 2.6 %collective-permute-done.12.refs_2_ = bf16[64,1664]{1,0:T(8,128)(2,1)S(1)} collective-permute-done((bf16[64,1664]{1,0:T(8,128)(2,1)S(1)}, bf16[64,1664]{1,0:T(8,128)(2,1)S(1)}, u32[]{:S(2)}, u32[]{:S(2)}) %collective-permute-start.12) | collective-permute-done | bytes 213024 | tf_op jit(solution)/shard_map/ppermute | solution.py:283
  43.5 1.8 %collective-permute-start.16 = (bf16[64,1664]{1,0:T(8,128)(2,1)S(1)}, bf16[64,1664]{1,0:T(8,128)(2,1)S(1)}, u32[]{:S(2)}, u32[]{:S(2)}) collective-permute-start(bf16[64,1664]{1,0:T(8,128)(2,1)S(1)} %pad_maximum_fusion.2.refs_6_), channel_id=1, source_target_pairs={{0,2},{2,0},{4,6},{6,4},{8,10},{10,8},{12,14},{14,12},{16,18},{18,... | collective-permute-start | bytes 638984 | tf_op jit(solution)/shard_map/ppermute | solution.py:283
  45.5 1.5 %collective-permute-start.18 = (bf16[64,1664]{1,0:T(8,128)(2,1)S(1)}, bf16[64,1664]{1,0:T(8,128)(2,1)S(1)}, u32[]{:S(2)}, u32[]{:S(2)}) collective-permute-start(bf16[64,1664]{1,0:T(8,128)(2,1)S(1)} %pad_maximum_fusion.3.refs_7_), channel_id=1, source_target_pairs={{0,4},{2,6},{4,0},{6,2},{8,12},{10,14},{12,8},{14,10},{16,20},{18,... | collective-permute-start | bytes 638984 | tf_op jit(solution)/shard_map/ppermute | solution.py:283
  47.1 3.0 %collective-permute-done.14.refs_2_ = bf16[64,1664]{1,0:T(8,128)(2,1)S(1)} collective-permute-done((bf16[64,1664]{1,0:T(8,128)(2,1)S(1)}, bf16[64,1664]{1,0:T(8,128)(2,1)S(1)}, u32[]{:S(2)}, u32[]{:S(2)}) %collective-permute-start.14) | collective-permute-done | bytes 213024 | tf_op jit(solution)/shard_map/ppermute | solution.py:283
  50.1 1.5 %collective-permute-start.11 = (bf16[64,1664]{1,0:T(8,128)(2,1)S(1)}, bf16[64,1664]{1,0:T(8,128)(2,1)S(1)}, u32[]{:S(2)}, u32[]{:S(2)}) collective-permute-start(bf16[64,1664]{1,0:T(8,128)(2,1)S(1)} %collective-permute-done.3.refs_5_), channel_id=1, source_target_pairs={{0,4},{2,6},{4,0},{6,2},{8,12},{10,14},{12,8},{14,10},{16,20},{18,... | collective-permute-start | bytes 638984 | tf_op jit(solution)/shard_map/ppermute | solution.py:283
  52.7 1.6 %collective-permute-start.17 = (bf16[64,1664]{1,0:T(8,128)(2,1)S(1)}, bf16[64,1664]{1,0:T(8,128)(2,1)S(1)}, u32[]{:S(2)}, u32[]{:S(2)}) collective-permute-start(bf16[64,1664]{1,0:T(8,128)(2,1)S(1)} %collective-permute-done.16.refs_4_), channel_id=1, source_target_pairs={{0,4},{2,6},{4,0},{6,2},{8,12},{10,14},{12,8},{14,10},{16,20},{18,... | collective-permute-start | bytes 638984 | tf_op jit(solution)/shard_map/ppermute | solution.py:283
  54.7 1.5 %collective-permute-start.19 = (bf16[64,1664]{1,0:T(8,128)(2,1)S(1)}, bf16[64,1664]{1,0:T(8,128)(2,1)S(1)}, u32[]{:S(2)}, u32[]{:S(2)}) collective-permute-start(bf16[64,1664]{1,0:T(8,128)(2,1)S(1)} %collective-permute-done.18.refs_5_), channel_id=1, source_target_pairs={{0,2},{2,0},{4,6},{6,4},{8,10},{10,8},{12,14},{14,12},{16,18},{18,... | collective-permute-start | bytes 638984 | tf_op jit(solution)/shard_map/ppermute | solution.py:283
  56.2 2.9 %collective-permute-done.11.refs_1_ = bf16[64,1664]{1,0:T(8,128)(2,1)S(1)} collective-permute-done((bf16[64,1664]{1,0:T(8,128)(2,1)S(1)}, bf16[64,1664]{1,0:T(8,128)(2,1)S(1)}, u32[]{:S(2)}, u32[]{:S(2)}) %collective-permute-start.11) | collective-permute-done | bytes 213024 | tf_op jit(solution)/shard_map/ppermute | solution.py:283
  59.1 3.1 %shard_map.134.total_ref = f32[512,1536]{1,0:T(8,128)S(1)} custom-call(bf16[64,1664]{1,0:T(8,128)(2,1)S(1)} %collective-permute-done.10.refs_0_, bf16[64,1664]{1,0:T(8,128)(2,1)S(1)} %collective-permute-done.11.refs_1_, bf16[64,1664]{1,0:T(8,128)(2,1)S(1)} %collective-permute-done.12.refs_2_, bf16[64,1664]{1,0:T(8,128)(2,1)S(1)} %collective-permute-done.13.refs_3_, ...), custom_call_target="tpu_custom_call" | custom-call | bytes 9437184 | tf_op jit(solution)/shard_map/pallas_call | solution.py:86
  62.3 3.1 %shard_map.135.total_ref = f32[512,1536]{1,0:T(8,128)S(1)} custom-call(bf16[64,1664]{1,0:T(8,128)(2,1)S(1)} %collective-permute-done.17.refs_0_, bf16[64,1664]{1,0:T(8,128)(2,1)S(1)} %collective-permute-done.19.refs_1_, bf16[64,1664]{1,0:T(8,128)(2,1)S(1)} %collective-permute-done.14.refs_2_, bf16[64,1664]{1,0:T(8,128)(2,1)S(1)} %collective-permute-done.15.refs_3_, ...), custom_call_target="tpu_custom_call" | custom-call | bytes 9437184 | tf_op jit(solution)/shard_map/pallas_call | solution.py:86
  67.3 2.3 %collective-permute-done.20.refs_9_ = bf16[768,1024]{1,0:T(8,128)(2,1)S(1)} collective-permute-done((bf16[768,1024]{1,0:T(8,128)(2,1)S(1)}, bf16[768,1024]{1,0:T(8,128)(2,1)S(1)}, u32[]{:S(2)}, u32[]{:S(2)}) %collective-permute-start.20) | collective-permute-done | bytes 1572896 | tf_op jit(solution)/shard_map/ppermute | solution.py:287
  69.7 2.1 %shard_map.137 = (bf16[512,512]{1,0:T(8,128)(2,1)S(1)}, f32[512,128]{1,0:T(8,128)S(1)}) custom-call(bf16[64,1664]{1,0:T(8,128)(2,1)S(1)} %collective-permute-done.17.refs_0_, bf16[64,1664]{1,0:T(8,128)(2,1)S(1)} %collective-permute-done.19.refs_1_, bf16[64,1664]{1,0:T(8,128)(2,1)S(1)} %collective-permute-done.14.refs_2_, ...), custom_call_target="tpu_custom_call" | custom-call | flops 1610612736 | bytes 4718592 | tf_op jit(solution)/shard_map/pallas_call | solution.py:86
  71.8 2.1 %shard_map.136 = (bf16[512,512]{1,0:T(8,128)(2,1)S(1)}, f32[512,128]{1,0:T(8,128)S(1)}) custom-call(bf16[64,1664]{1,0:T(8,128)(2,1)S(1)} %collective-permute-done.10.refs_0_, bf16[64,1664]{1,0:T(8,128)(2,1)S(1)} %collective-permute-done.11.refs_1_, bf16[64,1664]{1,0:T(8,128)(2,1)S(1)} %collective-permute-done.12.refs_2_, ...), custom_call_target="tpu_custom_call" | custom-call | flops 1610612736 | bytes 4718592 | tf_op jit(solution)/shard_map/pallas_call | solution.py:86
  74.0 3.8 %collective-permute-done.7.last_a = bf16[256,768]{1,0:T(8,128)(2,1)S(1)} collective-permute-done((bf16[256,768]{1,0:T(8,128)(2,1)S(1)}, bf16[256,768]{1,0:T(8,128)(2,1)S(1)}, u32[]{:S(2)}, u32[]{:S(2)}) %collective-permute-start.7) | collective-permute-done | bytes 393248 | tf_op jit(solution)/shard_map/ppermute | solution.py:283
  77.8 1.7 %collective-permute-done.21.last_b = bf16[256,768]{1,0:T(8,128)(2,1)S(1)} collective-permute-done((bf16[256,768]{1,0:T(8,128)(2,1)S(1)}, bf16[256,768]{1,0:T(8,128)(2,1)S(1)}, u32[]{:S(2)}, u32[]{:S(2)}) %collective-permute-start.21) | collective-permute-done | bytes 393248 | tf_op jit(solution)/shard_map/ppermute | solution.py:287
  80.5 1.6 %collective-permute-start.23 = (bf16[128,1536]{1,0:T(8,128)(2,1)S(1)}, bf16[128,1536]{1,0:T(8,128)(2,1)S(1)}, u32[]{:S(2)}, u32[]{:S(2)}) collective-permute-start(bf16[128,1536]{1,0:T(8,128)(2,1)S(1)} %get-tuple-element.115), channel_id=1, source_target_pairs={{0,2},{2,0},{4,6},{6,4},{8,10},{10,8},{12,14},{14,12},{16,18},{18,... | collective-permute-start | bytes 1179656 | tf_op jit(solution)/shard_map/ppermute | solution.py:283
  85.7 6.8 %collective-permute-done.23.got_ref = bf16[128,1536]{1,0:T(8,128)(2,1)S(1)} collective-permute-done((bf16[128,1536]{1,0:T(8,128)(2,1)S(1)}, bf16[128,1536]{1,0:T(8,128)(2,1)S(1)}, u32[]{:S(2)}, u32[]{:S(2)}) %collective-permute-start.23) | collective-permute-done | bytes 393248 | tf_op jit(solution)/shard_map/ppermute | solution.py:283
  92.6 1.5 %collective-permute-done.22.got_ref = bf16[128,1536]{1,0:T(8,128)(2,1)S(1)} collective-permute-done((bf16[128,1536]{1,0:T(8,128)(2,1)S(1)}, bf16[128,1536]{1,0:T(8,128)(2,1)S(1)}, u32[]{:S(2)}, u32[]{:S(2)}) %collective-permute-start.22) | collective-permute-done | bytes 393248 | tf_op jit(solution)/shard_map/ppermute | solution.py:283
  99.0 2.5 %collective-permute-done.24.got_a = bf16[64,1536]{1,0:T(8,128)(2,1)S(1)} collective-permute-done((bf16[64,1536]{1,0:T(8,128)(2,1)S(1)}, bf16[64,1536]{1,0:T(8,128)(2,1)S(1)}, u32[]{:S(2)}, u32[]{:S(2)}) %collective-permute-start.24) | collective-permute-done | bytes 196640 | tf_op jit(solution)/shard_map/ppermute | solution.py:283
  106.8 5.5 %collective-permute-done.26.got_ref = bf16[64,1536]{1,0:T(8,128)(2,1)S(1)} collective-permute-done((bf16[64,1536]{1,0:T(8,128)(2,1)S(1)}, bf16[64,1536]{1,0:T(8,128)(2,1)S(1)}, u32[]{:S(2)}, u32[]{:S(2)}) %collective-permute-start.26) | collective-permute-done | bytes 196640 | tf_op jit(solution)/shard_map/ppermute | solution.py:283
  113.3 9.7 %collective-permute-done.33.got_ref = bf16[64,1536]{1,0:T(8,128)(2,1)S(1)} collective-permute-done((bf16[64,1536]{1,0:T(8,128)(2,1)S(1)}, bf16[64,1536]{1,0:T(8,128)(2,1)S(1)}, u32[]{:S(2)}, u32[]{:S(2)}) %collective-permute-start.33) | collective-permute-done | bytes 196640 | tf_op jit(solution)/shard_map/ppermute | solution.py:283
  (72 shorter events, 24.5 us)
Async XLA Ops:
  2.8 14.8 %collective-permute-start.1 = (bf16[64,1664]{1,0:T(8,128)(2,1)}, bf16[64,1664]{1,0:T(8,128)(2,1)S(1)}, u32[]{:S(2)}, u32[]{:S(2)}) collective-permute-start(bf16[64,1664]{1,0:T(8,128)(2,1)} %get-tuple-element.76), channel_id=1, source_target_pairs={{0,16},{2,18},{4,20},{6,22},{8,24},{10,26},{12,28},{14,30},{16,0},... | collective-permute-start | bytes 638984 | tf_op jit(solution)/shard_map/ppermute | solution.py:283
  6.9 31.9 %collective-permute-start.6 = (bf16[512,768]{1,0:T(8,128)(2,1)}, bf16[512,768]{1,0:T(8,128)(2,1)S(1)}, u32[]{:S(2)}, u32[]{:S(2)}) collective-permute-start(bf16[512,768]{1,0:T(8,128)(2,1)} %bitcast.7), channel_id=1, source_target_pairs={{0,1},{1,0},{2,3},{3,2},{4,5},{5,4},{6,7},{7,6},{8,9},{9,8},{10,11... | collective-permute-start | bytes 2359304 | tf_op jit(solution)/shard_map/ppermute | solution.py:287
  9.0 19.8 %collective-permute-start.2 = (bf16[256,768]{1,0:T(8,128)(2,1)}, bf16[256,768]{1,0:T(8,128)(2,1)S(1)}, u32[]{:S(2)}, u32[]{:S(2)}) collective-permute-start(bf16[256,768]{1,0:T(8,128)(2,1)} %get-tuple-element.77), channel_id=1, source_target_pairs={{0,8},{2,10},{4,12},{6,14},{8,0},{10,2},{12,4},{14,6},{16,24},{18,... | collective-permute-start | bytes 1179656 | tf_op jit(solution)/shard_map/ppermute | solution.py:283
  12.0 26.8 %collective-permute-start.5 = (bf16[768,1024]{1,0:T(8,128)(2,1)S(1)}, bf16[768,1024]{1,0:T(8,128)(2,1)S(1)}, u32[]{:S(2)}, u32[]{:S(2)}) collective-permute-start(bf16[768,1024]{1,0:T(8,128)(2,1)S(1)} %shard_map.133.refs_8_), channel_id=1, source_target_pairs={{0,1},{1,0},{2,3},{3,2},{4,5},{5,4},{6,7},{7,6},{8,9},{9,8},{10,11... | collective-permute-start | bytes 4718600 | tf_op jit(solution)/shard_map/ppermute | solution.py:287
  12.7 17.8 %collective-permute-start = (bf16[64,1664]{1,0:T(8,128)(2,1)S(1)}, bf16[64,1664]{1,0:T(8,128)(2,1)S(1)}, u32[]{:S(2)}, u32[]{:S(2)}) collective-permute-start(bf16[64,1664]{1,0:T(8,128)(2,1)S(1)} %copy-done.3), channel_id=1, source_target_pairs={{0,16},{2,18},{4,20},{6,22},{8,24},{10,26},{12,28},{14,30},{16,0},... | collective-permute-start | bytes 638984 | tf_op jit(solution)/shard_map/ppermute | solution.py:283
  28.8 7.0 %collective-permute-start.4 = (bf16[64,1664]{1,0:T(8,128)(2,1)S(1)}, bf16[64,1664]{1,0:T(8,128)(2,1)S(1)}, u32[]{:S(2)}, u32[]{:S(2)}) collective-permute-start(bf16[64,1664]{1,0:T(8,128)(2,1)S(1)} %pad_maximum_fusion.1.refs_6_), channel_id=1, source_target_pairs={{0,4},{2,6},{4,0},{6,2},{8,12},{10,14},{12,8},{14,10},{16,20},{18,... | collective-permute-start | bytes 638984 | tf_op jit(solution)/shard_map/ppermute | solution.py:283
  30.4 35.8 %collective-permute-start.9 = (bf16[768,1024]{1,0:T(8,128)(2,1)S(1)}, bf16[768,1024]{1,0:T(8,128)(2,1)S(1)}, u32[]{:S(2)}, u32[]{:S(2)}) collective-permute-start(bf16[768,1024]{1,0:T(8,128)(2,1)S(1)} %shard_map.133.refs_8_), channel_id=1, source_target_pairs={{0,8},{2,10},{4,12},{6,14},{8,0},{10,2},{12,4},{14,6},{16,24},{18,... | collective-permute-start | bytes 4718600 | tf_op jit(solution)/shard_map/ppermute | solution.py:283
  30.5 6.9 %collective-permute-start.3 = (bf16[64,1664]{1,0:T(8,128)(2,1)S(1)}, bf16[64,1664]{1,0:T(8,128)(2,1)S(1)}, u32[]{:S(2)}, u32[]{:S(2)}) collective-permute-start(bf16[64,1664]{1,0:T(8,128)(2,1)S(1)} %pad_maximum_fusion.refs_4_), channel_id=1, source_target_pairs={{0,2},{2,0},{4,6},{6,4},{8,10},{10,8},{12,14},{14,12},{16,18},{18,... | collective-permute-start | bytes 638984 | tf_op jit(solution)/shard_map/ppermute | solution.py:283
  35.8 7.7 %collective-permute-start.12 = (bf16[64,1664]{1,0:T(8,128)(2,1)S(1)}, bf16[64,1664]{1,0:T(8,128)(2,1)S(1)}, u32[]{:S(2)}, u32[]{:S(2)}) collective-permute-start(bf16[64,1664]{1,0:T(8,128)(2,1)S(1)} %pad_maximum_fusion.1.refs_6_), channel_id=1, source_target_pairs={{0,2},{2,0},{4,6},{6,4},{8,10},{10,8},{12,14},{14,12},{16,18},{18,... | collective-permute-start | bytes 638984 | tf_op jit(solution)/shard_map/ppermute | solution.py:283
  37.4 8.2 %collective-permute-start.10 = (bf16[64,1664]{1,0:T(8,128)(2,1)S(1)}, bf16[64,1664]{1,0:T(8,128)(2,1)S(1)}, u32[]{:S(2)}, u32[]{:S(2)}) collective-permute-start(bf16[64,1664]{1,0:T(8,128)(2,1)S(1)} %pad_maximum_fusion.refs_4_), channel_id=1, source_target_pairs={{0,4},{2,6},{4,0},{6,2},{8,12},{10,14},{12,8},{14,10},{16,20},{18,... | collective-permute-start | bytes 638984 | tf_op jit(solution)/shard_map/ppermute | solution.py:283
  38.9 11.2 %collective-permute-start.14 = (bf16[64,1664]{1,0:T(8,128)(2,1)S(1)}, bf16[64,1664]{1,0:T(8,128)(2,1)S(1)}, u32[]{:S(2)}, u32[]{:S(2)}) collective-permute-start(bf16[64,1664]{1,0:T(8,128)(2,1)S(1)} %pad_maximum_fusion.2.refs_6_), channel_id=1, source_target_pairs={{0,4},{2,6},{4,0},{6,2},{8,12},{10,14},{12,8},{14,10},{16,20},{18,... | collective-permute-start | bytes 638984 | tf_op jit(solution)/shard_map/ppermute | solution.py:283
  39.5 12.1 %collective-permute-start.15 = (bf16[64,1664]{1,0:T(8,128)(2,1)S(1)}, bf16[64,1664]{1,0:T(8,128)(2,1)S(1)}, u32[]{:S(2)}, u32[]{:S(2)}) collective-permute-start(bf16[64,1664]{1,0:T(8,128)(2,1)S(1)} %pad_maximum_fusion.3.refs_7_), channel_id=1, source_target_pairs={{0,2},{2,0},{4,6},{6,4},{8,10},{10,8},{12,14},{14,12},{16,18},{18,... | collective-permute-start | bytes 638984 | tf_op jit(solution)/shard_map/ppermute | solution.py:283
  43.5 9.1 %collective-permute-start.16 = (bf16[64,1664]{1,0:T(8,128)(2,1)S(1)}, bf16[64,1664]{1,0:T(8,128)(2,1)S(1)}, u32[]{:S(2)}, u32[]{:S(2)}) collective-permute-start(bf16[64,1664]{1,0:T(8,128)(2,1)S(1)} %pad_maximum_fusion.2.refs_6_), channel_id=1, source_target_pairs={{0,2},{2,0},{4,6},{6,4},{8,10},{10,8},{12,14},{14,12},{16,18},{18,... | collective-permute-start | bytes 638984 | tf_op jit(solution)/shard_map/ppermute | solution.py:283
  45.5 9.1 %collective-permute-start.18 = (bf16[64,1664]{1,0:T(8,128)(2,1)S(1)}, bf16[64,1664]{1,0:T(8,128)(2,1)S(1)}, u32[]{:S(2)}, u32[]{:S(2)}) collective-permute-start(bf16[64,1664]{1,0:T(8,128)(2,1)S(1)} %pad_maximum_fusion.3.refs_7_), channel_id=1, source_target_pairs={{0,4},{2,6},{4,0},{6,2},{8,12},{10,14},{12,8},{14,10},{16,20},{18,... | collective-permute-start | bytes 638984 | tf_op jit(solution)/shard_map/ppermute | solution.py:283
  50.1 9.0 %collective-permute-start.11 = (bf16[64,1664]{1,0:T(8,128)(2,1)S(1)}, bf16[64,1664]{1,0:T(8,128)(2,1)S(1)}, u32[]{:S(2)}, u32[]{:S(2)}) collective-permute-start(bf16[64,1664]{1,0:T(8,128)(2,1)S(1)} %collective-permute-done.3.refs_5_), channel_id=1, source_target_pairs={{0,4},{2,6},{4,0},{6,2},{8,12},{10,14},{12,8},{14,10},{16,20},{18,... | collective-permute-start | bytes 638984 | tf_op jit(solution)/shard_map/ppermute | solution.py:283
  51.6 7.5 %collective-permute-start.13 = (bf16[64,1664]{1,0:T(8,128)(2,1)S(1)}, bf16[64,1664]{1,0:T(8,128)(2,1)S(1)}, u32[]{:S(2)}, u32[]{:S(2)}) collective-permute-start(bf16[64,1664]{1,0:T(8,128)(2,1)S(1)} %collective-permute-done.4.refs_7_), channel_id=1, source_target_pairs={{0,2},{2,0},{4,6},{6,4},{8,10},{10,8},{12,14},{14,12},{16,18},{18,... | collective-permute-start | bytes 638984 | tf_op jit(solution)/shard_map/ppermute | solution.py:283
  52.7 9.6 %collective-permute-start.17 = (bf16[64,1664]{1,0:T(8,128)(2,1)S(1)}, bf16[64,1664]{1,0:T(8,128)(2,1)S(1)}, u32[]{:S(2)}, u32[]{:S(2)}) collective-permute-start(bf16[64,1664]{1,0:T(8,128)(2,1)S(1)} %collective-permute-done.16.refs_4_), channel_id=1, source_target_pairs={{0,4},{2,6},{4,0},{6,2},{8,12},{10,14},{12,8},{14,10},{16,20},{18,... | collective-permute-start | bytes 638984 | tf_op jit(solution)/shard_map/ppermute | solution.py:283
  54.7 7.6 %collective-permute-start.19 = (bf16[64,1664]{1,0:T(8,128)(2,1)S(1)}, bf16[64,1664]{1,0:T(8,128)(2,1)S(1)}, u32[]{:S(2)}, u32[]{:S(2)}) collective-permute-start(bf16[64,1664]{1,0:T(8,128)(2,1)S(1)} %collective-permute-done.18.refs_5_), channel_id=1, source_target_pairs={{0,2},{2,0},{4,6},{6,4},{8,10},{10,8},{12,14},{14,12},{16,18},{18,... | collective-permute-start | bytes 638984 | tf_op jit(solution)/shard_map/ppermute | solution.py:283
  66.2 7.7 %collective-permute-start.8 = (bf16[256,768]{1,0:T(8,128)(2,1)S(1)}, bf16[256,768]{1,0:T(8,128)(2,1)S(1)}, u32[]{:S(2)}, u32[]{:S(2)}) collective-permute-start(bf16[256,768]{1,0:T(8,128)(2,1)S(1)} %collective-permute-done.2.first_a), channel_id=1, source_target_pairs={{0,1},{1,0},{2,3},{3,2},{4,5},{5,4},{6,7},{7,6},{8,9},{9,8},{10,11... | collective-permute-start | bytes 1179656 | tf_op jit(solution)/shard_map/ppermute | solution.py:287
  66.8 11.0 %collective-permute-start.7 = (bf16[256,768]{1,0:T(8,128)(2,1)S(1)}, bf16[256,768]{1,0:T(8,128)(2,1)S(1)}, u32[]{:S(2)}, u32[]{:S(2)}) collective-permute-start(bf16[256,768]{1,0:T(8,128)(2,1)S(1)} %copy-done.5), channel_id=1, source_target_pairs={{0,8},{2,10},{4,12},{6,14},{8,0},{10,2},{12,4},{14,6},{16,24},{18,... | collective-permute-start | bytes 1179656 | tf_op jit(solution)/shard_map/ppermute | solution.py:283
  80.5 12.0 %collective-permute-start.23 = (bf16[128,1536]{1,0:T(8,128)(2,1)S(1)}, bf16[128,1536]{1,0:T(8,128)(2,1)S(1)}, u32[]{:S(2)}, u32[]{:S(2)}) collective-permute-start(bf16[128,1536]{1,0:T(8,128)(2,1)S(1)} %get-tuple-element.115), channel_id=1, source_target_pairs={{0,2},{2,0},{4,6},{6,4},{8,10},{10,8},{12,14},{14,12},{16,18},{18,... | collective-permute-start | bytes 1179656 | tf_op jit(solution)/shard_map/ppermute | solution.py:283
  82.1 12.0 %collective-permute-start.22 = (bf16[128,1536]{1,0:T(8,128)(2,1)S(1)}, bf16[128,1536]{1,0:T(8,128)(2,1)S(1)}, u32[]{:S(2)}, u32[]{:S(2)}) collective-permute-start(bf16[128,1536]{1,0:T(8,128)(2,1)S(1)} %get-tuple-element.111), channel_id=1, source_target_pairs={{0,4},{2,6},{4,0},{6,2},{8,12},{10,14},{12,8},{14,10},{16,20},{18,... | collective-permute-start | bytes 1179656 | tf_op jit(solution)/shard_map/ppermute | solution.py:283
  83.6 13.2 %collective-permute-start.29 = (bf16[64,1536]{1,0:T(8,128)(2,1)S(1)}, bf16[64,1536]{1,0:T(8,128)(2,1)S(1)}, u32[]{:S(2)}, u32[]{:S(2)}) collective-permute-start(bf16[64,1536]{1,0:T(8,128)(2,1)S(1)} %get-tuple-element.132), channel_id=1, source_target_pairs={{0,2},{2,0},{4,6},{6,4},{8,10},{10,8},{12,14},{14,12},{16,18},{18,... | collective-permute-start | bytes 589832 | tf_op jit(solution)/shard_map/ppermute | solution.py:283
  84.6 13.7 %collective-permute-start.27 = (bf16[64,1536]{1,0:T(8,128)(2,1)S(1)}, bf16[64,1536]{1,0:T(8,128)(2,1)S(1)}, u32[]{:S(2)}, u32[]{:S(2)}) collective-permute-start(bf16[64,1536]{1,0:T(8,128)(2,1)S(1)} %get-tuple-element.130), channel_id=1, source_target_pairs={{0,4},{2,6},{4,0},{6,2},{8,12},{10,14},{12,8},{14,10},{16,20},{18,... | collective-permute-start | bytes 589832 | tf_op jit(solution)/shard_map/ppermute | solution.py:283
  94.1 7.3 %collective-permute-start.24 = (bf16[64,1536]{1,0:T(8,128)(2,1)S(1)}, bf16[64,1536]{1,0:T(8,128)(2,1)S(1)}, u32[]{:S(2)}, u32[]{:S(2)}) collective-permute-start(bf16[64,1536]{1,0:T(8,128)(2,1)S(1)} %get-tuple-element.124), channel_id=1, source_target_pairs={{0,2},{2,0},{4,6},{6,4},{8,10},{10,8},{12,14},{14,12},{16,18},{18,... | collective-permute-start | bytes 589832 | tf_op jit(solution)/shard_map/ppermute | solution.py:283
  94.7 7.8 %collective-permute-start.25 = (bf16[64,1536]{1,0:T(8,128)(2,1)S(1)}, bf16[64,1536]{1,0:T(8,128)(2,1)S(1)}, u32[]{:S(2)}, u32[]{:S(2)}) collective-permute-start(bf16[64,1536]{1,0:T(8,128)(2,1)S(1)} %get-tuple-element.126), channel_id=1, source_target_pairs={{0,4},{2,6},{4,0},{6,2},{8,12},{10,14},{12,8},{14,10},{16,20},{18,... | collective-permute-start | bytes 589832 | tf_op jit(solution)/shard_map/ppermute | solution.py:283
  96.8 10.0 %collective-permute-start.30 = (bf16[64,1536]{1,0:T(8,128)(2,1)S(1)}, bf16[64,1536]{1,0:T(8,128)(2,1)S(1)}, u32[]{:S(2)}, u32[]{:S(2)}) collective-permute-start(bf16[64,1536]{1,0:T(8,128)(2,1)S(1)} %shard_map.144), channel_id=1, source_target_pairs={{0,4},{2,6},{4,0},{6,2},{8,12},{10,14},{12,8},{14,10},{16,20},{18,... | collective-permute-start | bytes 589832 | tf_op jit(solution)/shard_map/ppermute | solution.py:283
  98.3 8.5 %collective-permute-start.28 = (bf16[64,1536]{1,0:T(8,128)(2,1)S(1)}, bf16[64,1536]{1,0:T(8,128)(2,1)S(1)}, u32[]{:S(2)}, u32[]{:S(2)}) collective-permute-start(bf16[64,1536]{1,0:T(8,128)(2,1)S(1)} %shard_map.143), channel_id=1, source_target_pairs={{0,2},{2,0},{4,6},{6,4},{8,10},{10,8},{12,14},{14,12},{16,18},{18,... | collective-permute-start | bytes 589832 | tf_op jit(solution)/shard_map/ppermute | solution.py:283
  102.7 9.7 %collective-permute-start.26 = (bf16[64,1536]{1,0:T(8,128)(2,1)S(1)}, bf16[64,1536]{1,0:T(8,128)(2,1)S(1)}, u32[]{:S(2)}, u32[]{:S(2)}) collective-permute-start(bf16[64,1536]{1,0:T(8,128)(2,1)S(1)} %get-tuple-element.128), channel_id=1, source_target_pairs={{0,16},{2,18},{4,20},{6,22},{8,24},{10,26},{12,28},{14,30},{16,0},... | collective-permute-start | bytes 589832 | tf_op jit(solution)/shard_map/ppermute | solution.py:283
  104.1 8.2 %collective-permute-start.31 = (bf16[64,1536]{1,0:T(8,128)(2,1)S(1)}, bf16[64,1536]{1,0:T(8,128)(2,1)S(1)}, u32[]{:S(2)}, u32[]{:S(2)}) collective-permute-start(bf16[64,1536]{1,0:T(8,128)(2,1)S(1)} %get-tuple-element.135), channel_id=1, source_target_pairs={{0,4},{2,6},{4,0},{6,2},{8,12},{10,14},{12,8},{14,10},{16,20},{18,... | collective-permute-start | bytes 589832 | tf_op jit(solution)/shard_map/ppermute | solution.py:283
  104.8 7.6 %collective-permute-start.32 = (bf16[64,1536]{1,0:T(8,128)(2,1)S(1)}, bf16[64,1536]{1,0:T(8,128)(2,1)S(1)}, u32[]{:S(2)}, u32[]{:S(2)}) collective-permute-start(bf16[64,1536]{1,0:T(8,128)(2,1)S(1)} %get-tuple-element.138), channel_id=1, source_target_pairs={{0,2},{2,0},{4,6},{6,4},{8,10},{10,8},{12,14},{14,12},{16,18},{18,... | collective-permute-start | bytes 589832 | tf_op jit(solution)/shard_map/ppermute | solution.py:283
  112.5 10.5 %collective-permute-start.33 = (bf16[64,1536]{1,0:T(8,128)(2,1)S(1)}, bf16[64,1536]{1,0:T(8,128)(2,1)S(1)}, u32[]{:S(2)}, u32[]{:S(2)}) collective-permute-start(bf16[64,1536]{1,0:T(8,128)(2,1)S(1)} %get-tuple-element.141), channel_id=1, source_target_pairs={{0,16},{2,18},{4,20},{6,22},{8,24},{10,26},{12,28},{14,30},{16,0},... | collective-permute-start | bytes 589832 | tf_op jit(solution)/shard_map/ppermute | solution.py:283
  (8 other events, 70.1 us)

commit v14 on v13

--- a/solution.py
+++ b/solution.py
@@ -388,11 +388,13 @@
     by_first = swap(down_first, Z_LOW)
     twins = (swap_core(both), swap_core(down))
     far = [swap(x, Z_HIGH) for x in own]
-    far[0], by_first, both_later = lax.optimization_barrier((far[0], by_first, both))
+    far[0], both_later = lax.optimization_barrier((far[0], both))
     both_by = swap(both_later, Z_LOW)
     first_one = halves(own[0], far[0])
     second_one = swap(first_one[0], X), swap(first_one[1], Y)
-    far[1], second_one, twins = lax.optimization_barrier((far[1], second_one, twins))
+    far[1], second_one, twins, by_first = lax.optimization_barrier(
+        (far[1], second_one, twins, by_first)
+    )
     first_two = halves(own[1], far[1])
     second_two = swap(first_two[0], X), swap(first_two[1], Y)
     a1, b1, a2, b2, a3, b3, a4, b4 = spread(*first_one, *second_one)

time: 124 us -> 126 us (1.016)
  waiting for transfers between devices: 67.4 us -> 60.1 us
  starting transfers between devices: 35 us -> 42.2 us
  local copies, waits for them, and re-layouts: 1.57 us -> 3.4 us
    ppermute x29, waiting for transfers between devices: 63.3 us -> 55.5 us  [swap(): lax.ppermute(block, 'expert', [(i, i ^ distance) for i in range(count)])]
    ppermute x29, starting transfers between devices: 34.2 us -> 41.3 us  [swap(): lax.ppermute(block, 'expert', [(i, i ^ distance) for i in range(count)])]
  transfers between devices with their start and end apart: 34 -> 34, of which waited for: 22 -> 20; matrix products, arithmetic and copies ran while one was open for 0% -> 1% of each run, Pallas kernels for 12% -> 12%
where the time goes in v14:
time: 126 us; the launch traced here: 125 us
  waiting for transfers between devices  60.1 us (48%)
  starting transfers between devices  42.2 us (33%)
  Pallas kernels  18.8 us (15%)
  local copies, waits for them, and re-layouts  3.4 us (3%)
    ppermute x29, waiting for transfers between devices, swap(): lax.ppermute(block, 'expert', [(i, i ^ distance) for i in range(count)])  55.5 us
    ppermute x29, starting transfers between devices, swap(): lax.ppermute(block, 'expert', [(i, i ^ distance) for i in range(count)])  41.3 us
    pallas_call x17, Pallas kernels, call(): pl.pallas_call(body, out_shape=outs, in_specs=specs or [smem if x.ndim ==...  18.8 us
    ppermute x5, waiting for transfers between devices, swap_core(): return lax.ppermute(block, 'tensor', [(0, 1), (1, 0)])  4.62 us
  transfers between devices with their start and end apart: 34, of which 20 were waited for; matrix products, arithmetic and copies ran while one was open for 1% of the time, Pallas kernels for 12%

profile of v14, /device:TPU:0, one launch (start us, length us, event | category | flops | bytes accessed | tf_op | source)
XLA Modules:
  0.0 125.5 jit_solution(1510222384321840289)
XLA Ops:
  0.6 2.1 %shard_map.132 = (bf16[64,1664]{1,0:T(8,128)(2,1)}, bf16[64,1664]{1,0:T(8,128)(2,1)}) custom-call(bf16[1536]{0:T(1024)(128)(2,1)} %refs_0_.1, bf16[64,1536]{1,0:T(8,128)(2,1)} %refs_1_.1, bf16[64,1536]{1,0:T(8,128)(2,1)} %refs_2_.1, s32[8,64]{1,0:T(8,128)} %bitcast.13, s32[8,64]{1,0:T(8,128)} %bitcast.14, f32[8,64]{1,0:T(8,128)} %bitcast.15, ...), custom_call_target="tpu_custom_call" | custom-call | flops 983040 | bytes 786432 | tf_op jit(solution)/shard_map/pallas_call | solution.py:86
  2.8 4.1 %collective-permute-start.1 = (bf16[64,1664]{1,0:T(8,128)(2,1)}, bf16[64,1664]{1,0:T(8,128)(2,1)S(1)}, u32[]{:S(2)}, u32[]{:S(2)}) collective-permute-start(bf16[64,1664]{1,0:T(8,128)(2,1)} %get-tuple-element.76), channel_id=1, source_target_pairs={{0,16},{2,18},{4,20},{6,22},{8,24},{10,26},{12,28},{14,30},{16,0},... | collective-permute-start | bytes 638984 | tf_op jit(solution)/shard_map/ppermute | solution.py:283
  10.0 2.0 %shard_map.131 = (bf16[256,768]{1,0:T(8,128)(2,1)}, bf16[256,768]{1,0:T(8,128)(2,1)}) custom-call(bf16[512,768]{1,0:T(8,128)(2,1)} %bitcast.7), custom_call_target="tpu_custom_call" | custom-call | bytes 1572864 | tf_op jit(solution)/shard_map/pallas_call | solution.py:86
  12.0 1.7 %collective-permute-start.6 = (bf16[256,768]{1,0:T(8,128)(2,1)}, bf16[256,768]{1,0:T(8,128)(2,1)S(1)}, u32[]{:S(2)}, u32[]{:S(2)}) collective-permute-start(bf16[256,768]{1,0:T(8,128)(2,1)} %get-tuple-element.80), channel_id=1, source_target_pairs={{0,8},{2,10},{4,12},{6,14},{8,0},{10,2},{12,4},{14,6},{16,24},{18,... | collective-permute-start | bytes 1179656 | tf_op jit(solution)/shard_map/ppermute | solution.py:283
  14.8 7.6 %collective-permute-done.1 = bf16[64,1664]{1,0:T(8,128)(2,1)S(1)} collective-permute-done((bf16[64,1664]{1,0:T(8,128)(2,1)}, bf16[64,1664]{1,0:T(8,128)(2,1)S(1)}, u32[]{:S(2)}, u32[]{:S(2)}) %collective-permute-start.1) | collective-permute-done | bytes 213024 | tf_op jit(solution)/shard_map/ppermute | solution.py:283
  22.5 3.6 %collective-permute-done = bf16[64,1664]{1,0:T(8,128)(2,1)S(1)} collective-permute-done((bf16[64,1664]{1,0:T(8,128)(2,1)}, bf16[64,1664]{1,0:T(8,128)(2,1)S(1)}, u32[]{:S(2)}, u32[]{:S(2)}) %collective-permute-start) | collective-permute-done | bytes 213024 | tf_op jit(solution)/shard_map/ppermute | solution.py:283
  27.7 3.2 %collective-permute-done.6.first_a = bf16[256,768]{1,0:T(8,128)(2,1)S(1)} collective-permute-done((bf16[256,768]{1,0:T(8,128)(2,1)}, bf16[256,768]{1,0:T(8,128)(2,1)S(1)}, u32[]{:S(2)}, u32[]{:S(2)}) %collective-permute-start.6) | collective-permute-done | bytes 393248 | tf_op jit(solution)/shard_map/ppermute | solution.py:283
  30.9 1.6 %collective-permute-start.2 = (bf16[64,1664]{1,0:T(8,128)(2,1)S(1)}, bf16[64,1664]{1,0:T(8,128)(2,1)S(1)}, u32[]{:S(2)}, u32[]{:S(2)}) collective-permute-start(bf16[64,1664]{1,0:T(8,128)(2,1)S(1)} %pad_maximum_fusion.refs_4_), channel_id=1, source_target_pairs={{0,2},{2,0},{4,6},{6,4},{8,10},{10,8},{12,14},{14,12},{16,18},{18,... | collective-permute-start | bytes 638984 | tf_op jit(solution)/shard_map/ppermute | solution.py:283
  33.7 5.3 %collective-permute-done.2.refs_5_ = bf16[64,1664]{1,0:T(8,128)(2,1)S(1)} collective-permute-done((bf16[64,1664]{1,0:T(8,128)(2,1)S(1)}, bf16[64,1664]{1,0:T(8,128)(2,1)S(1)}, u32[]{:S(2)}, u32[]{:S(2)}) %collective-permute-start.2) | collective-permute-done | bytes 213024 | tf_op jit(solution)/shard_map/ppermute | solution.py:283
  39.1 1.6 %collective-permute-start.10 = (bf16[64,1664]{1,0:T(8,128)(2,1)S(1)}, bf16[64,1664]{1,0:T(8,128)(2,1)S(1)}, u32[]{:S(2)}, u32[]{:S(2)}) collective-permute-start(bf16[64,1664]{1,0:T(8,128)(2,1)S(1)} %pad_maximum_fusion.refs_4_), channel_id=1, source_target_pairs={{0,4},{2,6},{4,0},{6,2},{8,12},{10,14},{12,8},{14,10},{16,20},{18,... | collective-permute-start | bytes 638984 | tf_op jit(solution)/shard_map/ppermute | solution.py:283
  41.2 1.7 %collective-permute-start.15 = (bf16[64,1664]{1,0:T(8,128)(2,1)S(1)}, bf16[64,1664]{1,0:T(8,128)(2,1)S(1)}, u32[]{:S(2)}, u32[]{:S(2)}) collective-permute-start(bf16[64,1664]{1,0:T(8,128)(2,1)S(1)} %pad_maximum_fusion.3.refs_7_), channel_id=1, source_target_pairs={{0,2},{2,0},{4,6},{6,4},{8,10},{10,8},{12,14},{14,12},{16,18},{18,... | collective-permute-start | bytes 638984 | tf_op jit(solution)/shard_map/ppermute | solution.py:283
  43.6 1.7 %collective-permute-start.16 = (bf16[64,1664]{1,0:T(8,128)(2,1)S(1)}, bf16[64,1664]{1,0:T(8,128)(2,1)S(1)}, u32[]{:S(2)}, u32[]{:S(2)}) collective-permute-start(bf16[64,1664]{1,0:T(8,128)(2,1)S(1)} %pad_maximum_fusion.2.refs_6_), channel_id=1, source_target_pairs={{0,2},{2,0},{4,6},{6,4},{8,10},{10,8},{12,14},{14,12},{16,18},{18,... | collective-permute-start | bytes 638984 | tf_op jit(solution)/shard_map/ppermute | solution.py:283
  46.3 1.7 %collective-permute-start.18 = (bf16[64,1664]{1,0:T(8,128)(2,1)S(1)}, bf16[64,1664]{1,0:T(8,128)(2,1)S(1)}, u32[]{:S(2)}, u32[]{:S(2)}) collective-permute-start(bf16[64,1664]{1,0:T(8,128)(2,1)S(1)} %pad_maximum_fusion.3.refs_7_), channel_id=1, source_target_pairs={{0,4},{2,6},{4,0},{6,2},{8,12},{10,14},{12,8},{14,10},{16,20},{18,... | collective-permute-start | bytes 638984 | tf_op jit(solution)/shard_map/ppermute | solution.py:283
  48.1 2.8 %collective-permute-done.14.refs_2_ = bf16[64,1664]{1,0:T(8,128)(2,1)S(1)} collective-permute-done((bf16[64,1664]{1,0:T(8,128)(2,1)S(1)}, bf16[64,1664]{1,0:T(8,128)(2,1)S(1)}, u32[]{:S(2)}, u32[]{:S(2)}) %collective-permute-start.14) | collective-permute-done | bytes 213024 | tf_op jit(solution)/shard_map/ppermute | solution.py:283
  50.9 1.7 %collective-permute-start.11 = (bf16[64,1664]{1,0:T(8,128)(2,1)S(1)}, bf16[64,1664]{1,0:T(8,128)(2,1)S(1)}, u32[]{:S(2)}, u32[]{:S(2)}) collective-permute-start(bf16[64,1664]{1,0:T(8,128)(2,1)S(1)} %collective-permute-done.2.refs_5_), channel_id=1, source_target_pairs={{0,4},{2,6},{4,0},{6,2},{8,12},{10,14},{12,8},{14,10},{16,20},{18,... | collective-permute-start | bytes 638984 | tf_op jit(solution)/shard_map/ppermute | solution.py:283
  52.6 2.2 %collective-permute-start.13 = (bf16[64,1664]{1,0:T(8,128)(2,1)S(1)}, bf16[64,1664]{1,0:T(8,128)(2,1)S(1)}, u32[]{:S(2)}, u32[]{:S(2)}) collective-permute-start(bf16[64,1664]{1,0:T(8,128)(2,1)S(1)} %collective-permute-done.3.refs_7_), channel_id=1, source_target_pairs={{0,2},{2,0},{4,6},{6,4},{8,10},{10,8},{12,14},{14,12},{16,18},{18,... | collective-permute-start | bytes 638984 | tf_op jit(solution)/shard_map/ppermute | solution.py:283
  55.7 2.2 %collective-permute-start.19 = (bf16[64,1664]{1,0:T(8,128)(2,1)S(1)}, bf16[64,1664]{1,0:T(8,128)(2,1)S(1)}, u32[]{:S(2)}, u32[]{:S(2)}) collective-permute-start(bf16[64,1664]{1,0:T(8,128)(2,1)S(1)} %collective-permute-done.18.refs_5_), channel_id=1, source_target_pairs={{0,2},{2,0},{4,6},{6,4},{8,10},{10,8},{12,14},{14,12},{16,18},{18,... | collective-permute-start | bytes 638984 | tf_op jit(solution)/shard_map/ppermute | solution.py:283
  58.7 3.1 %shard_map.134.total_ref = f32[512,1536]{1,0:T(8,128)S(1)} custom-call(bf16[64,1664]{1,0:T(8,128)(2,1)S(1)} %collective-permute-done.10.refs_0_, bf16[64,1664]{1,0:T(8,128)(2,1)S(1)} %collective-permute-done.11.refs_1_, bf16[64,1664]{1,0:T(8,128)(2,1)S(1)} %collective-permute-done.12.refs_2_, bf16[64,1664]{1,0:T(8,128)(2,1)S(1)} %collective-permute-done.13.refs_3_, ...), custom_call_target="tpu_custom_call" | custom-call | bytes 9437184 | tf_op jit(solution)/shard_map/pallas_call | solution.py:86
  61.9 3.1 %shard_map.135.total_ref = f32[512,1536]{1,0:T(8,128)S(1)} custom-call(bf16[64,1664]{1,0:T(8,128)(2,1)S(1)} %collective-permute-done.17.refs_0_, bf16[64,1664]{1,0:T(8,128)(2,1)S(1)} %collective-permute-done.19.refs_1_, bf16[64,1664]{1,0:T(8,128)(2,1)S(1)} %collective-permute-done.14.refs_2_, bf16[64,1664]{1,0:T(8,128)(2,1)S(1)} %collective-permute-done.15.refs_3_, ...), custom_call_target="tpu_custom_call" | custom-call | bytes 9437184 | tf_op jit(solution)/shard_map/pallas_call | solution.py:86
  65.6 2.9 %collective-permute-done.20.refs_9_ = bf16[768,1024]{1,0:T(8,128)(2,1)S(1)} collective-permute-done((bf16[768,1024]{1,0:T(8,128)(2,1)S(1)}, bf16[768,1024]{1,0:T(8,128)(2,1)S(1)}, u32[]{:S(2)}, u32[]{:S(2)}) %collective-permute-start.20) | collective-permute-done | bytes 1572896 | tf_op jit(solution)/shard_map/ppermute | solution.py:287
  68.5 2.1 %shard_map.137 = (bf16[512,512]{1,0:T(8,128)(2,1)S(1)}, f32[512,128]{1,0:T(8,128)S(1)}) custom-call(bf16[64,1664]{1,0:T(8,128)(2,1)S(1)} %collective-permute-done.17.refs_0_, bf16[64,1664]{1,0:T(8,128)(2,1)S(1)} %collective-permute-done.19.refs_1_, bf16[64,1664]{1,0:T(8,128)(2,1)S(1)} %collective-permute-done.14.refs_2_, ...), custom_call_target="tpu_custom_call" | custom-call | flops 1610612736 | bytes 4718592 | tf_op jit(solution)/shard_map/pallas_call | solution.py:86
  70.7 2.1 %shard_map.136 = (bf16[512,512]{1,0:T(8,128)(2,1)S(1)}, f32[512,128]{1,0:T(8,128)S(1)}) custom-call(bf16[64,1664]{1,0:T(8,128)(2,1)S(1)} %collective-permute-done.10.refs_0_, bf16[64,1664]{1,0:T(8,128)(2,1)S(1)} %collective-permute-done.11.refs_1_, bf16[64,1664]{1,0:T(8,128)(2,1)S(1)} %collective-permute-done.12.refs_2_, ...), custom_call_target="tpu_custom_call" | custom-call | flops 1610612736 | bytes 4718592 | tf_op jit(solution)/shard_map/pallas_call | solution.py:86
  72.8 3.8 %collective-permute-done.7.last_a = bf16[256,768]{1,0:T(8,128)(2,1)S(1)} collective-permute-done((bf16[256,768]{1,0:T(8,128)(2,1)S(1)}, bf16[256,768]{1,0:T(8,128)(2,1)S(1)}, u32[]{:S(2)}, u32[]{:S(2)}) %collective-permute-start.7) | collective-permute-done | bytes 393248 | tf_op jit(solution)/shard_map/ppermute | solution.py:283
  76.7 1.7 %collective-permute-done.21.last_b = bf16[256,768]{1,0:T(8,128)(2,1)S(1)} collective-permute-done((bf16[256,768]{1,0:T(8,128)(2,1)S(1)}, bf16[256,768]{1,0:T(8,128)(2,1)S(1)}, u32[]{:S(2)}, u32[]{:S(2)}) %collective-permute-start.21) | collective-permute-done | bytes 393248 | tf_op jit(solution)/shard_map/ppermute | solution.py:287
  79.4 2.1 %collective-permute-start.23 = (bf16[128,1536]{1,0:T(8,128)(2,1)S(1)}, bf16[128,1536]{1,0:T(8,128)(2,1)S(1)}, u32[]{:S(2)}, u32[]{:S(2)}) collective-permute-start(bf16[128,1536]{1,0:T(8,128)(2,1)S(1)} %get-tuple-element.115), channel_id=1, source_target_pairs={{0,2},{2,0},{4,6},{6,4},{8,10},{10,8},{12,14},{14,12},{16,18},{18,... | collective-permute-start | bytes 1179656 | tf_op jit(solution)/shard_map/ppermute | solution.py:283
  84.7 6.7 %collective-permute-done.23.got_ref = bf16[128,1536]{1,0:T(8,128)(2,1)S(1)} collective-permute-done((bf16[128,1536]{1,0:T(8,128)(2,1)S(1)}, bf16[128,1536]{1,0:T(8,128)(2,1)S(1)}, u32[]{:S(2)}, u32[]{:S(2)}) %collective-permute-start.23) | collective-permute-done | bytes 393248 | tf_op jit(solution)/shard_map/ppermute | solution.py:283
  91.5 2.0 %collective-permute-done.22.got_ref = bf16[128,1536]{1,0:T(8,128)(2,1)S(1)} collective-permute-done((bf16[128,1536]{1,0:T(8,128)(2,1)S(1)}, bf16[128,1536]{1,0:T(8,128)(2,1)S(1)}, u32[]{:S(2)}, u32[]{:S(2)}) %collective-permute-start.22) | collective-permute-done | bytes 393248 | tf_op jit(solution)/shard_map/ppermute | solution.py:283
  95.6 1.6 %collective-permute-start.30 = (bf16[64,1536]{1,0:T(8,128)(2,1)S(1)}, bf16[64,1536]{1,0:T(8,128)(2,1)S(1)}, u32[]{:S(2)}, u32[]{:S(2)}) collective-permute-start(bf16[64,1536]{1,0:T(8,128)(2,1)S(1)} %shard_map.144), channel_id=1, source_target_pairs={{0,4},{2,6},{4,0},{6,2},{8,12},{10,14},{12,8},{14,10},{16,20},{18,... | collective-permute-start | bytes 589832 | tf_op jit(solution)/shard_map/ppermute | solution.py:283
  100.1 1.8 %collective-permute-done.25.got_b = bf16[64,1536]{1,0:T(8,128)(2,1)S(1)} collective-permute-done((bf16[64,1536]{1,0:T(8,128)(2,1)S(1)}, bf16[64,1536]{1,0:T(8,128)(2,1)S(1)}, u32[]{:S(2)}, u32[]{:S(2)}) %collective-permute-start.25) | collective-permute-done | bytes 196640 | tf_op jit(solution)/shard_map/ppermute | solution.py:283
  102.0 4.8 %collective-permute-start.26 = (bf16[64,1536]{1,0:T(8,128)(2,1)S(1)}, bf16[64,1536]{1,0:T(8,128)(2,1)S(1)}, u32[]{:S(2)}, u32[]{:S(2)}) collective-permute-start(bf16[64,1536]{1,0:T(8,128)(2,1)S(1)} %get-tuple-element.128), channel_id=1, source_target_pairs={{0,16},{2,18},{4,20},{6,22},{8,24},{10,26},{12,28},{14,30},{16,0},... | collective-permute-start | bytes 589832 | tf_op jit(solution)/shard_map/ppermute | solution.py:283
  109.5 4.4 %collective-permute-done.26.got_ref = bf16[64,1536]{1,0:T(8,128)(2,1)S(1)} collective-permute-done((bf16[64,1536]{1,0:T(8,128)(2,1)S(1)}, bf16[64,1536]{1,0:T(8,128)(2,1)S(1)}, u32[]{:S(2)}, u32[]{:S(2)}) %collective-permute-start.26) | collective-permute-done | bytes 196640 | tf_op jit(solution)/shard_map/ppermute | solution.py:283
  114.8 9.9 %collective-permute-done.33.got_ref = bf16[64,1536]{1,0:T(8,128)(2,1)S(1)} collective-permute-done((bf16[64,1536]{1,0:T(8,128)(2,1)S(1)}, bf16[64,1536]{1,0:T(8,128)(2,1)S(1)}, u32[]{:S(2)}, u32[]{:S(2)}) %collective-permute-start.33) | collective-permute-done | bytes 196640 | tf_op jit(solution)/shard_map/ppermute | solution.py:283
  (70 shorter events, 25.3 us)
Async XLA Ops:
  2.8 19.6 %collective-permute-start.1 = (bf16[64,1664]{1,0:T(8,128)(2,1)}, bf16[64,1664]{1,0:T(8,128)(2,1)S(1)}, u32[]{:S(2)}, u32[]{:S(2)}) collective-permute-start(bf16[64,1664]{1,0:T(8,128)(2,1)} %get-tuple-element.76), channel_id=1, source_target_pairs={{0,16},{2,18},{4,20},{6,22},{8,24},{10,26},{12,28},{14,30},{16,0},... | collective-permute-start | bytes 638984 | tf_op jit(solution)/shard_map/ppermute | solution.py:283
  9.4 31.3 %collective-permute-start.4 = (bf16[768,1024]{1,0:T(8,128)(2,1)S(1)}, bf16[768,1024]{1,0:T(8,128)(2,1)S(1)}, u32[]{:S(2)}, u32[]{:S(2)}) collective-permute-start(bf16[768,1024]{1,0:T(8,128)(2,1)S(1)} %shard_map.133.refs_8_), channel_id=1, source_target_pairs={{0,1},{1,0},{2,3},{3,2},{4,5},{5,4},{6,7},{7,6},{8,9},{9,8},{10,11... | collective-permute-start | bytes 4718600 | tf_op jit(solution)/shard_map/ppermute | solution.py:287
  9.5 16.6 %collective-permute-start = (bf16[64,1664]{1,0:T(8,128)(2,1)}, bf16[64,1664]{1,0:T(8,128)(2,1)S(1)}, u32[]{:S(2)}, u32[]{:S(2)}) collective-permute-start(bf16[64,1664]{1,0:T(8,128)(2,1)} %get-tuple-element.75), channel_id=1, source_target_pairs={{0,16},{2,18},{4,20},{6,22},{8,24},{10,26},{12,28},{14,30},{16,0},... | collective-permute-start | bytes 638984 | tf_op jit(solution)/shard_map/ppermute | solution.py:283
  9.6 31.1 %collective-permute-start.5 = (bf16[512,768]{1,0:T(8,128)(2,1)S(1)}, bf16[512,768]{1,0:T(8,128)(2,1)S(1)}, u32[]{:S(2)}, u32[]{:S(2)}) collective-permute-start(bf16[512,768]{1,0:T(8,128)(2,1)S(1)} %bitcast.8), channel_id=1, source_target_pairs={{0,1},{1,0},{2,3},{3,2},{4,5},{5,4},{6,7},{7,6},{8,9},{9,8},{10,11... | collective-permute-start | bytes 2359304 | tf_op jit(solution)/shard_map/ppermute | solution.py:287
  12.0 18.9 %collective-permute-start.6 = (bf16[256,768]{1,0:T(8,128)(2,1)}, bf16[256,768]{1,0:T(8,128)(2,1)S(1)}, u32[]{:S(2)}, u32[]{:S(2)}) collective-permute-start(bf16[256,768]{1,0:T(8,128)(2,1)} %get-tuple-element.80), channel_id=1, source_target_pairs={{0,8},{2,10},{4,12},{6,14},{8,0},{10,2},{12,4},{14,6},{16,24},{18,... | collective-permute-start | bytes 1179656 | tf_op jit(solution)/shard_map/ppermute | solution.py:283
  22.4 42.6 %collective-permute-start.9 = (bf16[768,1024]{1,0:T(8,128)(2,1)S(1)}, bf16[768,1024]{1,0:T(8,128)(2,1)S(1)}, u32[]{:S(2)}, u32[]{:S(2)}) collective-permute-start(bf16[768,1024]{1,0:T(8,128)(2,1)S(1)} %shard_map.133.refs_8_), channel_id=1, source_target_pairs={{0,8},{2,10},{4,12},{6,14},{8,0},{10,2},{12,4},{14,6},{16,24},{18,... | collective-permute-start | bytes 4718600 | tf_op jit(solution)/shard_map/ppermute | solution.py:283
  26.1 6.4 %collective-permute-start.3 = (bf16[64,1664]{1,0:T(8,128)(2,1)S(1)}, bf16[64,1664]{1,0:T(8,128)(2,1)S(1)}, u32[]{:S(2)}, u32[]{:S(2)}) collective-permute-start(bf16[64,1664]{1,0:T(8,128)(2,1)S(1)} %pad_maximum_fusion.1.refs_6_), channel_id=1, source_target_pairs={{0,4},{2,6},{4,0},{6,2},{8,12},{10,14},{12,8},{14,10},{16,20},{18,... | collective-permute-start | bytes 638984 | tf_op jit(solution)/shard_map/ppermute | solution.py:283
  30.9 8.2 %collective-permute-start.2 = (bf16[64,1664]{1,0:T(8,128)(2,1)S(1)}, bf16[64,1664]{1,0:T(8,128)(2,1)S(1)}, u32[]{:S(2)}, u32[]{:S(2)}) collective-permute-start(bf16[64,1664]{1,0:T(8,128)(2,1)S(1)} %pad_maximum_fusion.refs_4_), channel_id=1, source_target_pairs={{0,2},{2,0},{4,6},{6,4},{8,10},{10,8},{12,14},{14,12},{16,18},{18,... | collective-permute-start | bytes 638984 | tf_op jit(solution)/shard_map/ppermute | solution.py:283
  32.5 11.1 %collective-permute-start.12 = (bf16[64,1664]{1,0:T(8,128)(2,1)S(1)}, bf16[64,1664]{1,0:T(8,128)(2,1)S(1)}, u32[]{:S(2)}, u32[]{:S(2)}) collective-permute-start(bf16[64,1664]{1,0:T(8,128)(2,1)S(1)} %pad_maximum_fusion.1.refs_6_), channel_id=1, source_target_pairs={{0,2},{2,0},{4,6},{6,4},{8,10},{10,8},{12,14},{14,12},{16,18},{18,... | collective-permute-start | bytes 638984 | tf_op jit(solution)/shard_map/ppermute | solution.py:283
  39.1 7.2 %collective-permute-start.10 = (bf16[64,1664]{1,0:T(8,128)(2,1)S(1)}, bf16[64,1664]{1,0:T(8,128)(2,1)S(1)}, u32[]{:S(2)}, u32[]{:S(2)}) collective-permute-start(bf16[64,1664]{1,0:T(8,128)(2,1)S(1)} %pad_maximum_fusion.refs_4_), channel_id=1, source_target_pairs={{0,4},{2,6},{4,0},{6,2},{8,12},{10,14},{12,8},{14,10},{16,20},{18,... | collective-permute-start | bytes 638984 | tf_op jit(solution)/shard_map/ppermute | solution.py:283
  40.8 10.1 %collective-permute-start.14 = (bf16[64,1664]{1,0:T(8,128)(2,1)S(1)}, bf16[64,1664]{1,0:T(8,128)(2,1)S(1)}, u32[]{:S(2)}, u32[]{:S(2)}) collective-permute-start(bf16[64,1664]{1,0:T(8,128)(2,1)S(1)} %pad_maximum_fusion.2.refs_6_), channel_id=1, source_target_pairs={{0,4},{2,6},{4,0},{6,2},{8,12},{10,14},{12,8},{14,10},{16,20},{18,... | collective-permute-start | bytes 638984 | tf_op jit(solution)/shard_map/ppermute | solution.py:283
  41.2 11.4 %collective-permute-start.15 = (bf16[64,1664]{1,0:T(8,128)(2,1)S(1)}, bf16[64,1664]{1,0:T(8,128)(2,1)S(1)}, u32[]{:S(2)}, u32[]{:S(2)}) collective-permute-start(bf16[64,1664]{1,0:T(8,128)(2,1)S(1)} %pad_maximum_fusion.3.refs_7_), channel_id=1, source_target_pairs={{0,2},{2,0},{4,6},{6,4},{8,10},{10,8},{12,14},{14,12},{16,18},{18,... | collective-permute-start | bytes 638984 | tf_op jit(solution)/shard_map/ppermute | solution.py:283
  43.6 11.3 %collective-permute-start.16 = (bf16[64,1664]{1,0:T(8,128)(2,1)S(1)}, bf16[64,1664]{1,0:T(8,128)(2,1)S(1)}, u32[]{:S(2)}, u32[]{:S(2)}) collective-permute-start(bf16[64,1664]{1,0:T(8,128)(2,1)S(1)} %pad_maximum_fusion.2.refs_6_), channel_id=1, source_target_pairs={{0,2},{2,0},{4,6},{6,4},{8,10},{10,8},{12,14},{14,12},{16,18},{18,... | collective-permute-start | bytes 638984 | tf_op jit(solution)/shard_map/ppermute | solution.py:283
  46.3 9.4 %collective-permute-start.18 = (bf16[64,1664]{1,0:T(8,128)(2,1)S(1)}, bf16[64,1664]{1,0:T(8,128)(2,1)S(1)}, u32[]{:S(2)}, u32[]{:S(2)}) collective-permute-start(bf16[64,1664]{1,0:T(8,128)(2,1)S(1)} %pad_maximum_fusion.3.refs_7_), channel_id=1, source_target_pairs={{0,4},{2,6},{4,0},{6,2},{8,12},{10,14},{12,8},{14,10},{16,20},{18,... | collective-permute-start | bytes 638984 | tf_op jit(solution)/shard_map/ppermute | solution.py:283
  50.9 7.7 %collective-permute-start.11 = (bf16[64,1664]{1,0:T(8,128)(2,1)S(1)}, bf16[64,1664]{1,0:T(8,128)(2,1)S(1)}, u32[]{:S(2)}, u32[]{:S(2)}) collective-permute-start(bf16[64,1664]{1,0:T(8,128)(2,1)S(1)} %collective-permute-done.2.refs_5_), channel_id=1, source_target_pairs={{0,4},{2,6},{4,0},{6,2},{8,12},{10,14},{12,8},{14,10},{16,20},{18,... | collective-permute-start | bytes 638984 | tf_op jit(solution)/shard_map/ppermute | solution.py:283
  52.6 6.1 %collective-permute-start.13 = (bf16[64,1664]{1,0:T(8,128)(2,1)S(1)}, bf16[64,1664]{1,0:T(8,128)(2,1)S(1)}, u32[]{:S(2)}, u32[]{:S(2)}) collective-permute-start(bf16[64,1664]{1,0:T(8,128)(2,1)S(1)} %collective-permute-done.3.refs_7_), channel_id=1, source_target_pairs={{0,2},{2,0},{4,6},{6,4},{8,10},{10,8},{12,14},{14,12},{16,18},{18,... | collective-permute-start | bytes 638984 | tf_op jit(solution)/shard_map/ppermute | solution.py:283
  54.9 7.0 %collective-permute-start.17 = (bf16[64,1664]{1,0:T(8,128)(2,1)S(1)}, bf16[64,1664]{1,0:T(8,128)(2,1)S(1)}, u32[]{:S(2)}, u32[]{:S(2)}) collective-permute-start(bf16[64,1664]{1,0:T(8,128)(2,1)S(1)} %collective-permute-done.16.refs_4_), channel_id=1, source_target_pairs={{0,4},{2,6},{4,0},{6,2},{8,12},{10,14},{12,8},{14,10},{16,20},{18,... | collective-permute-start | bytes 638984 | tf_op jit(solution)/shard_map/ppermute | solution.py:283
  55.7 6.2 %collective-permute-start.19 = (bf16[64,1664]{1,0:T(8,128)(2,1)S(1)}, bf16[64,1664]{1,0:T(8,128)(2,1)S(1)}, u32[]{:S(2)}, u32[]{:S(2)}) collective-permute-start(bf16[64,1664]{1,0:T(8,128)(2,1)S(1)} %collective-permute-done.18.refs_5_), channel_id=1, source_target_pairs={{0,2},{2,0},{4,6},{6,4},{8,10},{10,8},{12,14},{14,12},{16,18},{18,... | collective-permute-start | bytes 638984 | tf_op jit(solution)/shard_map/ppermute | solution.py:283
  65.1 11.5 %collective-permute-start.7 = (bf16[256,768]{1,0:T(8,128)(2,1)S(1)}, bf16[256,768]{1,0:T(8,128)(2,1)S(1)}, u32[]{:S(2)}, u32[]{:S(2)}) collective-permute-start(bf16[256,768]{1,0:T(8,128)(2,1)S(1)} %copy-done.4), channel_id=1, source_target_pairs={{0,8},{2,10},{4,12},{6,14},{8,0},{10,2},{12,4},{14,6},{16,24},{18,... | collective-permute-start | bytes 1179656 | tf_op jit(solution)/shard_map/ppermute | solution.py:283
  65.2 11.4 %collective-permute-start.8 = (bf16[256,768]{1,0:T(8,128)(2,1)S(1)}, bf16[256,768]{1,0:T(8,128)(2,1)S(1)}, u32[]{:S(2)}, u32[]{:S(2)}) collective-permute-start(bf16[256,768]{1,0:T(8,128)(2,1)S(1)} %collective-permute-done.6.first_a), channel_id=1, source_target_pairs={{0,1},{1,0},{2,3},{3,2},{4,5},{5,4},{6,7},{7,6},{8,9},{9,8},{10,11... | collective-permute-start | bytes 1179656 | tf_op jit(solution)/shard_map/ppermute | solution.py:287
  79.4 12.0 %collective-permute-start.23 = (bf16[128,1536]{1,0:T(8,128)(2,1)S(1)}, bf16[128,1536]{1,0:T(8,128)(2,1)S(1)}, u32[]{:S(2)}, u32[]{:S(2)}) collective-permute-start(bf16[128,1536]{1,0:T(8,128)(2,1)S(1)} %get-tuple-element.115), channel_id=1, source_target_pairs={{0,2},{2,0},{4,6},{6,4},{8,10},{10,8},{12,14},{14,12},{16,18},{18,... | collective-permute-start | bytes 1179656 | tf_op jit(solution)/shard_map/ppermute | solution.py:283
  81.5 12.0 %collective-permute-start.22 = (bf16[128,1536]{1,0:T(8,128)(2,1)S(1)}, bf16[128,1536]{1,0:T(8,128)(2,1)S(1)}, u32[]{:S(2)}, u32[]{:S(2)}) collective-permute-start(bf16[128,1536]{1,0:T(8,128)(2,1)S(1)} %get-tuple-element.111), channel_id=1, source_target_pairs={{0,4},{2,6},{4,0},{6,2},{8,12},{10,14},{12,8},{14,10},{16,20},{18,... | collective-permute-start | bytes 1179656 | tf_op jit(solution)/shard_map/ppermute | solution.py:283
  83.9 11.7 %collective-permute-start.29 = (bf16[64,1536]{1,0:T(8,128)(2,1)S(1)}, bf16[64,1536]{1,0:T(8,128)(2,1)S(1)}, u32[]{:S(2)}, u32[]{:S(2)}) collective-permute-start(bf16[64,1536]{1,0:T(8,128)(2,1)S(1)} %get-tuple-element.132), channel_id=1, source_target_pairs={{0,2},{2,0},{4,6},{6,4},{8,10},{10,8},{12,14},{14,12},{16,18},{18,... | collective-permute-start | bytes 589832 | tf_op jit(solution)/shard_map/ppermute | solution.py:283
  84.1 13.6 %collective-permute-start.27 = (bf16[64,1536]{1,0:T(8,128)(2,1)S(1)}, bf16[64,1536]{1,0:T(8,128)(2,1)S(1)}, u32[]{:S(2)}, u32[]{:S(2)}) collective-permute-start(bf16[64,1536]{1,0:T(8,128)(2,1)S(1)} %get-tuple-element.130), channel_id=1, source_target_pairs={{0,4},{2,6},{4,0},{6,2},{8,12},{10,14},{12,8},{14,10},{16,20},{18,... | collective-permute-start | bytes 589832 | tf_op jit(solution)/shard_map/ppermute | solution.py:283
  93.5 6.6 %collective-permute-start.24 = (bf16[64,1536]{1,0:T(8,128)(2,1)S(1)}, bf16[64,1536]{1,0:T(8,128)(2,1)S(1)}, u32[]{:S(2)}, u32[]{:S(2)}) collective-permute-start(bf16[64,1536]{1,0:T(8,128)(2,1)S(1)} %get-tuple-element.124), channel_id=1, source_target_pairs={{0,2},{2,0},{4,6},{6,4},{8,10},{10,8},{12,14},{14,12},{16,18},{18,... | collective-permute-start | bytes 589832 | tf_op jit(solution)/shard_map/ppermute | solution.py:283
  93.7 8.2 %collective-permute-start.25 = (bf16[64,1536]{1,0:T(8,128)(2,1)S(1)}, bf16[64,1536]{1,0:T(8,128)(2,1)S(1)}, u32[]{:S(2)}, u32[]{:S(2)}) collective-permute-start(bf16[64,1536]{1,0:T(8,128)(2,1)S(1)} %get-tuple-element.126), channel_id=1, source_target_pairs={{0,4},{2,6},{4,0},{6,2},{8,12},{10,14},{12,8},{14,10},{16,20},{18,... | collective-permute-start | bytes 589832 | tf_op jit(solution)/shard_map/ppermute | solution.py:283
  95.6 13.9 %collective-permute-start.30 = (bf16[64,1536]{1,0:T(8,128)(2,1)S(1)}, bf16[64,1536]{1,0:T(8,128)(2,1)S(1)}, u32[]{:S(2)}, u32[]{:S(2)}) collective-permute-start(bf16[64,1536]{1,0:T(8,128)(2,1)S(1)} %shard_map.144), channel_id=1, source_target_pairs={{0,4},{2,6},{4,0},{6,2},{8,12},{10,14},{12,8},{14,10},{16,20},{18,... | collective-permute-start | bytes 589832 | tf_op jit(solution)/shard_map/ppermute | solution.py:283
  97.7 11.8 %collective-permute-start.28 = (bf16[64,1536]{1,0:T(8,128)(2,1)S(1)}, bf16[64,1536]{1,0:T(8,128)(2,1)S(1)}, u32[]{:S(2)}, u32[]{:S(2)}) collective-permute-start(bf16[64,1536]{1,0:T(8,128)(2,1)S(1)} %shard_map.143), channel_id=1, source_target_pairs={{0,2},{2,0},{4,6},{6,4},{8,10},{10,8},{12,14},{14,12},{16,18},{18,... | collective-permute-start | bytes 589832 | tf_op jit(solution)/shard_map/ppermute | solution.py:283
  102.0 12.0 %collective-permute-start.26 = (bf16[64,1536]{1,0:T(8,128)(2,1)S(1)}, bf16[64,1536]{1,0:T(8,128)(2,1)S(1)}, u32[]{:S(2)}, u32[]{:S(2)}) collective-permute-start(bf16[64,1536]{1,0:T(8,128)(2,1)S(1)} %get-tuple-element.128), channel_id=1, source_target_pairs={{0,16},{2,18},{4,20},{6,22},{8,24},{10,26},{12,28},{14,30},{16,0},... | collective-permute-start | bytes 589832 | tf_op jit(solution)/shard_map/ppermute | solution.py:283
  106.8 7.2 %collective-permute-start.31 = (bf16[64,1536]{1,0:T(8,128)(2,1)S(1)}, bf16[64,1536]{1,0:T(8,128)(2,1)S(1)}, u32[]{:S(2)}, u32[]{:S(2)}) collective-permute-start(bf16[64,1536]{1,0:T(8,128)(2,1)S(1)} %get-tuple-element.135), channel_id=1, source_target_pairs={{0,4},{2,6},{4,0},{6,2},{8,12},{10,14},{12,8},{14,10},{16,20},{18,... | collective-permute-start | bytes 589832 | tf_op jit(solution)/shard_map/ppermute | solution.py:283
  108.2 5.8 %collective-permute-start.32 = (bf16[64,1536]{1,0:T(8,128)(2,1)S(1)}, bf16[64,1536]{1,0:T(8,128)(2,1)S(1)}, u32[]{:S(2)}, u32[]{:S(2)}) collective-permute-start(bf16[64,1536]{1,0:T(8,128)(2,1)S(1)} %get-tuple-element.138), channel_id=1, source_target_pairs={{0,2},{2,0},{4,6},{6,4},{8,10},{10,8},{12,14},{14,12},{16,18},{18,... | collective-permute-start | bytes 589832 | tf_op jit(solution)/shard_map/ppermute | solution.py:283
  114.0 10.7 %collective-permute-start.33 = (bf16[64,1536]{1,0:T(8,128)(2,1)S(1)}, bf16[64,1536]{1,0:T(8,128)(2,1)S(1)}, u32[]{:S(2)}, u32[]{:S(2)}) collective-permute-start(bf16[64,1536]{1,0:T(8,128)(2,1)S(1)} %get-tuple-element.141), channel_id=1, source_target_pairs={{0,16},{2,18},{4,20},{6,22},{8,24},{10,26},{12,28},{14,30},{16,0},... | collective-permute-start | bytes 589832 | tf_op jit(solution)/shard_map/ppermute | solution.py:283
  (7 other events, 64.3 us)

commit v15 on v12

--- a/solution.py
+++ b/solution.py
@@ -377,6 +377,7 @@
     a1, b1, a2, b2, a3, b3, a4, b4 = spread(*first_one, *second_one)
     pieces_one = [a3, a4, b3, b4, a1, a2, b1, b2]
     a1, b1, a2, b2, a3, b3, a4, b4 = spread(*first_two, *second_two)
+    pieces_one, a3, b3 = lax.optimization_barrier((pieces_one, a3, b3))
     pieces = [pieces_one, [a4, b4, a3, b3, a2, b2, a1, b1]]
 
     rows = 8 * tok
@@ -419,13 +420,12 @@
             2 * width * ff + 8 * rows * width,
         )
 
-    total_one = own_total(pieces[0])
+    total_one, total_two = own_total(pieces[0]), own_total(pieces[1])
     down_last, far[1] = lax.optimization_barrier((down_last, far[1]))
     by_last = swap(down_last, Z_LOW)
-    both_by, total_one, pieces = lax.optimization_barrier((both_by, total_one, pieces))
+    both_by, total_one, total_two = lax.optimization_barrier((both_by, total_one, total_two))
     twin_first = swap_core(by_first)
     both_twin = swap_core(both_by)
-    total_two = own_total(pieces[1])
     hidden_one, hidden_two = beside_hidden(pieces[0]), beside_hidden(pieces[1])
     by_last, twin_first, total_two, hidden_one, hidden_two = lax.optimization_barrier(
         (by_last, twin_first, total_two, hidden_one, hidden_two)

time: 120 us -> 120 us (level)
    ppermute x29, waiting for transfers between devices: 58.1 us -> 56.2 us  [swap(): lax.ppermute(block, 'expert', [(i, i ^ distance) for i in range(count)])]
    ppermute x5, waiting for transfers between devices: 1.73 us -> 3.58 us  [swap_core(): return lax.ppermute(block, 'tensor', [(0, 1), (1, 0)])]
  transfers between devices with their start and end apart: 34 -> 34, of which waited for: 17 -> 18; matrix products, arithmetic and copies ran while one was open for 0% -> 0% of each run, Pallas kernels for 12% -> 12%
where the time goes in v15:
time: 120 us
  waiting for transfers between devices  59.8 us (50%)
  starting transfers between devices  40.3 us (34%)
  Pallas kernels  18.9 us (16%)
    ppermute x29, waiting for transfers between devices, swap(): lax.ppermute(block, 'expert', [(i, i ^ distance) for i in range(count)])  56.2 us
    ppermute x29, starting transfers between devices, swap(): lax.ppermute(block, 'expert', [(i, i ^ distance) for i in range(count)])  39.4 us
    pallas_call x16, Pallas kernels, call(): pl.pallas_call(body, out_shape=outs, in_specs=specs or [smem if x.ndim ==...  18.9 us
    ppermute x5, waiting for transfers between devices, swap_core(): return lax.ppermute(block, 'tensor', [(0, 1), (1, 0)])  3.58 us
  transfers between devices with their start and end apart: 34, of which 18 were waited for; matrix products, arithmetic and copies ran while one was open for 0% of the time, Pallas kernels for 12%

profile of v15, /device:TPU:0, one launch (start us, length us, event | category | flops | bytes accessed | tf_op | source)
XLA Modules:
  0.0 120.1 jit_solution(1787177708897817143)
XLA Ops:
  0.7 3.2 %shard_map.131 = (bf16[768,1024]{1,0:T(8,128)(2,1)}, bf16[256,768]{1,0:T(8,128)(2,1)}, bf16[256,768]{1,0:T(8,128)(2,1)}) custom-call(bf16[768,512]{1,0:T(8,128)(2,1)} %bitcast.15, bf16[768,512]{1,0:T(8,128)(2,1)} %bitcast.16, bf16[512,768]{1,0:T(8,128)(2,1)} %bitcast.7), custom_call_target="tpu_custom_call" | custom-call | bytes 4718592 | tf_op jit(solution)/shard_map/pallas_call | solution.py:86
  6.0 4.1 %collective-permute-start.1 = (bf16[64,1664]{1,0:T(8,128)(2,1)S(1)}, bf16[64,1664]{1,0:T(8,128)(2,1)S(1)}, u32[]{:S(2)}, u32[]{:S(2)}) collective-permute-start(bf16[64,1664]{1,0:T(8,128)(2,1)S(1)} %get-tuple-element.71), channel_id=1, source_target_pairs={{0,16},{2,18},{4,20},{6,22},{8,24},{10,26},{12,28},{14,30},{16,0},... | collective-permute-start | bytes 638984 | tf_op jit(solution)/shard_map/ppermute | solution.py:273
  10.0 1.6 %collective-permute-start.6 = (bf16[256,768]{1,0:T(8,128)(2,1)}, bf16[256,768]{1,0:T(8,128)(2,1)S(1)}, u32[]{:S(2)}, u32[]{:S(2)}) collective-permute-start(bf16[256,768]{1,0:T(8,128)(2,1)} %get-tuple-element.74), channel_id=1, source_target_pairs={{0,8},{2,10},{4,12},{6,14},{8,0},{10,2},{12,4},{14,6},{16,24},{18,... | collective-permute-start | bytes 1179656 | tf_op jit(solution)/shard_map/ppermute | solution.py:273
  12.0 8.8 %collective-permute-done.1 = bf16[64,1664]{1,0:T(8,128)(2,1)S(1)} collective-permute-done((bf16[64,1664]{1,0:T(8,128)(2,1)S(1)}, bf16[64,1664]{1,0:T(8,128)(2,1)S(1)}, u32[]{:S(2)}, u32[]{:S(2)}) %collective-permute-start.1) | collective-permute-done | bytes 213024 | tf_op jit(solution)/shard_map/ppermute | solution.py:273
  20.8 2.0 %collective-permute-start.5 = (bf16[64,1664]{1,0:T(8,128)(2,1)S(1)}, bf16[64,1664]{1,0:T(8,128)(2,1)S(1)}, u32[]{:S(2)}, u32[]{:S(2)}) collective-permute-start(bf16[64,1664]{1,0:T(8,128)(2,1)S(1)} %pad_maximum_fusion.1.refs_6_), channel_id=1, source_target_pairs={{0,4},{2,6},{4,0},{6,2},{8,12},{10,14},{12,8},{14,10},{16,20},{18,... | collective-permute-start | bytes 638984 | tf_op jit(solution)/shard_map/ppermute | solution.py:273
  22.8 1.6 %collective-permute-start.4 = (bf16[64,1664]{1,0:T(8,128)(2,1)S(1)}, bf16[64,1664]{1,0:T(8,128)(2,1)S(1)}, u32[]{:S(2)}, u32[]{:S(2)}) collective-permute-start(bf16[64,1664]{1,0:T(8,128)(2,1)S(1)} %pad_maximum_fusion.refs_4_), channel_id=1, source_target_pairs={{0,2},{2,0},{4,6},{6,4},{8,10},{10,8},{12,14},{14,12},{16,18},{18,... | collective-permute-start | bytes 638984 | tf_op jit(solution)/shard_map/ppermute | solution.py:273
  24.4 4.4 %collective-permute-done = bf16[64,1664]{1,0:T(8,128)(2,1)S(1)} collective-permute-done((bf16[64,1664]{1,0:T(8,128)(2,1)S(1)}, bf16[64,1664]{1,0:T(8,128)(2,1)S(1)}, u32[]{:S(2)}, u32[]{:S(2)}) %collective-permute-start) | collective-permute-done | bytes 213024 | tf_op jit(solution)/shard_map/ppermute | solution.py:273
  30.3 1.6 %collective-permute-start.10 = (bf16[64,1664]{1,0:T(8,128)(2,1)S(1)}, bf16[64,1664]{1,0:T(8,128)(2,1)S(1)}, u32[]{:S(2)}, u32[]{:S(2)}) collective-permute-start(bf16[64,1664]{1,0:T(8,128)(2,1)S(1)} %pad_maximum_fusion.refs_4_), channel_id=1, source_target_pairs={{0,4},{2,6},{4,0},{6,2},{8,12},{10,14},{12,8},{14,10},{16,20},{18,... | collective-permute-start | bytes 638984 | tf_op jit(solution)/shard_map/ppermute | solution.py:273
  32.4 1.6 %collective-permute-start.15 = (bf16[64,1664]{1,0:T(8,128)(2,1)S(1)}, bf16[64,1664]{1,0:T(8,128)(2,1)S(1)}, u32[]{:S(2)}, u32[]{:S(2)}) collective-permute-start(bf16[64,1664]{1,0:T(8,128)(2,1)S(1)} %pad_maximum_fusion.3.refs_7_), channel_id=1, source_target_pairs={{0,2},{2,0},{4,6},{6,4},{8,10},{10,8},{12,14},{14,12},{16,18},{18,... | collective-permute-start | bytes 638984 | tf_op jit(solution)/shard_map/ppermute | solution.py:273
  34.0 2.6 %collective-permute-done.12.refs_2_ = bf16[64,1664]{1,0:T(8,128)(2,1)S(1)} collective-permute-done((bf16[64,1664]{1,0:T(8,128)(2,1)S(1)}, bf16[64,1664]{1,0:T(8,128)(2,1)S(1)}, u32[]{:S(2)}, u32[]{:S(2)}) %collective-permute-start.12) | collective-permute-done | bytes 213024 | tf_op jit(solution)/shard_map/ppermute | solution.py:273
  36.6 1.8 %collective-permute-start.16 = (bf16[64,1664]{1,0:T(8,128)(2,1)S(1)}, bf16[64,1664]{1,0:T(8,128)(2,1)S(1)}, u32[]{:S(2)}, u32[]{:S(2)}) collective-permute-start(bf16[64,1664]{1,0:T(8,128)(2,1)S(1)} %pad_maximum_fusion.2.refs_6_), channel_id=1, source_target_pairs={{0,2},{2,0},{4,6},{6,4},{8,10},{10,8},{12,14},{14,12},{16,18},{18,... | collective-permute-start | bytes 638984 | tf_op jit(solution)/shard_map/ppermute | solution.py:273
  38.4 1.6 %collective-permute-start.18 = (bf16[64,1664]{1,0:T(8,128)(2,1)S(1)}, bf16[64,1664]{1,0:T(8,128)(2,1)S(1)}, u32[]{:S(2)}, u32[]{:S(2)}) collective-permute-start(bf16[64,1664]{1,0:T(8,128)(2,1)S(1)} %pad_maximum_fusion.3.refs_7_), channel_id=1, source_target_pairs={{0,4},{2,6},{4,0},{6,2},{8,12},{10,14},{12,8},{14,10},{16,20},{18,... | collective-permute-start | bytes 638984 | tf_op jit(solution)/shard_map/ppermute | solution.py:273
  40.0 3.0 %collective-permute-done.14.refs_2_ = bf16[64,1664]{1,0:T(8,128)(2,1)S(1)} collective-permute-done((bf16[64,1664]{1,0:T(8,128)(2,1)S(1)}, bf16[64,1664]{1,0:T(8,128)(2,1)S(1)}, u32[]{:S(2)}, u32[]{:S(2)}) %collective-permute-start.14) | collective-permute-done | bytes 213024 | tf_op jit(solution)/shard_map/ppermute | solution.py:273
  43.0 1.6 %collective-permute-start.11 = (bf16[64,1664]{1,0:T(8,128)(2,1)S(1)}, bf16[64,1664]{1,0:T(8,128)(2,1)S(1)}, u32[]{:S(2)}, u32[]{:S(2)}) collective-permute-start(bf16[64,1664]{1,0:T(8,128)(2,1)S(1)} %collective-permute-done.4.refs_5_), channel_id=1, source_target_pairs={{0,4},{2,6},{4,0},{6,2},{8,12},{10,14},{12,8},{14,10},{16,20},{18,... | collective-permute-start | bytes 638984 | tf_op jit(solution)/shard_map/ppermute | solution.py:273
  47.6 1.5 %collective-permute-start.19 = (bf16[64,1664]{1,0:T(8,128)(2,1)S(1)}, bf16[64,1664]{1,0:T(8,128)(2,1)S(1)}, u32[]{:S(2)}, u32[]{:S(2)}) collective-permute-start(bf16[64,1664]{1,0:T(8,128)(2,1)S(1)} %collective-permute-done.18.refs_5_), channel_id=1, source_target_pairs={{0,2},{2,0},{4,6},{6,4},{8,10},{10,8},{12,14},{14,12},{16,18},{18,... | collective-permute-start | bytes 638984 | tf_op jit(solution)/shard_map/ppermute | solution.py:273
  49.1 2.4 %collective-permute-done.11.refs_1_ = bf16[64,1664]{1,0:T(8,128)(2,1)S(1)} collective-permute-done((bf16[64,1664]{1,0:T(8,128)(2,1)S(1)}, bf16[64,1664]{1,0:T(8,128)(2,1)S(1)}, u32[]{:S(2)}, u32[]{:S(2)}) %collective-permute-start.11) | collective-permute-done | bytes 213024 | tf_op jit(solution)/shard_map/ppermute | solution.py:273
  51.5 3.1 %shard_map.133.total_ref = f32[512,1536]{1,0:T(8,128)S(1)} custom-call(bf16[64,1664]{1,0:T(8,128)(2,1)S(1)} %collective-permute-done.10.refs_0_, bf16[64,1664]{1,0:T(8,128)(2,1)S(1)} %collective-permute-done.11.refs_1_, bf16[64,1664]{1,0:T(8,128)(2,1)S(1)} %collective-permute-done.12.refs_2_, bf16[64,1664]{1,0:T(8,128)(2,1)S(1)} %collective-permute-done.13.refs_3_, ...), custom_call_target="tpu_custom_call" | custom-call | bytes 9437184 | tf_op jit(solution)/shard_map/pallas_call | solution.py:86
  54.7 3.1 %shard_map.134.total_ref = f32[512,1536]{1,0:T(8,128)S(1)} custom-call(bf16[64,1664]{1,0:T(8,128)(2,1)S(1)} %collective-permute-done.17.refs_0_, bf16[64,1664]{1,0:T(8,128)(2,1)S(1)} %collective-permute-done.19.refs_1_, bf16[64,1664]{1,0:T(8,128)(2,1)S(1)} %collective-permute-done.14.refs_2_, bf16[64,1664]{1,0:T(8,128)(2,1)S(1)} %collective-permute-done.15.refs_3_, ...), custom_call_target="tpu_custom_call" | custom-call | bytes 9437184 | tf_op jit(solution)/shard_map/pallas_call | solution.py:86
  57.8 4.9 %collective-permute-done.9.refs_8_ = bf16[768,1024]{1,0:T(8,128)(2,1)S(1)} collective-permute-done((bf16[768,1024]{1,0:T(8,128)(2,1)S(1)}, bf16[768,1024]{1,0:T(8,128)(2,1)S(1)}, u32[]{:S(2)}, u32[]{:S(2)}) %collective-permute-start.9) | collective-permute-done | bytes 1572896 | tf_op jit(solution)/shard_map/ppermute | solution.py:273
  64.3 1.9 %collective-permute-done.20.refs_9_ = bf16[768,1024]{1,0:T(8,128)(2,1)S(1)} collective-permute-done((bf16[768,1024]{1,0:T(8,128)(2,1)S(1)}, bf16[768,1024]{1,0:T(8,128)(2,1)S(1)}, u32[]{:S(2)}, u32[]{:S(2)}) %collective-permute-start.20) | collective-permute-done | bytes 1572896 | tf_op jit(solution)/shard_map/ppermute | solution.py:277
  66.2 2.1 %shard_map.136 = (bf16[512,512]{1,0:T(8,128)(2,1)S(1)}, f32[512,128]{1,0:T(8,128)S(1)}) custom-call(bf16[64,1664]{1,0:T(8,128)(2,1)S(1)} %collective-permute-done.17.refs_0_, bf16[64,1664]{1,0:T(8,128)(2,1)S(1)} %collective-permute-done.19.refs_1_, bf16[64,1664]{1,0:T(8,128)(2,1)S(1)} %collective-permute-done.14.refs_2_, ...), custom_call_target="tpu_custom_call" | custom-call | flops 1610612736 | bytes 4718592 | tf_op jit(solution)/shard_map/pallas_call | solution.py:86
  68.3 2.1 %shard_map.135 = (bf16[512,512]{1,0:T(8,128)(2,1)S(1)}, f32[512,128]{1,0:T(8,128)S(1)}) custom-call(bf16[64,1664]{1,0:T(8,128)(2,1)S(1)} %collective-permute-done.10.refs_0_, bf16[64,1664]{1,0:T(8,128)(2,1)S(1)} %collective-permute-done.11.refs_1_, bf16[64,1664]{1,0:T(8,128)(2,1)S(1)} %collective-permute-done.12.refs_2_, ...), custom_call_target="tpu_custom_call" | custom-call | flops 1610612736 | bytes 4718592 | tf_op jit(solution)/shard_map/pallas_call | solution.py:86
  70.5 3.8 %collective-permute-done.7.last_a = bf16[256,768]{1,0:T(8,128)(2,1)S(1)} collective-permute-done((bf16[256,768]{1,0:T(8,128)(2,1)S(1)}, bf16[256,768]{1,0:T(8,128)(2,1)S(1)}, u32[]{:S(2)}, u32[]{:S(2)}) %collective-permute-start.7) | collective-permute-done | bytes 393248 | tf_op jit(solution)/shard_map/ppermute | solution.py:273
  74.3 1.7 %collective-permute-done.21.last_b = bf16[256,768]{1,0:T(8,128)(2,1)S(1)} collective-permute-done((bf16[256,768]{1,0:T(8,128)(2,1)S(1)}, bf16[256,768]{1,0:T(8,128)(2,1)S(1)}, u32[]{:S(2)}, u32[]{:S(2)}) %collective-permute-start.21) | collective-permute-done | bytes 393248 | tf_op jit(solution)/shard_map/ppermute | solution.py:277
  77.0 1.6 %collective-permute-start.23 = (bf16[128,1536]{1,0:T(8,128)(2,1)S(1)}, bf16[128,1536]{1,0:T(8,128)(2,1)S(1)}, u32[]{:S(2)}, u32[]{:S(2)}) collective-permute-start(bf16[128,1536]{1,0:T(8,128)(2,1)S(1)} %get-tuple-element.109), channel_id=1, source_target_pairs={{0,2},{2,0},{4,6},{6,4},{8,10},{10,8},{12,14},{14,12},{16,18},{18,... | collective-permute-start | bytes 1179656 | tf_op jit(solution)/shard_map/ppermute | solution.py:273
  82.2 6.8 %collective-permute-done.23.got_ref = bf16[128,1536]{1,0:T(8,128)(2,1)S(1)} collective-permute-done((bf16[128,1536]{1,0:T(8,128)(2,1)S(1)}, bf16[128,1536]{1,0:T(8,128)(2,1)S(1)}, u32[]{:S(2)}, u32[]{:S(2)}) %collective-permute-start.23) | collective-permute-done | bytes 393248 | tf_op jit(solution)/shard_map/ppermute | solution.py:273
  91.3 1.6 %collective-permute-start.25 = (bf16[64,1536]{1,0:T(8,128)(2,1)S(1)}, bf16[64,1536]{1,0:T(8,128)(2,1)S(1)}, u32[]{:S(2)}, u32[]{:S(2)}) collective-permute-start(bf16[64,1536]{1,0:T(8,128)(2,1)S(1)} %get-tuple-element.120), channel_id=1, source_target_pairs={{0,4},{2,6},{4,0},{6,2},{8,12},{10,14},{12,8},{14,10},{16,20},{18,... | collective-permute-start | bytes 589832 | tf_op jit(solution)/shard_map/ppermute | solution.py:273
  93.3 1.6 %collective-permute-start.30 = (bf16[64,1536]{1,0:T(8,128)(2,1)S(1)}, bf16[64,1536]{1,0:T(8,128)(2,1)S(1)}, u32[]{:S(2)}, u32[]{:S(2)}) collective-permute-start(bf16[64,1536]{1,0:T(8,128)(2,1)S(1)} %shard_map.143), channel_id=1, source_target_pairs={{0,4},{2,6},{4,0},{6,2},{8,12},{10,14},{12,8},{14,10},{16,20},{18,... | collective-permute-start | bytes 589832 | tf_op jit(solution)/shard_map/ppermute | solution.py:273
  95.0 1.6 %collective-permute-start.28 = (bf16[64,1536]{1,0:T(8,128)(2,1)S(1)}, bf16[64,1536]{1,0:T(8,128)(2,1)S(1)}, u32[]{:S(2)}, u32[]{:S(2)}) collective-permute-start(bf16[64,1536]{1,0:T(8,128)(2,1)S(1)} %shard_map.142), channel_id=1, source_target_pairs={{0,2},{2,0},{4,6},{6,4},{8,10},{10,8},{12,14},{14,12},{16,18},{18,... | collective-permute-start | bytes 589832 | tf_op jit(solution)/shard_map/ppermute | solution.py:273
  97.4 1.6 %collective-permute-done.25.got_b = bf16[64,1536]{1,0:T(8,128)(2,1)S(1)} collective-permute-done((bf16[64,1536]{1,0:T(8,128)(2,1)S(1)}, bf16[64,1536]{1,0:T(8,128)(2,1)S(1)}, u32[]{:S(2)}, u32[]{:S(2)}) %collective-permute-start.25) | collective-permute-done | bytes 196640 | tf_op jit(solution)/shard_map/ppermute | solution.py:273
  103.6 5.4 %collective-permute-done.26.got_ref = bf16[64,1536]{1,0:T(8,128)(2,1)S(1)} collective-permute-done((bf16[64,1536]{1,0:T(8,128)(2,1)S(1)}, bf16[64,1536]{1,0:T(8,128)(2,1)S(1)}, u32[]{:S(2)}, u32[]{:S(2)}) %collective-permute-start.26) | collective-permute-done | bytes 196640 | tf_op jit(solution)/shard_map/ppermute | solution.py:273
  110.3 9.1 %collective-permute-done.33.got_ref = bf16[64,1536]{1,0:T(8,128)(2,1)S(1)} collective-permute-done((bf16[64,1536]{1,0:T(8,128)(2,1)S(1)}, bf16[64,1536]{1,0:T(8,128)(2,1)S(1)}, u32[]{:S(2)}, u32[]{:S(2)}) %collective-permute-start.33) | collective-permute-done | bytes 196640 | tf_op jit(solution)/shard_map/ppermute | solution.py:273
  (83 shorter events, 23.9 us)
Async XLA Ops:
  3.9 16.9 %collective-permute-start.2 = (bf16[768,1024]{1,0:T(8,128)(2,1)}, bf16[768,1024]{1,0:T(8,128)(2,1)S(1)}, u32[]{:S(2)}, u32[]{:S(2)}) collective-permute-start(bf16[768,1024]{1,0:T(8,128)(2,1)} %get-tuple-element.78.refs_8_), channel_id=1, source_target_pairs={{0,1},{1,0},{2,3},{3,2},{4,5},{5,4},{6,7},{7,6},{8,9},{9,8},{10,11... | collective-permute-start | bytes 4718600 | tf_op jit(solution)/shard_map/ppermute | solution.py:277
  4.4 16.3 %collective-permute-start.3 = (bf16[512,768]{1,0:T(8,128)(2,1)S(1)}, bf16[512,768]{1,0:T(8,128)(2,1)S(1)}, u32[]{:S(2)}, u32[]{:S(2)}) collective-permute-start(bf16[512,768]{1,0:T(8,128)(2,1)S(1)} %bitcast.8), channel_id=1, source_target_pairs={{0,1},{1,0},{2,3},{3,2},{4,5},{5,4},{6,7},{7,6},{8,9},{9,8},{10,11... | collective-permute-start | bytes 2359304 | tf_op jit(solution)/shard_map/ppermute | solution.py:277
  6.0 14.8 %collective-permute-start.1 = (bf16[64,1664]{1,0:T(8,128)(2,1)S(1)}, bf16[64,1664]{1,0:T(8,128)(2,1)S(1)}, u32[]{:S(2)}, u32[]{:S(2)}) collective-permute-start(bf16[64,1664]{1,0:T(8,128)(2,1)S(1)} %get-tuple-element.71), channel_id=1, source_target_pairs={{0,16},{2,18},{4,20},{6,22},{8,24},{10,26},{12,28},{14,30},{16,0},... | collective-permute-start | bytes 638984 | tf_op jit(solution)/shard_map/ppermute | solution.py:273
  10.0 20.2 %collective-permute-start.6 = (bf16[256,768]{1,0:T(8,128)(2,1)}, bf16[256,768]{1,0:T(8,128)(2,1)S(1)}, u32[]{:S(2)}, u32[]{:S(2)}) collective-permute-start(bf16[256,768]{1,0:T(8,128)(2,1)} %get-tuple-element.74), channel_id=1, source_target_pairs={{0,8},{2,10},{4,12},{6,14},{8,0},{10,2},{12,4},{14,6},{16,24},{18,... | collective-permute-start | bytes 1179656 | tf_op jit(solution)/shard_map/ppermute | solution.py:273
  11.6 17.1 %collective-permute-start = (bf16[64,1664]{1,0:T(8,128)(2,1)S(1)}, bf16[64,1664]{1,0:T(8,128)(2,1)S(1)}, u32[]{:S(2)}, u32[]{:S(2)}) collective-permute-start(bf16[64,1664]{1,0:T(8,128)(2,1)S(1)} %get-tuple-element.70), channel_id=1, source_target_pairs={{0,16},{2,18},{4,20},{6,22},{8,24},{10,26},{12,28},{14,30},{16,0},... | collective-permute-start | bytes 638984 | tf_op jit(solution)/shard_map/ppermute | solution.py:273
  20.8 11.0 %collective-permute-start.5 = (bf16[64,1664]{1,0:T(8,128)(2,1)S(1)}, bf16[64,1664]{1,0:T(8,128)(2,1)S(1)}, u32[]{:S(2)}, u32[]{:S(2)}) collective-permute-start(bf16[64,1664]{1,0:T(8,128)(2,1)S(1)} %pad_maximum_fusion.1.refs_6_), channel_id=1, source_target_pairs={{0,4},{2,6},{4,0},{6,2},{8,12},{10,14},{12,8},{14,10},{16,20},{18,... | collective-permute-start | bytes 638984 | tf_op jit(solution)/shard_map/ppermute | solution.py:273
  22.8 40.0 %collective-permute-start.9 = (bf16[768,1024]{1,0:T(8,128)(2,1)S(1)}, bf16[768,1024]{1,0:T(8,128)(2,1)S(1)}, u32[]{:S(2)}, u32[]{:S(2)}) collective-permute-start(bf16[768,1024]{1,0:T(8,128)(2,1)S(1)} %copy-done.1), channel_id=1, source_target_pairs={{0,8},{2,10},{4,12},{6,14},{8,0},{10,2},{12,4},{14,6},{16,24},{18,... | collective-permute-start | bytes 4718600 | tf_op jit(solution)/shard_map/ppermute | solution.py:273
  22.8 9.0 %collective-permute-start.4 = (bf16[64,1664]{1,0:T(8,128)(2,1)S(1)}, bf16[64,1664]{1,0:T(8,128)(2,1)S(1)}, u32[]{:S(2)}, u32[]{:S(2)}) collective-permute-start(bf16[64,1664]{1,0:T(8,128)(2,1)S(1)} %pad_maximum_fusion.refs_4_), channel_id=1, source_target_pairs={{0,2},{2,0},{4,6},{6,4},{8,10},{10,8},{12,14},{14,12},{16,18},{18,... | collective-permute-start | bytes 638984 | tf_op jit(solution)/shard_map/ppermute | solution.py:273
  28.8 7.8 %collective-permute-start.12 = (bf16[64,1664]{1,0:T(8,128)(2,1)S(1)}, bf16[64,1664]{1,0:T(8,128)(2,1)S(1)}, u32[]{:S(2)}, u32[]{:S(2)}) collective-permute-start(bf16[64,1664]{1,0:T(8,128)(2,1)S(1)} %pad_maximum_fusion.1.refs_6_), channel_id=1, source_target_pairs={{0,2},{2,0},{4,6},{6,4},{8,10},{10,8},{12,14},{14,12},{16,18},{18,... | collective-permute-start | bytes 638984 | tf_op jit(solution)/shard_map/ppermute | solution.py:273
  30.3 8.2 %collective-permute-start.10 = (bf16[64,1664]{1,0:T(8,128)(2,1)S(1)}, bf16[64,1664]{1,0:T(8,128)(2,1)S(1)}, u32[]{:S(2)}, u32[]{:S(2)}) collective-permute-start(bf16[64,1664]{1,0:T(8,128)(2,1)S(1)} %pad_maximum_fusion.refs_4_), channel_id=1, source_target_pairs={{0,4},{2,6},{4,0},{6,2},{8,12},{10,14},{12,8},{14,10},{16,20},{18,... | collective-permute-start | bytes 638984 | tf_op jit(solution)/shard_map/ppermute | solution.py:273
  31.9 11.1 %collective-permute-start.14 = (bf16[64,1664]{1,0:T(8,128)(2,1)S(1)}, bf16[64,1664]{1,0:T(8,128)(2,1)S(1)}, u32[]{:S(2)}, u32[]{:S(2)}) collective-permute-start(bf16[64,1664]{1,0:T(8,128)(2,1)S(1)} %pad_maximum_fusion.2.refs_6_), channel_id=1, source_target_pairs={{0,4},{2,6},{4,0},{6,2},{8,12},{10,14},{12,8},{14,10},{16,20},{18,... | collective-permute-start | bytes 638984 | tf_op jit(solution)/shard_map/ppermute | solution.py:273
  32.4 12.1 %collective-permute-start.15 = (bf16[64,1664]{1,0:T(8,128)(2,1)S(1)}, bf16[64,1664]{1,0:T(8,128)(2,1)S(1)}, u32[]{:S(2)}, u32[]{:S(2)}) collective-permute-start(bf16[64,1664]{1,0:T(8,128)(2,1)S(1)} %pad_maximum_fusion.3.refs_7_), channel_id=1, source_target_pairs={{0,2},{2,0},{4,6},{6,4},{8,10},{10,8},{12,14},{14,12},{16,18},{18,... | collective-permute-start | bytes 638984 | tf_op jit(solution)/shard_map/ppermute | solution.py:273
  36.6 9.5 %collective-permute-start.16 = (bf16[64,1664]{1,0:T(8,128)(2,1)S(1)}, bf16[64,1664]{1,0:T(8,128)(2,1)S(1)}, u32[]{:S(2)}, u32[]{:S(2)}) collective-permute-start(bf16[64,1664]{1,0:T(8,128)(2,1)S(1)} %pad_maximum_fusion.2.refs_6_), channel_id=1, source_target_pairs={{0,2},{2,0},{4,6},{6,4},{8,10},{10,8},{12,14},{14,12},{16,18},{18,... | collective-permute-start | bytes 638984 | tf_op jit(solution)/shard_map/ppermute | solution.py:273
  38.4 9.1 %collective-permute-start.18 = (bf16[64,1664]{1,0:T(8,128)(2,1)S(1)}, bf16[64,1664]{1,0:T(8,128)(2,1)S(1)}, u32[]{:S(2)}, u32[]{:S(2)}) collective-permute-start(bf16[64,1664]{1,0:T(8,128)(2,1)S(1)} %pad_maximum_fusion.3.refs_7_), channel_id=1, source_target_pairs={{0,4},{2,6},{4,0},{6,2},{8,12},{10,14},{12,8},{14,10},{16,20},{18,... | collective-permute-start | bytes 638984 | tf_op jit(solution)/shard_map/ppermute | solution.py:273
  43.0 8.5 %collective-permute-start.11 = (bf16[64,1664]{1,0:T(8,128)(2,1)S(1)}, bf16[64,1664]{1,0:T(8,128)(2,1)S(1)}, u32[]{:S(2)}, u32[]{:S(2)}) collective-permute-start(bf16[64,1664]{1,0:T(8,128)(2,1)S(1)} %collective-permute-done.4.refs_5_), channel_id=1, source_target_pairs={{0,4},{2,6},{4,0},{6,2},{8,12},{10,14},{12,8},{14,10},{16,20},{18,... | collective-permute-start | bytes 638984 | tf_op jit(solution)/shard_map/ppermute | solution.py:273
  44.6 6.9 %collective-permute-start.13 = (bf16[64,1664]{1,0:T(8,128)(2,1)S(1)}, bf16[64,1664]{1,0:T(8,128)(2,1)S(1)}, u32[]{:S(2)}, u32[]{:S(2)}) collective-permute-start(bf16[64,1664]{1,0:T(8,128)(2,1)S(1)} %collective-permute-done.5.refs_7_), channel_id=1, source_target_pairs={{0,2},{2,0},{4,6},{6,4},{8,10},{10,8},{12,14},{14,12},{16,18},{18,... | collective-permute-start | bytes 638984 | tf_op jit(solution)/shard_map/ppermute | solution.py:273
  46.1 8.6 %collective-permute-start.17 = (bf16[64,1664]{1,0:T(8,128)(2,1)S(1)}, bf16[64,1664]{1,0:T(8,128)(2,1)S(1)}, u32[]{:S(2)}, u32[]{:S(2)}) collective-permute-start(bf16[64,1664]{1,0:T(8,128)(2,1)S(1)} %collective-permute-done.16.refs_4_), channel_id=1, source_target_pairs={{0,4},{2,6},{4,0},{6,2},{8,12},{10,14},{12,8},{14,10},{16,20},{18,... | collective-permute-start | bytes 638984 | tf_op jit(solution)/shard_map/ppermute | solution.py:273
  47.6 7.1 %collective-permute-start.19 = (bf16[64,1664]{1,0:T(8,128)(2,1)S(1)}, bf16[64,1664]{1,0:T(8,128)(2,1)S(1)}, u32[]{:S(2)}, u32[]{:S(2)}) collective-permute-start(bf16[64,1664]{1,0:T(8,128)(2,1)S(1)} %collective-permute-done.18.refs_5_), channel_id=1, source_target_pairs={{0,2},{2,0},{4,6},{6,4},{8,10},{10,8},{12,14},{14,12},{16,18},{18,... | collective-permute-start | bytes 638984 | tf_op jit(solution)/shard_map/ppermute | solution.py:273
  62.8 11.5 %collective-permute-start.7 = (bf16[256,768]{1,0:T(8,128)(2,1)S(1)}, bf16[256,768]{1,0:T(8,128)(2,1)S(1)}, u32[]{:S(2)}, u32[]{:S(2)}) collective-permute-start(bf16[256,768]{1,0:T(8,128)(2,1)S(1)} %copy-done.11), channel_id=1, source_target_pairs={{0,8},{2,10},{4,12},{6,14},{8,0},{10,2},{12,4},{14,6},{16,24},{18,... | collective-permute-start | bytes 1179656 | tf_op jit(solution)/shard_map/ppermute | solution.py:273
  64.1 10.2 %collective-permute-start.8 = (bf16[256,768]{1,0:T(8,128)(2,1)S(1)}, bf16[256,768]{1,0:T(8,128)(2,1)S(1)}, u32[]{:S(2)}, u32[]{:S(2)}) collective-permute-start(bf16[256,768]{1,0:T(8,128)(2,1)S(1)} %collective-permute-done.6.first_a), channel_id=1, source_target_pairs={{0,1},{1,0},{2,3},{3,2},{4,5},{5,4},{6,7},{7,6},{8,9},{9,8},{10,11... | collective-permute-start | bytes 1179656 | tf_op jit(solution)/shard_map/ppermute | solution.py:277
  77.0 12.0 %collective-permute-start.23 = (bf16[128,1536]{1,0:T(8,128)(2,1)S(1)}, bf16[128,1536]{1,0:T(8,128)(2,1)S(1)}, u32[]{:S(2)}, u32[]{:S(2)}) collective-permute-start(bf16[128,1536]{1,0:T(8,128)(2,1)S(1)} %get-tuple-element.109), channel_id=1, source_target_pairs={{0,2},{2,0},{4,6},{6,4},{8,10},{10,8},{12,14},{14,12},{16,18},{18,... | collective-permute-start | bytes 1179656 | tf_op jit(solution)/shard_map/ppermute | solution.py:273
  78.6 12.0 %collective-permute-start.22 = (bf16[128,1536]{1,0:T(8,128)(2,1)S(1)}, bf16[128,1536]{1,0:T(8,128)(2,1)S(1)}, u32[]{:S(2)}, u32[]{:S(2)}) collective-permute-start(bf16[128,1536]{1,0:T(8,128)(2,1)S(1)} %get-tuple-element.105), channel_id=1, source_target_pairs={{0,4},{2,6},{4,0},{6,2},{8,12},{10,14},{12,8},{14,10},{16,20},{18,... | collective-permute-start | bytes 1179656 | tf_op jit(solution)/shard_map/ppermute | solution.py:273
  81.2 12.1 %collective-permute-start.29 = (bf16[64,1536]{1,0:T(8,128)(2,1)S(1)}, bf16[64,1536]{1,0:T(8,128)(2,1)S(1)}, u32[]{:S(2)}, u32[]{:S(2)}) collective-permute-start(bf16[64,1536]{1,0:T(8,128)(2,1)S(1)} %get-tuple-element.126), channel_id=1, source_target_pairs={{0,2},{2,0},{4,6},{6,4},{8,10},{10,8},{12,14},{14,12},{16,18},{18,... | collective-permute-start | bytes 589832 | tf_op jit(solution)/shard_map/ppermute | solution.py:273
  81.8 13.2 %collective-permute-start.27 = (bf16[64,1536]{1,0:T(8,128)(2,1)S(1)}, bf16[64,1536]{1,0:T(8,128)(2,1)S(1)}, u32[]{:S(2)}, u32[]{:S(2)}) collective-permute-start(bf16[64,1536]{1,0:T(8,128)(2,1)S(1)} %get-tuple-element.124), channel_id=1, source_target_pairs={{0,4},{2,6},{4,0},{6,2},{8,12},{10,14},{12,8},{14,10},{16,20},{18,... | collective-permute-start | bytes 589832 | tf_op jit(solution)/shard_map/ppermute | solution.py:273
  90.7 6.7 %collective-permute-start.24 = (bf16[64,1536]{1,0:T(8,128)(2,1)S(1)}, bf16[64,1536]{1,0:T(8,128)(2,1)S(1)}, u32[]{:S(2)}, u32[]{:S(2)}) collective-permute-start(bf16[64,1536]{1,0:T(8,128)(2,1)S(1)} %get-tuple-element.118), channel_id=1, source_target_pairs={{0,2},{2,0},{4,6},{6,4},{8,10},{10,8},{12,14},{14,12},{16,18},{18,... | collective-permute-start | bytes 589832 | tf_op jit(solution)/shard_map/ppermute | solution.py:273
  91.3 7.8 %collective-permute-start.25 = (bf16[64,1536]{1,0:T(8,128)(2,1)S(1)}, bf16[64,1536]{1,0:T(8,128)(2,1)S(1)}, u32[]{:S(2)}, u32[]{:S(2)}) collective-permute-start(bf16[64,1536]{1,0:T(8,128)(2,1)S(1)} %get-tuple-element.120), channel_id=1, source_target_pairs={{0,4},{2,6},{4,0},{6,2},{8,12},{10,14},{12,8},{14,10},{16,20},{18,... | collective-permute-start | bytes 589832 | tf_op jit(solution)/shard_map/ppermute | solution.py:273
  93.3 10.2 %collective-permute-start.30 = (bf16[64,1536]{1,0:T(8,128)(2,1)S(1)}, bf16[64,1536]{1,0:T(8,128)(2,1)S(1)}, u32[]{:S(2)}, u32[]{:S(2)}) collective-permute-start(bf16[64,1536]{1,0:T(8,128)(2,1)S(1)} %shard_map.143), channel_id=1, source_target_pairs={{0,4},{2,6},{4,0},{6,2},{8,12},{10,14},{12,8},{14,10},{16,20},{18,... | collective-permute-start | bytes 589832 | tf_op jit(solution)/shard_map/ppermute | solution.py:273
  95.0 8.6 %collective-permute-start.28 = (bf16[64,1536]{1,0:T(8,128)(2,1)S(1)}, bf16[64,1536]{1,0:T(8,128)(2,1)S(1)}, u32[]{:S(2)}, u32[]{:S(2)}) collective-permute-start(bf16[64,1536]{1,0:T(8,128)(2,1)S(1)} %shard_map.142), channel_id=1, source_target_pairs={{0,2},{2,0},{4,6},{6,4},{8,10},{10,8},{12,14},{14,12},{16,18},{18,... | collective-permute-start | bytes 589832 | tf_op jit(solution)/shard_map/ppermute | solution.py:273
  99.1 9.9 %collective-permute-start.26 = (bf16[64,1536]{1,0:T(8,128)(2,1)S(1)}, bf16[64,1536]{1,0:T(8,128)(2,1)S(1)}, u32[]{:S(2)}, u32[]{:S(2)}) collective-permute-start(bf16[64,1536]{1,0:T(8,128)(2,1)S(1)} %get-tuple-element.122), channel_id=1, source_target_pairs={{0,16},{2,18},{4,20},{6,22},{8,24},{10,26},{12,28},{14,30},{16,0},... | collective-permute-start | bytes 589832 | tf_op jit(solution)/shard_map/ppermute | solution.py:273
  100.6 8.4 %collective-permute-start.31 = (bf16[64,1536]{1,0:T(8,128)(2,1)S(1)}, bf16[64,1536]{1,0:T(8,128)(2,1)S(1)}, u32[]{:S(2)}, u32[]{:S(2)}) collective-permute-start(bf16[64,1536]{1,0:T(8,128)(2,1)S(1)} %get-tuple-element.129), channel_id=1, source_target_pairs={{0,4},{2,6},{4,0},{6,2},{8,12},{10,14},{12,8},{14,10},{16,20},{18,... | collective-permute-start | bytes 589832 | tf_op jit(solution)/shard_map/ppermute | solution.py:273
  102.1 6.9 %collective-permute-start.32 = (bf16[64,1536]{1,0:T(8,128)(2,1)S(1)}, bf16[64,1536]{1,0:T(8,128)(2,1)S(1)}, u32[]{:S(2)}, u32[]{:S(2)}) collective-permute-start(bf16[64,1536]{1,0:T(8,128)(2,1)S(1)} %get-tuple-element.132), channel_id=1, source_target_pairs={{0,2},{2,0},{4,6},{6,4},{8,10},{10,8},{12,14},{14,12},{16,18},{18,... | collective-permute-start | bytes 589832 | tf_op jit(solution)/shard_map/ppermute | solution.py:273
  109.1 10.3 %collective-permute-start.33 = (bf16[64,1536]{1,0:T(8,128)(2,1)S(1)}, bf16[64,1536]{1,0:T(8,128)(2,1)S(1)}, u32[]{:S(2)}, u32[]{:S(2)}) collective-permute-start(bf16[64,1536]{1,0:T(8,128)(2,1)S(1)} %get-tuple-element.135), channel_id=1, source_target_pairs={{0,16},{2,18},{4,20},{6,22},{8,24},{10,26},{12,28},{14,30},{16,0},... | collective-permute-start | bytes 589832 | tf_op jit(solution)/shard_map/ppermute | solution.py:273
  (14 other events, 70.6 us)
